TPU v7x, 512 devices: a whole 4x8x8 slice. The times are simulated.
512 devices in a mesh: dp: 32 (over z_hi, y, core), mp: 16 (over z_lo, x).
Axes of the slice: x: 4, y: 8, z: 8 (z_hi: 2, z_lo: 4; z = z_hi * 4 + z_lo), core: 2. Of those that a mesh axis runs over, the one named last changes fastest.
Arguments:
- teacher_in: bfloat16 [8192, 6144], P('dp', 'mp'), may hold values from -8 to 8
- teacher_gain: float32 [6144], P('mp'), may hold values from 0.5 to 1.5
- qkv_weight: bfloat16 [6144, 3, 4096], P('dp', None, 'mp'), may hold values from -5 to 5
- qk_gain: float32 [32, 128], P('mp'), may hold values from 0.5 to 5
- student_in: bfloat16 [8192, 1024], P('dp'), may hold values from -6 to 6
- student_gain: float32 [1024], replicated, may hold values from 0.25 to 1.75
- up_weight: bfloat16 [1024, 4096], P(None, 'mp'), may hold values from -0.1875 to 0.1875
- down_weight: bfloat16 [4096, 1024], P('mp'), may hold values from -0.09375 to 0.09375
- projector: bfloat16 [1024, 4096], P(None, 'mp'), may hold values from -0.1875 to 0.1875
Outputs:
- grad_up: bfloat16 [1024, 4096], P('dp', 'mp')
- grad_down: bfloat16 [4096, 1024], P('mp', 'dp')
- grad_projector: bfloat16 [1024, 4096], P('dp', 'mp')
All inputs are finite; a program needn't handle non-finite values.
Results may differ from a plain program's by a relative error of at most 0.022.
Values may be sent and summed in bfloat16 or wider, within the bound.
No kernel may reach another device: no remote copies, remote signals or barrier semaphores. Data moves between devices by JAX's collectives and lax.ppermute only.
A program may use at most 64 MiB of HBM per device.

v0:
```python
import math

import jax
import jax.numpy as jnp
from jax import lax
from jax.sharding import PartitionSpec as P

HEAD = 128
PATCH = 256


EPSILON = 1e-06


def normalize(values):
    row_mean = jnp.mean(values, axis=-1, keepdims=True)
    centered = values - row_mean
    row_var = jnp.mean(centered * centered, axis=-1, keepdims=True)
    return centered * lax.rsqrt(row_var + EPSILON)


def gelu_parts(pre_act):
    cdf_part = 0.5 * (1.0 + lax.erf(pre_act * 0.7071067811865476))
    density = jnp.exp(-0.5 * pre_act * pre_act) * 0.3989422804014327
    return (pre_act * cdf_part, cdf_part + pre_act * density)


def shards(
    teacher_in,
    teacher_gain,
    qkv_weight,
    qk_gain,
    student_in,
    student_gain,
    up_weight,
    down_weight,
    projector,
):
    tok_rows = teacher_in.shape[0]
    head_count = qk_gain.shape[0]
    local_width = head_count * HEAD
    gain_row = teacher_gain.reshape(1, -1)
    gathered, gain_all = (
        lax.all_gather(teacher_in, "mp", axis=1, tiled=True),
        lax.all_gather(gain_row.astype(jnp.bfloat16), "mp", axis=1, tiled=True).astype(
            gain_row.dtype
        ),
    )
    normed = (normalize(gathered.astype(jnp.float32)) * gain_all).astype(jnp.bfloat16)
    part_rows = lax.all_gather(qkv_weight, "dp", axis=0, tiled=True)
    span_rows = part_rows.shape[0]
    projected = jnp.dot(
        normed, part_rows.reshape(span_rows, 3 * local_width), preferred_element_type=jnp.float32
    )
    projected = projected.reshape(tok_rows, 3, head_count, HEAD)

    def head_norm(values):
        return (normalize(values) * qk_gain).astype(jnp.bfloat16)

    image_count = tok_rows // PATCH
    queries = head_norm(projected[:, 0]).reshape(image_count, PATCH, head_count, HEAD)
    keys_all = head_norm(projected[:, 1]).reshape(image_count, PATCH, head_count, HEAD)
    values_all = projected[:, 2].astype(jnp.bfloat16).reshape(image_count, PATCH, head_count, HEAD)
    scores = jnp.einsum(
        "iqhc,ikhc->ihqk", queries, keys_all, preferred_element_type=jnp.float32
    ) * HEAD ** (-0.5)
    attn = jax.nn.softmax(scores, axis=-1).astype(jnp.bfloat16)
    features = jnp.einsum("ihqk,ikhc->iqhc", attn, values_all, preferred_element_type=jnp.float32)
    features = features.reshape(tok_rows, local_width)
    total_width = local_width * lax.axis_size("mp")
    feat_mean = lax.psum(jnp.sum(features, axis=1), "mp") / total_width
    centered = features - feat_mean[:, None]
    feat_var = lax.psum(jnp.sum(centered * centered, axis=1), "mp") / total_width
    target = centered * lax.rsqrt(feat_var + EPSILON)[:, None]
    student_normed = (normalize(student_in.astype(jnp.float32)) * student_gain).astype(jnp.bfloat16)
    pre_act = jnp.dot(student_normed, up_weight, preferred_element_type=jnp.float32)
    gated, slope = gelu_parts(pre_act)
    activ = gated.astype(jnp.bfloat16)
    mlp_term = jnp.dot(activ, down_weight, preferred_element_type=jnp.float32)
    mlp_sum = lax.psum(mlp_term.astype(jnp.bfloat16), "mp").astype(jnp.float32)
    block_out = (student_in.astype(jnp.float32) + mlp_sum).astype(jnp.bfloat16)
    predicted = jnp.dot(block_out, projector, preferred_element_type=jnp.float32)
    loss_factor = 1.0 / math.sqrt(tok_rows * lax.axis_size("dp"))
    grad_pred = ((predicted - target) * loss_factor).astype(jnp.bfloat16)
    proj_term = jnp.einsum("tc,tf->cf", block_out, grad_pred, preferred_element_type=jnp.float32)
    block_term = jnp.einsum("tf,cf->tc", grad_pred, projector, preferred_element_type=jnp.float32)
    grad_block = lax.psum(block_term.astype(jnp.bfloat16), "mp")
    down_term = jnp.einsum("tf,tc->fc", activ, grad_block, preferred_element_type=jnp.float32)
    grad_act = jnp.einsum("tc,fc->tf", grad_block, down_weight, preferred_element_type=jnp.float32)
    grad_pre = (grad_act * slope).astype(jnp.bfloat16)
    up_term = jnp.einsum("tc,tf->cf", student_normed, grad_pre, preferred_element_type=jnp.float32)
    grad_up, grad_down, grad_projector = (
        lax.psum_scatter(
            up_term.astype(jnp.bfloat16), "dp", scatter_dimension=0, tiled=True
        ).astype(jnp.float32),
        lax.psum_scatter(
            down_term.astype(jnp.bfloat16), "dp", scatter_dimension=1, tiled=True
        ).astype(jnp.float32),
        lax.psum_scatter(
            proj_term.astype(jnp.bfloat16), "dp", scatter_dimension=0, tiled=True
        ).astype(jnp.float32),
    )
    return (
        grad_up.astype(jnp.bfloat16),
        grad_down.astype(jnp.bfloat16),
        grad_projector.astype(jnp.bfloat16),
    )


def solution(mesh):
    in_specs = (
        P("dp", "mp"),
        P("mp"),
        P("dp", None, "mp"),
        P("mp", None),
        P("dp", None),
        P(),
        P(None, "mp"),
        P("mp", None),
        P(None, "mp"),
    )
    out_specs = (P("dp", "mp"), P("mp", "dp"), P("dp", "mp"))
    return jax.shard_map(shards, mesh=mesh, in_specs=in_specs, out_specs=out_specs, check_vma=False)
```

profile of v0, /device:TPU:2, one launch (start us, length us, event | category | flops | bytes accessed | tf_op | source)
XLA Modules:
  0.0 967.8 jit_solution(2176426721089531205)
XLA Ops:
  8.0 0.7 all-gather.7.cloned.1.call-update
  8.7 1.2 convert_reduce_fusion.1
  9.9 1.3 fusion.19
  11.2 1.6 fusion.46
  12.8 1.1 convolution_convert_fusion.4
  14.7 42.7 %all-gather.1 = bf16[16,1,384]{2,1,0:T(2,128)(2,1)S(1)} all-gather(bf16[1,1,384]{2,1,0:T(2,128)(2,1)S(1)} %reshape.110), channel_id=2, replica_groups=mesh['dp'=32,'mp'=16] {'mp'}, dimensions={0}, use_global_device_ids=true | all-gather | bytes 13056 | tf_op jit(solution)/shard_map/all_gather | solution.py:45
  57.5 45.8 %all-gather.5.cloned.1.call-done = bf16[256,6144]{1,0:T(8,128)(2,1)} async-done(((bf16[256,384]{1,0:T(8,128)(2,1)}), bf16[256,6144]{1,0:T(8,128)(2,1)}) %all-gather.5.cloned.1.call-update) | async-done | bytes 3145744 | tf_op jit(solution)/shard_map/all_gather | solution.py:44
  103.3 2.4 convert_reduce_fusion
  105.7 2.9 fusion.3
  108.6 136.9 %all-gather.7.cloned.1.call-done = bf16[6144,3,256]{2,0,1:T(8,128)(2,1)} async-done(((bf16[192,3,256]{2,0,1:T(8,128)(2,1)}), bf16[6144,3,256]{2,0,1:T(8,128)(2,1)}) %all-gather.7.cloned.1.call-update) | async-done | bytes 9437200 | tf_op jit(solution)/shard_map/all_gather | solution.py:50
  245.5 12.7 %copy.21 = bf16[6144,3,256]{0,2,1:T(8,128)(2,1)} copy(bf16[6144,3,256]{2,0,1:T(8,128)(2,1)} %all-gather.7.cloned.1.call-done) | data formatting | bytes 18874368 | tf_op jit(solution)/shard_map/all_gather | solution.py:50
  258.2 6.6 fusion.7
  265.9 38.3 %psum.29 = f32[256]{0:T(256)S(1)} all-reduce(f32[256]{0:T(256)S(1)} %get-tuple-element.7), channel_id=1, replica_groups=mesh['dp'=32,'mp'=16] {'mp'}, use_global_device_ids=true, to_apply=%region_12.0 | all-reduce | flops 256 | bytes 2048 | tf_op jit(solution)/shard_map/psum | solution.py:71
  304.3 41.6 %psum.30 = f32[256]{0:T(256)S(1)} all-reduce(f32[256]{0:T(256)S(1)} %fusion.29), channel_id=1, replica_groups=mesh['dp'=32,'mp'=16] {'mp'}, use_global_device_ids=true, to_apply=%region_14.0 | all-reduce | flops 256 | bytes 2048 | tf_op jit(solution)/shard_map/psum | solution.py:73
  345.9 64.2 %all-reduce.3.cloned.1.call-done = bf16[256,1024]{1,0:T(8,128)(2,1)} async-done(((bf16[256,1024]{1,0:T(8,128)(2,1)}), bf16[256,1024]{1,0:T(8,128)(2,1)}) %all-reduce.3.cloned.1.call-update) | async-done | bytes 524304 | tf_op jit(solution)/shard_map/psum | solution.py:80
  410.1 1.4 fusion.18
  411.5 1.2 convolution_convert_fusion.3
  412.7 2.2 convolution_convert_fusion
  415.0 163.6 %all-reduce.5.cloned.1.call-done = bf16[256,1024]{1,0:T(8,128)(2,1)} async-done(((bf16[256,1024]{1,0:T(8,128)(2,1)}), bf16[256,1024]{1,0:T(8,128)(2,1)}) %all-reduce.5.cloned.1.call-update) | async-done | bytes 524304 | tf_op jit(solution)/shard_map/psum | solution.py:87
  578.6 2.7 convolution_convert_fusion.2
  581.4 2.2 convolution_convert_fusion.1
  583.7 124.1 %reduce-scatter.8.cloned.1.call-done = bf16[32,256]{1,0:T(8,128)(2,1)} async-done(((bf16[1024,256]{1,0:T(8,128)(2,1)}), bf16[32,256]{1,0:T(8,128)(2,1)}) %reduce-scatter.8.cloned.1.call-update) | async-done | bytes 16400 | tf_op jit(solution)/shard_map/reduce_scatter | solution.py:99
  707.8 126.8 %reduce-scatter.4.cloned.1.call-done = bf16[32,256]{1,0:T(8,128)(2,1)} async-done(((bf16[1024,256]{1,0:T(8,128)(2,1)}), bf16[32,256]{1,0:T(8,128)(2,1)}) %reduce-scatter.4.cloned.1.call-update) | async-done | bytes 16400 | tf_op jit(solution)/shard_map/reduce_scatter | solution.py:93
  834.6 126.3 %reduce-scatter.6.cloned.1.call-done = bf16[256,32]{0,1:T(8,128)(2,1)} async-done(((bf16[256,1024]{0,1:T(8,128)(2,1)}), bf16[256,32]{0,1:T(8,128)(2,1)}) %reduce-scatter.6.cloned.1.call-update) | async-done | bytes 16400 | tf_op jit(solution)/shard_map/reduce_scatter | solution.py:96
  (42 shorter events, 3.0 us)
Async XLA Ops:
  7.2 5.7 copy-start
  7.2 96.1 %all-gather.5.cloned.1.call-start = ((), (), s32[]{:S(2)}) async-start(), calls=%async_computation.4 | async-start | bytes 3342336 | tf_op jit(solution)/shard_map/all_gather | solution.py:44
  7.9 237.6 %all-gather.7.cloned.1.call-start = ((), (), s32[]{:S(2)}) async-start(), calls=%async_computation.5 | async-start | bytes 9732096 | tf_op jit(solution)/shard_map/all_gather | solution.py:50
  8.7 401.5 %all-reduce.3.cloned.1.call-start = ((), (), s32[]{:S(2)}) async-start(), calls=%async_computation.3 | async-start | bytes 1048576 | tf_op jit(solution)/shard_map/psum | solution.py:80
  14.0 564.6 %all-reduce.5.cloned.1.call-start = ((), (), s32[]{:S(2)}) async-start(), calls=%async_computation.6 | async-start | bytes 1048576 | tf_op jit(solution)/shard_map/psum | solution.py:87
  258.2 6.8 copy-start.3
  258.2 151.9 %copy-start.1 = (bf16[256,1024]{1,0:T(8,128)(2,1)S(1)}, bf16[256,1024]{1,0:T(8,128)(2,1)}, u32[]{:S(2)}) copy-start(bf16[256,1024]{1,0:T(8,128)(2,1)} %param.13) | copy-start | bytes 1572868
  258.2 151.9 %copy-start.2 = (bf16[1024,256]{1,0:T(8,128)(2,1)S(1)}, bf16[1024,256]{1,0:T(8,128)(2,1)}, u32[]{:S(2)}) copy-start(bf16[1024,256]{1,0:T(8,128)(2,1)} %param.17) | copy-start | bytes 1572868
  264.8 313.8 %copy-start.4 = (f32[1024]{0:T(1024)S(1)}, f32[1024]{0:T(1024)}, u32[]{:S(2)}) copy-start(f32[1024]{0:T(1024)} %param.14) | copy-start | bytes 12292
  412.7 295.1 %reduce-scatter.8.cloned.1.call-start = ((), (), s32[]{:S(2)}) async-start(), calls=%async_computation.9 | async-start | bytes 540672 | tf_op jit(solution)/shard_map/reduce_scatter | solution.py:99
  414.9 419.7 %reduce-scatter.4.cloned.1.call-start = ((), (), s32[]{:S(2)}) async-start(), calls=%async_computation.7 | async-start | bytes 540672 | tf_op jit(solution)/shard_map/reduce_scatter | solution.py:93
  581.4 379.6 %reduce-scatter.6.cloned.1.call-start = ((), (), s32[]{:S(2)}) async-start(), calls=%async_computation.8 | async-start | bytes 540672 | tf_op jit(solution)/shard_map/reduce_scatter | solution.py:96
Sparse Core Ops, SparseCore 0:
  10.1 93.1 all-gather.4
  106.6 138.8 all-gather.6
  248.4 161.6 all-reduce.2
  413.1 165.4 all-reduce.4
  583.6 124.1 reduce-scatter.7
  713.5 121.1 reduce-scatter.3
  839.8 121.1 reduce-scatter.5
where the time goes:
time: 969 us; the launch traced here: 968 us
  waiting for transfers between devices  789 us (81%)
  blocking collectives  123 us (13%)
  matrix products  19.6 us (2%)
  between operations  14.2 us (1%)
  local copies, waits for them, and re-layouts  12.9 us (1%)
    psum x1, waiting for transfers between devices, shards(): grad_block = lax.psum(block_term.astype(jnp.bfloat16), 'mp')  164 us
    all_gather x1, waiting for transfers between devices, shards(): part_rows = lax.all_gather(qkv_weight, 'dp', axis=0, tiled=True)  137 us
    reduce_scatter x1, waiting for transfers between devices, shards(): lax.psum_scatter(up_term.astype(jnp.bfloat16), 'dp', scatter_dimension=0,...  127 us
    reduce_scatter x1, waiting for transfers between devices, shards(): lax.psum_scatter(down_term.astype(jnp.bfloat16), 'dp', scatter_dimension=...  126 us
    reduce_scatter x1, waiting for transfers between devices, shards(): lax.psum_scatter(proj_term.astype(jnp.bfloat16), 'dp', scatter_dimension=...  124 us
    psum x1, waiting for transfers between devices, shards(): mlp_sum = lax.psum(mlp_term.astype(jnp.bfloat16), 'mp').astype(jnp.float32)  64.2 us
    all_gather x1, waiting for transfers between devices, shards(): lax.all_gather(teacher_in, 'mp', axis=1, tiled=True)  45.8 us
    all_gather x1, blocking collectives, shards(): lax.all_gather(gain_row.astype(jnp.bfloat16), 'mp', axis=1, tiled=True)  42.7 us
  transfers between devices with their start and end apart: 7, of which 7 were waited for; matrix products, arithmetic and copies ran while one was open for 4% of the time, Pallas kernels for 0%

commit v1 on v0

v1 whole, which is shorter than its diff:
```python
import functools
import math

import jax
import jax.numpy as jnp
from jax import lax
from jax.experimental import pallas as pl
from jax.experimental.pallas import tpu as pltpu
from jax.sharding import Mesh, PartitionSpec as P

HEAD = 128
PATCH = 256
EPSILON = 1e-06
F32 = jnp.float32
BF16 = jnp.bfloat16

SIZES = {"zh": 2, "y": 8, "c": 2, "zl": 4, "x": 4}
DP = ("zh", "y", "c")
MP = ("zl", "x")
RING_ORDER = (0, -1, 1, -2, 2, -3, 3, 4)


def normalize(values):
    row_mean = jnp.mean(values, axis=-1, keepdims=True)
    centered = values - row_mean
    row_var = jnp.mean(centered * centered, axis=-1, keepdims=True)
    return centered * lax.rsqrt(row_var + EPSILON)


def gelu_parts(pre_act):
    cdf_part = 0.5 * (1.0 + lax.erf(pre_act * 0.7071067811865476))
    density = jnp.exp(-0.5 * pre_act * pre_act) * 0.3989422804014327
    return (pre_act * cdf_part, cdf_part + pre_act * density)


def shift(values, axis, step):
    size = SIZES[axis]
    return lax.ppermute(values, axis, [(i, (i + step) % size) for i in range(size)])


def swap(values, axis):
    return lax.all_to_all(values, axis, split_axis=0, concat_axis=0)


def spread(values, axis):
    return swap(jnp.broadcast_to(values[None], (SIZES[axis],) + values.shape), axis)


def ring_gather(chunk, forward_last):
    plus = [chunk]
    minus = [chunk]
    for unused in range(3):
        plus.append(shift(plus[-1], "y", 1))
        minus.append(shift(minus[-1], "y", -1))
    last = shift(plus[3], "y", 1) if forward_last else shift(minus[3], "y", -1)
    return [chunk, plus[1], minus[1], plus[2], minus[2], plus[3], minus[3], last]


def sum_parts(parts):
    return jnp.sum(parts.astype(F32), axis=0)


def reduce_mp(term):
    rows, cols = term.shape
    part = sum_parts(swap(term.reshape(4, rows // 4, cols), "x")).astype(BF16)
    part = sum_parts(swap(part.reshape(4, rows // 16, cols), "zl")).astype(BF16)
    part = spread(part, "zl").reshape(rows // 4, cols)
    return spread(part, "x").reshape(rows, cols)


def merge_stats(stats, count, axis):
    parts = spread(stats, axis)
    size = parts.shape[0]
    means = parts[:, 0] / count
    total = jnp.sum(parts[:, 0], axis=0)
    mean = total / (count * size)
    moved = means - mean[None]
    spreads = jnp.sum(parts[:, 1], axis=0) + count * jnp.sum(moved * moved, axis=0)
    return jnp.stack([total, spreads])


def teacher_kernel(
    place, a_ref, wa_ref, wa2_ref, wb_ref, wb2_ref, qg_ref, f_ref, n_ref, acc_ref
):
    zh, y, c = place[0], place[1], place[2]
    width = 16 * 384

    def block(b):
        return a_ref[b % 4, b // 4, :256, :].astype(F32)

    def fold(values):
        return values[:, :128] + values[:, 128:256] + values[:, 256:]

    total = lax.fori_loop(
        0, 16, lambda b, t: t + fold(block(b)), jnp.zeros((256, 128), F32)
    )
    mean = jnp.sum(total, axis=1, keepdims=True) / width

    def squares(b, t):
        d = block(b) - mean
        return t + fold(d * d)

    total = lax.fori_loop(0, 16, squares, jnp.zeros((256, 128), F32))
    rstd = lax.rsqrt(jnp.sum(total, axis=1, keepdims=True) / width + EPSILON)

    def write(b, carry):
        rows = a_ref[b % 4, b // 4, 256:272, :].astype(F32)
        gain = rows[0:1] + rows[1:2] + rows[2:3]
        n_ref[b] = ((block(b) - mean) * rstd * gain).astype(BF16)
        return carry

    lax.fori_loop(0, 16, write, 0)

    acc_ref[...] = jnp.zeros_like(acc_ref)
    for own, other, hi in ((wa_ref, wa2_ref, zh), (wb_ref, wb2_ref, 1 - zh)):
        for j, off in enumerate(RING_ORDER):
            b = hi * 8 + lax.rem(y + off + 8, 8)
            left = n_ref[b]
            right = jnp.concatenate(
                [own[j, 0], own[j, 1], own[j, 2], other[j, 0], other[j, 1], other[j, 2]],
                axis=1,
            )
            acc_ref[...] += jnp.dot(left, right, preferred_element_type=F32)

    def head(base, row):
        gain = jnp.where(row == 0, qg_ref[0:1, :], qg_ref[1:2, :])
        query = (normalize(acc_ref[:, base : base + 128]) * gain).astype(BF16)
        key = (normalize(acc_ref[:, base + 128 : base + 256]) * gain).astype(BF16)
        value = acc_ref[:, base + 256 : base + 384].astype(BF16)
        scores = lax.dot_general(
            query, key, (((1,), (1,)), ((), ())), preferred_element_type=F32
        ) * (HEAD ** (-0.5))
        scores = jnp.exp(scores - jnp.max(scores, axis=1, keepdims=True))
        attn = (scores / jnp.sum(scores, axis=1, keepdims=True)).astype(BF16)
        return jnp.dot(attn, value, preferred_element_type=F32)

    mine = head(0, c)
    theirs = head(384, 1 - c)
    f_ref[:, :128] = jnp.where(c == 0, mine, theirs)
    f_ref[:, 128:] = jnp.where(c == 0, theirs, mine)


def shards(
    teacher_in,
    teacher_gain,
    qkv_weight,
    qk_gain,
    student_in,
    student_gain,
    up_weight,
    down_weight,
    projector,
):
    tok_rows = teacher_in.shape[0]

    weight = qkv_weight.transpose(1, 0, 2).reshape(3, 192, 2, 128)
    weight = lax.all_to_all(weight, "c", split_axis=2, concat_axis=1).reshape(3, 384, 128)
    weight_far = shift(weight, "zh", 1)

    hi = lax.reduce_precision(teacher_gain, 8, 7)
    mid = lax.reduce_precision(teacher_gain - hi, 8, 7)
    low = teacher_gain - hi - mid
    gain_rows = jnp.stack([hi, mid, low] + [jnp.zeros_like(hi)] * 13).astype(BF16)
    shard = jnp.concatenate([teacher_in, gain_rows], axis=0)
    gathered = lax.all_gather(lax.all_gather(shard, "zl"), "x")

    near = jnp.stack(ring_gather(weight, True))
    far = jnp.stack(ring_gather(weight_far, False))
    near_other = shift(near, "c", 1)
    far_other = shift(far, "c", 1)

    place = jnp.stack([lax.axis_index("zh"), lax.axis_index("y"), lax.axis_index("c")])
    vmem = pl.BlockSpec(memory_space=pltpu.VMEM)
    features = pl.pallas_call(
        teacher_kernel,
        out_shape=jax.ShapeDtypeStruct((256, 256), F32),
        in_specs=[pl.BlockSpec(memory_space=pltpu.SMEM)] + [vmem] * 6,
        out_specs=vmem,
        scratch_shapes=[pltpu.VMEM((16, 256, 384), BF16), pltpu.VMEM((256, 768), F32)],
        compiler_params=pltpu.CompilerParams(vmem_limit_bytes=40 * 1024 * 1024),
        cost_estimate=pl.CostEstimate(
            flops=2 * 256 * 6144 * 768, bytes_accessed=13_000_000, transcendentals=131072
        ),
        name="teacher",
    )(place, gathered, near, near_other, far, far_other, qk_gain)

    student_normed = (normalize(student_in.astype(F32)) * student_gain).astype(BF16)
    pre_act = jnp.dot(student_normed, up_weight, preferred_element_type=F32)
    gated, slope = gelu_parts(pre_act)
    activ = gated.astype(BF16)
    mlp_term = jnp.dot(activ, down_weight, preferred_element_type=F32).astype(BF16)
    mlp_sum = reduce_mp(mlp_term).astype(F32)
    block_out = (student_in.astype(F32) + mlp_sum).astype(BF16)
    predicted = jnp.dot(block_out, projector, preferred_element_type=F32)

    local_sum = jnp.sum(features, axis=1)
    local_dev = features - (local_sum / 256)[:, None]
    stats = jnp.stack([local_sum, jnp.sum(local_dev * local_dev, axis=1)])
    stats = merge_stats(merge_stats(stats, 256, "x"), 1024, "zl")
    target = (features - (stats[0] / 4096)[:, None]) * lax.rsqrt(stats[1] / 4096 + EPSILON)[:, None]

    loss_factor = 1.0 / math.sqrt(tok_rows * 32)
    grad_pred = ((predicted - target) * loss_factor).astype(BF16)
    block_term = jnp.einsum("tf,cf->tc", grad_pred, projector, preferred_element_type=F32)
    grad_block = reduce_mp(block_term.astype(BF16))
    proj_term = jnp.einsum("tc,tf->cf", block_out, grad_pred, preferred_element_type=F32)
    down_term = jnp.einsum("tc,tf->cf", grad_block, activ, preferred_element_type=F32)
    grad_act = jnp.einsum("tc,fc->tf", grad_block, down_weight, preferred_element_type=F32)
    grad_pre = (grad_act * slope).astype(BF16)
    up_term = jnp.einsum("tc,tf->cf", student_normed, grad_pre, preferred_element_type=F32)

    terms = jnp.stack([t.astype(BF16) for t in (up_term, down_term, proj_term)])
    terms = terms.reshape(3, 2, 8, 2, 32, 256)
    terms = lax.all_to_all(terms, "c", split_axis=3, concat_axis=0)
    terms = sum_parts(terms).astype(BF16)
    terms = lax.all_to_all(terms, "y", split_axis=2, concat_axis=0)
    terms = sum_parts(terms).astype(BF16)
    terms = sum_parts(lax.all_to_all(terms, "zh", split_axis=1, concat_axis=0)).astype(BF16)
    return terms[0], terms[1].T, terms[2]


def solution(mesh):
    fine = Mesh(mesh.devices.reshape(tuple(SIZES.values())), tuple(SIZES))
    in_specs = (
        P(DP, MP),
        P(MP),
        P(DP, None, MP),
        P(MP, None),
        P(DP, None),
        P(),
        P(None, MP),
        P(MP, None),
        P(None, MP),
    )
    out_specs = (P(DP, MP), P(MP, DP), P(DP, MP))
    return jax.shard_map(shards, mesh=fine, in_specs=in_specs, out_specs=out_specs, check_vma=False)
```

time: 969 us -> 295 us (0.30)
  the two profiles are of different devices: /device:TPU:2 before, /device:TPU:64 now
where the time goes in v1:
time: 295 us; the launch traced here: 293 us
  blocking collectives  127 us (43%)
  starting transfers between devices  81 us (27%)
  waiting for transfers between devices  36.3 us (12%)
  local copies, waits for them, and re-layouts  16 us (5%)
  between operations  14.7 us (5%)
  Pallas kernels  11.5 us (4%)
  other arithmetic  4.34 us (1%)
  matrix products  3.01 us (1%)
    ppermute x17, starting transfers between devices, shift(): lax.ppermute(values, axis, [(i, (i + step) % size) for i in range(size)])  60.5 us
    all_to_all x5, blocking collectives, swap(): return lax.all_to_all(values, axis, split_axis=0, concat_axis=0)  53.3 us
    all_to_all x1, blocking collectives, shards(): terms = lax.all_to_all(terms, 'y', split_axis=2, concat_axis=0)  29.5 us
    all_gather x1, blocking collectives, shards(): gathered = lax.all_gather(lax.all_gather(shard, 'zl'), 'x')  20.8 us
    all_to_all x5, starting transfers between devices, swap(): return lax.all_to_all(values, axis, split_axis=0, concat_axis=0)  20.5 us
    all_to_all x5, waiting for transfers between devices, swap(): return lax.all_to_all(values, axis, split_axis=0, concat_axis=0)  20.5 us
    ppermute x17, waiting for transfers between devices, shift(): lax.ppermute(values, axis, [(i, (i + step) % size) for i in range(size)])  15.8 us
    all_to_all x1, blocking collectives, shards(): lax.all_to_all(terms, 'zh', split_axis=1, concat_axis=0)  14 us
  transfers between devices with their start and end apart: 23, of which 6 were waited for; matrix products, arithmetic and copies ran while one was open for 5% of the time, Pallas kernels for 4%

profile of v1, /device:TPU:64, one launch (start us, length us, event | category | flops | bytes accessed | tf_op | source)
XLA Modules:
  0.0 293.5 jit_solution(13297251081415370970)
XLA Ops:
  12.4 10.0 %collective-permute-start.8 = (bf16[3,384,128]{2,1,0:T(8,128)(2,1)S(1)}, bf16[3,384,128]{2,1,0:T(8,128)(2,1)}, u32[]{:S(2)}, u32[]{:S(2)}) collective-permute-start(bf16[3,384,128]{2,1,0:T(8,128)(2,1)S(1)} %bitcast.98), channel_id=1, source_target_pairs={{0,256},{256,0},{1,257},{257,1},{2,258},{258,2},{3,259},{259,3},{4... | collective-permute-start | bytes 884744 | tf_op jit(solution)/shard_map/ppermute | solution.py:38
  30.0 20.8 %all-gather = bf16[1088,384]{1,0:T(8,128)(2,1)} all-gather(bf16[272,384]{1,0:T(8,128)(2,1)S(1)} %concatenate.5), channel_id=2, replica_groups=mesh['zh'=2,'y'=8,'c'=2,'zl'=4,'x'=4] {'zl'}, dimensions={0}, use_global_device_ids=true | all-gather | bytes 1044480 | tf_op jit(solution)/shard_map/all_gather | solution.py:165
  55.0 4.6 %collective-permute-start.10 = (bf16[3,384,128]{2,1,0:T(8,128)(2,1)}, bf16[3,384,128]{2,1,0:T(8,128)(2,1)S(1)}, u32[]{:S(2)}, u32[]{:S(2)}) collective-permute-start(bf16[3,384,128]{2,1,0:T(8,128)(2,1)} %collective-permute-done.8), channel_id=1, source_target_pairs={{0,224},{32,0},{64,32},{96,64},{128,96},{160,128},{192,160},{224,1... | collective-permute-start | bytes 884744 | tf_op jit(solution)/shard_map/ppermute | solution.py:38
  63.3 5.1 %collective-permute-start.3 = (bf16[3,384,128]{2,1,0:T(8,128)(2,1)S(1)}, bf16[3,384,128]{2,1,0:T(8,128)(2,1)S(1)}, u32[]{:S(2)}, u32[]{:S(2)}) collective-permute-start(bf16[3,384,128]{2,1,0:T(8,128)(2,1)S(1)} %collective-permute-done.1), channel_id=1, source_target_pairs={{0,224},{32,0},{64,32},{96,64},{128,96},{160,128},{192,160},{224,1... | collective-permute-start | bytes 884744 | tf_op jit(solution)/shard_map/ppermute | solution.py:38
  71.1 5.1 %collective-permute-start.12 = (bf16[3,384,128]{2,1,0:T(8,128)(2,1)S(1)}, bf16[3,384,128]{2,1,0:T(8,128)(2,1)S(1)}, u32[]{:S(2)}, u32[]{:S(2)}) collective-permute-start(bf16[3,384,128]{2,1,0:T(8,128)(2,1)S(1)} %collective-permute-done.10), channel_id=1, source_target_pairs={{0,224},{32,0},{64,32},{96,64},{128,96},{160,128},{192,160},{224,1... | collective-permute-start | bytes 884744 | tf_op jit(solution)/shard_map/ppermute | solution.py:38
  79.0 5.1 %collective-permute-start.5 = (bf16[3,384,128]{2,1,0:T(8,128)(2,1)S(1)}, bf16[3,384,128]{2,1,0:T(8,128)(2,1)S(1)}, u32[]{:S(2)}, u32[]{:S(2)}) collective-permute-start(bf16[3,384,128]{2,1,0:T(8,128)(2,1)S(1)} %collective-permute-done.3), channel_id=1, source_target_pairs={{0,224},{32,0},{64,32},{96,64},{128,96},{160,128},{192,160},{224,1... | collective-permute-start | bytes 884744 | tf_op jit(solution)/shard_map/ppermute | solution.py:38
  87.0 5.1 %collective-permute-start.14 = (bf16[3,384,128]{2,1,0:T(8,128)(2,1)S(1)}, bf16[3,384,128]{2,1,0:T(8,128)(2,1)S(1)}, u32[]{:S(2)}, u32[]{:S(2)}) collective-permute-start(bf16[3,384,128]{2,1,0:T(8,128)(2,1)S(1)} %collective-permute-done.12), channel_id=1, source_target_pairs={{0,224},{32,0},{64,32},{96,64},{128,96},{160,128},{192,160},{224,1... | collective-permute-start | bytes 884744 | tf_op jit(solution)/shard_map/ppermute | solution.py:38
  95.7 6.4 %collective-permute-done.6 = bf16[3,384,128]{2,1,0:T(8,128)(2,1)S(1)} collective-permute-done((bf16[3,384,128]{2,1,0:T(8,128)(2,1)S(1)}, bf16[3,384,128]{2,1,0:T(8,128)(2,1)S(1)}, u32[]{:S(2)}, u32[]{:S(2)}) %collective-permute-start.6) | collective-permute-done | bytes 294944 | tf_op jit(solution)/shard_map/ppermute | solution.py:38
  106.9 9.3 %collective-permute-done.15 = bf16[3,384,128]{2,1,0:T(8,128)(2,1)S(1)} collective-permute-done((bf16[3,384,128]{2,1,0:T(8,128)(2,1)S(1)}, bf16[3,384,128]{2,1,0:T(8,128)(2,1)S(1)}, u32[]{:S(2)}, u32[]{:S(2)}) %collective-permute-start.15) | collective-permute-done | bytes 294944 | tf_op jit(solution)/shard_map/ppermute | solution.py:38
  119.3 13.6 %all_to_all.93 = bf16[4,64,1024]{2,1,0:T(8,128)(2,1)} all-to-all(bf16[4,64,1024]{2,1,0:T(8,128)(2,1)S(1)} %bitcast.94), channel_id=1, replica_groups=mesh['zh'=2,'y'=8,'c'=2,'zl'=4,'x'=4] {'x'}, dimensions={0} | all-to-all | bytes 1048576 | tf_op jit(solution)/shard_map/all_to_all | solution.py:42
  134.0 11.0 %all_to_all.94 = bf16[4,16,1024]{2,1,0:T(8,128)(2,1)S(1)} all-to-all(bf16[4,16,1024]{2,1,0:T(8,128)(2,1)S(1)} %bitcast.105), channel_id=1, replica_groups=mesh['zh'=2,'y'=8,'c'=2,'zl'=4,'x'=4] {'zl'}, dimensions={0} | all-to-all | bytes 262144 | tf_op jit(solution)/shard_map/all_to_all | solution.py:42
  145.7 4.2 %all-to-all-start.2 = ((bf16[4,16,1024]{2,1,0:T(8,128)(2,1)}), bf16[4,16,1024]{2,1,0:T(8,128)(2,1)S(1)}, u32[]{:S(2)}, u32[]{:S(2)}) async-start(bf16[4,16,1024]{2,1,0:T(8,128)(2,1)} %broadcast_in_dim.20), calls=%async_computation.2 | async-start | bytes 262144 | tf_op jit(solution)/shard_map/all_to_all | solution.py:42
  150.0 5.1 %all-to-all-done.2 = bf16[4,16,1024]{2,1,0:T(8,128)(2,1)S(1)} async-done(((bf16[4,16,1024]{2,1,0:T(8,128)(2,1)}), bf16[4,16,1024]{2,1,0:T(8,128)(2,1)S(1)}, u32[]{:S(2)}, u32[]{:S(2)}) %all-to-all-start.2) | async-done | bytes 131104 | tf_op jit(solution)/shard_map/all_to_all | solution.py:42
  155.9 4.1 %all-to-all-start.3 = ((bf16[4,64,1024]{2,1,0:T(8,128)(2,1)}), bf16[4,64,1024]{2,1,0:T(8,128)(2,1)}, u32[]{:S(2)}, u32[]{:S(2)}) async-start(bf16[4,64,1024]{2,1,0:T(8,128)(2,1)} %broadcast_in_dim.22), calls=%async_computation.3 | async-start | bytes 1048576 | tf_op jit(solution)/shard_map/all_to_all | solution.py:42
  162.1 11.5 %teacher.1 = f32[256,256]{1,0:T(8,128)S(1)} custom-call(s32[3]{0:T(128)S(1)} %pad_add_fusion.place, bf16[4,4,272,384]{3,2,1,0:T(8,128)(2,1)S(1)} %bitcast.89, bf16[8,3,384,128]{3,2,1,0:T(8,128)(2,1)} %bitcast_dynamic-update-slice_fusion.8.wa_ref, bf16[8,3,384,128]{3,2,1,0:T(8,128)(2,1)} %collective-permute-done.7.wa2_ref, ...), custom_call_target="tpu_custom_call" | custom-call | flops 2415919104 | bytes 13000000 | tf_op jit(solution)/shard_map/teacher/pallas_call | solution.py:174
  174.6 4.7 %all-to-all-start.5 = ((f32[4,2,256]{2,1,0:T(2,128)}), f32[4,2,256]{2,1,0:T(2,128)S(1)}, u32[]{:S(2)}, u32[]{:S(2)}) async-start(f32[4,2,256]{2,1,0:T(2,128)} %broadcast_in_dim.23), calls=%async_computation.5 | async-start | bytes 16384 | tf_op jit(solution)/shard_map/all_to_all | solution.py:42
  185.3 4.0 %all-to-all-start.6 = ((f32[4,2,256]{2,1,0:T(2,128)}), f32[4,2,256]{2,1,0:T(2,128)S(1)}, u32[]{:S(2)}, u32[]{:S(2)}) async-start(f32[4,2,256]{2,1,0:T(2,128)} %broadcast_in_dim.24), calls=%async_computation.6 | async-start | bytes 16384 | tf_op jit(solution)/shard_map/all_to_all | solution.py:42
  193.9 10.5 %all_to_all.95 = bf16[4,64,1024]{2,1,0:T(8,128)(2,1)S(1)} all-to-all(bf16[4,64,1024]{2,1,0:T(8,128)(2,1)S(1)} %bitcast.95), channel_id=1, replica_groups=mesh['zh'=2,'y'=8,'c'=2,'zl'=4,'x'=4] {'x'}, dimensions={0} | all-to-all | bytes 1048576 | tf_op jit(solution)/shard_map/all_to_all | solution.py:42
  204.4 9.4 %all_to_all.96 = bf16[4,16,1024]{2,1,0:T(8,128)(2,1)S(1)} all-to-all(bf16[4,16,1024]{2,1,0:T(8,128)(2,1)S(1)} %bitcast.106), channel_id=1, replica_groups=mesh['zh'=2,'y'=8,'c'=2,'zl'=4,'x'=4] {'zl'}, dimensions={0} | all-to-all | bytes 262144 | tf_op jit(solution)/shard_map/all_to_all | solution.py:42
  213.9 9.0 %all_to_all.97 = bf16[4,16,1024]{2,1,0:T(8,128)(2,1)S(1)} all-to-all(bf16[4,16,1024]{2,1,0:T(8,128)(2,1)S(1)} %broadcast_in_dim.25), channel_id=1, replica_groups=mesh['zh'=2,'y'=8,'c'=2,'zl'=4,'x'=4] {'zl'}, dimensions={0} | all-to-all | bytes 262144 | tf_op jit(solution)/shard_map/all_to_all | solution.py:42
  227.6 7.6 %all-to-all-done.10 = bf16[4,64,1024]{2,1,0:T(8,128)(2,1)S(1)} async-done(((bf16[4,64,1024]{2,1,0:T(8,128)(2,1)}), bf16[4,64,1024]{2,1,0:T(8,128)(2,1)S(1)}, u32[]{:S(2)}, u32[]{:S(2)}) %all-to-all-start.10) | async-done | bytes 524320 | tf_op jit(solution)/shard_map/all_to_all | solution.py:42
  236.8 5.0 %all_to_all.98 = bf16[1,3,2,8,2,32,256]{6,5,3,2,1,0,4:T(8,128)(2,1)S(1)} all-to-all(bf16[1,3,2,8,2,32,256]{6,5,3,2,1,0,4:T(8,128)(2,1)S(1)} %copy.52), channel_id=1, replica_groups=mesh['zh'=2,'y'=8,'c'=2,'zl'=4,'x'=4] {'c'}, dimensions={4} | all-to-all | bytes 3145728 | tf_op jit(solution)/shard_map/all_to_all | solution.py:214
  242.3 29.5 %all_to_all.99 = bf16[1,3,2,8,32,256]{5,4,2,1,0,3:T(8,128)(2,1)S(1)} all-to-all(bf16[1,3,2,8,32,256]{5,4,2,1,0,3:T(8,128)(2,1)S(1)} %copy.50), channel_id=1, replica_groups=mesh['zh'=2,'y'=8,'c'=2,'zl'=4,'x'=4] {'y'}, dimensions={3} | all-to-all | bytes 1572864 | tf_op jit(solution)/shard_map/all_to_all | solution.py:216
  271.9 14.0 %all_to_all.100 = bf16[1,3,2,32,256]{4,3,1,0,2:T(8,128)(2,1)S(1)} all-to-all(bf16[1,3,2,32,256]{4,3,1,0,2:T(8,128)(2,1)S(1)} %copy.51), channel_id=1, replica_groups=mesh['zh'=2,'y'=8,'c'=2,'zl'=4,'x'=4] {'zh'}, dimensions={2} | all-to-all | bytes 196608 | tf_op jit(solution)/shard_map/all_to_all | solution.py:218
  (125 shorter events, 64.0 us)
Async XLA Ops:
  7.2 111.8 %copy-start = (bf16[256,1024]{1,0:T(8,128)(2,1)S(1)}, bf16[256,1024]{1,0:T(8,128)(2,1)}, u32[]{:S(2)}) copy-start(bf16[256,1024]{1,0:T(8,128)(2,1)} %param.16) | copy-start | bytes 1572868
  7.2 152.9 %all-gather.4.cloned.1.call-start = ((), (), s32[]{:S(2)}) async-start(), calls=%async_computation.14 | async-start | bytes 4177920 | tf_op jit(solution)/shard_map/all_gather | solution.py:165
  12.4 39.1 %collective-permute-start.8 = (bf16[3,384,128]{2,1,0:T(8,128)(2,1)S(1)}, bf16[3,384,128]{2,1,0:T(8,128)(2,1)}, u32[]{:S(2)}, u32[]{:S(2)}) collective-permute-start(bf16[3,384,128]{2,1,0:T(8,128)(2,1)S(1)} %bitcast.98), channel_id=1, source_target_pairs={{0,256},{256,0},{1,257},{257,1},{2,258},{258,2},{3,259},{259,3},{4... | collective-permute-start | bytes 884744 | tf_op jit(solution)/shard_map/ppermute | solution.py:38
  22.4 37.2 %collective-permute-start = (bf16[3,384,128]{2,1,0:T(8,128)(2,1)S(1)}, bf16[3,384,128]{2,1,0:T(8,128)(2,1)}, u32[]{:S(2)}, u32[]{:S(2)}) collective-permute-start(bf16[3,384,128]{2,1,0:T(8,128)(2,1)S(1)} %bitcast.99), channel_id=1, source_target_pairs={{0,32},{32,64},{64,96},{96,128},{128,160},{160,192},{192,224},{224... | collective-permute-start | bytes 884744 | tf_op jit(solution)/shard_map/ppermute | solution.py:38
  25.9 37.3 %collective-permute-start.1 = (bf16[3,384,128]{2,1,0:T(8,128)(2,1)S(1)}, bf16[3,384,128]{2,1,0:T(8,128)(2,1)S(1)}, u32[]{:S(2)}, u32[]{:S(2)}) collective-permute-start(bf16[3,384,128]{2,1,0:T(8,128)(2,1)S(1)} %bitcast.100), channel_id=1, source_target_pairs={{0,224},{32,0},{64,32},{96,64},{128,96},{160,128},{192,160},{224,1... | collective-permute-start | bytes 884744 | tf_op jit(solution)/shard_map/ppermute | solution.py:38
  51.5 17.6 %collective-permute-start.9 = (bf16[3,384,128]{2,1,0:T(8,128)(2,1)}, bf16[3,384,128]{2,1,0:T(8,128)(2,1)S(1)}, u32[]{:S(2)}, u32[]{:S(2)}) collective-permute-start(bf16[3,384,128]{2,1,0:T(8,128)(2,1)} %collective-permute-done.8), channel_id=1, source_target_pairs={{0,32},{32,64},{64,96},{96,128},{128,160},{160,192},{192,224},{224... | collective-permute-start | bytes 884744 | tf_op jit(solution)/shard_map/ppermute | solution.py:38
  55.0 16.1 %collective-permute-start.10 = (bf16[3,384,128]{2,1,0:T(8,128)(2,1)}, bf16[3,384,128]{2,1,0:T(8,128)(2,1)S(1)}, u32[]{:S(2)}, u32[]{:S(2)}) collective-permute-start(bf16[3,384,128]{2,1,0:T(8,128)(2,1)} %collective-permute-done.8), channel_id=1, source_target_pairs={{0,224},{32,0},{64,32},{96,64},{128,96},{160,128},{192,160},{224,1... | collective-permute-start | bytes 884744 | tf_op jit(solution)/shard_map/ppermute | solution.py:38
  59.6 16.7 %collective-permute-start.2 = (bf16[3,384,128]{2,1,0:T(8,128)(2,1)}, bf16[3,384,128]{2,1,0:T(8,128)(2,1)S(1)}, u32[]{:S(2)}, u32[]{:S(2)}) collective-permute-start(bf16[3,384,128]{2,1,0:T(8,128)(2,1)} %collective-permute-done), channel_id=1, source_target_pairs={{0,32},{32,64},{64,96},{96,128},{128,160},{160,192},{192,224},{224... | collective-permute-start | bytes 884744 | tf_op jit(solution)/shard_map/ppermute | solution.py:38
  63.3 15.7 %collective-permute-start.3 = (bf16[3,384,128]{2,1,0:T(8,128)(2,1)S(1)}, bf16[3,384,128]{2,1,0:T(8,128)(2,1)S(1)}, u32[]{:S(2)}, u32[]{:S(2)}) collective-permute-start(bf16[3,384,128]{2,1,0:T(8,128)(2,1)S(1)} %collective-permute-done.1), channel_id=1, source_target_pairs={{0,224},{32,0},{64,32},{96,64},{128,96},{160,128},{192,160},{224,1... | collective-permute-start | bytes 884744 | tf_op jit(solution)/shard_map/ppermute | solution.py:38
  69.1 15.8 %collective-permute-start.11 = (bf16[3,384,128]{2,1,0:T(8,128)(2,1)S(1)}, bf16[3,384,128]{2,1,0:T(8,128)(2,1)S(1)}, u32[]{:S(2)}, u32[]{:S(2)}) collective-permute-start(bf16[3,384,128]{2,1,0:T(8,128)(2,1)S(1)} %collective-permute-done.9), channel_id=1, source_target_pairs={{0,32},{32,64},{64,96},{96,128},{128,160},{160,192},{192,224},{224... | collective-permute-start | bytes 884744 | tf_op jit(solution)/shard_map/ppermute | solution.py:38
  71.1 15.9 %collective-permute-start.12 = (bf16[3,384,128]{2,1,0:T(8,128)(2,1)S(1)}, bf16[3,384,128]{2,1,0:T(8,128)(2,1)S(1)}, u32[]{:S(2)}, u32[]{:S(2)}) collective-permute-start(bf16[3,384,128]{2,1,0:T(8,128)(2,1)S(1)} %collective-permute-done.10), channel_id=1, source_target_pairs={{0,224},{32,0},{64,32},{96,64},{128,96},{160,128},{192,160},{224,1... | collective-permute-start | bytes 884744 | tf_op jit(solution)/shard_map/ppermute | solution.py:38
  76.3 15.9 %collective-permute-start.4 = (bf16[3,384,128]{2,1,0:T(8,128)(2,1)S(1)}, bf16[3,384,128]{2,1,0:T(8,128)(2,1)S(1)}, u32[]{:S(2)}, u32[]{:S(2)}) collective-permute-start(bf16[3,384,128]{2,1,0:T(8,128)(2,1)S(1)} %collective-permute-done.2), channel_id=1, source_target_pairs={{0,32},{32,64},{64,96},{96,128},{128,160},{160,192},{192,224},{224... | collective-permute-start | bytes 884744 | tf_op jit(solution)/shard_map/ppermute | solution.py:38
  79.0 16.0 %collective-permute-start.5 = (bf16[3,384,128]{2,1,0:T(8,128)(2,1)S(1)}, bf16[3,384,128]{2,1,0:T(8,128)(2,1)S(1)}, u32[]{:S(2)}, u32[]{:S(2)}) collective-permute-start(bf16[3,384,128]{2,1,0:T(8,128)(2,1)S(1)} %collective-permute-done.3), channel_id=1, source_target_pairs={{0,224},{32,0},{64,32},{96,64},{128,96},{160,128},{192,160},{224,1... | collective-permute-start | bytes 884744 | tf_op jit(solution)/shard_map/ppermute | solution.py:38
  84.9 21.9 %collective-permute-start.13 = (bf16[3,384,128]{2,1,0:T(8,128)(2,1)S(1)}, bf16[3,384,128]{2,1,0:T(8,128)(2,1)S(1)}, u32[]{:S(2)}, u32[]{:S(2)}) collective-permute-start(bf16[3,384,128]{2,1,0:T(8,128)(2,1)S(1)} %collective-permute-done.11), channel_id=1, source_target_pairs={{0,32},{32,64},{64,96},{96,128},{128,160},{160,192},{192,224},{224... | collective-permute-start | bytes 884744 | tf_op jit(solution)/shard_map/ppermute | solution.py:38
  87.0 17.8 %collective-permute-start.14 = (bf16[3,384,128]{2,1,0:T(8,128)(2,1)S(1)}, bf16[3,384,128]{2,1,0:T(8,128)(2,1)S(1)}, u32[]{:S(2)}, u32[]{:S(2)}) collective-permute-start(bf16[3,384,128]{2,1,0:T(8,128)(2,1)S(1)} %collective-permute-done.12), channel_id=1, source_target_pairs={{0,224},{32,0},{64,32},{96,64},{128,96},{160,128},{192,160},{224,1... | collective-permute-start | bytes 884744 | tf_op jit(solution)/shard_map/ppermute | solution.py:38
  92.2 10.0 %collective-permute-start.6 = (bf16[3,384,128]{2,1,0:T(8,128)(2,1)S(1)}, bf16[3,384,128]{2,1,0:T(8,128)(2,1)S(1)}, u32[]{:S(2)}, u32[]{:S(2)}) collective-permute-start(bf16[3,384,128]{2,1,0:T(8,128)(2,1)S(1)} %collective-permute-done.4), channel_id=1, source_target_pairs={{0,32},{32,64},{64,96},{96,128},{128,160},{160,192},{192,224},{224... | collective-permute-start | bytes 884744 | tf_op jit(solution)/shard_map/ppermute | solution.py:38
  102.9 57.2 %collective-permute-start.7 = (bf16[8,3,384,128]{3,2,1,0:T(8,128)(2,1)}, bf16[8,3,384,128]{3,2,1,0:T(8,128)(2,1)}, u32[]{:S(2)}, u32[]{:S(2)}) collective-permute-start(bf16[8,3,384,128]{3,2,1,0:T(8,128)(2,1)} %bitcast_dynamic-update-slice_fusion.8.wa_ref), channel_id=1, source_target_pairs={{0,16},{16,0},{1,17},{17,1},{2,18},{18,2},{3,19},{19,3},{4,20},{20... | collective-permute-start | bytes 7077896 | tf_op jit(solution)/shard_map/ppermute | solution.py:38
  104.9 11.3 %collective-permute-start.15 = (bf16[3,384,128]{2,1,0:T(8,128)(2,1)S(1)}, bf16[3,384,128]{2,1,0:T(8,128)(2,1)S(1)}, u32[]{:S(2)}, u32[]{:S(2)}) collective-permute-start(bf16[3,384,128]{2,1,0:T(8,128)(2,1)S(1)} %collective-permute-done.14), channel_id=1, source_target_pairs={{0,224},{32,0},{64,32},{96,64},{128,96},{160,128},{192,160},{224,1... | collective-permute-start | bytes 884744 | tf_op jit(solution)/shard_map/ppermute | solution.py:38
  116.2 43.9 %collective-permute-start.16 = (bf16[8,3,384,128]{3,2,1,0:T(8,128)(2,1)S(1)}, bf16[8,3,384,128]{3,2,1,0:T(8,128)(2,1)}, u32[]{:S(2)}, u32[]{:S(2)}) collective-permute-start(bf16[8,3,384,128]{3,2,1,0:T(8,128)(2,1)S(1)} %bitcast_dynamic-update-slice_fusion.wb_ref), channel_id=1, source_target_pairs={{0,16},{16,0},{1,17},{17,1},{2,18},{18,2},{3,19},{19,3},{4,20},{20... | collective-permute-start | bytes 7077896 | tf_op jit(solution)/shard_map/ppermute | solution.py:38
  145.7 9.4 %all-to-all-start.2 = ((bf16[4,16,1024]{2,1,0:T(8,128)(2,1)}), bf16[4,16,1024]{2,1,0:T(8,128)(2,1)S(1)}, u32[]{:S(2)}, u32[]{:S(2)}) async-start(bf16[4,16,1024]{2,1,0:T(8,128)(2,1)} %broadcast_in_dim.20), calls=%async_computation.2 | async-start | bytes 262144 | tf_op jit(solution)/shard_map/all_to_all | solution.py:42
  155.9 18.0 %all-to-all-start.3 = ((bf16[4,64,1024]{2,1,0:T(8,128)(2,1)}), bf16[4,64,1024]{2,1,0:T(8,128)(2,1)}, u32[]{:S(2)}, u32[]{:S(2)}) async-start(bf16[4,64,1024]{2,1,0:T(8,128)(2,1)} %broadcast_in_dim.22), calls=%async_computation.3 | async-start | bytes 1048576 | tf_op jit(solution)/shard_map/all_to_all | solution.py:42
  174.6 10.0 %all-to-all-start.5 = ((f32[4,2,256]{2,1,0:T(2,128)}), f32[4,2,256]{2,1,0:T(2,128)S(1)}, u32[]{:S(2)}, u32[]{:S(2)}) async-start(f32[4,2,256]{2,1,0:T(2,128)} %broadcast_in_dim.23), calls=%async_computation.5 | async-start | bytes 16384 | tf_op jit(solution)/shard_map/all_to_all | solution.py:42
  185.3 8.2 %all-to-all-start.6 = ((f32[4,2,256]{2,1,0:T(2,128)}), f32[4,2,256]{2,1,0:T(2,128)S(1)}, u32[]{:S(2)}, u32[]{:S(2)}) async-start(f32[4,2,256]{2,1,0:T(2,128)} %broadcast_in_dim.24), calls=%async_computation.6 | async-start | bytes 16384 | tf_op jit(solution)/shard_map/all_to_all | solution.py:42
  223.7 11.5 %all-to-all-start.10 = ((bf16[4,64,1024]{2,1,0:T(8,128)(2,1)}), bf16[4,64,1024]{2,1,0:T(8,128)(2,1)S(1)}, u32[]{:S(2)}, u32[]{:S(2)}) async-start(bf16[4,64,1024]{2,1,0:T(8,128)(2,1)} %broadcast_in_dim.27), calls=%async_computation.10 | async-start | bytes 1048576 | tf_op jit(solution)/shard_map/all_to_all | solution.py:42
  (9 other events, 220.5 us)
Sparse Core Ops, SparseCore 0:
  50.9 47.5 all-gather.3

commit v2 on v1

v2 whole, which is shorter than its diff:
```python
import math

import jax
import jax.numpy as jnp
from jax import lax
from jax.experimental import pallas as pl
from jax.experimental.pallas import tpu as pltpu
from jax.sharding import Mesh, PartitionSpec as P

HEAD = 128
PATCH = 256
EPSILON = 1e-06
F32 = jnp.float32
BF16 = jnp.bfloat16

SIZES = {"zh": 2, "y": 8, "c": 2, "zl": 4, "x": 4}
DP = ("zh", "y", "c")
MP = ("zl", "x")


def normalize(values):
    row_mean = jnp.mean(values, axis=-1, keepdims=True)
    centered = values - row_mean
    row_var = jnp.mean(centered * centered, axis=-1, keepdims=True)
    return centered * lax.rsqrt(row_var + EPSILON)


def gelu_parts(pre_act):
    cdf_part = 0.5 * (1.0 + lax.erf(pre_act * 0.7071067811865476))
    density = jnp.exp(-0.5 * pre_act * pre_act) * 0.3989422804014327
    return (pre_act * cdf_part, cdf_part + pre_act * density)


def shift(values, axis, step):
    size = SIZES[axis]
    return lax.ppermute(values, axis, [(i, (i + step) % size) for i in range(size)])


def flip(values, axes, bits):
    return lax.ppermute(values, axes, [(i, i ^ bits) for i in range(4)])


def tie(values, *others):
    return lax.optimization_barrier((values, *others))[0]


def swap(values, axis):
    return lax.all_to_all(values, axis, split_axis=0, concat_axis=0)


def spread(values, axis):
    return swap(jnp.broadcast_to(values[None], (SIZES[axis],) + values.shape), axis)


def sum_parts(parts):
    return jnp.sum(parts.astype(F32), axis=0)


def mp_scatter_x(term):
    rows, cols = term.shape
    return sum_parts(swap(term.reshape(4, rows // 4, cols), "x")).astype(BF16)


def mp_scatter_zl(term):
    rows, cols = term.shape
    return sum_parts(swap(term.reshape(4, rows // 4, cols), "zl")).astype(BF16)


def mp_gather_zl(part):
    rows, cols = part.shape
    return spread(part, "zl").reshape(4 * rows, cols)


def mp_gather_x(part):
    rows, cols = part.shape
    return spread(part, "x").reshape(4 * rows, cols)


def merge_stats(stats, count):
    parts = swap(jnp.broadcast_to(stats[None], (16,) + stats.shape), MP)
    total = jnp.sum(parts[:, 0], axis=0)
    mean = total / (count * 16)
    moved = parts[:, 0] / count - mean[None]
    spreads = jnp.sum(parts[:, 1], axis=0) + count * jnp.sum(moved * moved, axis=0)
    return mean, spreads / (count * 16)


def norm_kernel(place, a0_ref, am_ref, ap_ref, lo_ref, hi_ref, n_ref):
    x, my_zl, my_zh = place[0], place[1], place[2]
    blocks = []
    for i in range(4):
        blocks.append((a0_ref, i, i, 0))
        blocks.append((am_ref, i, i, 3))
        blocks.append((ap_ref, i, i, 1))
        blocks.append((lo_ref if i < 2 else hi_ref, i % 2, i, 2))
    width = 16 * 384

    def fold(values):
        return values[:, :128] + values[:, 128:256] + values[:, 256:]

    @pl.loop(0, 8)
    def _(t):
        rows = pl.ds(pl.multiple_of(t * 32, 32), 32)
        total = jnp.zeros((32, 128), F32)
        for ref, i, dz, off in blocks:
            total += fold(ref[i, rows, :].astype(F32))
        mean = jnp.sum(total, axis=1, keepdims=True) / width
        total = jnp.zeros((32, 128), F32)
        for ref, i, dz, off in blocks:
            d = ref[i, rows, :].astype(F32) - mean
            total += fold(d * d)
        rstd = lax.rsqrt(jnp.sum(total, axis=1, keepdims=True) / width + EPSILON)
        for ref, i, dz, off in blocks:
            gains = ref[i, 256:272, :].astype(F32)
            gain = gains[0:1] + gains[1:2] + gains[2:3]
            zl = my_zl ^ dz
            xs = lax.rem(x + off, 4)
            spot = ((zl & 1) * 4 + xs) * 2 + ((zl >> 1) ^ my_zh)
            d = ref[i, rows, :].astype(F32) - mean
            n_ref[rows, pl.ds(pl.multiple_of(spot * 384, 128), 384)] = (
                d * rstd * gain
            ).astype(BF16)


def attention_kernel(place, own_ref, other_ref, w_ref, qg_ref, f_ref):
    gain = jnp.where(place[0] == 0, qg_ref[0:1, :], qg_ref[1:2, :])
    for image, ref in enumerate((own_ref, other_ref)):
        projected = jnp.dot(ref[...], w_ref[...], preferred_element_type=F32)
        query = (normalize(projected[:, :128]) * gain).astype(BF16)
        key = (normalize(projected[:, 128:256]) * gain).astype(BF16)
        value = projected[:, 256:].astype(BF16)
        scores = lax.dot_general(
            query, key, (((1,), (1,)), ((), ())), preferred_element_type=F32
        ) * (HEAD ** (-0.5))
        scores = jnp.exp(scores - jnp.max(scores, axis=1, keepdims=True))
        attn = (scores / jnp.sum(scores, axis=1, keepdims=True)).astype(BF16)
        f_ref[image] = jnp.dot(attn, value, preferred_element_type=F32)


def reduce_dp(terms):
    k = terms.shape[0]
    terms = terms.reshape(k, 16, 2, 32, 256)
    terms = lax.all_to_all(terms, "c", split_axis=2, concat_axis=0)
    terms = sum_parts(terms).astype(BF16)
    terms = lax.all_to_all(terms, ("zh", "y"), split_axis=1, concat_axis=0)
    return sum_parts(terms).astype(BF16)


def shards(
    teacher_in,
    teacher_gain,
    qkv_weight,
    qk_gain,
    student_in,
    student_gain,
    up_weight,
    down_weight,
    projector,
):
    tok_rows = teacher_in.shape[0]

    first = lax.axis_index("c") == 0
    weight = qkv_weight.reshape(192, 3, 2, 128).transpose(2, 0, 1, 3).reshape(2, 192, 384)
    kept = jnp.where(first, weight[0], weight[1])
    given = jnp.where(first, weight[1], weight[0])
    zh_kept = flip(kept, ("zh", "c"), 2)
    zh_given = flip(given, ("zh", "c"), 3)
    c_given = flip(given, ("zh", "c"), 1)

    hi = lax.reduce_precision(teacher_gain, 8, 7)
    mid = lax.reduce_precision(teacher_gain - hi, 8, 7)
    low = teacher_gain - hi - mid
    gain_rows = jnp.stack([hi, mid, low] + [jnp.zeros_like(hi)] * 13).astype(BF16)
    shard = tie(jnp.concatenate([teacher_in, gain_rows], axis=0), c_given)
    pair = jnp.stack([shard, flip(shard, "zl", 1)])

    student_normed = (normalize(student_in.astype(F32)) * student_gain).astype(BF16)
    pre_act = jnp.dot(student_normed, up_weight, preferred_element_type=F32)
    gated, slope = gelu_parts(pre_act)
    activ = gated.astype(BF16)
    mlp_term = jnp.dot(activ, down_weight, preferred_element_type=F32).astype(BF16)

    def by_core(mine, theirs):
        return jnp.where(first, jnp.stack([mine, theirs]), jnp.stack([theirs, mine]))

    zh_kept, zh_given, pair, mlp_term = lax.optimization_barrier(
        (zh_kept, zh_given, pair, mlp_term)
    )
    rows = jnp.concatenate([by_core(kept, c_given), by_core(zh_kept, zh_given)])
    weight = lax.all_gather(rows, "y").reshape(6144, 384)

    part = mp_scatter_x(tie(mlp_term, rows))
    shard = tie(jnp.concatenate([pair, flip(pair, "zl", 2)]), part)
    from_left = shift(shard, "x", 1)
    from_right = shift(shard, "x", -1)
    part = mp_gather_zl(mp_scatter_zl(tie(part, shard)))
    from_left, from_right, part = lax.optimization_barrier((from_left, from_right, part))
    far_low = shift(from_left[:2], "x", 1)
    far_high = shift(from_right[2:], "x", -1)

    place_x = jnp.stack([lax.axis_index("x"), lax.axis_index("zl"), lax.axis_index("zh")])
    place_c = lax.axis_index("c").reshape(1)
    smem = pl.BlockSpec(memory_space=pltpu.SMEM)
    vmem = pl.BlockSpec(memory_space=pltpu.VMEM)
    params = pltpu.CompilerParams(vmem_limit_bytes=40 * 1024 * 1024)
    normed = pl.pallas_call(
        norm_kernel,
        out_shape=jax.ShapeDtypeStruct((256, 6144), BF16),
        in_specs=[smem] + [vmem] * 5,
        out_specs=vmem,
        compiler_params=params,
        cost_estimate=pl.CostEstimate(
            flops=1000, bytes_accessed=1000, transcendentals=0
        ),
        name="teacher_norm",
    )(place_x, shard, from_left, from_right, far_low, far_high)
    normed_other = shift(normed, "c", 1)
    mlp_sum = mp_gather_x(tie(part, normed))
    heads = pl.pallas_call(
        attention_kernel,
        out_shape=jax.ShapeDtypeStruct((2, 256, 128), F32),
        in_specs=[smem] + [vmem] * 4,
        out_specs=vmem,
        compiler_params=params,
        cost_estimate=pl.CostEstimate(
            flops=2 * 512 * 6144 * 384, bytes_accessed=11_000_000, transcendentals=131072
        ),
        name="teacher_heads",
    )(place_c, normed, normed_other, weight, qk_gain)
    crossed = shift(heads[1], "c", 1)
    features = jnp.where(
        place_c[0] == 0,
        jnp.concatenate([heads[0], crossed], axis=1),
        jnp.concatenate([crossed, heads[0]], axis=1),
    )

    block_out = (student_in.astype(F32) + mlp_sum.astype(F32)).astype(BF16)
    predicted = jnp.dot(block_out, projector, preferred_element_type=F32)

    local_sum = jnp.sum(features, axis=1)
    local_dev = features - (local_sum / 256)[:, None]
    stats = jnp.stack([local_sum, jnp.sum(local_dev * local_dev, axis=1)])
    feat_mean, feat_var = merge_stats(stats, 256)
    target = (features - feat_mean[:, None]) * lax.rsqrt(feat_var + EPSILON)[:, None]

    loss_factor = 1.0 / math.sqrt(tok_rows * 32)
    grad_pred = ((predicted - target) * loss_factor).astype(BF16)
    block_term = jnp.einsum("tf,cf->tc", grad_pred, projector, preferred_element_type=F32)
    proj_term = jnp.einsum("tc,tf->cf", block_out, grad_pred, preferred_element_type=F32)
    grad_block = mp_scatter_zl(mp_scatter_x(block_term.astype(BF16)))
    grad_block = mp_gather_x(mp_gather_zl(grad_block))
    down_term = jnp.einsum("tc,tf->cf", grad_block, activ, preferred_element_type=F32)
    grad_act = jnp.einsum("tc,fc->tf", grad_block, down_weight, preferred_element_type=F32)
    grad_pre = (grad_act * slope).astype(BF16)
    up_term = jnp.einsum("tc,tf->cf", student_normed, grad_pre, preferred_element_type=F32)
    terms = jnp.stack([t.astype(BF16) for t in (up_term, down_term, proj_term)])
    grad_up, grad_down, grad_projector = reduce_dp(terms)
    return grad_up, grad_down.T, grad_projector


def solution(mesh):
    fine = Mesh(mesh.devices.reshape(tuple(SIZES.values())), tuple(SIZES))
    in_specs = (
        P(DP, MP),
        P(MP),
        P(DP, None, MP),
        P(MP, None),
        P(DP, None),
        P(),
        P(None, MP),
        P(MP, None),
        P(None, MP),
    )
    out_specs = (P(DP, MP), P(MP, DP), P(DP, MP))
    return jax.shard_map(shards, mesh=fine, in_specs=in_specs, out_specs=out_specs, check_vma=False)
```

time: 295 us -> 240 us (0.81)
  the two profiles are of different devices: /device:TPU:64 before, /device:TPU:8 now
where the time goes in v2:
time: 240 us; the launch traced here: 239 us
  blocking collectives  97.4 us (41%)
  starting transfers between devices  53.1 us (22%)
  waiting for transfers between devices  45.2 us (19%)
  between operations  14.6 us (6%)
  Pallas kernels  13.3 us (6%)
  local copies, waits for them, and re-layouts  9 us (4%)
  other arithmetic  3.34 us (1%)
  matrix products  3.04 us (1%)
    all_to_all x6, blocking collectives, swap(): return lax.all_to_all(values, axis, split_axis=0, concat_axis=0)  59.1 us
    all_to_all x1, blocking collectives, reduce_dp(): terms = lax.all_to_all(terms, ('zh', 'y'), split_axis=1, concat_axis=0)  33.3 us
    ppermute x5, starting transfers between devices, flip(): return lax.ppermute(values, axes, [(i, i ^ bits) for i in range(4)])  20.6 us
    ppermute x5, waiting for transfers between devices, flip(): return lax.ppermute(values, axes, [(i, i ^ bits) for i in range(4)])  19.3 us
    ppermute x6, starting transfers between devices, shift(): lax.ppermute(values, axis, [(i, (i + step) % size) for i in range(size)])  18.3 us
    all_to_all x3, waiting for transfers between devices, swap(): return lax.all_to_all(values, axis, split_axis=0, concat_axis=0)  15.2 us
    all_to_all x3, starting transfers between devices, swap(): return lax.all_to_all(values, axis, split_axis=0, concat_axis=0)  14.2 us
    ppermute x6, waiting for transfers between devices, shift(): lax.ppermute(values, axis, [(i, (i + step) % size) for i in range(size)])  10.6 us
  transfers between devices with their start and end apart: 15, of which 9 were waited for; matrix products, arithmetic and copies ran while one was open for 2% of the time, Pallas kernels for 6%

profile of v2, /device:TPU:8, one launch (start us, length us, event | category | flops | bytes accessed | tf_op | source)
XLA Modules:
  0.0 239.0 jit_solution(3742769630735516420)
XLA Ops:
  10.8 11.0 %collective-permute-start.1 = (bf16[192,384]{1,0:T(8,128)(2,1)S(1)}, bf16[192,384]{1,0:T(8,128)(2,1)S(1)}, u32[]{:S(2)}, u32[]{:S(2)}) collective-permute-start(bf16[192,384]{1,0:T(8,128)(2,1)S(1)} %bitcast.87), channel_id=1, source_target_pairs={{0,272},{16,256},{256,16},{272,0},{1,273},{17,257},{257,17},{273,1... | collective-permute-start | bytes 442376 | tf_op jit(solution)/shard_map/ppermute | solution.py:40
  24.9 3.4 %collective-permute-start.3 = (bf16[272,384]{1,0:T(8,128)(2,1)S(1)}, bf16[272,384]{1,0:T(8,128)(2,1)S(1)}, u32[]{:S(2)}, u32[]{:S(2)}) collective-permute-start(bf16[272,384]{1,0:T(8,128)(2,1)S(1)} %concatenate.17), channel_id=1, source_target_pairs={{0,4},{4,0},{8,12},{12,8},{1,5},{5,1},{9,13},{13,9},{2,6},{6,2},{1... | collective-permute-start | bytes 626696 | tf_op jit(solution)/shard_map/ppermute | solution.py:40
  28.8 12.4 %collective-permute-done.3 = bf16[272,384]{1,0:T(8,128)(2,1)S(1)} collective-permute-done((bf16[272,384]{1,0:T(8,128)(2,1)S(1)}, bf16[272,384]{1,0:T(8,128)(2,1)S(1)}, u32[]{:S(2)}, u32[]{:S(2)}) %collective-permute-start.3) | collective-permute-done | bytes 208928 | tf_op jit(solution)/shard_map/ppermute | solution.py:40
  44.7 13.4 %all_to_all.63 = bf16[4,64,1024]{2,1,0:T(8,128)(2,1)S(1)} all-to-all(bf16[4,64,1024]{2,1,0:T(8,128)(2,1)S(1)} %bitcast.71), channel_id=1, replica_groups=mesh['zh'=2,'y'=8,'c'=2,'zl'=4,'x'=4] {'x'}, dimensions={0} | all-to-all | bytes 1048576 | tf_op jit(solution)/shard_map/all_to_all | solution.py:48
  58.2 6.9 %collective-permute-done.4 = bf16[2,272,384]{2,1,0:T(8,128)(2,1)S(1)} collective-permute-done((bf16[2,272,384]{2,1,0:T(8,128)(2,1)S(1)}, bf16[2,272,384]{2,1,0:T(8,128)(2,1)S(1)}, u32[]{:S(2)}, u32[]{:S(2)}) %collective-permute-start.4) | collective-permute-done | bytes 417824 | tf_op jit(solution)/shard_map/ppermute | solution.py:40
  65.2 3.4 %collective-permute-start.5 = (bf16[4,272,384]{2,1,0:T(8,128)(2,1)S(1)}, bf16[4,272,384]{2,1,0:T(8,128)(2,1)S(1)}, u32[]{:S(2)}, u32[]{:S(2)}) collective-permute-start(bf16[4,272,384]{2,1,0:T(8,128)(2,1)S(1)} %pad_maximum_fusion.1.a0_ref), channel_id=1, source_target_pairs={{0,1},{1,2},{2,3},{3,0},{4,5},{5,6},{6,7},{7,4},{8,9},{9,10},{10,1... | collective-permute-start | bytes 2506760 | tf_op jit(solution)/shard_map/ppermute | solution.py:36
  68.6 3.7 %collective-permute-start.6 = (bf16[4,272,384]{2,1,0:T(8,128)(2,1)S(1)}, bf16[4,272,384]{2,1,0:T(8,128)(2,1)S(1)}, u32[]{:S(2)}, u32[]{:S(2)}) collective-permute-start(bf16[4,272,384]{2,1,0:T(8,128)(2,1)S(1)} %pad_maximum_fusion.1.a0_ref), channel_id=1, source_target_pairs={{0,3},{1,0},{2,1},{3,2},{4,7},{5,4},{6,5},{7,6},{8,11},{9,8},{10,9... | collective-permute-start | bytes 2506760 | tf_op jit(solution)/shard_map/ppermute | solution.py:36
  72.3 8.8 %all_to_all.64 = bf16[4,16,1024]{2,1,0:T(8,128)(2,1)S(1)} all-to-all(bf16[4,16,1024]{2,1,0:T(8,128)(2,1)S(1)} %bitcast.81), channel_id=1, replica_groups=mesh['zh'=2,'y'=8,'c'=2,'zl'=4,'x'=4] {'zl'}, dimensions={0} | all-to-all | bytes 262144 | tf_op jit(solution)/shard_map/all_to_all | solution.py:48
  81.2 9.0 %all_to_all.65 = bf16[4,16,1024]{2,1,0:T(8,128)(2,1)} all-to-all(bf16[4,16,1024]{2,1,0:T(8,128)(2,1)S(1)} %broadcast_in_dim.14), channel_id=1, replica_groups=mesh['zh'=2,'y'=8,'c'=2,'zl'=4,'x'=4] {'zl'}, dimensions={0} | all-to-all | bytes 262144 | tf_op jit(solution)/shard_map/all_to_all | solution.py:48
  91.3 3.4 %collective-permute-start.7 = (bf16[2,272,384]{2,1,0:T(8,128)(2,1)}, bf16[2,272,384]{2,1,0:T(8,128)(2,1)S(1)}, u32[]{:S(2)}, u32[]{:S(2)}) collective-permute-start(bf16[2,272,384]{2,1,0:T(8,128)(2,1)} %slice.32), channel_id=1, source_target_pairs={{0,1},{1,2},{2,3},{3,0},{4,5},{5,6},{6,7},{7,4},{8,9},{9,10},{10,1... | collective-permute-start | bytes 1253384 | tf_op jit(solution)/shard_map/ppermute | solution.py:36
  95.6 3.6 %collective-permute-start.8 = (bf16[2,272,384]{2,1,0:T(8,128)(2,1)}, bf16[2,272,384]{2,1,0:T(8,128)(2,1)}, u32[]{:S(2)}, u32[]{:S(2)}) collective-permute-start(bf16[2,272,384]{2,1,0:T(8,128)(2,1)} %slice.33), channel_id=1, source_target_pairs={{0,3},{1,0},{2,1},{3,2},{4,7},{5,4},{6,5},{7,6},{8,11},{9,8},{10,9... | collective-permute-start | bytes 1253384 | tf_op jit(solution)/shard_map/ppermute | solution.py:36
  99.3 5.6 %collective-permute-done.7.lo_ref = bf16[2,272,384]{2,1,0:T(8,128)(2,1)S(1)} collective-permute-done((bf16[2,272,384]{2,1,0:T(8,128)(2,1)}, bf16[2,272,384]{2,1,0:T(8,128)(2,1)S(1)}, u32[]{:S(2)}, u32[]{:S(2)}) %collective-permute-start.7) | collective-permute-done | bytes 417824 | tf_op jit(solution)/shard_map/ppermute | solution.py:36
  107.7 5.8 %teacher_norm.1.own_ref = bf16[256,6144]{1,0:T(8,128)(2,1)} custom-call(s32[3]{0:T(128)S(1)} %pad_add_fusion.place, bf16[4,272,384]{2,1,0:T(8,128)(2,1)S(1)} %pad_maximum_fusion.1.a0_ref, bf16[4,272,384]{2,1,0:T(8,128)(2,1)S(1)} %collective-permute-done.5.am_ref, bf16[4,272,384]{2,1,0:T(8,128)(2,1)S(1)} %collective-permute-done.6.ap_ref, ...), custom_call_target="tpu_custom_call" | custom-call | flops 1000 | bytes 1000 | tf_op jit(solution)/shard_map/teacher_norm/pallas_call | solution.py:206
  116.4 4.2 %all-to-all-start.3 = ((bf16[4,64,1024]{2,1,0:T(8,128)(2,1)}), bf16[4,64,1024]{2,1,0:T(8,128)(2,1)S(1)}, u32[]{:S(2)}, u32[]{:S(2)}) async-start(bf16[4,64,1024]{2,1,0:T(8,128)(2,1)} %broadcast_in_dim.15), calls=%async_computation.3 | async-start | bytes 1048576 | tf_op jit(solution)/shard_map/all_to_all | solution.py:48
  123.8 7.5 %teacher_heads.1 = f32[2,256,128]{2,1,0:T(8,128)S(1)} custom-call(s32[1]{0:T(128)} %bitcast.13.place, bf16[256,6144]{1,0:T(8,128)(2,1)} %teacher_norm.1.own_ref, bf16[256,6144]{1,0:T(8,128)(2,1)} %collective-permute-done.9.other_ref, bf16[6144,384]{1,0:T(8,128)(2,1)S(1)} %bitcast.68, f32[2,128]{1,0:T(2,128)S(1)} %copy-done.2), custom_call_target="tpu_custom_call" | custom-call | flops 2415919104 | bytes 11000000 | tf_op jit(solution)/shard_map/teacher_heads/pallas_call | solution.py:219
  135.7 6.2 %all-to-all-start.4 = ((f32[16,2,256]{2,1,0:T(2,128)}), f32[16,2,256]{2,1,0:T(2,128)S(1)}, u32[]{:S(2)}, u32[]{:S(2)}) async-start(f32[16,2,256]{2,1,0:T(2,128)} %broadcast_in_dim.16), calls=%async_computation.4 | async-start | bytes 65536 | tf_op jit(solution)/shard_map/all_to_all | solution.py:48
  142.2 7.8 %all-to-all-done.4 = f32[16,2,256]{2,1,0:T(2,128)S(1)} async-done(((f32[16,2,256]{2,1,0:T(2,128)}), f32[16,2,256]{2,1,0:T(2,128)S(1)}, u32[]{:S(2)}, u32[]{:S(2)}) %all-to-all-start.4) | async-done | bytes 32800 | tf_op jit(solution)/shard_map/all_to_all | solution.py:48
  150.5 11.1 %all_to_all.66 = bf16[4,64,1024]{2,1,0:T(8,128)(2,1)S(1)} all-to-all(bf16[4,64,1024]{2,1,0:T(8,128)(2,1)S(1)} %bitcast.70), channel_id=1, replica_groups=mesh['zh'=2,'y'=8,'c'=2,'zl'=4,'x'=4] {'x'}, dimensions={0} | all-to-all | bytes 1048576 | tf_op jit(solution)/shard_map/all_to_all | solution.py:48
  161.7 8.3 %all_to_all.67 = bf16[4,16,1024]{2,1,0:T(8,128)(2,1)S(1)} all-to-all(bf16[4,16,1024]{2,1,0:T(8,128)(2,1)S(1)} %bitcast.82), channel_id=1, replica_groups=mesh['zh'=2,'y'=8,'c'=2,'zl'=4,'x'=4] {'zl'}, dimensions={0} | all-to-all | bytes 262144 | tf_op jit(solution)/shard_map/all_to_all | solution.py:48
  170.0 8.4 %all_to_all.68 = bf16[4,16,1024]{2,1,0:T(8,128)(2,1)S(1)} all-to-all(bf16[4,16,1024]{2,1,0:T(8,128)(2,1)S(1)} %broadcast_in_dim.17), channel_id=1, replica_groups=mesh['zh'=2,'y'=8,'c'=2,'zl'=4,'x'=4] {'zl'}, dimensions={0} | all-to-all | bytes 262144 | tf_op jit(solution)/shard_map/all_to_all | solution.py:48
  179.3 3.8 %all-to-all-start.8 = ((bf16[4,64,1024]{2,1,0:T(8,128)(2,1)}), bf16[4,64,1024]{2,1,0:T(8,128)(2,1)S(1)}, u32[]{:S(2)}, u32[]{:S(2)}) async-start(bf16[4,64,1024]{2,1,0:T(8,128)(2,1)} %broadcast_in_dim.19), calls=%async_computation.8 | async-start | bytes 1048576 | tf_op jit(solution)/shard_map/all_to_all | solution.py:48
  183.5 7.4 %all-to-all-done.8 = bf16[4,64,1024]{2,1,0:T(8,128)(2,1)S(1)} async-done(((bf16[4,64,1024]{2,1,0:T(8,128)(2,1)}), bf16[4,64,1024]{2,1,0:T(8,128)(2,1)S(1)}, u32[]{:S(2)}, u32[]{:S(2)}) %all-to-all-start.8) | async-done | bytes 524320 | tf_op jit(solution)/shard_map/all_to_all | solution.py:48
  192.6 5.0 %all_to_all.69 = bf16[1,3,16,2,32,256]{5,4,2,1,0,3:T(8,128)(2,1)S(1)} all-to-all(bf16[1,3,16,2,32,256]{5,4,2,1,0,3:T(8,128)(2,1)S(1)} %copy.37), channel_id=1, replica_groups=mesh['zh'=2,'y'=8,'c'=2,'zl'=4,'x'=4] {'c'}, dimensions={3} | all-to-all | bytes 3145728 | tf_op jit(solution)/shard_map/all_to_all | solution.py:143
  198.1 33.3 %all_to_all.70 = bf16[1,3,16,32,256]{4,3,1,0,2:T(8,128)(2,1)S(1)} all-to-all(bf16[1,3,16,32,256]{4,3,1,0,2:T(8,128)(2,1)S(1)} %copy.36), channel_id=1, replica_groups=mesh['zh'=2,'y'=8,'c'=2,'zl'=4,'x'=4] {'zh','y'}, dimensions={2} | all-to-all | bytes 1572864 | tf_op jit(solution)/shard_map/all_to_all | solution.py:145
  (101 shorter events, 30.9 us)
Async XLA Ops:
  7.2 21.2 %copy-start = (bf16[256,1024]{1,0:T(8,128)(2,1)S(1)}, bf16[256,1024]{1,0:T(8,128)(2,1)}, u32[]{:S(2)}) copy-start(bf16[256,1024]{1,0:T(8,128)(2,1)} %param.16) | copy-start | bytes 1572868
  7.2 16.6 %copy-start.10 = (f32[384]{0:T(512)S(1)}, f32[384]{0:T(512)}, u32[]{:S(2)}) copy-start(f32[384]{0:T(512)} %param.10) | copy-start | bytes 4612
  7.2 16.7 %copy-start.3 = (bf16[256,1024]{1,0:T(8,128)(2,1)S(1)}, bf16[256,1024]{1,0:T(8,128)(2,1)}, u32[]{:S(2)}) copy-start(bf16[256,1024]{1,0:T(8,128)(2,1)} %param.13) | copy-start | bytes 1572868
  7.2 114.3 %all-gather.3.cloned.1.call-start = ((), (), s32[]{:S(2)}) async-start(), calls=%async_computation.11 | async-start | bytes 5308416 | tf_op jit(solution)/shard_map/all_gather | solution.py:190
  8.4 16.0 %copy-start.9 = (bf16[256,384]{1,0:T(8,128)(2,1)S(1)}, bf16[256,384]{1,0:T(8,128)(2,1)}, u32[]{:S(2)}) copy-start(bf16[256,384]{1,0:T(8,128)(2,1)} %param.9) | copy-start | bytes 589828
  8.7 15.9 %copy-start.11 = (bf16[1024,256]{1,0:T(8,128)(2,1)S(1)}, bf16[1024,256]{1,0:T(8,128)(2,1)}, u32[]{:S(2)}) copy-start(bf16[1024,256]{1,0:T(8,128)(2,1)} %param.15) | copy-start | bytes 1572868
  8.7 15.9 %copy-start.12 = (f32[1024]{0:T(1024)S(1)}, f32[1024]{0:T(1024)}, u32[]{:S(2)}) copy-start(f32[1024]{0:T(1024)} %param.14) | copy-start | bytes 12292
  8.9 16.0 %collective-permute-start.2 = (bf16[192,384]{1,0:T(8,128)(2,1)S(1)}, bf16[192,384]{1,0:T(8,128)(2,1)S(1)}, u32[]{:S(2)}, u32[]{:S(2)}) collective-permute-start(bf16[192,384]{1,0:T(8,128)(2,1)S(1)} %bitcast.86), channel_id=1, source_target_pairs={{0,16},{16,0},{256,272},{272,256},{1,17},{17,1},{257,273},{273,257... | collective-permute-start | bytes 442376 | tf_op jit(solution)/shard_map/ppermute | solution.py:40
  10.8 30.5 %collective-permute-start.1 = (bf16[192,384]{1,0:T(8,128)(2,1)S(1)}, bf16[192,384]{1,0:T(8,128)(2,1)S(1)}, u32[]{:S(2)}, u32[]{:S(2)}) collective-permute-start(bf16[192,384]{1,0:T(8,128)(2,1)S(1)} %bitcast.87), channel_id=1, source_target_pairs={{0,272},{16,256},{256,16},{272,0},{1,273},{17,257},{257,17},{273,1... | collective-permute-start | bytes 442376 | tf_op jit(solution)/shard_map/ppermute | solution.py:40
  21.9 19.5 %collective-permute-start = (bf16[192,384]{1,0:T(8,128)(2,1)S(1)}, bf16[192,384]{1,0:T(8,128)(2,1)S(1)}, u32[]{:S(2)}, u32[]{:S(2)}) collective-permute-start(bf16[192,384]{1,0:T(8,128)(2,1)S(1)} %bitcast.90), channel_id=1, source_target_pairs={{0,256},{16,272},{256,0},{272,16},{1,257},{17,273},{257,1},{273,17... | collective-permute-start | bytes 442376 | tf_op jit(solution)/shard_map/ppermute | solution.py:40
  24.9 16.3 %collective-permute-start.3 = (bf16[272,384]{1,0:T(8,128)(2,1)S(1)}, bf16[272,384]{1,0:T(8,128)(2,1)S(1)}, u32[]{:S(2)}, u32[]{:S(2)}) collective-permute-start(bf16[272,384]{1,0:T(8,128)(2,1)S(1)} %concatenate.17), channel_id=1, source_target_pairs={{0,4},{4,0},{8,12},{12,8},{1,5},{5,1},{9,13},{13,9},{2,6},{6,2},{1... | collective-permute-start | bytes 626696 | tf_op jit(solution)/shard_map/ppermute | solution.py:40
  42.3 22.8 %collective-permute-start.4 = (bf16[2,272,384]{2,1,0:T(8,128)(2,1)S(1)}, bf16[2,272,384]{2,1,0:T(8,128)(2,1)S(1)}, u32[]{:S(2)}, u32[]{:S(2)}) collective-permute-start(bf16[2,272,384]{2,1,0:T(8,128)(2,1)S(1)} %pad_maximum_fusion.3), channel_id=1, source_target_pairs={{0,8},{4,12},{8,0},{12,4},{1,9},{5,13},{9,1},{13,5},{2,10},{6,14},... | collective-permute-start | bytes 1253384 | tf_op jit(solution)/shard_map/ppermute | solution.py:40
  65.2 24.9 %collective-permute-start.5 = (bf16[4,272,384]{2,1,0:T(8,128)(2,1)S(1)}, bf16[4,272,384]{2,1,0:T(8,128)(2,1)S(1)}, u32[]{:S(2)}, u32[]{:S(2)}) collective-permute-start(bf16[4,272,384]{2,1,0:T(8,128)(2,1)S(1)} %pad_maximum_fusion.1.a0_ref), channel_id=1, source_target_pairs={{0,1},{1,2},{2,3},{3,0},{4,5},{5,6},{6,7},{7,4},{8,9},{9,10},{10,1... | collective-permute-start | bytes 2506760 | tf_op jit(solution)/shard_map/ppermute | solution.py:36
  68.6 21.9 %collective-permute-start.6 = (bf16[4,272,384]{2,1,0:T(8,128)(2,1)S(1)}, bf16[4,272,384]{2,1,0:T(8,128)(2,1)S(1)}, u32[]{:S(2)}, u32[]{:S(2)}) collective-permute-start(bf16[4,272,384]{2,1,0:T(8,128)(2,1)S(1)} %pad_maximum_fusion.1.a0_ref), channel_id=1, source_target_pairs={{0,3},{1,0},{2,1},{3,2},{4,7},{5,4},{6,5},{7,6},{8,11},{9,8},{10,9... | collective-permute-start | bytes 2506760 | tf_op jit(solution)/shard_map/ppermute | solution.py:36
  91.3 13.5 %collective-permute-start.7 = (bf16[2,272,384]{2,1,0:T(8,128)(2,1)}, bf16[2,272,384]{2,1,0:T(8,128)(2,1)S(1)}, u32[]{:S(2)}, u32[]{:S(2)}) collective-permute-start(bf16[2,272,384]{2,1,0:T(8,128)(2,1)} %slice.32), channel_id=1, source_target_pairs={{0,1},{1,2},{2,3},{3,0},{4,5},{5,6},{6,7},{7,4},{8,9},{9,10},{10,1... | collective-permute-start | bytes 1253384 | tf_op jit(solution)/shard_map/ppermute | solution.py:36
  95.6 12.1 %collective-permute-start.8 = (bf16[2,272,384]{2,1,0:T(8,128)(2,1)}, bf16[2,272,384]{2,1,0:T(8,128)(2,1)}, u32[]{:S(2)}, u32[]{:S(2)}) collective-permute-start(bf16[2,272,384]{2,1,0:T(8,128)(2,1)} %slice.33), channel_id=1, source_target_pairs={{0,3},{1,0},{2,1},{3,2},{4,7},{5,4},{6,5},{7,6},{8,11},{9,8},{10,9... | collective-permute-start | bytes 1253384 | tf_op jit(solution)/shard_map/ppermute | solution.py:36
  99.3 16.2 %copy-start.8 = (bf16[4,16,1024]{2,1,0:T(8,128)(2,1)S(1)}, bf16[4,16,1024]{2,1,0:T(8,128)(2,1)}, u32[]{:S(2)}) copy-start(bf16[4,16,1024]{2,1,0:T(8,128)(2,1)} %all_to_all.65) | copy-start | bytes 393220
  113.5 8.0 %collective-permute-start.9 = (bf16[256,6144]{1,0:T(8,128)(2,1)}, bf16[256,6144]{1,0:T(8,128)(2,1)}, u32[]{:S(2)}, u32[]{:S(2)}) collective-permute-start(bf16[256,6144]{1,0:T(8,128)(2,1)} %teacher_norm.1.own_ref), channel_id=1, source_target_pairs={{0,16},{16,0},{1,17},{17,1},{2,18},{18,2},{3,19},{19,3},{4,20},{20... | collective-permute-start | bytes 9437192 | tf_op jit(solution)/shard_map/ppermute | solution.py:36
  116.4 17.2 %all-to-all-start.3 = ((bf16[4,64,1024]{2,1,0:T(8,128)(2,1)}), bf16[4,64,1024]{2,1,0:T(8,128)(2,1)S(1)}, u32[]{:S(2)}, u32[]{:S(2)}) async-start(bf16[4,64,1024]{2,1,0:T(8,128)(2,1)} %broadcast_in_dim.15), calls=%async_computation.3 | async-start | bytes 1048576 | tf_op jit(solution)/shard_map/all_to_all | solution.py:48
  131.3 10.5 %copy-start.5 = (bf16[1024,256]{1,0:T(8,128)(2,1)S(1)}, bf16[1024,256]{1,0:T(8,128)(2,1)}, u32[]{:S(2)}) copy-start(bf16[1024,256]{1,0:T(8,128)(2,1)} %param.17) | copy-start | bytes 1572868
  131.4 3.4 %collective-permute-start.10 = (f32[256,128]{1,0:T(8,128)S(1)}, f32[256,128]{1,0:T(8,128)S(1)}, u32[]{:S(2)}, u32[]{:S(2)}) collective-permute-start(f32[256,128]{1,0:T(8,128)S(1)} %get-tuple-element.31), channel_id=1, source_target_pairs={{0,16},{16,0},{1,17},{17,1},{2,18},{18,2},{3,19},{19,3},{4,20},{20... | collective-permute-start | bytes 393224 | tf_op jit(solution)/shard_map/ppermute | solution.py:36
  135.7 14.3 %all-to-all-start.4 = ((f32[16,2,256]{2,1,0:T(2,128)}), f32[16,2,256]{2,1,0:T(2,128)S(1)}, u32[]{:S(2)}, u32[]{:S(2)}) async-start(f32[16,2,256]{2,1,0:T(2,128)} %broadcast_in_dim.16), calls=%async_computation.4 | async-start | bytes 65536 | tf_op jit(solution)/shard_map/all_to_all | solution.py:48
  179.3 11.7 %copy-start.7 = (f32[256,256]{1,0:T(8,128)S(1)}, f32[256,256]{1,0:T(8,128)}, u32[]{:S(2)}) copy-start(f32[256,256]{1,0:T(8,128)} %copy-done.6) | copy-start | bytes 786436
  179.3 11.7 %all-to-all-start.8 = ((bf16[4,64,1024]{2,1,0:T(8,128)(2,1)}), bf16[4,64,1024]{2,1,0:T(8,128)(2,1)S(1)}, u32[]{:S(2)}, u32[]{:S(2)}) async-start(bf16[4,64,1024]{2,1,0:T(8,128)(2,1)} %broadcast_in_dim.19), calls=%async_computation.8 | async-start | bytes 1048576 | tf_op jit(solution)/shard_map/all_to_all | solution.py:48
  (4 other events, 23.5 us)
Sparse Core Ops, SparseCore 0:
  42.4 59.6 all-gather.2

commit v3 on v2

--- a/solution.py
+++ b/solution.py
@@ -36,8 +36,8 @@
     return lax.ppermute(values, axis, [(i, (i + step) % size) for i in range(size)])
 
 
-def flip(values, axes, bits):
-    return lax.ppermute(values, axes, [(i, i ^ bits) for i in range(4)])
+def flip(values, axes, bits=1):
+    return lax.ppermute(values, axes, [(i, i ^ bits) for i in range(SIZES[axes])])
 
 
 def tie(values, *others):
@@ -85,14 +85,18 @@
     return mean, spreads / (count * 16)
 
 
-def norm_kernel(place, a0_ref, am_ref, ap_ref, lo_ref, hi_ref, n_ref):
+def norm_kernel(place, *refs):
+    n_ref = refs[-1]
     x, my_zl, my_zh = place[0], place[1], place[2]
     blocks = []
-    for i in range(4):
-        blocks.append((a0_ref, i, i, 0))
-        blocks.append((am_ref, i, i, 3))
-        blocks.append((ap_ref, i, i, 1))
-        blocks.append((lo_ref if i < 2 else hi_ref, i % 2, i, 2))
+    for half in range(2):
+        own, left, right, low, high = refs[5 * half : 5 * half + 5]
+        for i in range(2):
+            blocks.append((own, i, 2 * half + i, 0))
+            blocks.append((left, i, 2 * half + i, 3))
+            blocks.append((right, i, 2 * half + i, 1))
+        blocks.append((low, 0, 2 * half, 2))
+        blocks.append((high, 0, 2 * half + 1, 2))
     width = 16 * 384
 
     def fold(values):
@@ -146,6 +150,19 @@
     return sum_parts(terms).astype(BF16)
 
 
+def reduce_projector(term, first):
+    term = term.reshape(2, 8, 2, 32, 256)
+    mine = jnp.where(first, term[:, :, 0], term[:, :, 1])
+    theirs = flip(jnp.where(first, term[:, :, 1], term[:, :, 0]), "c")
+    term = (mine.astype(F32) + theirs.astype(F32)).astype(BF16)
+    term = term.transpose(1, 0, 2, 3).reshape(8 * 64, 256)
+    term = lax.psum_scatter(term, "y", scatter_dimension=0, tiled=True).reshape(2, 32, 256)
+    low = lax.axis_index("zh") == 0
+    theirs = flip(jnp.where(low, term[1], term[0]), "zh")
+    mine = jnp.where(low, term[0], term[1])
+    return (mine.astype(F32) + theirs.astype(F32)).astype(BF16)
+
+
 def shards(
     teacher_in,
     teacher_gain,
@@ -161,17 +178,15 @@
 
     first = lax.axis_index("c") == 0
     weight = qkv_weight.reshape(192, 3, 2, 128).transpose(2, 0, 1, 3).reshape(2, 192, 384)
-    kept = jnp.where(first, weight[0], weight[1])
-    given = jnp.where(first, weight[1], weight[0])
-    zh_kept = flip(kept, ("zh", "c"), 2)
-    zh_given = flip(given, ("zh", "c"), 3)
-    c_given = flip(given, ("zh", "c"), 1)
+    near = jnp.where(first, weight, weight[::-1])
+    far = flip(near, "zh")
+    given = flip(jnp.stack([near[1], far[1]]), "c")
 
     hi = lax.reduce_precision(teacher_gain, 8, 7)
     mid = lax.reduce_precision(teacher_gain - hi, 8, 7)
     low = teacher_gain - hi - mid
     gain_rows = jnp.stack([hi, mid, low] + [jnp.zeros_like(hi)] * 13).astype(BF16)
-    shard = tie(jnp.concatenate([teacher_in, gain_rows], axis=0), c_given)
+    shard = tie(jnp.concatenate([teacher_in, gain_rows], axis=0), near)
     pair = jnp.stack([shard, flip(shard, "zl", 1)])
 
     student_normed = (normalize(student_in.astype(F32)) * student_gain).astype(BF16)
@@ -183,20 +198,24 @@
     def by_core(mine, theirs):
         return jnp.where(first, jnp.stack([mine, theirs]), jnp.stack([theirs, mine]))
 
-    zh_kept, zh_given, pair, mlp_term = lax.optimization_barrier(
-        (zh_kept, zh_given, pair, mlp_term)
+    given, pair, mlp_term = lax.optimization_barrier((given, pair, mlp_term))
+    rows = jnp.concatenate([by_core(near[0], given[0]), by_core(far[0], given[1])])
+    weight = lax.all_gather(rows, "y").reshape(6144, 384)
+
+    late = flip(pair, "zl", 2)
+    left, right = shift(pair, "x", 1), shift(pair, "x", -1)
+    part = mp_scatter_x(tie(mlp_term, rows))
+    late = tie(late, part)
+    late_left, late_right = shift(late, "x", 1), shift(late, "x", -1)
+    low, high = shift(left[:1], "x", 1), shift(right[1:], "x", -1)
+    part = mp_scatter_zl(tie(part, left, right))
+    late_left, late_right, part, low, high = lax.optimization_barrier(
+        (late_left, late_right, part, low, high)
     )
-    rows = jnp.concatenate([by_core(kept, c_given), by_core(zh_kept, zh_given)])
-    weight = lax.all_gather(rows, "y").reshape(6144, 384)
-
-    part = mp_scatter_x(tie(mlp_term, rows))
-    shard = tie(jnp.concatenate([pair, flip(pair, "zl", 2)]), part)
-    from_left = shift(shard, "x", 1)
-    from_right = shift(shard, "x", -1)
-    part = mp_gather_zl(mp_scatter_zl(tie(part, shard)))
-    from_left, from_right, part = lax.optimization_barrier((from_left, from_right, part))
-    far_low = shift(from_left[:2], "x", 1)
-    far_high = shift(from_right[2:], "x", -1)
+    late_low, late_high = shift(late_left[:1], "x", 1), shift(late_right[1:], "x", -1)
+    part = mp_gather_zl(part)
+    late_low, part = lax.optimization_barrier((late_low, part))
+    blocks = (pair, left, right, low, high, late, late_left, late_right, late_low, late_high)
 
     place_x = jnp.stack([lax.axis_index("x"), lax.axis_index("zl"), lax.axis_index("zh")])
     place_c = lax.axis_index("c").reshape(1)
@@ -206,14 +225,14 @@
     normed = pl.pallas_call(
         norm_kernel,
         out_shape=jax.ShapeDtypeStruct((256, 6144), BF16),
-        in_specs=[smem] + [vmem] * 5,
+        in_specs=[smem] + [vmem] * 10,
         out_specs=vmem,
         compiler_params=params,
         cost_estimate=pl.CostEstimate(
             flops=1000, bytes_accessed=1000, transcendentals=0
         ),
         name="teacher_norm",
-    )(place_x, shard, from_left, from_right, far_low, far_high)
+    )(place_x, *blocks)
     normed_other = shift(normed, "c", 1)
     mlp_sum = mp_gather_x(tie(part, normed))
     heads = pl.pallas_call(
@@ -247,14 +266,14 @@
     grad_pred = ((predicted - target) * loss_factor).astype(BF16)
     block_term = jnp.einsum("tf,cf->tc", grad_pred, projector, preferred_element_type=F32)
     proj_term = jnp.einsum("tc,tf->cf", block_out, grad_pred, preferred_element_type=F32)
+    grad_projector = reduce_projector(proj_term.astype(BF16), first)
     grad_block = mp_scatter_zl(mp_scatter_x(block_term.astype(BF16)))
     grad_block = mp_gather_x(mp_gather_zl(grad_block))
     down_term = jnp.einsum("tc,tf->cf", grad_block, activ, preferred_element_type=F32)
     grad_act = jnp.einsum("tc,fc->tf", grad_block, down_weight, preferred_element_type=F32)
     grad_pre = (grad_act * slope).astype(BF16)
     up_term = jnp.einsum("tc,tf->cf", student_normed, grad_pre, preferred_element_type=F32)
-    terms = jnp.stack([t.astype(BF16) for t in (up_term, down_term, proj_term)])
-    grad_up, grad_down, grad_projector = reduce_dp(terms)
+    grad_up, grad_down = reduce_dp(jnp.stack([up_term.astype(BF16), down_term.astype(BF16)]))
     return grad_up, grad_down.T, grad_projector
 
 

time: 240 us -> 254 us (1.058)
  the two profiles are of different devices: /device:TPU:8 before, /device:TPU:28 now
where the time goes in v3:
time: 254 us; the launch traced here: 252 us
  starting transfers between devices  106 us (42%)
  waiting for transfers between devices  66.4 us (26%)
  blocking collectives  25.4 us (10%)
  local copies, waits for them, and re-layouts  14.8 us (6%)
  between operations  14.6 us (6%)
  Pallas kernels  13.3 us (5%)
  other arithmetic  8.1 us (3%)
  matrix products  3.79 us (1%)
    all_to_all x7, starting transfers between devices, swap(): return lax.all_to_all(values, axis, split_axis=0, concat_axis=0)  34.8 us
    ppermute x6, starting transfers between devices, flip(): lax.ppermute(values, axes, [(i, i ^ bits) for i in range(SIZES[axes])])  31.3 us
    ppermute x10, starting transfers between devices, shift(): lax.ppermute(values, axis, [(i, (i + step) % size) for i in range(size)])  27.3 us
    all_to_all x7, waiting for transfers between devices, swap(): return lax.all_to_all(values, axis, split_axis=0, concat_axis=0)  26.5 us
    all_to_all x2, blocking collectives, swap(): return lax.all_to_all(values, axis, split_axis=0, concat_axis=0)  20.8 us
    reduce_scatter x1, waiting for transfers between devices, reduce_projector(): lax.psum_scatter(term, 'y', scatter_dimension=0, tiled=True)  20.6 us
    ppermute x6, waiting for transfers between devices, flip(): lax.ppermute(values, axes, [(i, i ^ bits) for i in range(SIZES[axes])])  18.4 us
    all_to_all x1, starting transfers between devices, reduce_dp(): terms = lax.all_to_all(terms, ('zh', 'y'), split_axis=1, concat_axis=0)  12.5 us
  transfers between devices with their start and end apart: 26, of which 12 were waited for; matrix products, arithmetic and copies ran while one was open for 7% of the time, Pallas kernels for 5%

profile of v3, /device:TPU:28, one launch (start us, length us, event | category | flops | bytes accessed | tf_op | source)
XLA Modules:
  0.0 252.4 jit_solution(2573587140614672940)
XLA Ops:
  9.0 10.9 %collective-permute-start = (bf16[2,192,384]{2,1,0:T(8,128)(2,1)S(1)}, bf16[2,192,384]{2,1,0:T(8,128)(2,1)S(1)}, u32[]{:S(2)}, u32[]{:S(2)}) collective-permute-start(bf16[2,192,384]{2,1,0:T(8,128)(2,1)S(1)} %reverse_select_fusion), channel_id=1, source_target_pairs={{0,256},{256,0},{1,257},{257,1},{2,258},{258,2},{3,259},{259,3},{4... | collective-permute-start | bytes 884744 | tf_op jit(solution)/shard_map/ppermute | solution.py:40
  21.7 3.4 %collective-permute-start.2 = (bf16[272,384]{1,0:T(8,128)(2,1)S(1)}, bf16[272,384]{1,0:T(8,128)(2,1)S(1)}, u32[]{:S(2)}, u32[]{:S(2)}) collective-permute-start(bf16[272,384]{1,0:T(8,128)(2,1)S(1)} %concatenate.14), channel_id=1, source_target_pairs={{0,4},{4,0},{8,12},{12,8},{1,5},{5,1},{9,13},{13,9},{2,6},{6,2},{1... | collective-permute-start | bytes 626696 | tf_op jit(solution)/shard_map/ppermute | solution.py:40
  26.0 7.6 %collective-permute-done = bf16[2,192,384]{2,1,0:T(8,128)(2,1)S(1)} collective-permute-done((bf16[2,192,384]{2,1,0:T(8,128)(2,1)S(1)}, bf16[2,192,384]{2,1,0:T(8,128)(2,1)S(1)}, u32[]{:S(2)}, u32[]{:S(2)}) %collective-permute-start) | collective-permute-done | bytes 294944 | tf_op jit(solution)/shard_map/ppermute | solution.py:40
  42.4 4.8 %all-to-all-start = ((bf16[4,64,1024]{2,1,0:T(8,128)(2,1)}), bf16[4,64,1024]{2,1,0:T(8,128)(2,1)S(1)}, u32[]{:S(2)}, u32[]{:S(2)}) async-start(bf16[4,64,1024]{2,1,0:T(8,128)(2,1)} %bitcast.3), calls=%async_computation | async-start | bytes 1048576 | tf_op jit(solution)/shard_map/all_to_all | solution.py:48
  55.4 6.9 %collective-permute-done.3.refs_5_ = bf16[2,272,384]{2,1,0:T(8,128)(2,1)S(1)} collective-permute-done((bf16[2,272,384]{2,1,0:T(8,128)(2,1)S(1)}, bf16[2,272,384]{2,1,0:T(8,128)(2,1)S(1)}, u32[]{:S(2)}, u32[]{:S(2)}) %collective-permute-start.3) | collective-permute-done | bytes 417824 | tf_op jit(solution)/shard_map/ppermute | solution.py:40
  75.4 9.9 %all_to_all.63 = bf16[4,16,1024]{2,1,0:T(8,128)(2,1)} all-to-all(bf16[4,16,1024]{2,1,0:T(8,128)(2,1)} %bitcast.89), channel_id=1, replica_groups=mesh['zh'=2,'y'=8,'c'=2,'zl'=4,'x'=4] {'zl'}, dimensions={0} | all-to-all | bytes 262144 | tf_op jit(solution)/shard_map/all_to_all | solution.py:48
  94.2 3.9 %all-to-all-start.2 = ((bf16[4,16,1024]{2,1,0:T(8,128)(2,1)}), bf16[4,16,1024]{2,1,0:T(8,128)(2,1)}, u32[]{:S(2)}, u32[]{:S(2)}) async-start(bf16[4,16,1024]{2,1,0:T(8,128)(2,1)} %broadcast_in_dim.14), calls=%async_computation.2 | async-start | bytes 262144 | tf_op jit(solution)/shard_map/all_to_all | solution.py:48
  98.3 5.9 %all-to-all-done.2 = bf16[4,16,1024]{2,1,0:T(8,128)(2,1)} async-done(((bf16[4,16,1024]{2,1,0:T(8,128)(2,1)}), bf16[4,16,1024]{2,1,0:T(8,128)(2,1)}, u32[]{:S(2)}, u32[]{:S(2)}) %all-to-all-start.2) | async-done | bytes 131104 | tf_op jit(solution)/shard_map/all_to_all | solution.py:48
  104.2 5.8 %teacher_norm.1.own_ref = bf16[256,6144]{1,0:T(8,128)(2,1)} custom-call(s32[3]{0:T(128)S(1)} %pad_add_fusion.place, bf16[2,272,384]{2,1,0:T(8,128)(2,1)S(1)} %pad_maximum_fusion.2.refs_0_, bf16[2,272,384]{2,1,0:T(8,128)(2,1)S(1)} %collective-permute-done.6.refs_1_, bf16[2,272,384]{2,1,0:T(8,128)(2,1)S(1)} %collective-permute-done.7.refs_2_, ...), custom_call_target="tpu_custom_call" | custom-call | flops 1000 | bytes 1000 | tf_op jit(solution)/shard_map/teacher_norm/pallas_call | solution.py:225
  113.7 7.6 %all-to-all-start.3 = ((bf16[4,64,1024]{2,1,0:T(8,128)(2,1)}), bf16[4,64,1024]{2,1,0:T(8,128)(2,1)S(1)}, u32[]{:S(2)}, u32[]{:S(2)}) async-start(bf16[4,64,1024]{2,1,0:T(8,128)(2,1)} %broadcast_in_dim.15), calls=%async_computation.3 | async-start | bytes 1048576 | tf_op jit(solution)/shard_map/all_to_all | solution.py:48
  123.6 7.4 %teacher_heads.1 = f32[2,256,128]{2,1,0:T(8,128)S(1)} custom-call(s32[1]{0:T(128)} %bitcast.10.place, bf16[256,6144]{1,0:T(8,128)(2,1)} %teacher_norm.1.own_ref, bf16[256,6144]{1,0:T(8,128)(2,1)} %collective-permute-done.12.other_ref, bf16[6144,384]{1,0:T(8,128)(2,1)S(1)} %bitcast.77, f32[2,128]{1,0:T(2,128)S(1)} %copy-done.2), custom_call_target="tpu_custom_call" | custom-call | flops 2415919104 | bytes 11000000 | tf_op jit(solution)/shard_map/teacher_heads/pallas_call | solution.py:238
  135.3 5.7 %all-to-all-start.4 = ((f32[16,2,256]{2,1,0:T(2,128)}), f32[16,2,256]{2,1,0:T(2,128)S(1)}, u32[]{:S(2)}, u32[]{:S(2)}) async-start(f32[16,2,256]{2,1,0:T(2,128)} %broadcast_in_dim.16), calls=%async_computation.4 | async-start | bytes 65536 | tf_op jit(solution)/shard_map/all_to_all | solution.py:48
  141.3 5.5 %all-to-all-done.4 = f32[16,2,256]{2,1,0:T(2,128)S(1)} async-done(((f32[16,2,256]{2,1,0:T(2,128)}), f32[16,2,256]{2,1,0:T(2,128)S(1)}, u32[]{:S(2)}, u32[]{:S(2)}) %all-to-all-start.4) | async-done | bytes 32800 | tf_op jit(solution)/shard_map/all_to_all | solution.py:48
  147.2 10.9 %all_to_all.64 = bf16[4,64,1024]{2,1,0:T(8,128)(2,1)S(1)} all-to-all(bf16[4,64,1024]{2,1,0:T(8,128)(2,1)S(1)} %bitcast.78), channel_id=1, replica_groups=mesh['zh'=2,'y'=8,'c'=2,'zl'=4,'x'=4] {'x'}, dimensions={0} | all-to-all | bytes 1048576 | tf_op jit(solution)/shard_map/all_to_all | solution.py:48
  158.8 3.3 %all-to-all-start.6 = ((bf16[4,16,1024]{2,1,0:T(8,128)(2,1)}), bf16[4,16,1024]{2,1,0:T(8,128)(2,1)S(1)}, u32[]{:S(2)}, u32[]{:S(2)}) async-start(bf16[4,16,1024]{2,1,0:T(8,128)(2,1)} %bitcast.17), calls=%async_computation.6 | async-start | bytes 262144 | tf_op jit(solution)/shard_map/all_to_all | solution.py:48
  162.6 5.4 %all-to-all-done.6 = bf16[4,16,1024]{2,1,0:T(8,128)(2,1)S(1)} async-done(((bf16[4,16,1024]{2,1,0:T(8,128)(2,1)}), bf16[4,16,1024]{2,1,0:T(8,128)(2,1)S(1)}, u32[]{:S(2)}, u32[]{:S(2)}) %all-to-all-start.6) | async-done | bytes 131104 | tf_op jit(solution)/shard_map/all_to_all | solution.py:48
  168.7 3.3 %all-to-all-start.7 = ((bf16[4,16,1024]{2,1,0:T(8,128)(2,1)}), bf16[4,16,1024]{2,1,0:T(8,128)(2,1)S(1)}, u32[]{:S(2)}, u32[]{:S(2)}) async-start(bf16[4,16,1024]{2,1,0:T(8,128)(2,1)} %broadcast_in_dim.17), calls=%async_computation.7 | async-start | bytes 262144 | tf_op jit(solution)/shard_map/all_to_all | solution.py:48
  174.0 3.9 %all-to-all-done.7 = bf16[4,16,1024]{2,1,0:T(8,128)(2,1)S(1)} async-done(((bf16[4,16,1024]{2,1,0:T(8,128)(2,1)}), bf16[4,16,1024]{2,1,0:T(8,128)(2,1)S(1)}, u32[]{:S(2)}, u32[]{:S(2)}) %all-to-all-start.7) | async-done | bytes 131104 | tf_op jit(solution)/shard_map/all_to_all | solution.py:48
  178.8 6.1 %all-to-all-start.8 = ((bf16[4,64,1024]{2,1,0:T(8,128)(2,1)}), bf16[4,64,1024]{2,1,0:T(8,128)(2,1)S(1)}, u32[]{:S(2)}, u32[]{:S(2)}) async-start(bf16[4,64,1024]{2,1,0:T(8,128)(2,1)} %broadcast_in_dim.19), calls=%async_computation.8 | async-start | bytes 1048576 | tf_op jit(solution)/shard_map/all_to_all | solution.py:48
  185.8 4.2 %all-to-all-done.8 = bf16[4,64,1024]{2,1,0:T(8,128)(2,1)S(1)} async-done(((bf16[4,64,1024]{2,1,0:T(8,128)(2,1)}), bf16[4,64,1024]{2,1,0:T(8,128)(2,1)S(1)}, u32[]{:S(2)}, u32[]{:S(2)}) %all-to-all-start.8) | async-done | bytes 524320 | tf_op jit(solution)/shard_map/all_to_all | solution.py:48
  191.5 4.6 %all_to_all.65 = bf16[1,2,16,2,32,256]{5,4,2,1,0,3:T(8,128)(2,1)S(1)} all-to-all(bf16[1,2,16,2,32,256]{5,4,2,1,0,3:T(8,128)(2,1)S(1)} %copy.61), channel_id=1, replica_groups=mesh['zh'=2,'y'=8,'c'=2,'zl'=4,'x'=4] {'c'}, dimensions={3} | all-to-all | bytes 2097152 | tf_op jit(solution)/shard_map/all_to_all | solution.py:147
  197.1 12.5 %all-to-all-start.10 = ((bf16[1,2,16,32,256]{4,3,1,0,2:T(8,128)(2,1)}), bf16[1,2,16,32,256]{4,3,1,0,2:T(8,128)(2,1)S(1)}, u32[]{:S(2)}, u32[]{:S(2)}) async-start(bf16[1,2,16,32,256]{4,3,1,0,2:T(8,128)(2,1)} %copy.55), calls=%async_computation.10 | async-start | bytes 1048576 | tf_op jit(solution)/shard_map/all_to_all | solution.py:149
  209.6 20.6 %reduce-scatter.2.cloned.1.call-done = bf16[64,256]{1,0:T(8,128)(2,1)} async-done(((bf16[512,256]{1,0:T(8,128)(2,1)}), bf16[64,256]{1,0:T(8,128)(2,1)}) %reduce-scatter.2.cloned.1.call-update) | async-done | bytes 32784 | tf_op jit(solution)/shard_map/reduce_scatter | solution.py:159
  231.0 10.8 %collective-permute-start.15 = (bf16[32,256]{1,0:T(8,128)(2,1)S(1)}, bf16[32,256]{1,0:T(8,128)(2,1)S(1)}, u32[]{:S(2)}, u32[]{:S(2)}) collective-permute-start(bf16[32,256]{1,0:T(8,128)(2,1)S(1)} %broadcast_select_fusion), channel_id=1, source_target_pairs={{0,256},{256,0},{1,257},{257,1},{2,258},{258,2},{3,259},{259,3},{4... | collective-permute-start | bytes 49160 | tf_op jit(solution)/shard_map/ppermute | solution.py:40
  (120 shorter events, 66.7 us)
Async XLA Ops:
  7.2 114.1 %all-gather.3.cloned.1.call-start = ((), (), s32[]{:S(2)}) async-start(), calls=%async_computation.13 | async-start | bytes 5308416 | tf_op jit(solution)/shard_map/all_gather | solution.py:203
  9.0 24.5 %collective-permute-start = (bf16[2,192,384]{2,1,0:T(8,128)(2,1)S(1)}, bf16[2,192,384]{2,1,0:T(8,128)(2,1)S(1)}, u32[]{:S(2)}, u32[]{:S(2)}) collective-permute-start(bf16[2,192,384]{2,1,0:T(8,128)(2,1)S(1)} %reverse_select_fusion), channel_id=1, source_target_pairs={{0,256},{256,0},{1,257},{257,1},{2,258},{258,2},{3,259},{259,3},{4... | collective-permute-start | bytes 884744 | tf_op jit(solution)/shard_map/ppermute | solution.py:40
  21.7 17.2 %collective-permute-start.2 = (bf16[272,384]{1,0:T(8,128)(2,1)S(1)}, bf16[272,384]{1,0:T(8,128)(2,1)S(1)}, u32[]{:S(2)}, u32[]{:S(2)}) collective-permute-start(bf16[272,384]{1,0:T(8,128)(2,1)S(1)} %concatenate.14), channel_id=1, source_target_pairs={{0,4},{4,0},{8,12},{12,8},{1,5},{5,1},{9,13},{13,9},{2,6},{6,2},{1... | collective-permute-start | bytes 626696 | tf_op jit(solution)/shard_map/ppermute | solution.py:40
  40.0 22.3 %collective-permute-start.3 = (bf16[2,272,384]{2,1,0:T(8,128)(2,1)S(1)}, bf16[2,272,384]{2,1,0:T(8,128)(2,1)S(1)}, u32[]{:S(2)}, u32[]{:S(2)}) collective-permute-start(bf16[2,272,384]{2,1,0:T(8,128)(2,1)S(1)} %pad_maximum_fusion.2.refs_0_), channel_id=1, source_target_pairs={{0,8},{4,12},{8,0},{12,4},{1,9},{5,13},{9,1},{13,5},{2,10},{6,14},... | collective-permute-start | bytes 1253384 | tf_op jit(solution)/shard_map/ppermute | solution.py:40
  42.4 12.2 %all-to-all-start = ((bf16[4,64,1024]{2,1,0:T(8,128)(2,1)}), bf16[4,64,1024]{2,1,0:T(8,128)(2,1)S(1)}, u32[]{:S(2)}, u32[]{:S(2)}) async-start(bf16[4,64,1024]{2,1,0:T(8,128)(2,1)} %bitcast.3), calls=%async_computation | async-start | bytes 1048576 | tf_op jit(solution)/shard_map/all_to_all | solution.py:48
  47.2 20.9 %collective-permute-start.6 = (bf16[2,272,384]{2,1,0:T(8,128)(2,1)S(1)}, bf16[2,272,384]{2,1,0:T(8,128)(2,1)S(1)}, u32[]{:S(2)}, u32[]{:S(2)}) collective-permute-start(bf16[2,272,384]{2,1,0:T(8,128)(2,1)S(1)} %pad_maximum_fusion.2.refs_0_), channel_id=1, source_target_pairs={{0,1},{1,2},{2,3},{3,0},{4,5},{5,6},{6,7},{7,4},{8,9},{9,10},{10,1... | collective-permute-start | bytes 1253384 | tf_op jit(solution)/shard_map/ppermute | solution.py:36
  50.3 21.7 %collective-permute-start.7 = (bf16[2,272,384]{2,1,0:T(8,128)(2,1)S(1)}, bf16[2,272,384]{2,1,0:T(8,128)(2,1)S(1)}, u32[]{:S(2)}, u32[]{:S(2)}) collective-permute-start(bf16[2,272,384]{2,1,0:T(8,128)(2,1)S(1)} %pad_maximum_fusion.2.refs_0_), channel_id=1, source_target_pairs={{0,3},{1,0},{2,1},{3,2},{4,7},{5,4},{6,5},{7,6},{8,11},{9,8},{10,9... | collective-permute-start | bytes 1253384 | tf_op jit(solution)/shard_map/ppermute | solution.py:36
  62.3 24.0 %collective-permute-start.4 = (bf16[2,272,384]{2,1,0:T(8,128)(2,1)S(1)}, bf16[2,272,384]{2,1,0:T(8,128)(2,1)S(1)}, u32[]{:S(2)}, u32[]{:S(2)}) collective-permute-start(bf16[2,272,384]{2,1,0:T(8,128)(2,1)S(1)} %collective-permute-done.3.refs_5_), channel_id=1, source_target_pairs={{0,1},{1,2},{2,3},{3,0},{4,5},{5,6},{6,7},{7,4},{8,9},{9,10},{10,1... | collective-permute-start | bytes 1253384 | tf_op jit(solution)/shard_map/ppermute | solution.py:36
  65.4 20.9 %collective-permute-start.5 = (bf16[2,272,384]{2,1,0:T(8,128)(2,1)S(1)}, bf16[2,272,384]{2,1,0:T(8,128)(2,1)S(1)}, u32[]{:S(2)}, u32[]{:S(2)}) collective-permute-start(bf16[2,272,384]{2,1,0:T(8,128)(2,1)S(1)} %collective-permute-done.3.refs_5_), channel_id=1, source_target_pairs={{0,3},{1,0},{2,1},{3,2},{4,7},{5,4},{6,5},{7,6},{8,11},{9,8},{10,9... | collective-permute-start | bytes 1253384 | tf_op jit(solution)/shard_map/ppermute | solution.py:36
  68.9 17.4 %collective-permute-start.8 = (bf16[1,272,384]{2,1,0:T(8,128)(2,1)}, bf16[1,272,384]{2,1,0:T(8,128)(2,1)S(1)}, u32[]{:S(2)}, u32[]{:S(2)}) collective-permute-start(bf16[1,272,384]{2,1,0:T(8,128)(2,1)} %slice.84), channel_id=1, source_target_pairs={{0,1},{1,2},{2,3},{3,0},{4,5},{5,6},{6,7},{7,4},{8,9},{9,10},{10,1... | collective-permute-start | bytes 626696 | tf_op jit(solution)/shard_map/ppermute | solution.py:36
  72.7 13.6 %collective-permute-start.9 = (bf16[1,272,384]{2,1,0:T(8,128)(2,1)}, bf16[1,272,384]{2,1,0:T(8,128)(2,1)S(1)}, u32[]{:S(2)}, u32[]{:S(2)}) collective-permute-start(bf16[1,272,384]{2,1,0:T(8,128)(2,1)} %slice.85), channel_id=1, source_target_pairs={{0,3},{1,0},{2,1},{3,2},{4,7},{5,4},{6,5},{7,6},{8,11},{9,8},{10,9... | collective-permute-start | bytes 626696 | tf_op jit(solution)/shard_map/ppermute | solution.py:36
  87.0 17.2 %collective-permute-start.10 = (bf16[1,272,384]{2,1,0:T(8,128)(2,1)}, bf16[1,272,384]{2,1,0:T(8,128)(2,1)}, u32[]{:S(2)}, u32[]{:S(2)}) collective-permute-start(bf16[1,272,384]{2,1,0:T(8,128)(2,1)} %slice.70), channel_id=1, source_target_pairs={{0,1},{1,2},{2,3},{3,0},{4,5},{5,6},{6,7},{7,4},{8,9},{9,10},{10,1... | collective-permute-start | bytes 626696 | tf_op jit(solution)/shard_map/ppermute | solution.py:36
  90.8 13.4 %collective-permute-start.11 = (bf16[1,272,384]{2,1,0:T(8,128)(2,1)}, bf16[1,272,384]{2,1,0:T(8,128)(2,1)}, u32[]{:S(2)}, u32[]{:S(2)}) collective-permute-start(bf16[1,272,384]{2,1,0:T(8,128)(2,1)} %slice.71), channel_id=1, source_target_pairs={{0,3},{1,0},{2,1},{3,2},{4,7},{5,4},{6,5},{7,6},{8,11},{9,8},{10,9... | collective-permute-start | bytes 626696 | tf_op jit(solution)/shard_map/ppermute | solution.py:36
  94.2 9.9 %all-to-all-start.2 = ((bf16[4,16,1024]{2,1,0:T(8,128)(2,1)}), bf16[4,16,1024]{2,1,0:T(8,128)(2,1)}, u32[]{:S(2)}, u32[]{:S(2)}) async-start(bf16[4,16,1024]{2,1,0:T(8,128)(2,1)} %broadcast_in_dim.14), calls=%async_computation.2 | async-start | bytes 262144 | tf_op jit(solution)/shard_map/all_to_all | solution.py:48
  110.0 11.3 %collective-permute-start.12 = (bf16[256,6144]{1,0:T(8,128)(2,1)}, bf16[256,6144]{1,0:T(8,128)(2,1)}, u32[]{:S(2)}, u32[]{:S(2)}) collective-permute-start(bf16[256,6144]{1,0:T(8,128)(2,1)} %teacher_norm.1.own_ref), channel_id=1, source_target_pairs={{0,16},{16,0},{1,17},{17,1},{2,18},{18,2},{3,19},{19,3},{4,20},{20... | collective-permute-start | bytes 9437192 | tf_op jit(solution)/shard_map/ppermute | solution.py:36
  113.7 19.5 %all-to-all-start.3 = ((bf16[4,64,1024]{2,1,0:T(8,128)(2,1)}), bf16[4,64,1024]{2,1,0:T(8,128)(2,1)S(1)}, u32[]{:S(2)}, u32[]{:S(2)}) async-start(bf16[4,64,1024]{2,1,0:T(8,128)(2,1)} %broadcast_in_dim.15), calls=%async_computation.3 | async-start | bytes 1048576 | tf_op jit(solution)/shard_map/all_to_all | solution.py:48
  135.3 11.4 %all-to-all-start.4 = ((f32[16,2,256]{2,1,0:T(2,128)}), f32[16,2,256]{2,1,0:T(2,128)S(1)}, u32[]{:S(2)}, u32[]{:S(2)}) async-start(f32[16,2,256]{2,1,0:T(2,128)} %broadcast_in_dim.16), calls=%async_computation.4 | async-start | bytes 65536 | tf_op jit(solution)/shard_map/all_to_all | solution.py:48
  158.8 9.2 %all-to-all-start.6 = ((bf16[4,16,1024]{2,1,0:T(8,128)(2,1)}), bf16[4,16,1024]{2,1,0:T(8,128)(2,1)S(1)}, u32[]{:S(2)}, u32[]{:S(2)}) async-start(bf16[4,16,1024]{2,1,0:T(8,128)(2,1)} %bitcast.17), calls=%async_computation.6 | async-start | bytes 262144 | tf_op jit(solution)/shard_map/all_to_all | solution.py:48
  168.7 9.2 %all-to-all-start.7 = ((bf16[4,16,1024]{2,1,0:T(8,128)(2,1)}), bf16[4,16,1024]{2,1,0:T(8,128)(2,1)S(1)}, u32[]{:S(2)}, u32[]{:S(2)}) async-start(bf16[4,16,1024]{2,1,0:T(8,128)(2,1)} %broadcast_in_dim.17), calls=%async_computation.7 | async-start | bytes 262144 | tf_op jit(solution)/shard_map/all_to_all | solution.py:48
  172.1 12.9 %collective-permute-start.14 = (bf16[2,8,32,256]{3,2,1,0:T(8,128)(2,1)S(1)}, bf16[2,8,32,256]{3,2,1,0:T(8,128)(2,1)S(1)}, u32[]{:S(2)}, u32[]{:S(2)}) collective-permute-start(bf16[2,8,32,256]{3,2,1,0:T(8,128)(2,1)S(1)} %fusion.13), channel_id=1, source_target_pairs={{0,16},{16,0},{1,17},{17,1},{2,18},{18,2},{3,19},{19,3},{4,20},{20... | collective-permute-start | bytes 786440 | tf_op jit(solution)/shard_map/ppermute | solution.py:40
  178.8 11.3 %all-to-all-start.8 = ((bf16[4,64,1024]{2,1,0:T(8,128)(2,1)}), bf16[4,64,1024]{2,1,0:T(8,128)(2,1)S(1)}, u32[]{:S(2)}, u32[]{:S(2)}) async-start(bf16[4,64,1024]{2,1,0:T(8,128)(2,1)} %broadcast_in_dim.19), calls=%async_computation.8 | async-start | bytes 1048576 | tf_op jit(solution)/shard_map/all_to_all | solution.py:48
  184.9 45.3 %reduce-scatter.2.cloned.1.call-start = ((), (), s32[]{:S(2)}) async-start(), calls=%async_computation.12 | async-start | bytes 294912 | tf_op jit(solution)/shard_map/reduce_scatter | solution.py:159
  197.1 47.7 %all-to-all-start.10 = ((bf16[1,2,16,32,256]{4,3,1,0,2:T(8,128)(2,1)}), bf16[1,2,16,32,256]{4,3,1,0,2:T(8,128)(2,1)S(1)}, u32[]{:S(2)}, u32[]{:S(2)}) async-start(bf16[1,2,16,32,256]{4,3,1,0,2:T(8,128)(2,1)} %copy.55), calls=%async_computation.10 | async-start | bytes 1048576 | tf_op jit(solution)/shard_map/all_to_all | solution.py:149
  231.0 12.5 %collective-permute-start.15 = (bf16[32,256]{1,0:T(8,128)(2,1)S(1)}, bf16[32,256]{1,0:T(8,128)(2,1)S(1)}, u32[]{:S(2)}, u32[]{:S(2)}) collective-permute-start(bf16[32,256]{1,0:T(8,128)(2,1)S(1)} %broadcast_select_fusion), channel_id=1, source_target_pairs={{0,256},{256,0},{1,257},{257,1},{2,258},{258,2},{3,259},{259,3},{4... | collective-permute-start | bytes 49160 | tf_op jit(solution)/shard_map/ppermute | solution.py:40
  (12 other events, 179.0 us)
Sparse Core Ops, SparseCore 0:
  40.2 61.7 all-gather.2
  188.5 41.6 reduce-scatter.1

commit v4 on v2

--- a/solution.py
+++ b/solution.py
@@ -36,8 +36,8 @@
     return lax.ppermute(values, axis, [(i, (i + step) % size) for i in range(size)])
 
 
-def flip(values, axes, bits):
-    return lax.ppermute(values, axes, [(i, i ^ bits) for i in range(4)])
+def flip(values, axes, bits=1):
+    return lax.ppermute(values, axes, [(i, i ^ bits) for i in range(SIZES[axes])])
 
 
 def tie(values, *others):
@@ -115,17 +115,24 @@
             gain = gains[0:1] + gains[1:2] + gains[2:3]
             zl = my_zl ^ dz
             xs = lax.rem(x + off, 4)
-            spot = ((zl & 1) * 4 + xs) * 2 + ((zl >> 1) ^ my_zh)
+            spot = ((zl >> 1) ^ my_zh) * 8 + (zl & 1) * 4 + xs
             d = ref[i, rows, :].astype(F32) - mean
             n_ref[rows, pl.ds(pl.multiple_of(spot * 384, 128), 384)] = (
                 d * rstd * gain
             ).astype(BF16)
 
 
-def attention_kernel(place, own_ref, other_ref, w_ref, qg_ref, f_ref):
+def near_kernel(own_ref, other_ref, w_ref, p_ref):
+    for image, ref in enumerate((own_ref, other_ref)):
+        p_ref[image] = jnp.dot(ref[:, :3072], w_ref[...], preferred_element_type=F32)
+
+
+def attention_kernel(place, own_ref, other_ref, w_ref, p_ref, qg_ref, f_ref):
     gain = jnp.where(place[0] == 0, qg_ref[0:1, :], qg_ref[1:2, :])
     for image, ref in enumerate((own_ref, other_ref)):
-        projected = jnp.dot(ref[...], w_ref[...], preferred_element_type=F32)
+        projected = p_ref[image] + jnp.dot(
+            ref[:, 3072:], w_ref[...], preferred_element_type=F32
+        )
         query = (normalize(projected[:, :128]) * gain).astype(BF16)
         key = (normalize(projected[:, 128:256]) * gain).astype(BF16)
         value = projected[:, 256:].astype(BF16)
@@ -144,6 +151,18 @@
     terms = sum_parts(terms).astype(BF16)
     terms = lax.all_to_all(terms, ("zh", "y"), split_axis=1, concat_axis=0)
     return sum_parts(terms).astype(BF16)
+
+
+def reduce_projector(term, first):
+    term = term.reshape(2, 8, 2 * 32, 256).transpose(1, 0, 2, 3).reshape(8 * 128, 256)
+    term = lax.psum_scatter(term, "y", scatter_dimension=0, tiled=True).reshape(2, 2, 32, 256)
+    theirs = flip(jnp.where(first, term[:, 1], term[:, 0]), "c")
+    mine = jnp.where(first, term[:, 0], term[:, 1])
+    term = (mine.astype(F32) + theirs.astype(F32)).astype(BF16)
+    low = lax.axis_index("zh") == 0
+    theirs = flip(jnp.where(low, term[1], term[0]), "zh")
+    mine = jnp.where(low, term[0], term[1])
+    return (mine.astype(F32) + theirs.astype(F32)).astype(BF16)
 
 
 def shards(
@@ -161,17 +180,20 @@
 
     first = lax.axis_index("c") == 0
     weight = qkv_weight.reshape(192, 3, 2, 128).transpose(2, 0, 1, 3).reshape(2, 192, 384)
-    kept = jnp.where(first, weight[0], weight[1])
-    given = jnp.where(first, weight[1], weight[0])
-    zh_kept = flip(kept, ("zh", "c"), 2)
-    zh_given = flip(given, ("zh", "c"), 3)
-    c_given = flip(given, ("zh", "c"), 1)
+    near = jnp.where(first, weight, weight[::-1])
+
+    def by_core(pair):
+        given = flip(pair[1], "c")
+        return jnp.where(first, jnp.stack([pair[0], given]), jnp.stack([given, pair[0]]))
+
+    near_rows = by_core(near)
+    near_weight = lax.all_gather(near_rows, "y").reshape(3072, 384)
 
     hi = lax.reduce_precision(teacher_gain, 8, 7)
     mid = lax.reduce_precision(teacher_gain - hi, 8, 7)
     low = teacher_gain - hi - mid
     gain_rows = jnp.stack([hi, mid, low] + [jnp.zeros_like(hi)] * 13).astype(BF16)
-    shard = tie(jnp.concatenate([teacher_in, gain_rows], axis=0), c_given)
+    shard = jnp.concatenate([teacher_in, gain_rows], axis=0)
     pair = jnp.stack([shard, flip(shard, "zl", 1)])
 
     student_normed = (normalize(student_in.astype(F32)) * student_gain).astype(BF16)
@@ -180,23 +202,17 @@
     activ = gated.astype(BF16)
     mlp_term = jnp.dot(activ, down_weight, preferred_element_type=F32).astype(BF16)
 
-    def by_core(mine, theirs):
-        return jnp.where(first, jnp.stack([mine, theirs]), jnp.stack([theirs, mine]))
-
-    zh_kept, zh_given, pair, mlp_term = lax.optimization_barrier(
-        (zh_kept, zh_given, pair, mlp_term)
-    )
-    rows = jnp.concatenate([by_core(kept, c_given), by_core(zh_kept, zh_given)])
-    weight = lax.all_gather(rows, "y").reshape(6144, 384)
-
-    part = mp_scatter_x(tie(mlp_term, rows))
-    shard = tie(jnp.concatenate([pair, flip(pair, "zl", 2)]), part)
-    from_left = shift(shard, "x", 1)
-    from_right = shift(shard, "x", -1)
-    part = mp_gather_zl(mp_scatter_zl(tie(part, shard)))
-    from_left, from_right, part = lax.optimization_barrier((from_left, from_right, part))
-    far_low = shift(from_left[:2], "x", 1)
-    far_high = shift(from_right[2:], "x", -1)
+    pair, near_rows = lax.optimization_barrier((pair, near_rows))
+    late = flip(pair, "zl", 2)
+    part = mp_scatter_x(tie(mlp_term, pair))
+    far = flip(tie(near, part), "zh")
+    shard = jnp.concatenate([pair, late])
+    left, right = shift(shard, "x", 1), shift(shard, "x", -1)
+    far_weight = lax.all_gather(by_core(far), "y").reshape(3072, 384)
+    part = mp_gather_zl(mp_scatter_zl(part))
+    left, right, part = lax.optimization_barrier((left, right, part))
+    low, high = shift(left[:2], "x", 1), shift(right[2:], "x", -1)
+    blocks = (shard, left, right, low, high)
 
     place_x = jnp.stack([lax.axis_index("x"), lax.axis_index("zl"), lax.axis_index("zh")])
     place_c = lax.axis_index("c").reshape(1)
@@ -213,20 +229,31 @@
             flops=1000, bytes_accessed=1000, transcendentals=0
         ),
         name="teacher_norm",
-    )(place_x, shard, from_left, from_right, far_low, far_high)
+    )(place_x, *blocks)
     normed_other = shift(normed, "c", 1)
     mlp_sum = mp_gather_x(tie(part, normed))
+    partial = pl.pallas_call(
+        near_kernel,
+        out_shape=jax.ShapeDtypeStruct((2, 256, 384), F32),
+        in_specs=[vmem] * 3,
+        out_specs=vmem,
+        compiler_params=params,
+        cost_estimate=pl.CostEstimate(
+            flops=512 * 6144 * 384, bytes_accessed=6_000_000, transcendentals=0
+        ),
+        name="teacher_near",
+    )(normed, normed_other, near_weight)
     heads = pl.pallas_call(
         attention_kernel,
         out_shape=jax.ShapeDtypeStruct((2, 256, 128), F32),
-        in_specs=[smem] + [vmem] * 4,
+        in_specs=[smem] + [vmem] * 5,
         out_specs=vmem,
         compiler_params=params,
         cost_estimate=pl.CostEstimate(
-            flops=2 * 512 * 6144 * 384, bytes_accessed=11_000_000, transcendentals=131072
+            flops=512 * 6144 * 384, bytes_accessed=6_000_000, transcendentals=131072
         ),
         name="teacher_heads",
-    )(place_c, normed, normed_other, weight, qk_gain)
+    )(place_c, normed, normed_other, far_weight, partial, qk_gain)
     crossed = shift(heads[1], "c", 1)
     features = jnp.where(
         place_c[0] == 0,
@@ -247,14 +274,17 @@
     grad_pred = ((predicted - target) * loss_factor).astype(BF16)
     block_term = jnp.einsum("tf,cf->tc", grad_pred, projector, preferred_element_type=F32)
     proj_term = jnp.einsum("tc,tf->cf", block_out, grad_pred, preferred_element_type=F32)
-    grad_block = mp_scatter_zl(mp_scatter_x(block_term.astype(BF16)))
+    proj_term, block_term = lax.optimization_barrier(
+        (proj_term.astype(BF16), block_term.astype(BF16))
+    )
+    grad_projector = reduce_projector(proj_term.astype(F32), first)
+    grad_block = mp_scatter_zl(mp_scatter_x(block_term))
     grad_block = mp_gather_x(mp_gather_zl(grad_block))
     down_term = jnp.einsum("tc,tf->cf", grad_block, activ, preferred_element_type=F32)
     grad_act = jnp.einsum("tc,fc->tf", grad_block, down_weight, preferred_element_type=F32)
     grad_pre = (grad_act * slope).astype(BF16)
     up_term = jnp.einsum("tc,tf->cf", student_normed, grad_pre, preferred_element_type=F32)
-    terms = jnp.stack([t.astype(BF16) for t in (up_term, down_term, proj_term)])
-    grad_up, grad_down, grad_projector = reduce_dp(terms)
+    grad_up, grad_down = reduce_dp(jnp.stack([up_term.astype(BF16), down_term.astype(BF16)]))
     return grad_up, grad_down.T, grad_projector
 
 

time: 240 us -> 248 us (1.033)
  blocking collectives: 97.4 us -> 51.5 us
  starting transfers between devices: 53.1 us -> 83.8 us
  waiting for transfers between devices: 45.2 us -> 59.4 us
  Pallas kernels: 13.3 us -> 16.2 us
  other arithmetic: 3.34 us -> 5.88 us
    all_to_all x1 -> x0, blocking collectives: 33.3 us -> none  [reduce_dp(): terms = lax.all_to_all(terms, ('zh', 'y'), split_axis=1, concat_axis=0)]
    all_to_all x0 -> x1, starting transfers between devices: none -> 13.5 us  [reduce_dp(): terms = lax.all_to_all(terms, ('zh', 'y'), split_axis=1, concat_axis=0)]
    ppermute x5 -> x7, starting transfers between devices: 20.6 us -> 33.3 us  [flip(): lax.ppermute(values, axes, [(i, i ^ bits) for i in range(SIZES[axes])])]
    all_to_all x6 -> x5, blocking collectives: 59.1 us -> 47 us  [swap(): return lax.all_to_all(values, axis, split_axis=0, concat_axis=0)]
    all_to_all x0 -> x1, waiting for transfers between devices: none -> 6.6 us  [reduce_dp(): terms = lax.all_to_all(terms, ('zh', 'y'), split_axis=1, concat_axis=0)]
    ppermute x5 -> x7, waiting for transfers between devices: 19.3 us -> 25 us  [flip(): lax.ppermute(values, axes, [(i, i ^ bits) for i in range(SIZES[axes])])]
    pallas_call x0 -> x1, Pallas kernels: none -> 4.66 us  [shards(): pl.pallas_call(near_kernel, out_shape=jax.ShapeDtypeStruct((2, 256, 384),...]
    all_to_all x3 -> x4, starting transfers between devices: 14.2 us -> 18.8 us  [swap(): return lax.all_to_all(values, axis, split_axis=0, concat_axis=0)]
  transfers between devices with their start and end apart: 15 -> 21, of which waited for: 9 -> 13; matrix products, arithmetic and copies ran while one was open for 2% -> 5% of each run, Pallas kernels for 6% -> 7%
where the time goes in v4:
time: 248 us; the launch traced here: 247 us
  starting transfers between devices  83.8 us (34%)
  waiting for transfers between devices  59.4 us (24%)
  blocking collectives  51.5 us (21%)
  Pallas kernels  16.2 us (7%)
  between operations  14.4 us (6%)
  local copies, waits for them, and re-layouts  11.1 us (4%)
  other arithmetic  5.88 us (2%)
  matrix products  4.7 us (2%)
    all_to_all x5, blocking collectives, swap(): return lax.all_to_all(values, axis, split_axis=0, concat_axis=0)  47 us
    ppermute x7, starting transfers between devices, flip(): lax.ppermute(values, axes, [(i, i ^ bits) for i in range(SIZES[axes])])  33.3 us
    ppermute x7, waiting for transfers between devices, flip(): lax.ppermute(values, axes, [(i, i ^ bits) for i in range(SIZES[axes])])  25 us
    all_to_all x4, waiting for transfers between devices, swap(): return lax.all_to_all(values, axis, split_axis=0, concat_axis=0)  19 us
    all_to_all x4, starting transfers between devices, swap(): return lax.all_to_all(values, axis, split_axis=0, concat_axis=0)  18.8 us
    ppermute x6, starting transfers between devices, shift(): lax.ppermute(values, axis, [(i, (i + step) % size) for i in range(size)])  18 us
    all_to_all x1, starting transfers between devices, reduce_dp(): terms = lax.all_to_all(terms, ('zh', 'y'), split_axis=1, concat_axis=0)  13.5 us
    ppermute x6, waiting for transfers between devices, shift(): lax.ppermute(values, axis, [(i, (i + step) % size) for i in range(size)])  8.12 us
  transfers between devices with their start and end apart: 21, of which 13 were waited for; matrix products, arithmetic and copies ran while one was open for 5% of the time, Pallas kernels for 7%

profile of v4, /device:TPU:8, one launch (start us, length us, event | category | flops | bytes accessed | tf_op | source)
XLA Modules:
  0.0 247.0 jit_solution(13206821638966856309)
XLA Ops:
  13.4 4.3 %collective-permute-start = (bf16[272,384]{1,0:T(8,128)(2,1)S(1)}, bf16[272,384]{1,0:T(8,128)(2,1)S(1)}, u32[]{:S(2)}, u32[]{:S(2)}) collective-permute-start(bf16[272,384]{1,0:T(8,128)(2,1)S(1)} %concatenate.42), channel_id=1, source_target_pairs={{0,4},{4,0},{8,12},{12,8},{1,5},{5,1},{9,13},{13,9},{2,6},{6,2},{1... | collective-permute-start | bytes 626696 | tf_op jit(solution)/shard_map/ppermute | solution.py:40
  23.2 4.3 %all-to-all-start = ((bf16[4,64,1024]{2,1,0:T(8,128)(2,1)}), bf16[4,64,1024]{2,1,0:T(8,128)(2,1)S(1)}, u32[]{:S(2)}, u32[]{:S(2)}) async-start(bf16[4,64,1024]{2,1,0:T(8,128)(2,1)} %bitcast.2), calls=%async_computation | async-start | bytes 1048576 | tf_op jit(solution)/shard_map/all_to_all | solution.py:48
  27.5 6.1 %collective-permute-start.1 = (bf16[2,272,384]{2,1,0:T(8,128)(2,1)S(1)}, bf16[2,272,384]{2,1,0:T(8,128)(2,1)S(1)}, u32[]{:S(2)}, u32[]{:S(2)}) collective-permute-start(bf16[2,272,384]{2,1,0:T(8,128)(2,1)S(1)} %pad_maximum_fusion.2), channel_id=1, source_target_pairs={{0,8},{4,12},{8,0},{12,4},{1,9},{5,13},{9,1},{13,5},{2,10},{6,14},... | collective-permute-start | bytes 1253384 | tf_op jit(solution)/shard_map/ppermute | solution.py:40
  36.8 10.0 %collective-permute-start.7 = (bf16[2,192,384]{2,1,0:T(8,128)(2,1)S(1)}, bf16[2,192,384]{2,1,0:T(8,128)(2,1)S(1)}, u32[]{:S(2)}, u32[]{:S(2)}) collective-permute-start(bf16[2,192,384]{2,1,0:T(8,128)(2,1)S(1)} %reverse_select_fusion), channel_id=1, source_target_pairs={{0,256},{256,0},{1,257},{257,1},{2,258},{258,2},{3,259},{259,3},{4... | collective-permute-start | bytes 884744 | tf_op jit(solution)/shard_map/ppermute | solution.py:40
  46.8 17.6 %collective-permute-done.1 = bf16[2,272,384]{2,1,0:T(8,128)(2,1)S(1)} collective-permute-done((bf16[2,272,384]{2,1,0:T(8,128)(2,1)S(1)}, bf16[2,272,384]{2,1,0:T(8,128)(2,1)S(1)}, u32[]{:S(2)}, u32[]{:S(2)}) %collective-permute-start.1) | collective-permute-done | bytes 417824 | tf_op jit(solution)/shard_map/ppermute | solution.py:40
  64.5 3.7 %collective-permute-start.2 = (bf16[4,272,384]{2,1,0:T(8,128)(2,1)S(1)}, bf16[4,272,384]{2,1,0:T(8,128)(2,1)S(1)}, u32[]{:S(2)}, u32[]{:S(2)}) collective-permute-start(bf16[4,272,384]{2,1,0:T(8,128)(2,1)S(1)} %pad_maximum_fusion.1.a0_ref), channel_id=1, source_target_pairs={{0,1},{1,2},{2,3},{3,0},{4,5},{5,6},{6,7},{7,4},{8,9},{9,10},{10,1... | collective-permute-start | bytes 2506760 | tf_op jit(solution)/shard_map/ppermute | solution.py:36
  75.7 10.8 %all_to_all.63 = bf16[4,16,1024]{2,1,0:T(8,128)(2,1)S(1)} all-to-all(bf16[4,16,1024]{2,1,0:T(8,128)(2,1)S(1)} %bitcast.110), channel_id=1, replica_groups=mesh['zh'=2,'y'=8,'c'=2,'zl'=4,'x'=4] {'zl'}, dimensions={0} | all-to-all | bytes 262144 | tf_op jit(solution)/shard_map/all_to_all | solution.py:48
  86.5 9.0 %all_to_all.64 = bf16[4,16,1024]{2,1,0:T(8,128)(2,1)} all-to-all(bf16[4,16,1024]{2,1,0:T(8,128)(2,1)S(1)} %broadcast_in_dim.14), channel_id=1, replica_groups=mesh['zh'=2,'y'=8,'c'=2,'zl'=4,'x'=4] {'zl'}, dimensions={0} | all-to-all | bytes 262144 | tf_op jit(solution)/shard_map/all_to_all | solution.py:48
  99.5 4.6 %collective-permute-start.5 = (bf16[2,272,384]{2,1,0:T(8,128)(2,1)}, bf16[2,272,384]{2,1,0:T(8,128)(2,1)}, u32[]{:S(2)}, u32[]{:S(2)}) collective-permute-start(bf16[2,272,384]{2,1,0:T(8,128)(2,1)} %slice.51), channel_id=1, source_target_pairs={{0,3},{1,0},{2,1},{3,2},{4,7},{5,4},{6,5},{7,6},{8,11},{9,8},{10,9... | collective-permute-start | bytes 1253384 | tf_op jit(solution)/shard_map/ppermute | solution.py:36
  104.2 5.0 %collective-permute-done.4.lo_ref = bf16[2,272,384]{2,1,0:T(8,128)(2,1)S(1)} collective-permute-done((bf16[2,272,384]{2,1,0:T(8,128)(2,1)}, bf16[2,272,384]{2,1,0:T(8,128)(2,1)S(1)}, u32[]{:S(2)}, u32[]{:S(2)}) %collective-permute-start.4) | collective-permute-done | bytes 417824 | tf_op jit(solution)/shard_map/ppermute | solution.py:36
  111.2 5.7 %teacher_norm.1.own_ref = bf16[256,6144]{1,0:T(8,128)(2,1)} custom-call(s32[3]{0:T(128)S(1)} %pad_add_fusion.place, bf16[4,272,384]{2,1,0:T(8,128)(2,1)S(1)} %pad_maximum_fusion.1.a0_ref, bf16[4,272,384]{2,1,0:T(8,128)(2,1)S(1)} %collective-permute-done.2.am_ref, bf16[4,272,384]{2,1,0:T(8,128)(2,1)S(1)} %collective-permute-done.3.ap_ref, ...), custom_call_target="tpu_custom_call" | custom-call | flops 1000 | bytes 1000 | tf_op jit(solution)/shard_map/teacher_norm/pallas_call | solution.py:222
  119.7 5.0 %all-to-all-start.3 = ((bf16[4,64,1024]{2,1,0:T(8,128)(2,1)}), bf16[4,64,1024]{2,1,0:T(8,128)(2,1)S(1)}, u32[]{:S(2)}, u32[]{:S(2)}) async-start(bf16[4,64,1024]{2,1,0:T(8,128)(2,1)} %broadcast_in_dim.15), calls=%async_computation.3 | async-start | bytes 1048576 | tf_op jit(solution)/shard_map/all_to_all | solution.py:48
  126.5 4.7 %teacher_near.1.p_ref = f32[2,256,384]{2,1,0:T(8,128)S(1)} custom-call(bf16[256,6144]{1,0:T(8,128)(2,1)} %teacher_norm.1.own_ref, bf16[256,6144]{1,0:T(8,128)(2,1)} %collective-permute-done.6.other_ref, bf16[3072,384]{1,0:T(8,128)(2,1)S(1)} %bitcast.97), custom_call_target="tpu_custom_call" | custom-call | flops 1207959552 | bytes 6000000 | tf_op jit(solution)/shard_map/teacher_near/pallas_call | solution.py:235
  132.9 5.8 %teacher_heads.1 = f32[2,256,128]{2,1,0:T(8,128)S(1)} custom-call(s32[1]{0:T(128)} %bitcast.9.place, bf16[256,6144]{1,0:T(8,128)(2,1)} %teacher_norm.1.own_ref, bf16[256,6144]{1,0:T(8,128)(2,1)} %collective-permute-done.6.other_ref, bf16[3072,384]{1,0:T(8,128)(2,1)S(1)} %bitcast.96, f32[2,256,384]{2,1,0:T(8,128)S(1)} %teacher_near.1.p_ref, ...), custom_call_target="tpu_custom_call" | custom-call | flops 1207959552 | bytes 6000000 | tf_op jit(solution)/shard_map/teacher_heads/pallas_call | solution.py:246
  142.9 6.1 %all-to-all-start.4 = ((f32[16,2,256]{2,1,0:T(2,128)}), f32[16,2,256]{2,1,0:T(2,128)S(1)}, u32[]{:S(2)}, u32[]{:S(2)}) async-start(f32[16,2,256]{2,1,0:T(2,128)} %broadcast_in_dim.16), calls=%async_computation.4 | async-start | bytes 65536 | tf_op jit(solution)/shard_map/all_to_all | solution.py:48
  149.4 7.8 %all-to-all-done.4 = f32[16,2,256]{2,1,0:T(2,128)S(1)} async-done(((f32[16,2,256]{2,1,0:T(2,128)}), f32[16,2,256]{2,1,0:T(2,128)S(1)}, u32[]{:S(2)}, u32[]{:S(2)}) %all-to-all-start.4) | async-done | bytes 32800 | tf_op jit(solution)/shard_map/all_to_all | solution.py:48
  164.2 8.0 %all-to-all-done.5 = bf16[4,64,1024]{2,1,0:T(8,128)(2,1)S(1)} async-done(((bf16[4,64,1024]{2,1,0:T(8,128)(2,1)}), bf16[4,64,1024]{2,1,0:T(8,128)(2,1)S(1)}, u32[]{:S(2)}, u32[]{:S(2)}) %all-to-all-start.5) | async-done | bytes 524320 | tf_op jit(solution)/shard_map/all_to_all | solution.py:48
  172.3 8.3 %all_to_all.65 = bf16[4,16,1024]{2,1,0:T(8,128)(2,1)S(1)} all-to-all(bf16[4,16,1024]{2,1,0:T(8,128)(2,1)S(1)} %bitcast.111), channel_id=1, replica_groups=mesh['zh'=2,'y'=8,'c'=2,'zl'=4,'x'=4] {'zl'}, dimensions={0} | all-to-all | bytes 262144 | tf_op jit(solution)/shard_map/all_to_all | solution.py:48
  180.6 8.4 %all_to_all.66 = bf16[4,16,1024]{2,1,0:T(8,128)(2,1)S(1)} all-to-all(bf16[4,16,1024]{2,1,0:T(8,128)(2,1)S(1)} %broadcast_in_dim.17), channel_id=1, replica_groups=mesh['zh'=2,'y'=8,'c'=2,'zl'=4,'x'=4] {'zl'}, dimensions={0} | all-to-all | bytes 262144 | tf_op jit(solution)/shard_map/all_to_all | solution.py:48
  189.1 10.5 %all_to_all.67 = bf16[4,64,1024]{2,1,0:T(8,128)(2,1)S(1)} all-to-all(bf16[4,64,1024]{2,1,0:T(8,128)(2,1)S(1)} %broadcast_in_dim.19), channel_id=1, replica_groups=mesh['zh'=2,'y'=8,'c'=2,'zl'=4,'x'=4] {'x'}, dimensions={0} | all-to-all | bytes 1048576 | tf_op jit(solution)/shard_map/all_to_all | solution.py:48
  201.1 4.6 %all_to_all.68 = bf16[1,2,16,2,32,256]{5,4,2,1,0,3:T(8,128)(2,1)S(1)} all-to-all(bf16[1,2,16,2,32,256]{5,4,2,1,0,3:T(8,128)(2,1)S(1)} %copy.56), channel_id=1, replica_groups=mesh['zh'=2,'y'=8,'c'=2,'zl'=4,'x'=4] {'c'}, dimensions={3} | all-to-all | bytes 2097152 | tf_op jit(solution)/shard_map/all_to_all | solution.py:150
  206.8 13.5 %all-to-all-start.10 = ((bf16[1,2,16,32,256]{4,3,1,0,2:T(8,128)(2,1)}), bf16[1,2,16,32,256]{4,3,1,0,2:T(8,128)(2,1)S(1)}, u32[]{:S(2)}, u32[]{:S(2)}) async-start(bf16[1,2,16,32,256]{4,3,1,0,2:T(8,128)(2,1)} %copy.50), calls=%async_computation.10 | async-start | bytes 1048576 | tf_op jit(solution)/shard_map/all_to_all | solution.py:152
  225.3 7.3 %collective-permute-start.12 = (bf16[32,256]{1,0:T(8,128)(2,1)S(1)}, bf16[32,256]{1,0:T(8,128)(2,1)S(1)}, u32[]{:S(2)}, u32[]{:S(2)}) collective-permute-start(bf16[32,256]{1,0:T(8,128)(2,1)S(1)} %select_bitcast_fusion.1), channel_id=1, source_target_pairs={{0,256},{256,0},{1,257},{257,1},{2,258},{258,2},{3,259},{259,3},{4... | collective-permute-start | bytes 49160 | tf_op jit(solution)/shard_map/ppermute | solution.py:40
  232.5 6.6 %all-to-all-done.10 = bf16[1,2,16,32,256]{4,3,1,0,2:T(8,128)(2,1)S(1)} async-done(((bf16[1,2,16,32,256]{4,3,1,0,2:T(8,128)(2,1)}), bf16[1,2,16,32,256]{4,3,1,0,2:T(8,128)(2,1)S(1)}, u32[]{:S(2)}, u32[]{:S(2)}) %all-to-all-start.10) | async-done | bytes 524320 | tf_op jit(solution)/shard_map/all_to_all | solution.py:152
  (120 shorter events, 55.3 us)
Async XLA Ops:
  7.2 117.4 %all-gather.5.cloned.1.call-start = ((), (), s32[]{:S(2)}) async-start(), calls=%async_computation.13 | async-start | bytes 2654208 | tf_op jit(solution)/shard_map/all_gather | solution.py:190
  9.1 3.3 %collective-permute-start.9 = (bf16[192,384]{1,0:T(8,128)(2,1)S(1)}, bf16[192,384]{1,0:T(8,128)(2,1)S(1)}, u32[]{:S(2)}, u32[]{:S(2)}) collective-permute-start(bf16[192,384]{1,0:T(8,128)(2,1)S(1)} %get-tuple-element.22), channel_id=1, source_target_pairs={{0,16},{16,0},{1,17},{17,1},{2,18},{18,2},{3,19},{19,3},{4,20},{20... | collective-permute-start | bytes 442376 | tf_op jit(solution)/shard_map/ppermute | solution.py:40
  13.4 9.7 %collective-permute-start = (bf16[272,384]{1,0:T(8,128)(2,1)S(1)}, bf16[272,384]{1,0:T(8,128)(2,1)S(1)}, u32[]{:S(2)}, u32[]{:S(2)}) collective-permute-start(bf16[272,384]{1,0:T(8,128)(2,1)S(1)} %concatenate.42), channel_id=1, source_target_pairs={{0,4},{4,0},{8,12},{12,8},{1,5},{5,1},{9,13},{13,9},{2,6},{6,2},{1... | collective-permute-start | bytes 626696 | tf_op jit(solution)/shard_map/ppermute | solution.py:40
  18.5 28.3 %copy-start.7 = (f32[256,256]{1,0:T(8,128)}, f32[256,256]{1,0:T(8,128)S(1)}, u32[]{:S(2)}) copy-start(f32[256,256]{1,0:T(8,128)S(1)} %fusion.33) | copy-start | bytes 786436
  23.2 13.6 %all-to-all-start = ((bf16[4,64,1024]{2,1,0:T(8,128)(2,1)}), bf16[4,64,1024]{2,1,0:T(8,128)(2,1)S(1)}, u32[]{:S(2)}, u32[]{:S(2)}) async-start(bf16[4,64,1024]{2,1,0:T(8,128)(2,1)} %bitcast.2), calls=%async_computation | async-start | bytes 1048576 | tf_op jit(solution)/shard_map/all_to_all | solution.py:48
  27.5 103.7 %all-gather.3.cloned.1.call-start = ((), (), s32[]{:S(2)}) async-start(), calls=%async_computation.12 | async-start | bytes 2654208 | tf_op jit(solution)/shard_map/all_gather | solution.py:211
  27.5 36.9 %collective-permute-start.1 = (bf16[2,272,384]{2,1,0:T(8,128)(2,1)S(1)}, bf16[2,272,384]{2,1,0:T(8,128)(2,1)S(1)}, u32[]{:S(2)}, u32[]{:S(2)}) collective-permute-start(bf16[2,272,384]{2,1,0:T(8,128)(2,1)S(1)} %pad_maximum_fusion.2), channel_id=1, source_target_pairs={{0,8},{4,12},{8,0},{12,4},{1,9},{5,13},{9,1},{13,5},{2,10},{6,14},... | collective-permute-start | bytes 1253384 | tf_op jit(solution)/shard_map/ppermute | solution.py:40
  36.8 34.7 %collective-permute-start.7 = (bf16[2,192,384]{2,1,0:T(8,128)(2,1)S(1)}, bf16[2,192,384]{2,1,0:T(8,128)(2,1)S(1)}, u32[]{:S(2)}, u32[]{:S(2)}) collective-permute-start(bf16[2,192,384]{2,1,0:T(8,128)(2,1)S(1)} %reverse_select_fusion), channel_id=1, source_target_pairs={{0,256},{256,0},{1,257},{257,1},{2,258},{258,2},{3,259},{259,3},{4... | collective-permute-start | bytes 884744 | tf_op jit(solution)/shard_map/ppermute | solution.py:40
  64.5 31.0 %collective-permute-start.2 = (bf16[4,272,384]{2,1,0:T(8,128)(2,1)S(1)}, bf16[4,272,384]{2,1,0:T(8,128)(2,1)S(1)}, u32[]{:S(2)}, u32[]{:S(2)}) collective-permute-start(bf16[4,272,384]{2,1,0:T(8,128)(2,1)S(1)} %pad_maximum_fusion.1.a0_ref), channel_id=1, source_target_pairs={{0,1},{1,2},{2,3},{3,0},{4,5},{5,6},{6,7},{7,4},{8,9},{9,10},{10,1... | collective-permute-start | bytes 2506760 | tf_op jit(solution)/shard_map/ppermute | solution.py:36
  68.1 27.3 %collective-permute-start.3 = (bf16[4,272,384]{2,1,0:T(8,128)(2,1)S(1)}, bf16[4,272,384]{2,1,0:T(8,128)(2,1)S(1)}, u32[]{:S(2)}, u32[]{:S(2)}) collective-permute-start(bf16[4,272,384]{2,1,0:T(8,128)(2,1)S(1)} %pad_maximum_fusion.1.a0_ref), channel_id=1, source_target_pairs={{0,3},{1,0},{2,1},{3,2},{4,7},{5,4},{6,5},{7,6},{8,11},{9,8},{10,9... | collective-permute-start | bytes 2506760 | tf_op jit(solution)/shard_map/ppermute | solution.py:36
  71.6 3.3 %collective-permute-start.8 = (bf16[192,384]{1,0:T(8,128)(2,1)S(1)}, bf16[192,384]{1,0:T(8,128)(2,1)S(1)}, u32[]{:S(2)}, u32[]{:S(2)}) collective-permute-start(bf16[192,384]{1,0:T(8,128)(2,1)S(1)} %get-tuple-element.24), channel_id=1, source_target_pairs={{0,16},{16,0},{1,17},{17,1},{2,18},{18,2},{3,19},{19,3},{4,20},{20... | collective-permute-start | bytes 442376 | tf_op jit(solution)/shard_map/ppermute | solution.py:40
  96.3 12.9 %collective-permute-start.4 = (bf16[2,272,384]{2,1,0:T(8,128)(2,1)}, bf16[2,272,384]{2,1,0:T(8,128)(2,1)S(1)}, u32[]{:S(2)}, u32[]{:S(2)}) collective-permute-start(bf16[2,272,384]{2,1,0:T(8,128)(2,1)} %slice.50), channel_id=1, source_target_pairs={{0,1},{1,2},{2,3},{3,0},{4,5},{5,6},{6,7},{7,4},{8,9},{9,10},{10,1... | collective-permute-start | bytes 1253384 | tf_op jit(solution)/shard_map/ppermute | solution.py:36
  99.5 11.7 %collective-permute-start.5 = (bf16[2,272,384]{2,1,0:T(8,128)(2,1)}, bf16[2,272,384]{2,1,0:T(8,128)(2,1)}, u32[]{:S(2)}, u32[]{:S(2)}) collective-permute-start(bf16[2,272,384]{2,1,0:T(8,128)(2,1)} %slice.51), channel_id=1, source_target_pairs={{0,3},{1,0},{2,1},{3,2},{4,7},{5,4},{6,5},{7,6},{8,11},{9,8},{10,9... | collective-permute-start | bytes 1253384 | tf_op jit(solution)/shard_map/ppermute | solution.py:36
  116.9 7.9 %collective-permute-start.6 = (bf16[256,6144]{1,0:T(8,128)(2,1)}, bf16[256,6144]{1,0:T(8,128)(2,1)}, u32[]{:S(2)}, u32[]{:S(2)}) collective-permute-start(bf16[256,6144]{1,0:T(8,128)(2,1)} %teacher_norm.1.own_ref), channel_id=1, source_target_pairs={{0,16},{16,0},{1,17},{17,1},{2,18},{18,2},{3,19},{19,3},{4,20},{20... | collective-permute-start | bytes 9437192 | tf_op jit(solution)/shard_map/ppermute | solution.py:36
  119.7 21.1 %all-to-all-start.3 = ((bf16[4,64,1024]{2,1,0:T(8,128)(2,1)}), bf16[4,64,1024]{2,1,0:T(8,128)(2,1)S(1)}, u32[]{:S(2)}, u32[]{:S(2)}) async-start(bf16[4,64,1024]{2,1,0:T(8,128)(2,1)} %broadcast_in_dim.15), calls=%async_computation.3 | async-start | bytes 1048576 | tf_op jit(solution)/shard_map/all_to_all | solution.py:48
  132.9 16.2 %copy-start.6 = (bf16[1024,256]{1,0:T(8,128)(2,1)S(1)}, bf16[1024,256]{1,0:T(8,128)(2,1)}, u32[]{:S(2)}) copy-start(bf16[1024,256]{1,0:T(8,128)(2,1)} %param.17) | copy-start | bytes 1572868
  138.7 3.2 %collective-permute-start.10 = (f32[256,128]{1,0:T(8,128)S(1)}, f32[256,128]{1,0:T(8,128)S(1)}, u32[]{:S(2)}, u32[]{:S(2)}) collective-permute-start(f32[256,128]{1,0:T(8,128)S(1)} %get-tuple-element.25), channel_id=1, source_target_pairs={{0,16},{16,0},{1,17},{17,1},{2,18},{18,2},{3,19},{19,3},{4,20},{20... | collective-permute-start | bytes 393224 | tf_op jit(solution)/shard_map/ppermute | solution.py:36
  142.9 14.2 %all-to-all-start.4 = ((f32[16,2,256]{2,1,0:T(2,128)}), f32[16,2,256]{2,1,0:T(2,128)S(1)}, u32[]{:S(2)}, u32[]{:S(2)}) async-start(f32[16,2,256]{2,1,0:T(2,128)} %broadcast_in_dim.16), calls=%async_computation.4 | async-start | bytes 65536 | tf_op jit(solution)/shard_map/all_to_all | solution.py:48
  158.9 40.7 %copy-start.8 = (f32[256,256]{1,0:T(8,128)S(1)}, f32[256,256]{1,0:T(8,128)}, u32[]{:S(2)}) copy-start(f32[256,256]{1,0:T(8,128)} %copy-done.7) | copy-start | bytes 786436
  160.0 12.2 %all-to-all-start.5 = ((bf16[4,64,1024]{2,1,0:T(8,128)(2,1)}), bf16[4,64,1024]{2,1,0:T(8,128)(2,1)S(1)}, u32[]{:S(2)}, u32[]{:S(2)}) async-start(bf16[4,64,1024]{2,1,0:T(8,128)(2,1)} %bitcast.23), calls=%async_computation.5 | async-start | bytes 1048576 | tf_op jit(solution)/shard_map/all_to_all | solution.py:48
  163.5 56.8 %reduce-scatter.2.cloned.1.call-start = ((), (), s32[]{:S(2)}) async-start(), calls=%async_computation.14 | async-start | bytes 1179648 | tf_op jit(solution)/shard_map/reduce_scatter | solution.py:158
  206.8 32.3 %all-to-all-start.10 = ((bf16[1,2,16,32,256]{4,3,1,0,2:T(8,128)(2,1)}), bf16[1,2,16,32,256]{4,3,1,0,2:T(8,128)(2,1)S(1)}, u32[]{:S(2)}, u32[]{:S(2)}) async-start(bf16[1,2,16,32,256]{4,3,1,0,2:T(8,128)(2,1)} %copy.50), calls=%async_computation.10 | async-start | bytes 1048576 | tf_op jit(solution)/shard_map/all_to_all | solution.py:152
  221.2 3.1 %collective-permute-start.11 = (f32[2,32,256]{2,1,0:T(8,128)S(1)}, f32[2,32,256]{2,1,0:T(8,128)S(1)}, u32[]{:S(2)}, u32[]{:S(2)}) collective-permute-start(f32[2,32,256]{2,1,0:T(8,128)S(1)} %select_bitcast_fusion), channel_id=1, source_target_pairs={{0,16},{16,0},{1,17},{17,1},{2,18},{18,2},{3,19},{19,3},{4,20},{20... | collective-permute-start | bytes 196616 | tf_op jit(solution)/shard_map/ppermute | solution.py:40
  225.3 14.6 %collective-permute-start.12 = (bf16[32,256]{1,0:T(8,128)(2,1)S(1)}, bf16[32,256]{1,0:T(8,128)(2,1)S(1)}, u32[]{:S(2)}, u32[]{:S(2)}) collective-permute-start(bf16[32,256]{1,0:T(8,128)(2,1)S(1)} %select_bitcast_fusion.1), channel_id=1, source_target_pairs={{0,256},{256,0},{1,257},{257,1},{2,258},{258,2},{3,259},{259,3},{4... | collective-permute-start | bytes 49160 | tf_op jit(solution)/shard_map/ppermute | solution.py:40
  (11 other events, 86.1 us)
Sparse Core Ops, SparseCore 0:
  13.2 48.2 all-gather.4
  75.8 44.8 all-gather.2
  167.1 43.1 reduce-scatter.1

commit v5 on v4

--- a/solution.py
+++ b/solution.py
@@ -85,31 +85,62 @@
     return mean, spreads / (count * 16)
 
 
-def norm_kernel(place, a0_ref, am_ref, ap_ref, lo_ref, hi_ref, n_ref):
-    x, my_zl, my_zh = place[0], place[1], place[2]
+def block_list(refs):
     blocks = []
-    for i in range(4):
-        blocks.append((a0_ref, i, i, 0))
-        blocks.append((am_ref, i, i, 3))
-        blocks.append((ap_ref, i, i, 1))
-        blocks.append((lo_ref if i < 2 else hi_ref, i % 2, i, 2))
-    width = 16 * 384
-
+    for half in range(len(refs) // 5):
+        own, left, right, low, high = refs[5 * half : 5 * half + 5]
+        for i in range(2):
+            blocks.append((own, i, 2 * half + i, 0))
+            blocks.append((left, i, 2 * half + i, 3))
+            blocks.append((right, i, 2 * half + i, 1))
+        blocks.append((low, 0, 2 * half, 2))
+        blocks.append((high, 0, 2 * half + 1, 2))
+    return blocks
+
+
+def block_stats(blocks, rows):
     def fold(values):
         return values[:, :128] + values[:, 128:256] + values[:, 256:]
+
+    total = jnp.zeros((32, 128), F32)
+    for ref, i, dz, off in blocks:
+        total += fold(ref[i, rows, :].astype(F32))
+    total = jnp.sum(total, axis=1, keepdims=True)
+    mean = total / (len(blocks) * 384)
+    square = jnp.zeros((32, 128), F32)
+    for ref, i, dz, off in blocks:
+        d = ref[i, rows, :].astype(F32) - mean
+        square += fold(d * d)
+    return total, jnp.sum(square, axis=1, keepdims=True)
+
+
+def stats_kernel(*refs):
+    out_ref = refs[-1]
+    blocks = block_list(list(refs[:8]) + [None, None])[:14]
 
     @pl.loop(0, 8)
     def _(t):
         rows = pl.ds(pl.multiple_of(t * 32, 32), 32)
-        total = jnp.zeros((32, 128), F32)
-        for ref, i, dz, off in blocks:
-            total += fold(ref[i, rows, :].astype(F32))
-        mean = jnp.sum(total, axis=1, keepdims=True) / width
-        total = jnp.zeros((32, 128), F32)
-        for ref, i, dz, off in blocks:
-            d = ref[i, rows, :].astype(F32) - mean
-            total += fold(d * d)
-        rstd = lax.rsqrt(jnp.sum(total, axis=1, keepdims=True) / width + EPSILON)
+        total, square = block_stats(blocks, rows)
+        out_ref[0, rows, :] = jnp.broadcast_to(total, (32, 128))
+        out_ref[1, rows, :] = jnp.broadcast_to(square, (32, 128))
+
+
+def norm_kernel(place, stats_ref, *refs):
+    n_ref = refs[-1]
+    x, my_zl, my_zh = place[0], place[1], place[2]
+    blocks = block_list(refs[:10])
+    width, early, last = 16 * 384, 14 * 384, 2 * 384
+
+    @pl.loop(0, 8)
+    def _(t):
+        rows = pl.ds(pl.multiple_of(t * 32, 32), 32)
+        total, square = block_stats(blocks[14:], rows)
+        first_total = stats_ref[0, rows, :][:, :1]
+        mean = (first_total + total) / width
+        apart = first_total / early - total / last
+        square += stats_ref[1, rows, :][:, :1] + apart * apart * (early * last / width)
+        rstd = lax.rsqrt(square / width + EPSILON)
         for ref, i, dz, off in blocks:
             gains = ref[i, 256:272, :].astype(F32)
             gain = gains[0:1] + gains[1:2] + gains[2:3]
@@ -153,18 +184,6 @@
     return sum_parts(terms).astype(BF16)
 
 
-def reduce_projector(term, first):
-    term = term.reshape(2, 8, 2 * 32, 256).transpose(1, 0, 2, 3).reshape(8 * 128, 256)
-    term = lax.psum_scatter(term, "y", scatter_dimension=0, tiled=True).reshape(2, 2, 32, 256)
-    theirs = flip(jnp.where(first, term[:, 1], term[:, 0]), "c")
-    mine = jnp.where(first, term[:, 0], term[:, 1])
-    term = (mine.astype(F32) + theirs.astype(F32)).astype(BF16)
-    low = lax.axis_index("zh") == 0
-    theirs = flip(jnp.where(low, term[1], term[0]), "zh")
-    mine = jnp.where(low, term[0], term[1])
-    return (mine.astype(F32) + theirs.astype(F32)).astype(BF16)
-
-
 def shards(
     teacher_in,
     teacher_gain,
@@ -187,6 +206,7 @@
         return jnp.where(first, jnp.stack([pair[0], given]), jnp.stack([given, pair[0]]))
 
     near_rows = by_core(near)
+    far_rows = by_core(flip(near, "zh"))
     near_weight = lax.all_gather(near_rows, "y").reshape(3072, 384)
 
     hi = lax.reduce_precision(teacher_gain, 8, 7)
@@ -204,32 +224,49 @@
 
     pair, near_rows = lax.optimization_barrier((pair, near_rows))
     late = flip(pair, "zl", 2)
+    left, right = shift(pair, "x", 1), shift(pair, "x", -1)
     part = mp_scatter_x(tie(mlp_term, pair))
-    far = flip(tie(near, part), "zh")
-    shard = jnp.concatenate([pair, late])
-    left, right = shift(shard, "x", 1), shift(shard, "x", -1)
-    far_weight = lax.all_gather(by_core(far), "y").reshape(3072, 384)
-    part = mp_gather_zl(mp_scatter_zl(part))
-    left, right, part = lax.optimization_barrier((left, right, part))
-    low, high = shift(left[:2], "x", 1), shift(right[2:], "x", -1)
-    blocks = (shard, left, right, low, high)
+    part, far_rows = lax.optimization_barrier((part, far_rows))
+    part = mp_scatter_zl(part)
+    far_weight = lax.all_gather(far_rows, "y").reshape(3072, 384)
+    late = tie(late, part)
+    late_left, late_right = shift(late, "x", 1), shift(late, "x", -1)
+    low, high = shift(left[:1], "x", 1), shift(right[1:], "x", -1)
+    late_left, late_right, part, low, high = lax.optimization_barrier(
+        (late_left, late_right, part, low, high)
+    )
+    late_low, late_high = shift(late_left[:1], "x", 1), shift(late_right[1:], "x", -1)
+    part = mp_gather_zl(part)
+    late_low, part = lax.optimization_barrier((late_low, part))
+    blocks = (pair, left, right, low, high, late, late_left, late_right, late_low, late_high)
 
     place_x = jnp.stack([lax.axis_index("x"), lax.axis_index("zl"), lax.axis_index("zh")])
     place_c = lax.axis_index("c").reshape(1)
     smem = pl.BlockSpec(memory_space=pltpu.SMEM)
     vmem = pl.BlockSpec(memory_space=pltpu.VMEM)
     params = pltpu.CompilerParams(vmem_limit_bytes=40 * 1024 * 1024)
+    early_stats = pl.pallas_call(
+        stats_kernel,
+        out_shape=jax.ShapeDtypeStruct((2, 256, 128), F32),
+        in_specs=[vmem] * 8,
+        out_specs=vmem,
+        compiler_params=params,
+        cost_estimate=pl.CostEstimate(
+            flops=8_000_000, bytes_accessed=3_000_000, transcendentals=0
+        ),
+        name="teacher_stats",
+    )(*blocks[:8])
     normed = pl.pallas_call(
         norm_kernel,
         out_shape=jax.ShapeDtypeStruct((256, 6144), BF16),
-        in_specs=[smem] + [vmem] * 5,
+        in_specs=[smem] + [vmem] * 11,
         out_specs=vmem,
         compiler_params=params,
         cost_estimate=pl.CostEstimate(
             flops=1000, bytes_accessed=1000, transcendentals=0
         ),
         name="teacher_norm",
-    )(place_x, *blocks)
+    )(place_x, early_stats, *blocks)
     normed_other = shift(normed, "c", 1)
     mlp_sum = mp_gather_x(tie(part, normed))
     partial = pl.pallas_call(
@@ -274,17 +311,14 @@
     grad_pred = ((predicted - target) * loss_factor).astype(BF16)
     block_term = jnp.einsum("tf,cf->tc", grad_pred, projector, preferred_element_type=F32)
     proj_term = jnp.einsum("tc,tf->cf", block_out, grad_pred, preferred_element_type=F32)
-    proj_term, block_term = lax.optimization_barrier(
-        (proj_term.astype(BF16), block_term.astype(BF16))
-    )
-    grad_projector = reduce_projector(proj_term.astype(F32), first)
-    grad_block = mp_scatter_zl(mp_scatter_x(block_term))
+    grad_block = mp_scatter_zl(mp_scatter_x(block_term.astype(BF16)))
     grad_block = mp_gather_x(mp_gather_zl(grad_block))
     down_term = jnp.einsum("tc,tf->cf", grad_block, activ, preferred_element_type=F32)
     grad_act = jnp.einsum("tc,fc->tf", grad_block, down_weight, preferred_element_type=F32)
     grad_pre = (grad_act * slope).astype(BF16)
     up_term = jnp.einsum("tc,tf->cf", student_normed, grad_pre, preferred_element_type=F32)
-    grad_up, grad_down = reduce_dp(jnp.stack([up_term.astype(BF16), down_term.astype(BF16)]))
+    terms = jnp.stack([t.astype(BF16) for t in (up_term, down_term, proj_term)])
+    grad_up, grad_down, grad_projector = reduce_dp(terms)
     return grad_up, grad_down.T, grad_projector
 
 

time: 248 us -> 253 us (1.020)
  blocking collectives: 51.5 us -> 78.3 us
  waiting for transfers between devices: 59.4 us -> 46.1 us
  starting transfers between devices: 83.8 us -> 73.5 us
    all_to_all x0 -> x1, blocking collectives: none -> 33.1 us  [reduce_dp(): terms = lax.all_to_all(terms, ('zh', 'y'), split_axis=1, concat_axis=0)]
    ppermute x6 -> x10, starting transfers between devices: 18 us -> 32.3 us  [shift(): lax.ppermute(values, axis, [(i, (i + step) % size) for i in range(size)])]
    all_to_all x1 -> x0, starting transfers between devices: 13.5 us -> none  [reduce_dp(): terms = lax.all_to_all(terms, ('zh', 'y'), split_axis=1, concat_axis=0)]
    ppermute x7 -> x5, starting transfers between devices: 33.3 us -> 20.7 us  [flip(): lax.ppermute(values, axes, [(i, i ^ bits) for i in range(SIZES[axes])])]
    ppermute x7 -> x5, waiting for transfers between devices: 25 us -> 15 us  [flip(): lax.ppermute(values, axes, [(i, i ^ bits) for i in range(SIZES[axes])])]
    all_to_all x5 -> x4, blocking collectives: 47 us -> 40.2 us  [swap(): return lax.all_to_all(values, axis, split_axis=0, concat_axis=0)]
    all_to_all x1 -> x0, waiting for transfers between devices: 6.6 us -> none  [reduce_dp(): terms = lax.all_to_all(terms, ('zh', 'y'), split_axis=1, concat_axis=0)]
    all_to_all x4 -> x5, waiting for transfers between devices: 19 us -> 22 us  [swap(): return lax.all_to_all(values, axis, split_axis=0, concat_axis=0)]
  transfers between devices with their start and end apart: 21 -> 22, of which waited for: 13 -> 10; matrix products, arithmetic and copies ran while one was open for 5% -> 3% of each run, Pallas kernels for 7% -> 7%
where the time goes in v5:
time: 253 us; the launch traced here: 252 us
  blocking collectives  78.3 us (31%)
  starting transfers between devices  73.5 us (29%)
  waiting for transfers between devices  46.1 us (18%)
  Pallas kernels  18.2 us (7%)
  between operations  14.7 us (6%)
  local copies, waits for them, and re-layouts  13.3 us (5%)
  matrix products  3.85 us (2%)
  other arithmetic  3.67 us (1%)
    all_to_all x4, blocking collectives, swap(): return lax.all_to_all(values, axis, split_axis=0, concat_axis=0)  40.2 us
    all_to_all x1, blocking collectives, reduce_dp(): terms = lax.all_to_all(terms, ('zh', 'y'), split_axis=1, concat_axis=0)  33.1 us
    ppermute x10, starting transfers between devices, shift(): lax.ppermute(values, axis, [(i, (i + step) % size) for i in range(size)])  32.3 us
    all_to_all x5, waiting for transfers between devices, swap(): return lax.all_to_all(values, axis, split_axis=0, concat_axis=0)  22 us
    ppermute x5, starting transfers between devices, flip(): lax.ppermute(values, axes, [(i, i ^ bits) for i in range(SIZES[axes])])  20.7 us
    all_to_all x5, starting transfers between devices, swap(): return lax.all_to_all(values, axis, split_axis=0, concat_axis=0)  20.5 us
    ppermute x5, waiting for transfers between devices, flip(): lax.ppermute(values, axes, [(i, i ^ bits) for i in range(SIZES[axes])])  15 us
    ppermute x10, waiting for transfers between devices, shift(): lax.ppermute(values, axis, [(i, (i + step) % size) for i in range(size)])  9.09 us
  transfers between devices with their start and end apart: 22, of which 10 were waited for; matrix products, arithmetic and copies ran while one was open for 3% of the time, Pallas kernels for 7%

profile of v5, /device:TPU:8, one launch (start us, length us, event | category | flops | bytes accessed | tf_op | source)
XLA Modules:
  0.0 251.6 jit_solution(11065642638092852122)
XLA Ops:
  13.2 10.9 %collective-permute-start.2 = (bf16[2,192,384]{2,1,0:T(8,128)(2,1)S(1)}, bf16[2,192,384]{2,1,0:T(8,128)(2,1)S(1)}, u32[]{:S(2)}, u32[]{:S(2)}) collective-permute-start(bf16[2,192,384]{2,1,0:T(8,128)(2,1)S(1)} %reverse_select_fusion), channel_id=1, source_target_pairs={{0,256},{256,0},{1,257},{257,1},{2,258},{258,2},{3,259},{259,3},{4... | collective-permute-start | bytes 884744 | tf_op jit(solution)/shard_map/ppermute | solution.py:40
  29.7 13.7 %collective-permute-done = bf16[272,384]{1,0:T(8,128)(2,1)S(1)} collective-permute-done((bf16[272,384]{1,0:T(8,128)(2,1)S(1)}, bf16[272,384]{1,0:T(8,128)(2,1)S(1)}, u32[]{:S(2)}, u32[]{:S(2)}) %collective-permute-start) | collective-permute-done | bytes 208928 | tf_op jit(solution)/shard_map/ppermute | solution.py:40
  43.5 4.3 %all-to-all-start = ((bf16[4,64,1024]{2,1,0:T(8,128)(2,1)}), bf16[4,64,1024]{2,1,0:T(8,128)(2,1)S(1)}, u32[]{:S(2)}, u32[]{:S(2)}) async-start(bf16[4,64,1024]{2,1,0:T(8,128)(2,1)} %bitcast.2), calls=%async_computation | async-start | bytes 1048576 | tf_op jit(solution)/shard_map/all_to_all | solution.py:48
  52.9 3.9 %all-to-all-done = bf16[4,64,1024]{2,1,0:T(8,128)(2,1)S(1)} async-done(((bf16[4,64,1024]{2,1,0:T(8,128)(2,1)}), bf16[4,64,1024]{2,1,0:T(8,128)(2,1)S(1)}, u32[]{:S(2)}, u32[]{:S(2)}) %all-to-all-start) | async-done | bytes 524320 | tf_op jit(solution)/shard_map/all_to_all | solution.py:48
  59.4 4.6 %collective-permute-start.8 = (bf16[2,272,384]{2,1,0:T(8,128)(2,1)S(1)}, bf16[2,272,384]{2,1,0:T(8,128)(2,1)S(1)}, u32[]{:S(2)}, u32[]{:S(2)}) collective-permute-start(bf16[2,272,384]{2,1,0:T(8,128)(2,1)S(1)} %pad_maximum_fusion.1.refs_0_), channel_id=1, source_target_pairs={{0,3},{1,0},{2,1},{3,2},{4,7},{5,4},{6,5},{7,6},{8,11},{9,8},{10,9... | collective-permute-start | bytes 1253384 | tf_op jit(solution)/shard_map/ppermute | solution.py:36
  64.0 12.3 %all_to_all.63 = bf16[4,16,1024]{2,1,0:T(8,128)(2,1)S(1)} all-to-all(bf16[4,16,1024]{2,1,0:T(8,128)(2,1)S(1)} %bitcast.74), channel_id=1, replica_groups=mesh['zh'=2,'y'=8,'c'=2,'zl'=4,'x'=4] {'zl'}, dimensions={0} | all-to-all | bytes 262144 | tf_op jit(solution)/shard_map/all_to_all | solution.py:48
  76.4 3.9 %collective-permute-start.4 = (bf16[2,272,384]{2,1,0:T(8,128)(2,1)S(1)}, bf16[2,272,384]{2,1,0:T(8,128)(2,1)S(1)}, u32[]{:S(2)}, u32[]{:S(2)}) collective-permute-start(bf16[2,272,384]{2,1,0:T(8,128)(2,1)S(1)} %collective-permute-done.1.refs_5_), channel_id=1, source_target_pairs={{0,1},{1,2},{2,3},{3,0},{4,5},{5,6},{6,7},{7,4},{8,9},{9,10},{10,1... | collective-permute-start | bytes 1253384 | tf_op jit(solution)/shard_map/ppermute | solution.py:36
  86.3 4.3 %collective-permute-start.9 = (bf16[1,272,384]{2,1,0:T(8,128)(2,1)S(1)}, bf16[1,272,384]{2,1,0:T(8,128)(2,1)S(1)}, u32[]{:S(2)}, u32[]{:S(2)}) collective-permute-start(bf16[1,272,384]{2,1,0:T(8,128)(2,1)S(1)} %slice.55), channel_id=1, source_target_pairs={{0,3},{1,0},{2,1},{3,2},{4,7},{5,4},{6,5},{7,6},{8,11},{9,8},{10,9... | collective-permute-start | bytes 626696 | tf_op jit(solution)/shard_map/ppermute | solution.py:36
  90.6 5.3 %collective-permute-done.7.refs_3_ = bf16[1,272,384]{2,1,0:T(8,128)(2,1)S(1)} collective-permute-done((bf16[1,272,384]{2,1,0:T(8,128)(2,1)S(1)}, bf16[1,272,384]{2,1,0:T(8,128)(2,1)S(1)}, u32[]{:S(2)}, u32[]{:S(2)}) %collective-permute-start.7) | collective-permute-done | bytes 208928 | tf_op jit(solution)/shard_map/ppermute | solution.py:36
  102.9 3.7 %collective-permute-start.11 = (bf16[1,272,384]{2,1,0:T(8,128)(2,1)}, bf16[1,272,384]{2,1,0:T(8,128)(2,1)}, u32[]{:S(2)}, u32[]{:S(2)}) collective-permute-start(bf16[1,272,384]{2,1,0:T(8,128)(2,1)} %slice.45), channel_id=1, source_target_pairs={{0,3},{1,0},{2,1},{3,2},{4,7},{5,4},{6,5},{7,6},{8,11},{9,8},{10,9... | collective-permute-start | bytes 626696 | tf_op jit(solution)/shard_map/ppermute | solution.py:36
  107.2 3.9 %all-to-all-start.2 = ((bf16[4,16,1024]{2,1,0:T(8,128)(2,1)}), bf16[4,16,1024]{2,1,0:T(8,128)(2,1)}, u32[]{:S(2)}, u32[]{:S(2)}) async-start(bf16[4,16,1024]{2,1,0:T(8,128)(2,1)} %broadcast_in_dim.14), calls=%async_computation.2 | async-start | bytes 262144 | tf_op jit(solution)/shard_map/all_to_all | solution.py:48
  118.1 5.6 %teacher_norm.1.own_ref = bf16[256,6144]{1,0:T(8,128)(2,1)} custom-call(s32[3]{0:T(128)S(1)} %pad_add_fusion.place, f32[2,256,128]{2,1,0:T(8,128)S(1)} %teacher_stats.1.stats_ref, bf16[2,272,384]{2,1,0:T(8,128)(2,1)S(1)} %pad_maximum_fusion.1.refs_0_, bf16[2,272,384]{2,1,0:T(8,128)(2,1)S(1)} %collective-permute-done.6.refs_1_, ...), custom_call_target="tpu_custom_call" | custom-call | flops 1000 | bytes 1000 | tf_op jit(solution)/shard_map/teacher_norm/pallas_call | solution.py:259
  127.3 3.5 %all-to-all-start.3 = ((bf16[4,64,1024]{2,1,0:T(8,128)(2,1)}), bf16[4,64,1024]{2,1,0:T(8,128)(2,1)S(1)}, u32[]{:S(2)}, u32[]{:S(2)}) async-start(bf16[4,64,1024]{2,1,0:T(8,128)(2,1)} %broadcast_in_dim.15), calls=%async_computation.3 | async-start | bytes 1048576 | tf_op jit(solution)/shard_map/all_to_all | solution.py:48
  133.2 4.7 %teacher_near.1.p_ref = f32[2,256,384]{2,1,0:T(8,128)S(1)} custom-call(bf16[256,6144]{1,0:T(8,128)(2,1)} %teacher_norm.1.own_ref, bf16[256,6144]{1,0:T(8,128)(2,1)} %collective-permute-done.12.other_ref, bf16[3072,384]{1,0:T(8,128)(2,1)S(1)} %bitcast.65), custom_call_target="tpu_custom_call" | custom-call | flops 1207959552 | bytes 6000000 | tf_op jit(solution)/shard_map/teacher_near/pallas_call | solution.py:272
  139.6 5.8 %teacher_heads.1 = f32[2,256,128]{2,1,0:T(8,128)S(1)} custom-call(s32[1]{0:T(128)} %bitcast.12.place, bf16[256,6144]{1,0:T(8,128)(2,1)} %teacher_norm.1.own_ref, bf16[256,6144]{1,0:T(8,128)(2,1)} %collective-permute-done.12.other_ref, bf16[3072,384]{1,0:T(8,128)(2,1)S(1)} %bitcast.64, f32[2,256,384]{2,1,0:T(8,128)S(1)} %teacher_near.1.p_ref, ...), custom_call_target="tpu_custom_call" | custom-call | flops 1207959552 | bytes 6000000 | tf_op jit(solution)/shard_map/teacher_heads/pallas_call | solution.py:283
  149.8 5.0 %all-to-all-start.4 = ((f32[16,2,256]{2,1,0:T(2,128)}), f32[16,2,256]{2,1,0:T(2,128)S(1)}, u32[]{:S(2)}, u32[]{:S(2)}) async-start(f32[16,2,256]{2,1,0:T(2,128)} %broadcast_in_dim.16), calls=%async_computation.4 | async-start | bytes 65536 | tf_op jit(solution)/shard_map/all_to_all | solution.py:48
  155.1 7.8 %all-to-all-done.4 = f32[16,2,256]{2,1,0:T(2,128)S(1)} async-done(((f32[16,2,256]{2,1,0:T(2,128)}), f32[16,2,256]{2,1,0:T(2,128)S(1)}, u32[]{:S(2)}, u32[]{:S(2)}) %all-to-all-start.4) | async-done | bytes 32800 | tf_op jit(solution)/shard_map/all_to_all | solution.py:48
  163.4 11.1 %all_to_all.64 = bf16[4,64,1024]{2,1,0:T(8,128)(2,1)S(1)} all-to-all(bf16[4,64,1024]{2,1,0:T(8,128)(2,1)S(1)} %bitcast.67), channel_id=1, replica_groups=mesh['zh'=2,'y'=8,'c'=2,'zl'=4,'x'=4] {'x'}, dimensions={0} | all-to-all | bytes 1048576 | tf_op jit(solution)/shard_map/all_to_all | solution.py:48
  174.6 8.3 %all_to_all.65 = bf16[4,16,1024]{2,1,0:T(8,128)(2,1)S(1)} all-to-all(bf16[4,16,1024]{2,1,0:T(8,128)(2,1)S(1)} %bitcast.75), channel_id=1, replica_groups=mesh['zh'=2,'y'=8,'c'=2,'zl'=4,'x'=4] {'zl'}, dimensions={0} | all-to-all | bytes 262144 | tf_op jit(solution)/shard_map/all_to_all | solution.py:48
  182.9 8.4 %all_to_all.66 = bf16[4,16,1024]{2,1,0:T(8,128)(2,1)S(1)} all-to-all(bf16[4,16,1024]{2,1,0:T(8,128)(2,1)S(1)} %broadcast_in_dim.17), channel_id=1, replica_groups=mesh['zh'=2,'y'=8,'c'=2,'zl'=4,'x'=4] {'zl'}, dimensions={0} | all-to-all | bytes 262144 | tf_op jit(solution)/shard_map/all_to_all | solution.py:48
  192.2 3.8 %all-to-all-start.8 = ((bf16[4,64,1024]{2,1,0:T(8,128)(2,1)}), bf16[4,64,1024]{2,1,0:T(8,128)(2,1)S(1)}, u32[]{:S(2)}, u32[]{:S(2)}) async-start(bf16[4,64,1024]{2,1,0:T(8,128)(2,1)} %broadcast_in_dim.19), calls=%async_computation.8 | async-start | bytes 1048576 | tf_op jit(solution)/shard_map/all_to_all | solution.py:48
  196.4 7.4 %all-to-all-done.8 = bf16[4,64,1024]{2,1,0:T(8,128)(2,1)S(1)} async-done(((bf16[4,64,1024]{2,1,0:T(8,128)(2,1)}), bf16[4,64,1024]{2,1,0:T(8,128)(2,1)S(1)}, u32[]{:S(2)}, u32[]{:S(2)}) %all-to-all-start.8) | async-done | bytes 524320 | tf_op jit(solution)/shard_map/all_to_all | solution.py:48
  205.5 5.0 %all_to_all.67 = bf16[1,3,16,2,32,256]{5,4,2,1,0,3:T(8,128)(2,1)S(1)} all-to-all(bf16[1,3,16,2,32,256]{5,4,2,1,0,3:T(8,128)(2,1)S(1)} %copy.35), channel_id=1, replica_groups=mesh['zh'=2,'y'=8,'c'=2,'zl'=4,'x'=4] {'c'}, dimensions={3} | all-to-all | bytes 3145728 | tf_op jit(solution)/shard_map/all_to_all | solution.py:181
  210.9 33.1 %all_to_all.68 = bf16[1,3,16,32,256]{4,3,1,0,2:T(8,128)(2,1)S(1)} all-to-all(bf16[1,3,16,32,256]{4,3,1,0,2:T(8,128)(2,1)S(1)} %copy.34), channel_id=1, replica_groups=mesh['zh'=2,'y'=8,'c'=2,'zl'=4,'x'=4] {'zh','y'}, dimensions={2} | all-to-all | bytes 1572864 | tf_op jit(solution)/shard_map/all_to_all | solution.py:183
  (122 shorter events, 56.6 us)
Async XLA Ops:
  7.2 21.4 %copy-start = (bf16[256,1024]{1,0:T(8,128)(2,1)S(1)}, bf16[256,1024]{1,0:T(8,128)(2,1)}, u32[]{:S(2)}) copy-start(bf16[256,1024]{1,0:T(8,128)(2,1)} %param.16) | copy-start | bytes 1572868
  7.2 123.7 %all-gather.4.cloned.1.call-start = ((), (), s32[]{:S(2)}) async-start(), calls=%async_computation.11 | async-start | bytes 2654208 | tf_op jit(solution)/shard_map/all_gather | solution.py:210
  8.9 19.3 %copy-start.14 = (bf16[1024,256]{1,0:T(8,128)(2,1)S(1)}, bf16[1024,256]{1,0:T(8,128)(2,1)}, u32[]{:S(2)}) copy-start(bf16[1024,256]{1,0:T(8,128)(2,1)} %param.15) | copy-start | bytes 1572868
  9.0 3.4 %collective-permute-start.13 = (bf16[192,384]{1,0:T(8,128)(2,1)S(1)}, bf16[192,384]{1,0:T(8,128)(2,1)S(1)}, u32[]{:S(2)}, u32[]{:S(2)}) collective-permute-start(bf16[192,384]{1,0:T(8,128)(2,1)S(1)} %get-tuple-element.30), channel_id=1, source_target_pairs={{0,16},{16,0},{1,17},{17,1},{2,18},{18,2},{3,19},{19,3},{4,20},{20... | collective-permute-start | bytes 442376 | tf_op jit(solution)/shard_map/ppermute | solution.py:40
  13.2 34.6 %collective-permute-start.2 = (bf16[2,192,384]{2,1,0:T(8,128)(2,1)S(1)}, bf16[2,192,384]{2,1,0:T(8,128)(2,1)S(1)}, u32[]{:S(2)}, u32[]{:S(2)}) collective-permute-start(bf16[2,192,384]{2,1,0:T(8,128)(2,1)S(1)} %reverse_select_fusion), channel_id=1, source_target_pairs={{0,256},{256,0},{1,257},{257,1},{2,258},{258,2},{3,259},{259,3},{4... | collective-permute-start | bytes 884744 | tf_op jit(solution)/shard_map/ppermute | solution.py:40
  24.4 19.0 %collective-permute-start = (bf16[272,384]{1,0:T(8,128)(2,1)S(1)}, bf16[272,384]{1,0:T(8,128)(2,1)S(1)}, u32[]{:S(2)}, u32[]{:S(2)}) collective-permute-start(bf16[272,384]{1,0:T(8,128)(2,1)S(1)} %concatenate.25), channel_id=1, source_target_pairs={{0,4},{4,0},{8,12},{12,8},{1,5},{5,1},{9,13},{13,9},{2,6},{6,2},{1... | collective-permute-start | bytes 626696 | tf_op jit(solution)/shard_map/ppermute | solution.py:40
  43.5 13.4 %all-to-all-start = ((bf16[4,64,1024]{2,1,0:T(8,128)(2,1)}), bf16[4,64,1024]{2,1,0:T(8,128)(2,1)S(1)}, u32[]{:S(2)}, u32[]{:S(2)}) async-start(bf16[4,64,1024]{2,1,0:T(8,128)(2,1)} %bitcast.2), calls=%async_computation | async-start | bytes 1048576 | tf_op jit(solution)/shard_map/all_to_all | solution.py:48
  47.8 90.2 %all-gather.6.cloned.1.call-start = ((), (), s32[]{:S(2)}) async-start(), calls=%async_computation.12 | async-start | bytes 2654208 | tf_op jit(solution)/shard_map/all_gather | solution.py:231
  47.8 4.3 %collective-permute-start.3 = (bf16[192,384]{1,0:T(8,128)(2,1)S(1)}, bf16[192,384]{1,0:T(8,128)(2,1)S(1)}, u32[]{:S(2)}, u32[]{:S(2)}) collective-permute-start(bf16[192,384]{1,0:T(8,128)(2,1)S(1)} %get-tuple-element.32), channel_id=1, source_target_pairs={{0,16},{16,0},{1,17},{17,1},{2,18},{18,2},{3,19},{19,3},{4,20},{20... | collective-permute-start | bytes 442376 | tf_op jit(solution)/shard_map/ppermute | solution.py:40
  49.7 26.6 %collective-permute-start.1 = (bf16[2,272,384]{2,1,0:T(8,128)(2,1)S(1)}, bf16[2,272,384]{2,1,0:T(8,128)(2,1)S(1)}, u32[]{:S(2)}, u32[]{:S(2)}) collective-permute-start(bf16[2,272,384]{2,1,0:T(8,128)(2,1)S(1)} %pad_maximum_fusion.1.refs_0_), channel_id=1, source_target_pairs={{0,8},{4,12},{8,0},{12,4},{1,9},{5,13},{9,1},{13,5},{2,10},{6,14},... | collective-permute-start | bytes 1253384 | tf_op jit(solution)/shard_map/ppermute | solution.py:40
  56.9 26.5 %collective-permute-start.6 = (bf16[2,272,384]{2,1,0:T(8,128)(2,1)S(1)}, bf16[2,272,384]{2,1,0:T(8,128)(2,1)S(1)}, u32[]{:S(2)}, u32[]{:S(2)}) collective-permute-start(bf16[2,272,384]{2,1,0:T(8,128)(2,1)S(1)} %pad_maximum_fusion.1.refs_0_), channel_id=1, source_target_pairs={{0,1},{1,2},{2,3},{3,0},{4,5},{5,6},{6,7},{7,4},{8,9},{9,10},{10,1... | collective-permute-start | bytes 1253384 | tf_op jit(solution)/shard_map/ppermute | solution.py:36
  59.4 26.8 %collective-permute-start.8 = (bf16[2,272,384]{2,1,0:T(8,128)(2,1)S(1)}, bf16[2,272,384]{2,1,0:T(8,128)(2,1)S(1)}, u32[]{:S(2)}, u32[]{:S(2)}) collective-permute-start(bf16[2,272,384]{2,1,0:T(8,128)(2,1)S(1)} %pad_maximum_fusion.1.refs_0_), channel_id=1, source_target_pairs={{0,3},{1,0},{2,1},{3,2},{4,7},{5,4},{6,5},{7,6},{8,11},{9,8},{10,9... | collective-permute-start | bytes 1253384 | tf_op jit(solution)/shard_map/ppermute | solution.py:36
  76.4 21.6 %collective-permute-start.4 = (bf16[2,272,384]{2,1,0:T(8,128)(2,1)S(1)}, bf16[2,272,384]{2,1,0:T(8,128)(2,1)S(1)}, u32[]{:S(2)}, u32[]{:S(2)}) collective-permute-start(bf16[2,272,384]{2,1,0:T(8,128)(2,1)S(1)} %collective-permute-done.1.refs_5_), channel_id=1, source_target_pairs={{0,1},{1,2},{2,3},{3,0},{4,5},{5,6},{6,7},{7,4},{8,9},{9,10},{10,1... | collective-permute-start | bytes 1253384 | tf_op jit(solution)/shard_map/ppermute | solution.py:36
  80.3 17.7 %collective-permute-start.5 = (bf16[2,272,384]{2,1,0:T(8,128)(2,1)S(1)}, bf16[2,272,384]{2,1,0:T(8,128)(2,1)S(1)}, u32[]{:S(2)}, u32[]{:S(2)}) collective-permute-start(bf16[2,272,384]{2,1,0:T(8,128)(2,1)S(1)} %collective-permute-done.1.refs_5_), channel_id=1, source_target_pairs={{0,3},{1,0},{2,1},{3,2},{4,7},{5,4},{6,5},{7,6},{8,11},{9,8},{10,9... | collective-permute-start | bytes 1253384 | tf_op jit(solution)/shard_map/ppermute | solution.py:36
  83.5 12.4 %collective-permute-start.7 = (bf16[1,272,384]{2,1,0:T(8,128)(2,1)S(1)}, bf16[1,272,384]{2,1,0:T(8,128)(2,1)S(1)}, u32[]{:S(2)}, u32[]{:S(2)}) collective-permute-start(bf16[1,272,384]{2,1,0:T(8,128)(2,1)S(1)} %slice.54), channel_id=1, source_target_pairs={{0,1},{1,2},{2,3},{3,0},{4,5},{5,6},{6,7},{7,4},{8,9},{9,10},{10,1... | collective-permute-start | bytes 626696 | tf_op jit(solution)/shard_map/ppermute | solution.py:36
  86.3 11.8 %collective-permute-start.9 = (bf16[1,272,384]{2,1,0:T(8,128)(2,1)S(1)}, bf16[1,272,384]{2,1,0:T(8,128)(2,1)S(1)}, u32[]{:S(2)}, u32[]{:S(2)}) collective-permute-start(bf16[1,272,384]{2,1,0:T(8,128)(2,1)S(1)} %slice.55), channel_id=1, source_target_pairs={{0,3},{1,0},{2,1},{3,2},{4,7},{5,4},{6,5},{7,6},{8,11},{9,8},{10,9... | collective-permute-start | bytes 626696 | tf_op jit(solution)/shard_map/ppermute | solution.py:36
  98.8 18.3 %collective-permute-start.10 = (bf16[1,272,384]{2,1,0:T(8,128)(2,1)}, bf16[1,272,384]{2,1,0:T(8,128)(2,1)}, u32[]{:S(2)}, u32[]{:S(2)}) collective-permute-start(bf16[1,272,384]{2,1,0:T(8,128)(2,1)} %slice.44), channel_id=1, source_target_pairs={{0,1},{1,2},{2,3},{3,0},{4,5},{5,6},{6,7},{7,4},{8,9},{9,10},{10,1... | collective-permute-start | bytes 626696 | tf_op jit(solution)/shard_map/ppermute | solution.py:36
  102.9 14.3 %collective-permute-start.11 = (bf16[1,272,384]{2,1,0:T(8,128)(2,1)}, bf16[1,272,384]{2,1,0:T(8,128)(2,1)}, u32[]{:S(2)}, u32[]{:S(2)}) collective-permute-start(bf16[1,272,384]{2,1,0:T(8,128)(2,1)} %slice.45), channel_id=1, source_target_pairs={{0,3},{1,0},{2,1},{3,2},{4,7},{5,4},{6,5},{7,6},{8,11},{9,8},{10,9... | collective-permute-start | bytes 626696 | tf_op jit(solution)/shard_map/ppermute | solution.py:36
  107.2 9.9 %all-to-all-start.2 = ((bf16[4,16,1024]{2,1,0:T(8,128)(2,1)}), bf16[4,16,1024]{2,1,0:T(8,128)(2,1)}, u32[]{:S(2)}, u32[]{:S(2)}) async-start(bf16[4,16,1024]{2,1,0:T(8,128)(2,1)} %broadcast_in_dim.14), calls=%async_computation.2 | async-start | bytes 262144 | tf_op jit(solution)/shard_map/all_to_all | solution.py:48
  123.7 7.9 %collective-permute-start.12 = (bf16[256,6144]{1,0:T(8,128)(2,1)}, bf16[256,6144]{1,0:T(8,128)(2,1)}, u32[]{:S(2)}, u32[]{:S(2)}) collective-permute-start(bf16[256,6144]{1,0:T(8,128)(2,1)} %teacher_norm.1.own_ref), channel_id=1, source_target_pairs={{0,16},{16,0},{1,17},{17,1},{2,18},{18,2},{3,19},{19,3},{4,20},{20... | collective-permute-start | bytes 9437192 | tf_op jit(solution)/shard_map/ppermute | solution.py:36
  127.3 20.3 %all-to-all-start.3 = ((bf16[4,64,1024]{2,1,0:T(8,128)(2,1)}), bf16[4,64,1024]{2,1,0:T(8,128)(2,1)S(1)}, u32[]{:S(2)}, u32[]{:S(2)}) async-start(bf16[4,64,1024]{2,1,0:T(8,128)(2,1)} %broadcast_in_dim.15), calls=%async_computation.3 | async-start | bytes 1048576 | tf_op jit(solution)/shard_map/all_to_all | solution.py:48
  145.5 3.4 %collective-permute-start.14 = (f32[256,128]{1,0:T(8,128)S(1)}, f32[256,128]{1,0:T(8,128)S(1)}, u32[]{:S(2)}, u32[]{:S(2)}) collective-permute-start(f32[256,128]{1,0:T(8,128)S(1)} %get-tuple-element.33), channel_id=1, source_target_pairs={{0,16},{16,0},{1,17},{17,1},{2,18},{18,2},{3,19},{19,3},{4,20},{20... | collective-permute-start | bytes 393224 | tf_op jit(solution)/shard_map/ppermute | solution.py:36
  149.8 13.1 %all-to-all-start.4 = ((f32[16,2,256]{2,1,0:T(2,128)}), f32[16,2,256]{2,1,0:T(2,128)S(1)}, u32[]{:S(2)}, u32[]{:S(2)}) async-start(f32[16,2,256]{2,1,0:T(2,128)} %broadcast_in_dim.16), calls=%async_computation.4 | async-start | bytes 65536 | tf_op jit(solution)/shard_map/all_to_all | solution.py:48
  192.2 11.7 %all-to-all-start.8 = ((bf16[4,64,1024]{2,1,0:T(8,128)(2,1)}), bf16[4,64,1024]{2,1,0:T(8,128)(2,1)S(1)}, u32[]{:S(2)}, u32[]{:S(2)}) async-start(bf16[4,64,1024]{2,1,0:T(8,128)(2,1)} %broadcast_in_dim.19), calls=%async_computation.8 | async-start | bytes 1048576 | tf_op jit(solution)/shard_map/all_to_all | solution.py:48
  (14 other events, 137.0 us)
Sparse Core Ops, SparseCore 0:
  13.3 48.2 all-gather.3
  63.7 43.1 all-gather.5

commit v6 on v3

--- a/solution.py
+++ b/solution.py
@@ -150,19 +150,6 @@
     return sum_parts(terms).astype(BF16)
 
 
-def reduce_projector(term, first):
-    term = term.reshape(2, 8, 2, 32, 256)
-    mine = jnp.where(first, term[:, :, 0], term[:, :, 1])
-    theirs = flip(jnp.where(first, term[:, :, 1], term[:, :, 0]), "c")
-    term = (mine.astype(F32) + theirs.astype(F32)).astype(BF16)
-    term = term.transpose(1, 0, 2, 3).reshape(8 * 64, 256)
-    term = lax.psum_scatter(term, "y", scatter_dimension=0, tiled=True).reshape(2, 32, 256)
-    low = lax.axis_index("zh") == 0
-    theirs = flip(jnp.where(low, term[1], term[0]), "zh")
-    mine = jnp.where(low, term[0], term[1])
-    return (mine.astype(F32) + theirs.astype(F32)).astype(BF16)
-
-
 def shards(
     teacher_in,
     teacher_gain,
@@ -180,8 +167,6 @@
     weight = qkv_weight.reshape(192, 3, 2, 128).transpose(2, 0, 1, 3).reshape(2, 192, 384)
     near = jnp.where(first, weight, weight[::-1])
     far = flip(near, "zh")
-    given = flip(jnp.stack([near[1], far[1]]), "c")
-
     hi = lax.reduce_precision(teacher_gain, 8, 7)
     mid = lax.reduce_precision(teacher_gain - hi, 8, 7)
     low = teacher_gain - hi - mid
@@ -198,17 +183,18 @@
     def by_core(mine, theirs):
         return jnp.where(first, jnp.stack([mine, theirs]), jnp.stack([theirs, mine]))
 
-    given, pair, mlp_term = lax.optimization_barrier((given, pair, mlp_term))
+    part = mp_scatter_x(mlp_term)
+    given = flip(jnp.stack([near[1], far[1]]), "c")
+    given, part, pair = lax.optimization_barrier((given, part, pair))
     rows = jnp.concatenate([by_core(near[0], given[0]), by_core(far[0], given[1])])
     weight = lax.all_gather(rows, "y").reshape(6144, 384)
 
     late = flip(pair, "zl", 2)
     left, right = shift(pair, "x", 1), shift(pair, "x", -1)
-    part = mp_scatter_x(tie(mlp_term, rows))
+    part = mp_scatter_zl(tie(part, rows))
     late = tie(late, part)
     late_left, late_right = shift(late, "x", 1), shift(late, "x", -1)
     low, high = shift(left[:1], "x", 1), shift(right[1:], "x", -1)
-    part = mp_scatter_zl(tie(part, left, right))
     late_left, late_right, part, low, high = lax.optimization_barrier(
         (late_left, late_right, part, low, high)
     )
@@ -266,14 +252,14 @@
     grad_pred = ((predicted - target) * loss_factor).astype(BF16)
     block_term = jnp.einsum("tf,cf->tc", grad_pred, projector, preferred_element_type=F32)
     proj_term = jnp.einsum("tc,tf->cf", block_out, grad_pred, preferred_element_type=F32)
-    grad_projector = reduce_projector(proj_term.astype(BF16), first)
     grad_block = mp_scatter_zl(mp_scatter_x(block_term.astype(BF16)))
     grad_block = mp_gather_x(mp_gather_zl(grad_block))
     down_term = jnp.einsum("tc,tf->cf", grad_block, activ, preferred_element_type=F32)
     grad_act = jnp.einsum("tc,fc->tf", grad_block, down_weight, preferred_element_type=F32)
     grad_pre = (grad_act * slope).astype(BF16)
     up_term = jnp.einsum("tc,tf->cf", student_normed, grad_pre, preferred_element_type=F32)
-    grad_up, grad_down = reduce_dp(jnp.stack([up_term.astype(BF16), down_term.astype(BF16)]))
+    terms = jnp.stack([t.astype(BF16) for t in (up_term, down_term, proj_term)])
+    grad_up, grad_down, grad_projector = reduce_dp(terms)
     return grad_up, grad_down.T, grad_projector
 
 

time: 254 us -> 242 us (0.953)
  the two profiles are of different devices: /device:TPU:28 before, /device:TPU:8 now
where the time goes in v6:
time: 242 us; the launch traced here: 241 us
  blocking collectives  84.5 us (35%)
  starting transfers between devices  73.7 us (30%)
  waiting for transfers between devices  35.1 us (15%)
  between operations  14.6 us (6%)
  Pallas kernels  13.2 us (5%)
  local copies, waits for them, and re-layouts  11.2 us (5%)
  matrix products  5.38 us (2%)
  other arithmetic  3.2 us (1%)
    all_to_all x4, blocking collectives, swap(): return lax.all_to_all(values, axis, split_axis=0, concat_axis=0)  41.8 us
    all_to_all x1, blocking collectives, reduce_dp(): terms = lax.all_to_all(terms, ('zh', 'y'), split_axis=1, concat_axis=0)  37.8 us
    ppermute x10, starting transfers between devices, shift(): lax.ppermute(values, axis, [(i, (i + step) % size) for i in range(size)])  32.4 us
    all_to_all x5, starting transfers between devices, swap(): return lax.all_to_all(values, axis, split_axis=0, concat_axis=0)  21 us
    all_to_all x5, waiting for transfers between devices, swap(): return lax.all_to_all(values, axis, split_axis=0, concat_axis=0)  20.4 us
    ppermute x4, starting transfers between devices, flip(): lax.ppermute(values, axes, [(i, i ^ bits) for i in range(SIZES[axes])])  20.3 us
    ppermute x10, waiting for transfers between devices, shift(): lax.ppermute(values, axis, [(i, (i + step) % size) for i in range(size)])  7.65 us
    pallas_call x1, Pallas kernels, shards(): pl.pallas_call(attention_kernel, out_shape=jax.ShapeDtypeStruct((2, 256,...  7.4 us
  transfers between devices with their start and end apart: 20, of which 9 were waited for; matrix products, arithmetic and copies ran while one was open for 3% of the time, Pallas kernels for 5%

profile of v6, /device:TPU:8, one launch (start us, length us, event | category | flops | bytes accessed | tf_op | source)
XLA Modules:
  0.0 241.1 jit_solution(908773969715697051)
XLA Ops:
  9.0 10.9 %collective-permute-start = (bf16[2,192,384]{2,1,0:T(8,128)(2,1)S(1)}, bf16[2,192,384]{2,1,0:T(8,128)(2,1)S(1)}, u32[]{:S(2)}, u32[]{:S(2)}) collective-permute-start(bf16[2,192,384]{2,1,0:T(8,128)(2,1)S(1)} %reverse_select_fusion), channel_id=1, source_target_pairs={{0,256},{256,0},{1,257},{257,1},{2,258},{258,2},{3,259},{259,3},{4... | collective-permute-start | bytes 884744 | tf_op jit(solution)/shard_map/ppermute | solution.py:40
  25.5 4.3 %all-to-all-start = ((bf16[4,64,1024]{2,1,0:T(8,128)(2,1)}), bf16[4,64,1024]{2,1,0:T(8,128)(2,1)S(1)}, u32[]{:S(2)}, u32[]{:S(2)}) async-start(bf16[4,64,1024]{2,1,0:T(8,128)(2,1)} %bitcast.1), calls=%async_computation | async-start | bytes 1048576 | tf_op jit(solution)/shard_map/all_to_all | solution.py:48
  29.8 3.7 %collective-permute-done = bf16[2,192,384]{2,1,0:T(8,128)(2,1)S(1)} collective-permute-done((bf16[2,192,384]{2,1,0:T(8,128)(2,1)S(1)}, bf16[2,192,384]{2,1,0:T(8,128)(2,1)S(1)}, u32[]{:S(2)}, u32[]{:S(2)}) %collective-permute-start) | collective-permute-done | bytes 294944 | tf_op jit(solution)/shard_map/ppermute | solution.py:40
  40.1 4.1 %collective-permute-start.3 = (bf16[2,272,384]{2,1,0:T(8,128)(2,1)S(1)}, bf16[2,272,384]{2,1,0:T(8,128)(2,1)S(1)}, u32[]{:S(2)}, u32[]{:S(2)}) collective-permute-start(bf16[2,272,384]{2,1,0:T(8,128)(2,1)S(1)} %pad_maximum_fusion.2.refs_0_), channel_id=1, source_target_pairs={{0,8},{4,12},{8,0},{12,4},{1,9},{5,13},{9,1},{13,5},{2,10},{6,14},... | collective-permute-start | bytes 1253384 | tf_op jit(solution)/shard_map/ppermute | solution.py:40
  46.7 4.6 %collective-permute-start.8 = (bf16[2,272,384]{2,1,0:T(8,128)(2,1)S(1)}, bf16[2,272,384]{2,1,0:T(8,128)(2,1)S(1)}, u32[]{:S(2)}, u32[]{:S(2)}) collective-permute-start(bf16[2,272,384]{2,1,0:T(8,128)(2,1)S(1)} %pad_maximum_fusion.2.refs_0_), channel_id=1, source_target_pairs={{0,3},{1,0},{2,1},{3,2},{4,7},{5,4},{6,5},{7,6},{8,11},{9,8},{10,9... | collective-permute-start | bytes 1253384 | tf_op jit(solution)/shard_map/ppermute | solution.py:36
  51.3 13.9 %all_to_all.63 = bf16[4,16,1024]{2,1,0:T(8,128)(2,1)S(1)} all-to-all(bf16[4,16,1024]{2,1,0:T(8,128)(2,1)S(1)} %bitcast.64), channel_id=1, replica_groups=mesh['zh'=2,'y'=8,'c'=2,'zl'=4,'x'=4] {'zl'}, dimensions={0} | all-to-all | bytes 262144 | tf_op jit(solution)/shard_map/all_to_all | solution.py:48
  68.6 3.7 %collective-permute-start.5 = (bf16[2,272,384]{2,1,0:T(8,128)(2,1)S(1)}, bf16[2,272,384]{2,1,0:T(8,128)(2,1)S(1)}, u32[]{:S(2)}, u32[]{:S(2)}) collective-permute-start(bf16[2,272,384]{2,1,0:T(8,128)(2,1)S(1)} %collective-permute-done.3.refs_5_), channel_id=1, source_target_pairs={{0,3},{1,0},{2,1},{3,2},{4,7},{5,4},{6,5},{7,6},{8,11},{9,8},{10,9... | collective-permute-start | bytes 1253384 | tf_op jit(solution)/shard_map/ppermute | solution.py:36
  74.5 4.9 %collective-permute-start.9 = (bf16[1,272,384]{2,1,0:T(8,128)(2,1)S(1)}, bf16[1,272,384]{2,1,0:T(8,128)(2,1)S(1)}, u32[]{:S(2)}, u32[]{:S(2)}) collective-permute-start(bf16[1,272,384]{2,1,0:T(8,128)(2,1)S(1)} %slice.63), channel_id=1, source_target_pairs={{0,3},{1,0},{2,1},{3,2},{4,7},{5,4},{6,5},{7,6},{8,11},{9,8},{10,9... | collective-permute-start | bytes 626696 | tf_op jit(solution)/shard_map/ppermute | solution.py:36
  79.5 4.1 %collective-permute-done.7.refs_3_ = bf16[1,272,384]{2,1,0:T(8,128)(2,1)S(1)} collective-permute-done((bf16[1,272,384]{2,1,0:T(8,128)(2,1)S(1)}, bf16[1,272,384]{2,1,0:T(8,128)(2,1)S(1)}, u32[]{:S(2)}, u32[]{:S(2)}) %collective-permute-start.7) | collective-permute-done | bytes 208928 | tf_op jit(solution)/shard_map/ppermute | solution.py:36
  90.3 3.6 %collective-permute-start.11 = (bf16[1,272,384]{2,1,0:T(8,128)(2,1)}, bf16[1,272,384]{2,1,0:T(8,128)(2,1)}, u32[]{:S(2)}, u32[]{:S(2)}) collective-permute-start(bf16[1,272,384]{2,1,0:T(8,128)(2,1)} %slice.53), channel_id=1, source_target_pairs={{0,3},{1,0},{2,1},{3,2},{4,7},{5,4},{6,5},{7,6},{8,11},{9,8},{10,9... | collective-permute-start | bytes 626696 | tf_op jit(solution)/shard_map/ppermute | solution.py:36
  94.6 4.5 %all-to-all-start.2 = ((bf16[4,16,1024]{2,1,0:T(8,128)(2,1)}), bf16[4,16,1024]{2,1,0:T(8,128)(2,1)}, u32[]{:S(2)}, u32[]{:S(2)}) async-start(bf16[4,16,1024]{2,1,0:T(8,128)(2,1)} %broadcast_in_dim.14), calls=%async_computation.2 | async-start | bytes 262144 | tf_op jit(solution)/shard_map/all_to_all | solution.py:48
  99.1 5.9 %all-to-all-done.2 = bf16[4,16,1024]{2,1,0:T(8,128)(2,1)} async-done(((bf16[4,16,1024]{2,1,0:T(8,128)(2,1)}), bf16[4,16,1024]{2,1,0:T(8,128)(2,1)}, u32[]{:S(2)}, u32[]{:S(2)}) %all-to-all-start.2) | async-done | bytes 131104 | tf_op jit(solution)/shard_map/all_to_all | solution.py:48
  105.1 5.8 %teacher_norm.1.own_ref = bf16[256,6144]{1,0:T(8,128)(2,1)} custom-call(s32[3]{0:T(128)S(1)} %pad_add_fusion.place, bf16[2,272,384]{2,1,0:T(8,128)(2,1)S(1)} %pad_maximum_fusion.2.refs_0_, bf16[2,272,384]{2,1,0:T(8,128)(2,1)S(1)} %collective-permute-done.6.refs_1_, bf16[2,272,384]{2,1,0:T(8,128)(2,1)S(1)} %collective-permute-done.8.refs_2_, ...), custom_call_target="tpu_custom_call" | custom-call | flops 1000 | bytes 1000 | tf_op jit(solution)/shard_map/teacher_norm/pallas_call | solution.py:211
  114.8 3.5 %all-to-all-start.3 = ((bf16[4,64,1024]{2,1,0:T(8,128)(2,1)}), bf16[4,64,1024]{2,1,0:T(8,128)(2,1)S(1)}, u32[]{:S(2)}, u32[]{:S(2)}) async-start(bf16[4,64,1024]{2,1,0:T(8,128)(2,1)} %broadcast_in_dim.15), calls=%async_computation.3 | async-start | bytes 1048576 | tf_op jit(solution)/shard_map/all_to_all | solution.py:48
  121.3 7.4 %teacher_heads.1 = f32[2,256,128]{2,1,0:T(8,128)S(1)} custom-call(s32[1]{0:T(128)} %bitcast.10.place, bf16[256,6144]{1,0:T(8,128)(2,1)} %teacher_norm.1.own_ref, bf16[256,6144]{1,0:T(8,128)(2,1)} %collective-permute-done.12.other_ref, bf16[6144,384]{1,0:T(8,128)(2,1)S(1)} %bitcast.55, f32[2,128]{1,0:T(2,128)S(1)} %copy-done.2), custom_call_target="tpu_custom_call" | custom-call | flops 2415919104 | bytes 11000000 | tf_op jit(solution)/shard_map/teacher_heads/pallas_call | solution.py:224
  133.1 5.0 %all-to-all-start.4 = ((f32[16,2,256]{2,1,0:T(2,128)}), f32[16,2,256]{2,1,0:T(2,128)S(1)}, u32[]{:S(2)}, u32[]{:S(2)}) async-start(f32[16,2,256]{2,1,0:T(2,128)} %broadcast_in_dim.16), calls=%async_computation.4 | async-start | bytes 65536 | tf_op jit(solution)/shard_map/all_to_all | solution.py:48
  138.4 7.8 %all-to-all-done.4 = f32[16,2,256]{2,1,0:T(2,128)S(1)} async-done(((f32[16,2,256]{2,1,0:T(2,128)}), f32[16,2,256]{2,1,0:T(2,128)S(1)}, u32[]{:S(2)}, u32[]{:S(2)}) %all-to-all-start.4) | async-done | bytes 32800 | tf_op jit(solution)/shard_map/all_to_all | solution.py:48
  146.7 11.1 %all_to_all.64 = bf16[4,64,1024]{2,1,0:T(8,128)(2,1)S(1)} all-to-all(bf16[4,64,1024]{2,1,0:T(8,128)(2,1)S(1)} %bitcast.57), channel_id=1, replica_groups=mesh['zh'=2,'y'=8,'c'=2,'zl'=4,'x'=4] {'x'}, dimensions={0} | all-to-all | bytes 1048576 | tf_op jit(solution)/shard_map/all_to_all | solution.py:48
  157.9 8.3 %all_to_all.65 = bf16[4,16,1024]{2,1,0:T(8,128)(2,1)S(1)} all-to-all(bf16[4,16,1024]{2,1,0:T(8,128)(2,1)S(1)} %bitcast.65), channel_id=1, replica_groups=mesh['zh'=2,'y'=8,'c'=2,'zl'=4,'x'=4] {'zl'}, dimensions={0} | all-to-all | bytes 262144 | tf_op jit(solution)/shard_map/all_to_all | solution.py:48
  166.2 8.4 %all_to_all.66 = bf16[4,16,1024]{2,1,0:T(8,128)(2,1)S(1)} all-to-all(bf16[4,16,1024]{2,1,0:T(8,128)(2,1)S(1)} %broadcast_in_dim.17), channel_id=1, replica_groups=mesh['zh'=2,'y'=8,'c'=2,'zl'=4,'x'=4] {'zl'}, dimensions={0} | all-to-all | bytes 262144 | tf_op jit(solution)/shard_map/all_to_all | solution.py:48
  175.5 3.8 %all-to-all-start.8 = ((bf16[4,64,1024]{2,1,0:T(8,128)(2,1)}), bf16[4,64,1024]{2,1,0:T(8,128)(2,1)S(1)}, u32[]{:S(2)}, u32[]{:S(2)}) async-start(bf16[4,64,1024]{2,1,0:T(8,128)(2,1)} %broadcast_in_dim.19), calls=%async_computation.8 | async-start | bytes 1048576 | tf_op jit(solution)/shard_map/all_to_all | solution.py:48
  180.5 6.6 %all-to-all-done.8 = bf16[4,64,1024]{2,1,0:T(8,128)(2,1)S(1)} async-done(((bf16[4,64,1024]{2,1,0:T(8,128)(2,1)}), bf16[4,64,1024]{2,1,0:T(8,128)(2,1)S(1)}, u32[]{:S(2)}, u32[]{:S(2)}) %all-to-all-start.8) | async-done | bytes 524320 | tf_op jit(solution)/shard_map/all_to_all | solution.py:48
  190.2 5.0 %all_to_all.67 = bf16[1,3,16,2,32,256]{5,4,2,1,0,3:T(8,128)(2,1)S(1)} all-to-all(bf16[1,3,16,2,32,256]{5,4,2,1,0,3:T(8,128)(2,1)S(1)} %copy.35), channel_id=1, replica_groups=mesh['zh'=2,'y'=8,'c'=2,'zl'=4,'x'=4] {'c'}, dimensions={3} | all-to-all | bytes 3145728 | tf_op jit(solution)/shard_map/all_to_all | solution.py:147
  195.7 37.8 %all_to_all.68 = bf16[1,3,16,32,256]{4,3,1,0,2:T(8,128)(2,1)S(1)} all-to-all(bf16[1,3,16,32,256]{4,3,1,0,2:T(8,128)(2,1)S(1)} %copy.34), channel_id=1, replica_groups=mesh['zh'=2,'y'=8,'c'=2,'zl'=4,'x'=4] {'zh','y'}, dimensions={2} | all-to-all | bytes 1572864 | tf_op jit(solution)/shard_map/all_to_all | solution.py:149
  (113 shorter events, 47.6 us)
Async XLA Ops:
  7.2 17.2 %copy-start = (bf16[256,1024]{1,0:T(8,128)(2,1)S(1)}, bf16[256,1024]{1,0:T(8,128)(2,1)}, u32[]{:S(2)}) copy-start(bf16[256,1024]{1,0:T(8,128)(2,1)} %param.16) | copy-start | bytes 1572868
  7.2 16.3 %copy-start.3 = (bf16[256,1024]{1,0:T(8,128)(2,1)S(1)}, bf16[256,1024]{1,0:T(8,128)(2,1)}, u32[]{:S(2)}) copy-start(bf16[256,1024]{1,0:T(8,128)(2,1)} %param.13) | copy-start | bytes 1572868
  8.3 15.6 %copy-start.12 = (bf16[1024,256]{1,0:T(8,128)(2,1)S(1)}, bf16[1024,256]{1,0:T(8,128)(2,1)}, u32[]{:S(2)}) copy-start(bf16[1024,256]{1,0:T(8,128)(2,1)} %param.15) | copy-start | bytes 1572868
  8.4 15.6 %copy-start.13 = (f32[1024]{0:T(1024)S(1)}, f32[1024]{0:T(1024)}, u32[]{:S(2)}) copy-start(f32[1024]{0:T(1024)} %param.14) | copy-start | bytes 12292
  9.0 24.5 %collective-permute-start = (bf16[2,192,384]{2,1,0:T(8,128)(2,1)S(1)}, bf16[2,192,384]{2,1,0:T(8,128)(2,1)S(1)}, u32[]{:S(2)}, u32[]{:S(2)}) collective-permute-start(bf16[2,192,384]{2,1,0:T(8,128)(2,1)S(1)} %reverse_select_fusion), channel_id=1, source_target_pairs={{0,256},{256,0},{1,257},{257,1},{2,258},{258,2},{3,259},{259,3},{4... | collective-permute-start | bytes 884744 | tf_op jit(solution)/shard_map/ppermute | solution.py:40
  20.1 18.7 %collective-permute-start.2 = (bf16[272,384]{1,0:T(8,128)(2,1)S(1)}, bf16[272,384]{1,0:T(8,128)(2,1)S(1)}, u32[]{:S(2)}, u32[]{:S(2)}) collective-permute-start(bf16[272,384]{1,0:T(8,128)(2,1)S(1)} %concatenate.14), channel_id=1, source_target_pairs={{0,4},{4,0},{8,12},{12,8},{1,5},{5,1},{9,13},{13,9},{2,6},{6,2},{1... | collective-permute-start | bytes 626696 | tf_op jit(solution)/shard_map/ppermute | solution.py:40
  25.5 13.4 %all-to-all-start = ((bf16[4,64,1024]{2,1,0:T(8,128)(2,1)}), bf16[4,64,1024]{2,1,0:T(8,128)(2,1)S(1)}, u32[]{:S(2)}, u32[]{:S(2)}) async-start(bf16[4,64,1024]{2,1,0:T(8,128)(2,1)} %bitcast.1), calls=%async_computation | async-start | bytes 1048576 | tf_op jit(solution)/shard_map/all_to_all | solution.py:48
  29.8 89.2 %all-gather.3.cloned.1.call-start = ((), (), s32[]{:S(2)}) async-start(), calls=%async_computation.11 | async-start | bytes 5308416 | tf_op jit(solution)/shard_map/all_gather | solution.py:190
  33.6 5.4 %collective-permute-start.1 = (bf16[2,192,384]{2,1,0:T(8,128)(2,1)S(1)}, bf16[2,192,384]{2,1,0:T(8,128)(2,1)S(1)}, u32[]{:S(2)}, u32[]{:S(2)}) collective-permute-start(bf16[2,192,384]{2,1,0:T(8,128)(2,1)S(1)} %pad_maximum_fusion.3), channel_id=1, source_target_pairs={{0,16},{16,0},{1,17},{17,1},{2,18},{18,2},{3,19},{19,3},{4,20},{20... | collective-permute-start | bytes 884744 | tf_op jit(solution)/shard_map/ppermute | solution.py:40
  40.1 25.1 %collective-permute-start.3 = (bf16[2,272,384]{2,1,0:T(8,128)(2,1)S(1)}, bf16[2,272,384]{2,1,0:T(8,128)(2,1)S(1)}, u32[]{:S(2)}, u32[]{:S(2)}) collective-permute-start(bf16[2,272,384]{2,1,0:T(8,128)(2,1)S(1)} %pad_maximum_fusion.2.refs_0_), channel_id=1, source_target_pairs={{0,8},{4,12},{8,0},{12,4},{1,9},{5,13},{9,1},{13,5},{2,10},{6,14},... | collective-permute-start | bytes 1253384 | tf_op jit(solution)/shard_map/ppermute | solution.py:40
  44.2 28.1 %collective-permute-start.6 = (bf16[2,272,384]{2,1,0:T(8,128)(2,1)S(1)}, bf16[2,272,384]{2,1,0:T(8,128)(2,1)S(1)}, u32[]{:S(2)}, u32[]{:S(2)}) collective-permute-start(bf16[2,272,384]{2,1,0:T(8,128)(2,1)S(1)} %pad_maximum_fusion.2.refs_0_), channel_id=1, source_target_pairs={{0,1},{1,2},{2,3},{3,0},{4,5},{5,6},{6,7},{7,4},{8,9},{9,10},{10,1... | collective-permute-start | bytes 1253384 | tf_op jit(solution)/shard_map/ppermute | solution.py:36
  46.7 27.8 %collective-permute-start.8 = (bf16[2,272,384]{2,1,0:T(8,128)(2,1)S(1)}, bf16[2,272,384]{2,1,0:T(8,128)(2,1)S(1)}, u32[]{:S(2)}, u32[]{:S(2)}) collective-permute-start(bf16[2,272,384]{2,1,0:T(8,128)(2,1)S(1)} %pad_maximum_fusion.2.refs_0_), channel_id=1, source_target_pairs={{0,3},{1,0},{2,1},{3,2},{4,7},{5,4},{6,5},{7,6},{8,11},{9,8},{10,9... | collective-permute-start | bytes 1253384 | tf_op jit(solution)/shard_map/ppermute | solution.py:36
  65.2 20.2 %collective-permute-start.4 = (bf16[2,272,384]{2,1,0:T(8,128)(2,1)S(1)}, bf16[2,272,384]{2,1,0:T(8,128)(2,1)S(1)}, u32[]{:S(2)}, u32[]{:S(2)}) collective-permute-start(bf16[2,272,384]{2,1,0:T(8,128)(2,1)S(1)} %collective-permute-done.3.refs_5_), channel_id=1, source_target_pairs={{0,1},{1,2},{2,3},{3,0},{4,5},{5,6},{6,7},{7,4},{8,9},{9,10},{10,1... | collective-permute-start | bytes 1253384 | tf_op jit(solution)/shard_map/ppermute | solution.py:36
  68.6 16.8 %collective-permute-start.5 = (bf16[2,272,384]{2,1,0:T(8,128)(2,1)S(1)}, bf16[2,272,384]{2,1,0:T(8,128)(2,1)S(1)}, u32[]{:S(2)}, u32[]{:S(2)}) collective-permute-start(bf16[2,272,384]{2,1,0:T(8,128)(2,1)S(1)} %collective-permute-done.3.refs_5_), channel_id=1, source_target_pairs={{0,3},{1,0},{2,1},{3,2},{4,7},{5,4},{6,5},{7,6},{8,11},{9,8},{10,9... | collective-permute-start | bytes 1253384 | tf_op jit(solution)/shard_map/ppermute | solution.py:36
  72.3 11.2 %collective-permute-start.7 = (bf16[1,272,384]{2,1,0:T(8,128)(2,1)S(1)}, bf16[1,272,384]{2,1,0:T(8,128)(2,1)S(1)}, u32[]{:S(2)}, u32[]{:S(2)}) collective-permute-start(bf16[1,272,384]{2,1,0:T(8,128)(2,1)S(1)} %slice.62), channel_id=1, source_target_pairs={{0,1},{1,2},{2,3},{3,0},{4,5},{5,6},{6,7},{7,4},{8,9},{9,10},{10,1... | collective-permute-start | bytes 626696 | tf_op jit(solution)/shard_map/ppermute | solution.py:36
  74.5 10.9 %collective-permute-start.9 = (bf16[1,272,384]{2,1,0:T(8,128)(2,1)S(1)}, bf16[1,272,384]{2,1,0:T(8,128)(2,1)S(1)}, u32[]{:S(2)}, u32[]{:S(2)}) collective-permute-start(bf16[1,272,384]{2,1,0:T(8,128)(2,1)S(1)} %slice.63), channel_id=1, source_target_pairs={{0,3},{1,0},{2,1},{3,2},{4,7},{5,4},{6,5},{7,6},{8,11},{9,8},{10,9... | collective-permute-start | bytes 626696 | tf_op jit(solution)/shard_map/ppermute | solution.py:36
  86.2 18.9 %collective-permute-start.10 = (bf16[1,272,384]{2,1,0:T(8,128)(2,1)}, bf16[1,272,384]{2,1,0:T(8,128)(2,1)}, u32[]{:S(2)}, u32[]{:S(2)}) collective-permute-start(bf16[1,272,384]{2,1,0:T(8,128)(2,1)} %slice.52), channel_id=1, source_target_pairs={{0,1},{1,2},{2,3},{3,0},{4,5},{5,6},{6,7},{7,4},{8,9},{9,10},{10,1... | collective-permute-start | bytes 626696 | tf_op jit(solution)/shard_map/ppermute | solution.py:36
  90.3 14.8 %collective-permute-start.11 = (bf16[1,272,384]{2,1,0:T(8,128)(2,1)}, bf16[1,272,384]{2,1,0:T(8,128)(2,1)}, u32[]{:S(2)}, u32[]{:S(2)}) collective-permute-start(bf16[1,272,384]{2,1,0:T(8,128)(2,1)} %slice.53), channel_id=1, source_target_pairs={{0,3},{1,0},{2,1},{3,2},{4,7},{5,4},{6,5},{7,6},{8,11},{9,8},{10,9... | collective-permute-start | bytes 626696 | tf_op jit(solution)/shard_map/ppermute | solution.py:36
  94.6 10.5 %all-to-all-start.2 = ((bf16[4,16,1024]{2,1,0:T(8,128)(2,1)}), bf16[4,16,1024]{2,1,0:T(8,128)(2,1)}, u32[]{:S(2)}, u32[]{:S(2)}) async-start(bf16[4,16,1024]{2,1,0:T(8,128)(2,1)} %broadcast_in_dim.14), calls=%async_computation.2 | async-start | bytes 262144 | tf_op jit(solution)/shard_map/all_to_all | solution.py:48
  111.0 8.0 %collective-permute-start.12 = (bf16[256,6144]{1,0:T(8,128)(2,1)}, bf16[256,6144]{1,0:T(8,128)(2,1)}, u32[]{:S(2)}, u32[]{:S(2)}) collective-permute-start(bf16[256,6144]{1,0:T(8,128)(2,1)} %teacher_norm.1.own_ref), channel_id=1, source_target_pairs={{0,16},{16,0},{1,17},{17,1},{2,18},{18,2},{3,19},{19,3},{4,20},{20... | collective-permute-start | bytes 9437192 | tf_op jit(solution)/shard_map/ppermute | solution.py:36
  114.8 16.2 %all-to-all-start.3 = ((bf16[4,64,1024]{2,1,0:T(8,128)(2,1)}), bf16[4,64,1024]{2,1,0:T(8,128)(2,1)S(1)}, u32[]{:S(2)}, u32[]{:S(2)}) async-start(bf16[4,64,1024]{2,1,0:T(8,128)(2,1)} %broadcast_in_dim.15), calls=%async_computation.3 | async-start | bytes 1048576 | tf_op jit(solution)/shard_map/all_to_all | solution.py:48
  128.8 3.4 %collective-permute-start.13 = (f32[256,128]{1,0:T(8,128)S(1)}, f32[256,128]{1,0:T(8,128)S(1)}, u32[]{:S(2)}, u32[]{:S(2)}) collective-permute-start(f32[256,128]{1,0:T(8,128)S(1)} %get-tuple-element.39), channel_id=1, source_target_pairs={{0,16},{16,0},{1,17},{17,1},{2,18},{18,2},{3,19},{19,3},{4,20},{20... | collective-permute-start | bytes 393224 | tf_op jit(solution)/shard_map/ppermute | solution.py:36
  133.1 13.1 %all-to-all-start.4 = ((f32[16,2,256]{2,1,0:T(2,128)}), f32[16,2,256]{2,1,0:T(2,128)S(1)}, u32[]{:S(2)}, u32[]{:S(2)}) async-start(f32[16,2,256]{2,1,0:T(2,128)} %broadcast_in_dim.16), calls=%async_computation.4 | async-start | bytes 65536 | tf_op jit(solution)/shard_map/all_to_all | solution.py:48
  175.5 11.7 %all-to-all-start.8 = ((bf16[4,64,1024]{2,1,0:T(8,128)(2,1)}), bf16[4,64,1024]{2,1,0:T(8,128)(2,1)S(1)}, u32[]{:S(2)}, u32[]{:S(2)}) async-start(bf16[4,64,1024]{2,1,0:T(8,128)(2,1)} %broadcast_in_dim.19), calls=%async_computation.8 | async-start | bytes 1048576 | tf_op jit(solution)/shard_map/all_to_all | solution.py:48
  (10 other events, 70.7 us)
Sparse Core Ops, SparseCore 0:
  40.2 60.7 all-gather.2

commit v7 on v6

--- a/solution.py
+++ b/solution.py
@@ -64,6 +64,12 @@
 def mp_scatter_zl(term):
     rows, cols = term.shape
     return sum_parts(swap(term.reshape(4, rows // 4, cols), "zl")).astype(BF16)
+
+
+def mp_sum_zl(part):
+    for bits in (1, 2):
+        part = (part.astype(F32) + flip(part, "zl", bits).astype(F32)).astype(BF16)
+    return part
 
 
 def mp_gather_zl(part):
@@ -85,18 +91,12 @@
     return mean, spreads / (count * 16)
 
 
-def norm_kernel(place, *refs):
-    n_ref = refs[-1]
-    x, my_zl, my_zh = place[0], place[1], place[2]
+def norm_kernel(place, pair_ref, late_ref, n_ref):
+    my_zl, my_zh = place[0], place[1]
     blocks = []
-    for half in range(2):
-        own, left, right, low, high = refs[5 * half : 5 * half + 5]
-        for i in range(2):
-            blocks.append((own, i, 2 * half + i, 0))
-            blocks.append((left, i, 2 * half + i, 3))
-            blocks.append((right, i, 2 * half + i, 1))
-        blocks.append((low, 0, 2 * half, 2))
-        blocks.append((high, 0, 2 * half + 1, 2))
+    for dz in range(4):
+        for x in range(4):
+            blocks.append(((pair_ref, late_ref)[dz // 2], (x, dz % 2), dz, x))
     width = 16 * 384
 
     def fold(values):
@@ -106,21 +106,20 @@
     def _(t):
         rows = pl.ds(pl.multiple_of(t * 32, 32), 32)
         total = jnp.zeros((32, 128), F32)
-        for ref, i, dz, off in blocks:
-            total += fold(ref[i, rows, :].astype(F32))
+        for ref, (i, j), dz, x in blocks:
+            total += fold(ref[i, j, rows, :].astype(F32))
         mean = jnp.sum(total, axis=1, keepdims=True) / width
         total = jnp.zeros((32, 128), F32)
-        for ref, i, dz, off in blocks:
-            d = ref[i, rows, :].astype(F32) - mean
+        for ref, (i, j), dz, x in blocks:
+            d = ref[i, j, rows, :].astype(F32) - mean
             total += fold(d * d)
         rstd = lax.rsqrt(jnp.sum(total, axis=1, keepdims=True) / width + EPSILON)
-        for ref, i, dz, off in blocks:
-            gains = ref[i, 256:272, :].astype(F32)
+        for ref, (i, j), dz, x in blocks:
+            gains = ref[i, j, 256:272, :].astype(F32)
             gain = gains[0:1] + gains[1:2] + gains[2:3]
             zl = my_zl ^ dz
-            xs = lax.rem(x + off, 4)
-            spot = ((zl & 1) * 4 + xs) * 2 + ((zl >> 1) ^ my_zh)
-            d = ref[i, rows, :].astype(F32) - mean
+            spot = ((zl & 1) * 4 + x) * 2 + ((zl >> 1) ^ my_zh)
+            d = ref[i, j, rows, :].astype(F32) - mean
             n_ref[rows, pl.ds(pl.multiple_of(spot * 384, 128), 384)] = (
                 d * rstd * gain
             ).astype(BF16)
@@ -190,20 +189,11 @@
     weight = lax.all_gather(rows, "y").reshape(6144, 384)
 
     late = flip(pair, "zl", 2)
-    left, right = shift(pair, "x", 1), shift(pair, "x", -1)
-    part = mp_scatter_zl(tie(part, rows))
-    late = tie(late, part)
-    late_left, late_right = shift(late, "x", 1), shift(late, "x", -1)
-    low, high = shift(left[:1], "x", 1), shift(right[1:], "x", -1)
-    late_left, late_right, part, low, high = lax.optimization_barrier(
-        (late_left, late_right, part, low, high)
-    )
-    late_low, late_high = shift(late_left[:1], "x", 1), shift(late_right[1:], "x", -1)
-    part = mp_gather_zl(part)
-    late_low, part = lax.optimization_barrier((late_low, part))
-    blocks = (pair, left, right, low, high, late, late_left, late_right, late_low, late_high)
-
-    place_x = jnp.stack([lax.axis_index("x"), lax.axis_index("zl"), lax.axis_index("zh")])
+    pair = spread(pair, "x")
+    part = mp_sum_zl(tie(part, rows))
+    late, part = lax.optimization_barrier((spread(tie(late, pair), "x"), part))
+
+    place_z = jnp.stack([lax.axis_index("zl"), lax.axis_index("zh")])
     place_c = lax.axis_index("c").reshape(1)
     smem = pl.BlockSpec(memory_space=pltpu.SMEM)
     vmem = pl.BlockSpec(memory_space=pltpu.VMEM)
@@ -211,14 +201,14 @@
     normed = pl.pallas_call(
         norm_kernel,
         out_shape=jax.ShapeDtypeStruct((256, 6144), BF16),
-        in_specs=[smem] + [vmem] * 10,
+        in_specs=[smem] + [vmem] * 2,
         out_specs=vmem,
         compiler_params=params,
         cost_estimate=pl.CostEstimate(
             flops=1000, bytes_accessed=1000, transcendentals=0
         ),
         name="teacher_norm",
-    )(place_x, *blocks)
+    )(place_z, pair, late)
     normed_other = shift(normed, "c", 1)
     mlp_sum = mp_gather_x(tie(part, normed))
     heads = pl.pallas_call(

time: 242 us -> 232 us (0.959)
  waiting for transfers between devices: 35.1 us -> 58 us
  starting transfers between devices: 73.7 us -> 55.9 us
  blocking collectives: 84.5 us -> 69.8 us
    ppermute x10 -> x2, starting transfers between devices: 32.4 us -> 4.21 us  [shift(): lax.ppermute(values, axis, [(i, (i + step) % size) for i in range(size)])]
    ppermute x4 -> x6, waiting for transfers between devices: 7.01 us -> 34.4 us  [flip(): lax.ppermute(values, axes, [(i, i ^ bits) for i in range(SIZES[axes])])]
    all_to_all x4 -> x3, blocking collectives: 41.8 us -> 27.8 us  [swap(): return lax.all_to_all(values, axis, split_axis=0, concat_axis=0)]
    ppermute x4 -> x6, starting transfers between devices: 20.3 us -> 26 us  [flip(): lax.ppermute(values, axes, [(i, i ^ bits) for i in range(SIZES[axes])])]
    ppermute x10 -> x2, waiting for transfers between devices: 7.65 us -> 2.59 us  [shift(): lax.ppermute(values, axis, [(i, (i + step) % size) for i in range(size)])]
    all_to_all x5 -> x6, starting transfers between devices: 21 us -> 25.6 us  [swap(): return lax.all_to_all(values, axis, split_axis=0, concat_axis=0)]
    broadcast_in_dim x4 -> x5, local copies, waits for them, and re-layouts: 3.27 us -> 5.45 us  [spread(): jnp.broadcast_to(values[None], (SIZES[axis],) + values.shape)]
    all_to_all x5 -> x6, waiting for transfers between devices: 20.4 us -> 20.9 us  [swap(): return lax.all_to_all(values, axis, split_axis=0, concat_axis=0)]
  transfers between devices with their start and end apart: 20 -> 15, of which waited for: 9 -> 11; matrix products, arithmetic and copies ran while one was open for 3% -> 4% of each run, Pallas kernels for 5% -> 6%
where the time goes in v7:
time: 232 us; the launch traced here: 231 us
  blocking collectives  69.8 us (30%)
  waiting for transfers between devices  58 us (25%)
  starting transfers between devices  55.9 us (24%)
  between operations  14.5 us (6%)
  Pallas kernels  13.5 us (6%)
  local copies, waits for them, and re-layouts  11.2 us (5%)
  matrix products  4.83 us (2%)
  other arithmetic  3.25 us (1%)
    all_to_all x1, blocking collectives, reduce_dp(): terms = lax.all_to_all(terms, ('zh', 'y'), split_axis=1, concat_axis=0)  36.9 us
    ppermute x6, waiting for transfers between devices, flip(): lax.ppermute(values, axes, [(i, i ^ bits) for i in range(SIZES[axes])])  34.4 us
    all_to_all x3, blocking collectives, swap(): return lax.all_to_all(values, axis, split_axis=0, concat_axis=0)  27.8 us
    ppermute x6, starting transfers between devices, flip(): lax.ppermute(values, axes, [(i, i ^ bits) for i in range(SIZES[axes])])  26 us
    all_to_all x6, starting transfers between devices, swap(): return lax.all_to_all(values, axis, split_axis=0, concat_axis=0)  25.6 us
    all_to_all x6, waiting for transfers between devices, swap(): return lax.all_to_all(values, axis, split_axis=0, concat_axis=0)  20.9 us
    pallas_call x1, Pallas kernels, shards(): pl.pallas_call(attention_kernel, out_shape=jax.ShapeDtypeStruct((2, 256,...  7.35 us
    pallas_call x1, Pallas kernels, shards(): pl.pallas_call(norm_kernel, out_shape=jax.ShapeDtypeStruct((256, 6144), B...  6.15 us
  transfers between devices with their start and end apart: 15, of which 11 were waited for; matrix products, arithmetic and copies ran while one was open for 4% of the time, Pallas kernels for 6%

profile of v7, /device:TPU:8, one launch (start us, length us, event | category | flops | bytes accessed | tf_op | source)
XLA Modules:
  0.0 231.0 jit_solution(10189009538046699324)
XLA Ops:
  8.9 10.9 %collective-permute-start = (bf16[2,192,384]{2,1,0:T(8,128)(2,1)S(1)}, bf16[2,192,384]{2,1,0:T(8,128)(2,1)S(1)}, u32[]{:S(2)}, u32[]{:S(2)}) collective-permute-start(bf16[2,192,384]{2,1,0:T(8,128)(2,1)S(1)} %reverse_select_fusion), channel_id=1, source_target_pairs={{0,256},{256,0},{1,257},{257,1},{2,258},{258,2},{3,259},{259,3},{4... | collective-permute-start | bytes 884744 | tf_op jit(solution)/shard_map/ppermute | solution.py:40
  20.1 3.4 %collective-permute-start.2 = (bf16[272,384]{1,0:T(8,128)(2,1)S(1)}, bf16[272,384]{1,0:T(8,128)(2,1)S(1)}, u32[]{:S(2)}, u32[]{:S(2)}) collective-permute-start(bf16[272,384]{1,0:T(8,128)(2,1)S(1)} %concatenate.14), channel_id=1, source_target_pairs={{0,4},{4,0},{8,12},{12,8},{1,5},{5,1},{9,13},{13,9},{2,6},{6,2},{1... | collective-permute-start | bytes 626696 | tf_op jit(solution)/shard_map/ppermute | solution.py:40
  26.5 4.3 %all-to-all-start = ((bf16[4,64,1024]{2,1,0:T(8,128)(2,1)}), bf16[4,64,1024]{2,1,0:T(8,128)(2,1)S(1)}, u32[]{:S(2)}, u32[]{:S(2)}) async-start(bf16[4,64,1024]{2,1,0:T(8,128)(2,1)} %bitcast.1), calls=%async_computation | async-start | bytes 1048576 | tf_op jit(solution)/shard_map/all_to_all | solution.py:48
  35.5 3.4 %collective-permute-done.2 = bf16[272,384]{1,0:T(8,128)(2,1)S(1)} collective-permute-done((bf16[272,384]{1,0:T(8,128)(2,1)S(1)}, bf16[272,384]{1,0:T(8,128)(2,1)S(1)}, u32[]{:S(2)}, u32[]{:S(2)}) %collective-permute-start.2) | collective-permute-done | bytes 208928 | tf_op jit(solution)/shard_map/ppermute | solution.py:40
  42.3 3.6 %all-to-all-start.1 = ((bf16[4,2,272,384]{3,2,1,0:T(8,128)(2,1)}), bf16[4,2,272,384]{3,2,1,0:T(8,128)(2,1)S(1)}, u32[]{:S(2)}, u32[]{:S(2)}) async-start(bf16[4,2,272,384]{3,2,1,0:T(8,128)(2,1)} %broadcast_in_dim.16), calls=%async_computation.1 | async-start | bytes 3342336 | tf_op jit(solution)/shard_map/all_to_all | solution.py:48
  45.9 4.3 %collective-permute-start.3 = (bf16[2,272,384]{2,1,0:T(8,128)(2,1)S(1)}, bf16[2,272,384]{2,1,0:T(8,128)(2,1)}, u32[]{:S(2)}, u32[]{:S(2)}) collective-permute-start(bf16[2,272,384]{2,1,0:T(8,128)(2,1)S(1)} %pad_maximum_fusion.2), channel_id=1, source_target_pairs={{0,8},{4,12},{8,0},{12,4},{1,9},{5,13},{9,1},{13,5},{2,10},{6,14},... | collective-permute-start | bytes 1253384 | tf_op jit(solution)/shard_map/ppermute | solution.py:40
  50.2 17.6 %collective-permute-done.3 = bf16[2,272,384]{2,1,0:T(8,128)(2,1)} collective-permute-done((bf16[2,272,384]{2,1,0:T(8,128)(2,1)S(1)}, bf16[2,272,384]{2,1,0:T(8,128)(2,1)}, u32[]{:S(2)}, u32[]{:S(2)}) %collective-permute-start.3) | collective-permute-done | bytes 417824 | tf_op jit(solution)/shard_map/ppermute | solution.py:40
  70.2 4.5 %all-to-all-start.2 = ((bf16[4,2,272,384]{3,2,1,0:T(8,128)(2,1)}), bf16[4,2,272,384]{3,2,1,0:T(8,128)(2,1)}, u32[]{:S(2)}, u32[]{:S(2)}) async-start(bf16[4,2,272,384]{3,2,1,0:T(8,128)(2,1)} %broadcast_in_dim.17), calls=%async_computation.2 | async-start | bytes 3342336 | tf_op jit(solution)/shard_map/all_to_all | solution.py:48
  76.6 4.9 %collective-permute-done.4 = bf16[64,1024]{1,0:T(8,128)(2,1)S(1)} collective-permute-done((bf16[64,1024]{1,0:T(8,128)(2,1)S(1)}, bf16[64,1024]{1,0:T(8,128)(2,1)S(1)}, u32[]{:S(2)}, u32[]{:S(2)}) %collective-permute-start.4) | collective-permute-done | bytes 131104 | tf_op jit(solution)/shard_map/ppermute | solution.py:40
  81.6 3.6 %collective-permute-start.5 = (bf16[64,1024]{1,0:T(8,128)(2,1)S(1)}, bf16[64,1024]{1,0:T(8,128)(2,1)S(1)}, u32[]{:S(2)}, u32[]{:S(2)}) collective-permute-start(bf16[64,1024]{1,0:T(8,128)(2,1)S(1)} %add_convert_fusion.1), channel_id=1, source_target_pairs={{0,8},{4,12},{8,0},{12,4},{1,9},{5,13},{9,1},{13,5},{2,10},{6,14},... | collective-permute-start | bytes 393224 | tf_op jit(solution)/shard_map/ppermute | solution.py:40
  85.3 5.9 %collective-permute-done.5 = bf16[64,1024]{1,0:T(8,128)(2,1)S(1)} collective-permute-done((bf16[64,1024]{1,0:T(8,128)(2,1)S(1)}, bf16[64,1024]{1,0:T(8,128)(2,1)S(1)}, u32[]{:S(2)}, u32[]{:S(2)}) %collective-permute-start.5) | collective-permute-done | bytes 131104 | tf_op jit(solution)/shard_map/ppermute | solution.py:40
  91.2 4.8 %all-to-all-done.2.late_ref = bf16[4,2,272,384]{3,2,1,0:T(8,128)(2,1)} async-done(((bf16[4,2,272,384]{3,2,1,0:T(8,128)(2,1)}), bf16[4,2,272,384]{3,2,1,0:T(8,128)(2,1)}, u32[]{:S(2)}, u32[]{:S(2)}) %all-to-all-start.2) | async-done | bytes 1671200 | tf_op jit(solution)/shard_map/all_to_all | solution.py:48
  96.1 6.2 %teacher_norm.1.own_ref = bf16[256,6144]{1,0:T(8,128)(2,1)} custom-call(s32[2]{0:T(128)S(1)} %pad_add_fusion.place, bf16[4,2,272,384]{3,2,1,0:T(8,128)(2,1)S(1)} %all-to-all-done.1.pair_ref, bf16[4,2,272,384]{3,2,1,0:T(8,128)(2,1)} %all-to-all-done.2.late_ref), custom_call_target="tpu_custom_call" | custom-call | flops 1000 | bytes 1000 | tf_op jit(solution)/shard_map/teacher_norm/pallas_call | solution.py:201
  105.1 3.5 %all-to-all-start.3 = ((bf16[4,64,1024]{2,1,0:T(8,128)(2,1)}), bf16[4,64,1024]{2,1,0:T(8,128)(2,1)S(1)}, u32[]{:S(2)}, u32[]{:S(2)}) async-start(bf16[4,64,1024]{2,1,0:T(8,128)(2,1)} %broadcast_in_dim.18), calls=%async_computation.3 | async-start | bytes 1048576 | tf_op jit(solution)/shard_map/all_to_all | solution.py:48
  112.6 7.4 %teacher_heads.1 = f32[2,256,128]{2,1,0:T(8,128)S(1)} custom-call(s32[1]{0:T(128)} %bitcast.7.place, bf16[256,6144]{1,0:T(8,128)(2,1)} %teacher_norm.1.own_ref, bf16[256,6144]{1,0:T(8,128)(2,1)} %collective-permute-done.6.other_ref, bf16[6144,384]{1,0:T(8,128)(2,1)S(1)} %bitcast.52, f32[2,128]{1,0:T(2,128)S(1)} %copy-done.2), custom_call_target="tpu_custom_call" | custom-call | flops 2415919104 | bytes 11000000 | tf_op jit(solution)/shard_map/teacher_heads/pallas_call | solution.py:214
  124.3 6.0 %all-to-all-start.4 = ((f32[16,2,256]{2,1,0:T(2,128)}), f32[16,2,256]{2,1,0:T(2,128)S(1)}, u32[]{:S(2)}, u32[]{:S(2)}) async-start(f32[16,2,256]{2,1,0:T(2,128)} %broadcast_in_dim.19), calls=%async_computation.4 | async-start | bytes 65536 | tf_op jit(solution)/shard_map/all_to_all | solution.py:48
  130.6 7.8 %all-to-all-done.4 = f32[16,2,256]{2,1,0:T(2,128)S(1)} async-done(((f32[16,2,256]{2,1,0:T(2,128)}), f32[16,2,256]{2,1,0:T(2,128)S(1)}, u32[]{:S(2)}, u32[]{:S(2)}) %all-to-all-start.4) | async-done | bytes 32800 | tf_op jit(solution)/shard_map/all_to_all | solution.py:48
  138.9 11.1 %all_to_all.63 = bf16[4,64,1024]{2,1,0:T(8,128)(2,1)S(1)} all-to-all(bf16[4,64,1024]{2,1,0:T(8,128)(2,1)S(1)} %bitcast.54), channel_id=1, replica_groups=mesh['zh'=2,'y'=8,'c'=2,'zl'=4,'x'=4] {'x'}, dimensions={0} | all-to-all | bytes 1048576 | tf_op jit(solution)/shard_map/all_to_all | solution.py:48
  150.1 8.3 %all_to_all.64 = bf16[4,16,1024]{2,1,0:T(8,128)(2,1)S(1)} all-to-all(bf16[4,16,1024]{2,1,0:T(8,128)(2,1)S(1)} %bitcast.61), channel_id=1, replica_groups=mesh['zh'=2,'y'=8,'c'=2,'zl'=4,'x'=4] {'zl'}, dimensions={0} | all-to-all | bytes 262144 | tf_op jit(solution)/shard_map/all_to_all | solution.py:48
  158.4 8.4 %all_to_all.65 = bf16[4,16,1024]{2,1,0:T(8,128)(2,1)S(1)} all-to-all(bf16[4,16,1024]{2,1,0:T(8,128)(2,1)S(1)} %broadcast_in_dim.20), channel_id=1, replica_groups=mesh['zh'=2,'y'=8,'c'=2,'zl'=4,'x'=4] {'zl'}, dimensions={0} | all-to-all | bytes 262144 | tf_op jit(solution)/shard_map/all_to_all | solution.py:48
  167.7 3.8 %all-to-all-start.8 = ((bf16[4,64,1024]{2,1,0:T(8,128)(2,1)}), bf16[4,64,1024]{2,1,0:T(8,128)(2,1)S(1)}, u32[]{:S(2)}, u32[]{:S(2)}) async-start(bf16[4,64,1024]{2,1,0:T(8,128)(2,1)} %broadcast_in_dim.22), calls=%async_computation.8 | async-start | bytes 1048576 | tf_op jit(solution)/shard_map/all_to_all | solution.py:48
  171.9 7.4 %all-to-all-done.8 = bf16[4,64,1024]{2,1,0:T(8,128)(2,1)S(1)} async-done(((bf16[4,64,1024]{2,1,0:T(8,128)(2,1)}), bf16[4,64,1024]{2,1,0:T(8,128)(2,1)S(1)}, u32[]{:S(2)}, u32[]{:S(2)}) %all-to-all-start.8) | async-done | bytes 524320 | tf_op jit(solution)/shard_map/all_to_all | solution.py:48
  181.0 5.0 %all_to_all.66 = bf16[1,3,16,2,32,256]{5,4,2,1,0,3:T(8,128)(2,1)S(1)} all-to-all(bf16[1,3,16,2,32,256]{5,4,2,1,0,3:T(8,128)(2,1)S(1)} %copy.35), channel_id=1, replica_groups=mesh['zh'=2,'y'=8,'c'=2,'zl'=4,'x'=4] {'c'}, dimensions={3} | all-to-all | bytes 3145728 | tf_op jit(solution)/shard_map/all_to_all | solution.py:146
  186.4 36.9 %all_to_all.67 = bf16[1,3,16,32,256]{4,3,1,0,2:T(8,128)(2,1)S(1)} all-to-all(bf16[1,3,16,32,256]{4,3,1,0,2:T(8,128)(2,1)S(1)} %copy.34), channel_id=1, replica_groups=mesh['zh'=2,'y'=8,'c'=2,'zl'=4,'x'=4] {'zh','y'}, dimensions={2} | all-to-all | bytes 1572864 | tf_op jit(solution)/shard_map/all_to_all | solution.py:148
  (98 shorter events, 33.4 us)
Async XLA Ops:
  7.2 18.3 %copy-start = (bf16[256,1024]{1,0:T(8,128)(2,1)S(1)}, bf16[256,1024]{1,0:T(8,128)(2,1)}, u32[]{:S(2)}) copy-start(bf16[256,1024]{1,0:T(8,128)(2,1)} %param.16) | copy-start | bytes 1572868
  7.2 12.7 %copy-start.8 = (f32[384]{0:T(512)S(1)}, f32[384]{0:T(512)}, u32[]{:S(2)}) copy-start(f32[384]{0:T(512)} %param.10) | copy-start | bytes 4612
  7.2 12.8 %copy-start.5 = (bf16[256,384]{1,0:T(8,128)(2,1)S(1)}, bf16[256,384]{1,0:T(8,128)(2,1)}, u32[]{:S(2)}) copy-start(bf16[256,384]{1,0:T(8,128)(2,1)} %param.9) | copy-start | bytes 589828
  7.2 16.3 %copy-start.3 = (bf16[256,1024]{1,0:T(8,128)(2,1)S(1)}, bf16[256,1024]{1,0:T(8,128)(2,1)}, u32[]{:S(2)}) copy-start(bf16[256,1024]{1,0:T(8,128)(2,1)} %param.13) | copy-start | bytes 1572868
  8.3 15.6 %copy-start.11 = (f32[1024]{0:T(1024)S(1)}, f32[1024]{0:T(1024)}, u32[]{:S(2)}) copy-start(f32[1024]{0:T(1024)} %param.14) | copy-start | bytes 12292
  8.9 24.5 %collective-permute-start = (bf16[2,192,384]{2,1,0:T(8,128)(2,1)S(1)}, bf16[2,192,384]{2,1,0:T(8,128)(2,1)S(1)}, u32[]{:S(2)}, u32[]{:S(2)}) collective-permute-start(bf16[2,192,384]{2,1,0:T(8,128)(2,1)S(1)} %reverse_select_fusion), channel_id=1, source_target_pairs={{0,256},{256,0},{1,257},{257,1},{2,258},{258,2},{3,259},{259,3},{4... | collective-permute-start | bytes 884744 | tf_op jit(solution)/shard_map/ppermute | solution.py:40
  20.1 18.7 %collective-permute-start.2 = (bf16[272,384]{1,0:T(8,128)(2,1)S(1)}, bf16[272,384]{1,0:T(8,128)(2,1)S(1)}, u32[]{:S(2)}, u32[]{:S(2)}) collective-permute-start(bf16[272,384]{1,0:T(8,128)(2,1)S(1)} %concatenate.14), channel_id=1, source_target_pairs={{0,4},{4,0},{8,12},{12,8},{1,5},{5,1},{9,13},{13,9},{2,6},{6,2},{1... | collective-permute-start | bytes 626696 | tf_op jit(solution)/shard_map/ppermute | solution.py:40
  26.5 13.2 %all-to-all-start = ((bf16[4,64,1024]{2,1,0:T(8,128)(2,1)}), bf16[4,64,1024]{2,1,0:T(8,128)(2,1)S(1)}, u32[]{:S(2)}, u32[]{:S(2)}) async-start(bf16[4,64,1024]{2,1,0:T(8,128)(2,1)} %bitcast.1), calls=%async_computation | async-start | bytes 1048576 | tf_op jit(solution)/shard_map/all_to_all | solution.py:48
  30.8 79.4 %all-gather.3.cloned.1.call-start = ((), (), s32[]{:S(2)}) async-start(), calls=%async_computation.11 | async-start | bytes 5308416 | tf_op jit(solution)/shard_map/all_gather | solution.py:189
  33.6 6.3 %collective-permute-start.1 = (bf16[2,192,384]{2,1,0:T(8,128)(2,1)S(1)}, bf16[2,192,384]{2,1,0:T(8,128)(2,1)S(1)}, u32[]{:S(2)}, u32[]{:S(2)}) collective-permute-start(bf16[2,192,384]{2,1,0:T(8,128)(2,1)S(1)} %pad_maximum_fusion.3), channel_id=1, source_target_pairs={{0,16},{16,0},{1,17},{17,1},{2,18},{18,2},{3,19},{19,3},{4,20},{20... | collective-permute-start | bytes 884744 | tf_op jit(solution)/shard_map/ppermute | solution.py:40
  42.3 25.5 %all-to-all-start.1 = ((bf16[4,2,272,384]{3,2,1,0:T(8,128)(2,1)}), bf16[4,2,272,384]{3,2,1,0:T(8,128)(2,1)S(1)}, u32[]{:S(2)}, u32[]{:S(2)}) async-start(bf16[4,2,272,384]{3,2,1,0:T(8,128)(2,1)} %broadcast_in_dim.16), calls=%async_computation.1 | async-start | bytes 3342336 | tf_op jit(solution)/shard_map/all_to_all | solution.py:48
  45.9 21.9 %collective-permute-start.3 = (bf16[2,272,384]{2,1,0:T(8,128)(2,1)S(1)}, bf16[2,272,384]{2,1,0:T(8,128)(2,1)}, u32[]{:S(2)}, u32[]{:S(2)}) collective-permute-start(bf16[2,272,384]{2,1,0:T(8,128)(2,1)S(1)} %pad_maximum_fusion.2), channel_id=1, source_target_pairs={{0,8},{4,12},{8,0},{12,4},{1,9},{5,13},{9,1},{13,5},{2,10},{6,14},... | collective-permute-start | bytes 1253384 | tf_op jit(solution)/shard_map/ppermute | solution.py:40
  70.2 25.9 %all-to-all-start.2 = ((bf16[4,2,272,384]{3,2,1,0:T(8,128)(2,1)}), bf16[4,2,272,384]{3,2,1,0:T(8,128)(2,1)}, u32[]{:S(2)}, u32[]{:S(2)}) async-start(bf16[4,2,272,384]{3,2,1,0:T(8,128)(2,1)} %broadcast_in_dim.17), calls=%async_computation.2 | async-start | bytes 3342336 | tf_op jit(solution)/shard_map/all_to_all | solution.py:48
  74.7 6.8 %collective-permute-start.4 = (bf16[64,1024]{1,0:T(8,128)(2,1)S(1)}, bf16[64,1024]{1,0:T(8,128)(2,1)S(1)}, u32[]{:S(2)}, u32[]{:S(2)}) collective-permute-start(bf16[64,1024]{1,0:T(8,128)(2,1)S(1)} %reduce_sum.125), channel_id=1, source_target_pairs={{0,4},{4,0},{8,12},{12,8},{1,5},{5,1},{9,13},{13,9},{2,6},{6,2},{1... | collective-permute-start | bytes 393224 | tf_op jit(solution)/shard_map/ppermute | solution.py:40
  81.6 9.6 %collective-permute-start.5 = (bf16[64,1024]{1,0:T(8,128)(2,1)S(1)}, bf16[64,1024]{1,0:T(8,128)(2,1)S(1)}, u32[]{:S(2)}, u32[]{:S(2)}) collective-permute-start(bf16[64,1024]{1,0:T(8,128)(2,1)S(1)} %add_convert_fusion.1), channel_id=1, source_target_pairs={{0,8},{4,12},{8,0},{12,4},{1,9},{5,13},{9,1},{13,5},{2,10},{6,14},... | collective-permute-start | bytes 393224 | tf_op jit(solution)/shard_map/ppermute | solution.py:40
  102.2 8.0 %collective-permute-start.6 = (bf16[256,6144]{1,0:T(8,128)(2,1)}, bf16[256,6144]{1,0:T(8,128)(2,1)}, u32[]{:S(2)}, u32[]{:S(2)}) collective-permute-start(bf16[256,6144]{1,0:T(8,128)(2,1)} %teacher_norm.1.own_ref), channel_id=1, source_target_pairs={{0,16},{16,0},{1,17},{17,1},{2,18},{18,2},{3,19},{19,3},{4,20},{20... | collective-permute-start | bytes 9437192 | tf_op jit(solution)/shard_map/ppermute | solution.py:36
  105.1 17.0 %all-to-all-start.3 = ((bf16[4,64,1024]{2,1,0:T(8,128)(2,1)}), bf16[4,64,1024]{2,1,0:T(8,128)(2,1)S(1)}, u32[]{:S(2)}, u32[]{:S(2)}) async-start(bf16[4,64,1024]{2,1,0:T(8,128)(2,1)} %broadcast_in_dim.18), calls=%async_computation.3 | async-start | bytes 1048576 | tf_op jit(solution)/shard_map/all_to_all | solution.py:48
  119.9 10.4 %copy-start.4 = (bf16[1024,256]{1,0:T(8,128)(2,1)S(1)}, bf16[1024,256]{1,0:T(8,128)(2,1)}, u32[]{:S(2)}) copy-start(bf16[1024,256]{1,0:T(8,128)(2,1)} %param.17) | copy-start | bytes 1572868
  120.0 3.4 %collective-permute-start.7 = (f32[256,128]{1,0:T(8,128)S(1)}, f32[256,128]{1,0:T(8,128)S(1)}, u32[]{:S(2)}, u32[]{:S(2)}) collective-permute-start(f32[256,128]{1,0:T(8,128)S(1)} %get-tuple-element.29), channel_id=1, source_target_pairs={{0,16},{16,0},{1,17},{17,1},{2,18},{18,2},{3,19},{19,3},{4,20},{20... | collective-permute-start | bytes 393224 | tf_op jit(solution)/shard_map/ppermute | solution.py:36
  124.3 14.2 %all-to-all-start.4 = ((f32[16,2,256]{2,1,0:T(2,128)}), f32[16,2,256]{2,1,0:T(2,128)S(1)}, u32[]{:S(2)}, u32[]{:S(2)}) async-start(f32[16,2,256]{2,1,0:T(2,128)} %broadcast_in_dim.19), calls=%async_computation.4 | async-start | bytes 65536 | tf_op jit(solution)/shard_map/all_to_all | solution.py:48
  167.7 11.7 %copy-start.7 = (f32[256]{0:T(256)S(1)}, f32[256]{0:T(256)}, u32[]{:S(2)}) copy-start(f32[256]{0:T(256)} %copy-done.6) | copy-start | bytes 3076
  167.7 11.7 %copy-start.10 = (f32[256]{0:T(256)S(1)}, f32[256]{0:T(256)}, u32[]{:S(2)}) copy-start(f32[256]{0:T(256)} %copy-done.9) | copy-start | bytes 3076
  167.7 11.7 %copy-start.12 = (f32[1024]{0:T(1024)S(1)}, f32[1024]{0:T(1024)}, u32[]{:S(2)}) copy-start(f32[1024]{0:T(1024)} %param.14) | copy-start | bytes 12292
  167.7 11.7 %all-to-all-start.8 = ((bf16[4,64,1024]{2,1,0:T(8,128)(2,1)}), bf16[4,64,1024]{2,1,0:T(8,128)(2,1)S(1)}, u32[]{:S(2)}, u32[]{:S(2)}) async-start(bf16[4,64,1024]{2,1,0:T(8,128)(2,1)} %broadcast_in_dim.22), calls=%async_computation.8 | async-start | bytes 1048576 | tf_op jit(solution)/shard_map/all_to_all | solution.py:48
  (4 other events, 15.8 us)
Sparse Core Ops, SparseCore 0:
  41.0 59.8 all-gather.2

commit v8 on v7

--- a/solution.py
+++ b/solution.py
@@ -61,20 +61,10 @@
     return sum_parts(swap(term.reshape(4, rows // 4, cols), "x")).astype(BF16)
 
 
-def mp_scatter_zl(term):
-    rows, cols = term.shape
-    return sum_parts(swap(term.reshape(4, rows // 4, cols), "zl")).astype(BF16)
-
-
 def mp_sum_zl(part):
     for bits in (1, 2):
         part = (part.astype(F32) + flip(part, "zl", bits).astype(F32)).astype(BF16)
     return part
-
-
-def mp_gather_zl(part):
-    rows, cols = part.shape
-    return spread(part, "zl").reshape(4 * rows, cols)
 
 
 def mp_gather_x(part):
@@ -96,7 +86,7 @@
     blocks = []
     for dz in range(4):
         for x in range(4):
-            blocks.append(((pair_ref, late_ref)[dz // 2], (x, dz % 2), dz, x))
+            blocks.append(((pair_ref, late_ref)[dz % 2], (x, dz // 2), dz, x))
     width = 16 * 384
 
     def fold(values):
@@ -171,7 +161,7 @@
     low = teacher_gain - hi - mid
     gain_rows = jnp.stack([hi, mid, low] + [jnp.zeros_like(hi)] * 13).astype(BF16)
     shard = tie(jnp.concatenate([teacher_in, gain_rows], axis=0), near)
-    pair = jnp.stack([shard, flip(shard, "zl", 1)])
+    pair = jnp.stack([shard, flip(shard, "zl", 2)])
 
     student_normed = (normalize(student_in.astype(F32)) * student_gain).astype(BF16)
     pre_act = jnp.dot(student_normed, up_weight, preferred_element_type=F32)
@@ -188,7 +178,7 @@
     rows = jnp.concatenate([by_core(near[0], given[0]), by_core(far[0], given[1])])
     weight = lax.all_gather(rows, "y").reshape(6144, 384)
 
-    late = flip(pair, "zl", 2)
+    late = flip(pair, "zl", 1)
     pair = spread(pair, "x")
     part = mp_sum_zl(tie(part, rows))
     late, part = lax.optimization_barrier((spread(tie(late, pair), "x"), part))
@@ -242,8 +232,7 @@
     grad_pred = ((predicted - target) * loss_factor).astype(BF16)
     block_term = jnp.einsum("tf,cf->tc", grad_pred, projector, preferred_element_type=F32)
     proj_term = jnp.einsum("tc,tf->cf", block_out, grad_pred, preferred_element_type=F32)
-    grad_block = mp_scatter_zl(mp_scatter_x(block_term.astype(BF16)))
-    grad_block = mp_gather_x(mp_gather_zl(grad_block))
+    grad_block = mp_gather_x(mp_sum_zl(mp_scatter_x(block_term.astype(BF16))))
     down_term = jnp.einsum("tc,tf->cf", grad_block, activ, preferred_element_type=F32)
     grad_act = jnp.einsum("tc,fc->tf", grad_block, down_weight, preferred_element_type=F32)
     grad_pre = (grad_act * slope).astype(BF16)

time: 232 us -> 231 us (level)
  blocking collectives: 69.8 us -> 49.6 us
  waiting for transfers between devices: 58 us -> 74.6 us
    all_to_all x3 -> x1, blocking collectives: 27.8 us -> 11.1 us  [swap(): return lax.all_to_all(values, axis, split_axis=0, concat_axis=0)]
    all_to_all x6, waiting for transfers between devices: 20.9 us -> 29.3 us  [swap(): return lax.all_to_all(values, axis, split_axis=0, concat_axis=0)]
    ppermute x6 -> x8, waiting for transfers between devices: 34.4 us -> 42.7 us  [flip(): lax.ppermute(values, axes, [(i, i ^ bits) for i in range(SIZES[axes])])]
    all_to_all x1, blocking collectives: 36.9 us -> 33.5 us  [reduce_dp(): terms = lax.all_to_all(terms, ('zh', 'y'), split_axis=1, concat_axis=0)]
    ppermute x6 -> x8, starting transfers between devices: 26 us -> 28.6 us  [flip(): lax.ppermute(values, axes, [(i, i ^ bits) for i in range(SIZES[axes])])]
    broadcast_in_dim x5 -> x4, local copies, waits for them, and re-layouts: 5.45 us -> 5.48 us  [spread(): jnp.broadcast_to(values[None], (SIZES[axis],) + values.shape)]
  transfers between devices with their start and end apart: 15 -> 17, of which waited for: 11 -> 13; matrix products, arithmetic and copies ran while one was open for 4% -> 4% of each run, Pallas kernels for 6% -> 6%
where the time goes in v8:
time: 231 us; the launch traced here: 230 us
  waiting for transfers between devices  74.6 us (32%)
  starting transfers between devices  58.1 us (25%)
  blocking collectives  49.6 us (21%)
  between operations  14.6 us (6%)
  Pallas kernels  13.5 us (6%)
  local copies, waits for them, and re-layouts  11.3 us (5%)
  matrix products  4.83 us (2%)
  other arithmetic  3.31 us (1%)
    ppermute x8, waiting for transfers between devices, flip(): lax.ppermute(values, axes, [(i, i ^ bits) for i in range(SIZES[axes])])  42.7 us
    all_to_all x1, blocking collectives, reduce_dp(): terms = lax.all_to_all(terms, ('zh', 'y'), split_axis=1, concat_axis=0)  33.5 us
    all_to_all x6, waiting for transfers between devices, swap(): return lax.all_to_all(values, axis, split_axis=0, concat_axis=0)  29.3 us
    ppermute x8, starting transfers between devices, flip(): lax.ppermute(values, axes, [(i, i ^ bits) for i in range(SIZES[axes])])  28.6 us
    all_to_all x6, starting transfers between devices, swap(): return lax.all_to_all(values, axis, split_axis=0, concat_axis=0)  25.3 us
    all_to_all x1, blocking collectives, swap(): return lax.all_to_all(values, axis, split_axis=0, concat_axis=0)  11.1 us
    pallas_call x1, Pallas kernels, shards(): pl.pallas_call(attention_kernel, out_shape=jax.ShapeDtypeStruct((2, 256,...  7.35 us
    pallas_call x1, Pallas kernels, shards(): pl.pallas_call(norm_kernel, out_shape=jax.ShapeDtypeStruct((256, 6144), B...  6.14 us
  transfers between devices with their start and end apart: 17, of which 13 were waited for; matrix products, arithmetic and copies ran while one was open for 4% of the time, Pallas kernels for 6%

profile of v8, /device:TPU:8, one launch (start us, length us, event | category | flops | bytes accessed | tf_op | source)
XLA Modules:
  0.0 229.7 jit_solution(973636557502417429)
XLA Ops:
  8.9 10.9 %collective-permute-start = (bf16[2,192,384]{2,1,0:T(8,128)(2,1)S(1)}, bf16[2,192,384]{2,1,0:T(8,128)(2,1)S(1)}, u32[]{:S(2)}, u32[]{:S(2)}) collective-permute-start(bf16[2,192,384]{2,1,0:T(8,128)(2,1)S(1)} %reverse_select_fusion), channel_id=1, source_target_pairs={{0,256},{256,0},{1,257},{257,1},{2,258},{258,2},{3,259},{259,3},{4... | collective-permute-start | bytes 884744 | tf_op jit(solution)/shard_map/ppermute | solution.py:40
  20.1 4.3 %collective-permute-start.2 = (bf16[272,384]{1,0:T(8,128)(2,1)S(1)}, bf16[272,384]{1,0:T(8,128)(2,1)S(1)}, u32[]{:S(2)}, u32[]{:S(2)}) collective-permute-start(bf16[272,384]{1,0:T(8,128)(2,1)S(1)} %concatenate.14), channel_id=1, source_target_pairs={{0,8},{4,12},{8,0},{12,4},{1,9},{5,13},{9,1},{13,5},{2,10},{6,14},... | collective-permute-start | bytes 626696 | tf_op jit(solution)/shard_map/ppermute | solution.py:40
  27.5 4.3 %all-to-all-start = ((bf16[4,64,1024]{2,1,0:T(8,128)(2,1)}), bf16[4,64,1024]{2,1,0:T(8,128)(2,1)S(1)}, u32[]{:S(2)}, u32[]{:S(2)}) async-start(bf16[4,64,1024]{2,1,0:T(8,128)(2,1)} %bitcast.1), calls=%async_computation | async-start | bytes 1048576 | tf_op jit(solution)/shard_map/all_to_all | solution.py:48
  35.5 7.8 %collective-permute-done.2 = bf16[272,384]{1,0:T(8,128)(2,1)S(1)} collective-permute-done((bf16[272,384]{1,0:T(8,128)(2,1)S(1)}, bf16[272,384]{1,0:T(8,128)(2,1)S(1)}, u32[]{:S(2)}, u32[]{:S(2)}) %collective-permute-start.2) | collective-permute-done | bytes 208928 | tf_op jit(solution)/shard_map/ppermute | solution.py:40
  45.9 4.3 %all-to-all-start.1 = ((bf16[4,2,272,384]{3,2,1,0:T(8,128)(2,1)}), bf16[4,2,272,384]{3,2,1,0:T(8,128)(2,1)S(1)}, u32[]{:S(2)}, u32[]{:S(2)}) async-start(bf16[4,2,272,384]{3,2,1,0:T(8,128)(2,1)} %broadcast_in_dim.12), calls=%async_computation.1 | async-start | bytes 3342336 | tf_op jit(solution)/shard_map/all_to_all | solution.py:48
  52.1 11.4 %collective-permute-done.3 = bf16[2,272,384]{2,1,0:T(8,128)(2,1)} collective-permute-done((bf16[2,272,384]{2,1,0:T(8,128)(2,1)S(1)}, bf16[2,272,384]{2,1,0:T(8,128)(2,1)}, u32[]{:S(2)}, u32[]{:S(2)}) %collective-permute-start.3) | collective-permute-done | bytes 417824 | tf_op jit(solution)/shard_map/ppermute | solution.py:40
  63.5 8.7 %all-to-all-done.1.pair_ref = bf16[4,2,272,384]{3,2,1,0:T(8,128)(2,1)S(1)} async-done(((bf16[4,2,272,384]{3,2,1,0:T(8,128)(2,1)}), bf16[4,2,272,384]{3,2,1,0:T(8,128)(2,1)S(1)}, u32[]{:S(2)}, u32[]{:S(2)}) %all-to-all-start.1) | async-done | bytes 1671200 | tf_op jit(solution)/shard_map/all_to_all | solution.py:48
  74.6 4.4 %all-to-all-start.2 = ((bf16[4,2,272,384]{3,2,1,0:T(8,128)(2,1)}), bf16[4,2,272,384]{3,2,1,0:T(8,128)(2,1)}, u32[]{:S(2)}, u32[]{:S(2)}) async-start(bf16[4,2,272,384]{3,2,1,0:T(8,128)(2,1)} %broadcast_in_dim.13), calls=%async_computation.2 | async-start | bytes 3342336 | tf_op jit(solution)/shard_map/all_to_all | solution.py:48
  80.9 4.9 %collective-permute-done.4 = bf16[64,1024]{1,0:T(8,128)(2,1)S(1)} collective-permute-done((bf16[64,1024]{1,0:T(8,128)(2,1)S(1)}, bf16[64,1024]{1,0:T(8,128)(2,1)S(1)}, u32[]{:S(2)}, u32[]{:S(2)}) %collective-permute-start.4) | collective-permute-done | bytes 131104 | tf_op jit(solution)/shard_map/ppermute | solution.py:40
  85.9 2.8 %collective-permute-start.5 = (bf16[64,1024]{1,0:T(8,128)(2,1)S(1)}, bf16[64,1024]{1,0:T(8,128)(2,1)S(1)}, u32[]{:S(2)}, u32[]{:S(2)}) collective-permute-start(bf16[64,1024]{1,0:T(8,128)(2,1)S(1)} %add_convert_fusion.3), channel_id=1, source_target_pairs={{0,8},{4,12},{8,0},{12,4},{1,9},{5,13},{9,1},{13,5},{2,10},{6,14},... | collective-permute-start | bytes 393224 | tf_op jit(solution)/shard_map/ppermute | solution.py:40
  88.8 5.9 %collective-permute-done.5 = bf16[64,1024]{1,0:T(8,128)(2,1)S(1)} collective-permute-done((bf16[64,1024]{1,0:T(8,128)(2,1)S(1)}, bf16[64,1024]{1,0:T(8,128)(2,1)S(1)}, u32[]{:S(2)}, u32[]{:S(2)}) %collective-permute-start.5) | collective-permute-done | bytes 131104 | tf_op jit(solution)/shard_map/ppermute | solution.py:40
  94.7 5.3 %all-to-all-done.2.late_ref = bf16[4,2,272,384]{3,2,1,0:T(8,128)(2,1)} async-done(((bf16[4,2,272,384]{3,2,1,0:T(8,128)(2,1)}), bf16[4,2,272,384]{3,2,1,0:T(8,128)(2,1)}, u32[]{:S(2)}, u32[]{:S(2)}) %all-to-all-start.2) | async-done | bytes 1671200 | tf_op jit(solution)/shard_map/all_to_all | solution.py:48
  100.1 6.1 %teacher_norm.1.own_ref = bf16[256,6144]{1,0:T(8,128)(2,1)} custom-call(s32[2]{0:T(128)S(1)} %pad_add_fusion.place, bf16[4,2,272,384]{3,2,1,0:T(8,128)(2,1)S(1)} %all-to-all-done.1.pair_ref, bf16[4,2,272,384]{3,2,1,0:T(8,128)(2,1)} %all-to-all-done.2.late_ref), custom_call_target="tpu_custom_call" | custom-call | flops 1000 | bytes 1000 | tf_op jit(solution)/shard_map/teacher_norm/pallas_call | solution.py:191
  109.1 3.5 %all-to-all-start.3 = ((bf16[4,64,1024]{2,1,0:T(8,128)(2,1)}), bf16[4,64,1024]{2,1,0:T(8,128)(2,1)S(1)}, u32[]{:S(2)}, u32[]{:S(2)}) async-start(bf16[4,64,1024]{2,1,0:T(8,128)(2,1)} %broadcast_in_dim.14), calls=%async_computation.3 | async-start | bytes 1048576 | tf_op jit(solution)/shard_map/all_to_all | solution.py:48
  116.6 7.4 %teacher_heads.1 = f32[2,256,128]{2,1,0:T(8,128)S(1)} custom-call(s32[1]{0:T(128)} %bitcast.7.place, bf16[256,6144]{1,0:T(8,128)(2,1)} %teacher_norm.1.own_ref, bf16[256,6144]{1,0:T(8,128)(2,1)} %collective-permute-done.6.other_ref, bf16[6144,384]{1,0:T(8,128)(2,1)S(1)} %bitcast.50, f32[2,128]{1,0:T(2,128)S(1)} %copy-done.2), custom_call_target="tpu_custom_call" | custom-call | flops 2415919104 | bytes 11000000 | tf_op jit(solution)/shard_map/teacher_heads/pallas_call | solution.py:204
  128.3 5.0 %all-to-all-start.4 = ((f32[16,2,256]{2,1,0:T(2,128)}), f32[16,2,256]{2,1,0:T(2,128)S(1)}, u32[]{:S(2)}, u32[]{:S(2)}) async-start(f32[16,2,256]{2,1,0:T(2,128)} %broadcast_in_dim.15), calls=%async_computation.4 | async-start | bytes 65536 | tf_op jit(solution)/shard_map/all_to_all | solution.py:48
  133.7 7.8 %all-to-all-done.4 = f32[16,2,256]{2,1,0:T(2,128)S(1)} async-done(((f32[16,2,256]{2,1,0:T(2,128)}), f32[16,2,256]{2,1,0:T(2,128)S(1)}, u32[]{:S(2)}, u32[]{:S(2)}) %all-to-all-start.4) | async-done | bytes 32800 | tf_op jit(solution)/shard_map/all_to_all | solution.py:48
  141.9 11.1 %all_to_all.53 = bf16[4,64,1024]{2,1,0:T(8,128)(2,1)S(1)} all-to-all(bf16[4,64,1024]{2,1,0:T(8,128)(2,1)S(1)} %bitcast.52), channel_id=1, replica_groups=mesh['zh'=2,'y'=8,'c'=2,'zl'=4,'x'=4] {'x'}, dimensions={0} | all-to-all | bytes 1048576 | tf_op jit(solution)/shard_map/all_to_all | solution.py:48
  155.4 4.6 %collective-permute-done.8 = bf16[64,1024]{1,0:T(8,128)(2,1)S(1)} collective-permute-done((bf16[64,1024]{1,0:T(8,128)(2,1)S(1)}, bf16[64,1024]{1,0:T(8,128)(2,1)S(1)}, u32[]{:S(2)}, u32[]{:S(2)}) %collective-permute-start.8) | collective-permute-done | bytes 131104 | tf_op jit(solution)/shard_map/ppermute | solution.py:40
  162.6 6.4 %collective-permute-done.9 = bf16[64,1024]{1,0:T(8,128)(2,1)S(1)} collective-permute-done((bf16[64,1024]{1,0:T(8,128)(2,1)S(1)}, bf16[64,1024]{1,0:T(8,128)(2,1)S(1)}, u32[]{:S(2)}, u32[]{:S(2)}) %collective-permute-start.9) | collective-permute-done | bytes 131104 | tf_op jit(solution)/shard_map/ppermute | solution.py:40
  169.9 3.8 %all-to-all-start.6 = ((bf16[4,64,1024]{2,1,0:T(8,128)(2,1)}), bf16[4,64,1024]{2,1,0:T(8,128)(2,1)S(1)}, u32[]{:S(2)}, u32[]{:S(2)}) async-start(bf16[4,64,1024]{2,1,0:T(8,128)(2,1)} %broadcast_in_dim.16), calls=%async_computation.6 | async-start | bytes 1048576 | tf_op jit(solution)/shard_map/all_to_all | solution.py:48
  174.1 7.4 %all-to-all-done.6 = bf16[4,64,1024]{2,1,0:T(8,128)(2,1)S(1)} async-done(((bf16[4,64,1024]{2,1,0:T(8,128)(2,1)}), bf16[4,64,1024]{2,1,0:T(8,128)(2,1)S(1)}, u32[]{:S(2)}, u32[]{:S(2)}) %all-to-all-start.6) | async-done | bytes 524320 | tf_op jit(solution)/shard_map/all_to_all | solution.py:48
  183.1 5.0 %all_to_all.54 = bf16[1,3,16,2,32,256]{5,4,2,1,0,3:T(8,128)(2,1)S(1)} all-to-all(bf16[1,3,16,2,32,256]{5,4,2,1,0,3:T(8,128)(2,1)S(1)} %copy.35), channel_id=1, replica_groups=mesh['zh'=2,'y'=8,'c'=2,'zl'=4,'x'=4] {'c'}, dimensions={3} | all-to-all | bytes 3145728 | tf_op jit(solution)/shard_map/all_to_all | solution.py:136
  188.6 33.5 %all_to_all.55 = bf16[1,3,16,32,256]{4,3,1,0,2:T(8,128)(2,1)S(1)} all-to-all(bf16[1,3,16,32,256]{4,3,1,0,2:T(8,128)(2,1)S(1)} %copy.34), channel_id=1, replica_groups=mesh['zh'=2,'y'=8,'c'=2,'zl'=4,'x'=4] {'zh','y'}, dimensions={2} | all-to-all | bytes 1572864 | tf_op jit(solution)/shard_map/all_to_all | solution.py:138
  (100 shorter events, 38.6 us)
Async XLA Ops:
  7.2 19.2 %copy-start = (bf16[256,1024]{1,0:T(8,128)(2,1)S(1)}, bf16[256,1024]{1,0:T(8,128)(2,1)}, u32[]{:S(2)}) copy-start(bf16[256,1024]{1,0:T(8,128)(2,1)} %param.16) | copy-start | bytes 1572868
  7.2 12.7 %copy-start.8 = (f32[384]{0:T(512)S(1)}, f32[384]{0:T(512)}, u32[]{:S(2)}) copy-start(f32[384]{0:T(512)} %param.10) | copy-start | bytes 4612
  7.2 12.8 %copy-start.5 = (bf16[256,384]{1,0:T(8,128)(2,1)S(1)}, bf16[256,384]{1,0:T(8,128)(2,1)}, u32[]{:S(2)}) copy-start(bf16[256,384]{1,0:T(8,128)(2,1)} %param.9) | copy-start | bytes 589828
  7.2 17.2 %copy-start.3 = (bf16[256,1024]{1,0:T(8,128)(2,1)S(1)}, bf16[256,1024]{1,0:T(8,128)(2,1)}, u32[]{:S(2)}) copy-start(bf16[256,1024]{1,0:T(8,128)(2,1)} %param.13) | copy-start | bytes 1572868
  8.3 16.5 %copy-start.11 = (f32[1024]{0:T(1024)S(1)}, f32[1024]{0:T(1024)}, u32[]{:S(2)}) copy-start(f32[1024]{0:T(1024)} %param.14) | copy-start | bytes 12292
  8.9 24.6 %collective-permute-start = (bf16[2,192,384]{2,1,0:T(8,128)(2,1)S(1)}, bf16[2,192,384]{2,1,0:T(8,128)(2,1)S(1)}, u32[]{:S(2)}, u32[]{:S(2)}) collective-permute-start(bf16[2,192,384]{2,1,0:T(8,128)(2,1)S(1)} %reverse_select_fusion), channel_id=1, source_target_pairs={{0,256},{256,0},{1,257},{257,1},{2,258},{258,2},{3,259},{259,3},{4... | collective-permute-start | bytes 884744 | tf_op jit(solution)/shard_map/ppermute | solution.py:40
  20.1 23.2 %collective-permute-start.2 = (bf16[272,384]{1,0:T(8,128)(2,1)S(1)}, bf16[272,384]{1,0:T(8,128)(2,1)S(1)}, u32[]{:S(2)}, u32[]{:S(2)}) collective-permute-start(bf16[272,384]{1,0:T(8,128)(2,1)S(1)} %concatenate.14), channel_id=1, source_target_pairs={{0,8},{4,12},{8,0},{12,4},{1,9},{5,13},{9,1},{13,5},{2,10},{6,14},... | collective-permute-start | bytes 626696 | tf_op jit(solution)/shard_map/ppermute | solution.py:40
  27.5 15.9 %all-to-all-start = ((bf16[4,64,1024]{2,1,0:T(8,128)(2,1)}), bf16[4,64,1024]{2,1,0:T(8,128)(2,1)S(1)}, u32[]{:S(2)}, u32[]{:S(2)}) async-start(bf16[4,64,1024]{2,1,0:T(8,128)(2,1)} %bitcast.1), calls=%async_computation | async-start | bytes 1048576 | tf_op jit(solution)/shard_map/all_to_all | solution.py:48
  31.7 82.5 %all-gather.3.cloned.1.call-start = ((), (), s32[]{:S(2)}) async-start(), calls=%async_computation.9 | async-start | bytes 5308416 | tf_op jit(solution)/shard_map/all_gather | solution.py:179
  33.6 9.9 %collective-permute-start.1 = (bf16[2,192,384]{2,1,0:T(8,128)(2,1)S(1)}, bf16[2,192,384]{2,1,0:T(8,128)(2,1)S(1)}, u32[]{:S(2)}, u32[]{:S(2)}) collective-permute-start(bf16[2,192,384]{2,1,0:T(8,128)(2,1)S(1)} %pad_maximum_fusion.3), channel_id=1, source_target_pairs={{0,16},{16,0},{1,17},{17,1},{2,18},{18,2},{3,19},{19,3},{4,20},{20... | collective-permute-start | bytes 884744 | tf_op jit(solution)/shard_map/ppermute | solution.py:40
  45.9 26.2 %all-to-all-start.1 = ((bf16[4,2,272,384]{3,2,1,0:T(8,128)(2,1)}), bf16[4,2,272,384]{3,2,1,0:T(8,128)(2,1)S(1)}, u32[]{:S(2)}, u32[]{:S(2)}) async-start(bf16[4,2,272,384]{3,2,1,0:T(8,128)(2,1)} %broadcast_in_dim.12), calls=%async_computation.1 | async-start | bytes 3342336 | tf_op jit(solution)/shard_map/all_to_all | solution.py:48
  50.2 13.3 %collective-permute-start.3 = (bf16[2,272,384]{2,1,0:T(8,128)(2,1)S(1)}, bf16[2,272,384]{2,1,0:T(8,128)(2,1)}, u32[]{:S(2)}, u32[]{:S(2)}) collective-permute-start(bf16[2,272,384]{2,1,0:T(8,128)(2,1)S(1)} %pad_maximum_fusion.2), channel_id=1, source_target_pairs={{0,4},{4,0},{8,12},{12,8},{1,5},{5,1},{9,13},{13,9},{2,6},{6,2},{1... | collective-permute-start | bytes 1253384 | tf_op jit(solution)/shard_map/ppermute | solution.py:40
  74.6 25.5 %all-to-all-start.2 = ((bf16[4,2,272,384]{3,2,1,0:T(8,128)(2,1)}), bf16[4,2,272,384]{3,2,1,0:T(8,128)(2,1)}, u32[]{:S(2)}, u32[]{:S(2)}) async-start(bf16[4,2,272,384]{3,2,1,0:T(8,128)(2,1)} %broadcast_in_dim.13), calls=%async_computation.2 | async-start | bytes 3342336 | tf_op jit(solution)/shard_map/all_to_all | solution.py:48
  79.0 6.9 %collective-permute-start.4 = (bf16[64,1024]{1,0:T(8,128)(2,1)S(1)}, bf16[64,1024]{1,0:T(8,128)(2,1)S(1)}, u32[]{:S(2)}, u32[]{:S(2)}) collective-permute-start(bf16[64,1024]{1,0:T(8,128)(2,1)S(1)} %reduce_sum.113), channel_id=1, source_target_pairs={{0,4},{4,0},{8,12},{12,8},{1,5},{5,1},{9,13},{13,9},{2,6},{6,2},{1... | collective-permute-start | bytes 393224 | tf_op jit(solution)/shard_map/ppermute | solution.py:40
  85.9 8.8 %collective-permute-start.5 = (bf16[64,1024]{1,0:T(8,128)(2,1)S(1)}, bf16[64,1024]{1,0:T(8,128)(2,1)S(1)}, u32[]{:S(2)}, u32[]{:S(2)}) collective-permute-start(bf16[64,1024]{1,0:T(8,128)(2,1)S(1)} %add_convert_fusion.3), channel_id=1, source_target_pairs={{0,8},{4,12},{8,0},{12,4},{1,9},{5,13},{9,1},{13,5},{2,10},{6,14},... | collective-permute-start | bytes 393224 | tf_op jit(solution)/shard_map/ppermute | solution.py:40
  106.2 8.0 %collective-permute-start.6 = (bf16[256,6144]{1,0:T(8,128)(2,1)}, bf16[256,6144]{1,0:T(8,128)(2,1)}, u32[]{:S(2)}, u32[]{:S(2)}) collective-permute-start(bf16[256,6144]{1,0:T(8,128)(2,1)} %teacher_norm.1.own_ref), channel_id=1, source_target_pairs={{0,16},{16,0},{1,17},{17,1},{2,18},{18,2},{3,19},{19,3},{4,20},{20... | collective-permute-start | bytes 9437192 | tf_op jit(solution)/shard_map/ppermute | solution.py:36
  109.1 17.0 %all-to-all-start.3 = ((bf16[4,64,1024]{2,1,0:T(8,128)(2,1)}), bf16[4,64,1024]{2,1,0:T(8,128)(2,1)S(1)}, u32[]{:S(2)}, u32[]{:S(2)}) async-start(bf16[4,64,1024]{2,1,0:T(8,128)(2,1)} %broadcast_in_dim.14), calls=%async_computation.3 | async-start | bytes 1048576 | tf_op jit(solution)/shard_map/all_to_all | solution.py:48
  124.0 3.4 %collective-permute-start.7 = (f32[256,128]{1,0:T(8,128)S(1)}, f32[256,128]{1,0:T(8,128)S(1)}, u32[]{:S(2)}, u32[]{:S(2)}) collective-permute-start(f32[256,128]{1,0:T(8,128)S(1)} %get-tuple-element.29), channel_id=1, source_target_pairs={{0,16},{16,0},{1,17},{17,1},{2,18},{18,2},{3,19},{19,3},{4,20},{20... | collective-permute-start | bytes 393224 | tf_op jit(solution)/shard_map/ppermute | solution.py:36
  128.3 13.2 %all-to-all-start.4 = ((f32[16,2,256]{2,1,0:T(2,128)}), f32[16,2,256]{2,1,0:T(2,128)S(1)}, u32[]{:S(2)}, u32[]{:S(2)}) async-start(f32[16,2,256]{2,1,0:T(2,128)} %broadcast_in_dim.15), calls=%async_computation.4 | async-start | bytes 65536 | tf_op jit(solution)/shard_map/all_to_all | solution.py:48
  153.1 6.9 %collective-permute-start.8 = (bf16[64,1024]{1,0:T(8,128)(2,1)S(1)}, bf16[64,1024]{1,0:T(8,128)(2,1)S(1)}, u32[]{:S(2)}, u32[]{:S(2)}) collective-permute-start(bf16[64,1024]{1,0:T(8,128)(2,1)S(1)} %reduce_sum.119), channel_id=1, source_target_pairs={{0,4},{4,0},{8,12},{12,8},{1,5},{5,1},{9,13},{13,9},{2,6},{6,2},{1... | collective-permute-start | bytes 393224 | tf_op jit(solution)/shard_map/ppermute | solution.py:40
  160.0 9.0 %collective-permute-start.9 = (bf16[64,1024]{1,0:T(8,128)(2,1)S(1)}, bf16[64,1024]{1,0:T(8,128)(2,1)S(1)}, u32[]{:S(2)}, u32[]{:S(2)}) collective-permute-start(bf16[64,1024]{1,0:T(8,128)(2,1)S(1)} %add_convert_fusion.1), channel_id=1, source_target_pairs={{0,8},{4,12},{8,0},{12,4},{1,9},{5,13},{9,1},{13,5},{2,10},{6,14},... | collective-permute-start | bytes 393224 | tf_op jit(solution)/shard_map/ppermute | solution.py:40
  169.9 11.7 %copy-start.10 = (f32[256]{0:T(256)S(1)}, f32[256]{0:T(256)}, u32[]{:S(2)}) copy-start(f32[256]{0:T(256)} %copy-done.9) | copy-start | bytes 3076
  169.9 11.7 %copy-start.12 = (f32[1024]{0:T(1024)S(1)}, f32[1024]{0:T(1024)}, u32[]{:S(2)}) copy-start(f32[1024]{0:T(1024)} %param.14) | copy-start | bytes 12292
  169.9 11.7 %all-to-all-start.6 = ((bf16[4,64,1024]{2,1,0:T(8,128)(2,1)}), bf16[4,64,1024]{2,1,0:T(8,128)(2,1)S(1)}, u32[]{:S(2)}, u32[]{:S(2)}) async-start(bf16[4,64,1024]{2,1,0:T(8,128)(2,1)} %broadcast_in_dim.16), calls=%async_computation.6 | async-start | bytes 1048576 | tf_op jit(solution)/shard_map/all_to_all | solution.py:48
  (6 other events, 36.8 us)
Sparse Core Ops, SparseCore 0:
  44.7 58.5 all-gather.2

commit v9 on v8

--- a/solution.py
+++ b/solution.py
@@ -59,6 +59,17 @@
 def mp_scatter_x(term):
     rows, cols = term.shape
     return sum_parts(swap(term.reshape(4, rows // 4, cols), "x")).astype(BF16)
+
+
+def mp_scatter_x_beside(term):
+    rows, cols = term.shape
+    term = term.reshape(4, rows // 4, cols)
+    x = lax.axis_index("x")
+    total = lax.dynamic_index_in_dim(term, x, 0, False).astype(F32)
+    for bits in (1, 2, 3):
+        given = lax.dynamic_index_in_dim(term, x ^ bits, 0, False)
+        total += flip(given, "x", bits).astype(F32)
+    return total.astype(BF16)
 
 
 def mp_sum_zl(part):
@@ -81,12 +92,17 @@
     return mean, spreads / (count * 16)
 
 
-def norm_kernel(place, pair_ref, late_ref, n_ref):
+def norm_kernel(place, own_ref, near_ref, late_ref, n_ref, gain_ref):
     my_zl, my_zh = place[0], place[1]
     blocks = []
-    for dz in range(4):
-        for x in range(4):
-            blocks.append(((pair_ref, late_ref)[dz % 2], (x, dz // 2), dz, x))
+    for x in range(4):
+        blocks.append((own_ref, (x,), 0, x))
+        blocks.append((near_ref, (x,), 1, x))
+        blocks.append((late_ref, (x, 0), 2, x))
+        blocks.append((late_ref, (x, 1), 3, x))
+    for k, (ref, at, dz, x) in enumerate(blocks):
+        gains = ref[(*at, slice(256, 272), slice(None))].astype(F32)
+        gain_ref[k : k + 1, :] = gains[0:1] + gains[1:2] + gains[2:3]
     width = 16 * 384
 
     def fold(values):
@@ -95,39 +111,39 @@
     @pl.loop(0, 8)
     def _(t):
         rows = pl.ds(pl.multiple_of(t * 32, 32), 32)
+
+        def read(ref, at):
+            return ref[(*at, rows, slice(None))].astype(F32)
+
         total = jnp.zeros((32, 128), F32)
-        for ref, (i, j), dz, x in blocks:
-            total += fold(ref[i, j, rows, :].astype(F32))
+        for ref, at, dz, x in blocks:
+            total += fold(read(ref, at))
         mean = jnp.sum(total, axis=1, keepdims=True) / width
         total = jnp.zeros((32, 128), F32)
-        for ref, (i, j), dz, x in blocks:
-            d = ref[i, j, rows, :].astype(F32) - mean
+        for ref, at, dz, x in blocks:
+            d = read(ref, at) - mean
             total += fold(d * d)
         rstd = lax.rsqrt(jnp.sum(total, axis=1, keepdims=True) / width + EPSILON)
-        for ref, (i, j), dz, x in blocks:
-            gains = ref[i, j, 256:272, :].astype(F32)
-            gain = gains[0:1] + gains[1:2] + gains[2:3]
+        for k, (ref, at, dz, x) in enumerate(blocks):
             zl = my_zl ^ dz
             spot = ((zl & 1) * 4 + x) * 2 + ((zl >> 1) ^ my_zh)
-            d = ref[i, j, rows, :].astype(F32) - mean
             n_ref[rows, pl.ds(pl.multiple_of(spot * 384, 128), 384)] = (
-                d * rstd * gain
+                (read(ref, at) - mean) * rstd * gain_ref[k : k + 1, :]
             ).astype(BF16)
 
 
-def attention_kernel(place, own_ref, other_ref, w_ref, qg_ref, f_ref):
+def attention_kernel(place, n_ref, w_ref, qg_ref, f_ref):
     gain = jnp.where(place[0] == 0, qg_ref[0:1, :], qg_ref[1:2, :])
-    for image, ref in enumerate((own_ref, other_ref)):
-        projected = jnp.dot(ref[...], w_ref[...], preferred_element_type=F32)
-        query = (normalize(projected[:, :128]) * gain).astype(BF16)
-        key = (normalize(projected[:, 128:256]) * gain).astype(BF16)
-        value = projected[:, 256:].astype(BF16)
-        scores = lax.dot_general(
-            query, key, (((1,), (1,)), ((), ())), preferred_element_type=F32
-        ) * (HEAD ** (-0.5))
-        scores = jnp.exp(scores - jnp.max(scores, axis=1, keepdims=True))
-        attn = (scores / jnp.sum(scores, axis=1, keepdims=True)).astype(BF16)
-        f_ref[image] = jnp.dot(attn, value, preferred_element_type=F32)
+    projected = jnp.dot(n_ref[...], w_ref[...], preferred_element_type=F32)
+    query = (normalize(projected[:, :128]) * gain).astype(BF16)
+    key = (normalize(projected[:, 128:256]) * gain).astype(BF16)
+    value = projected[:, 256:].astype(BF16)
+    scores = lax.dot_general(
+        query, key, (((1,), (1,)), ((), ())), preferred_element_type=F32
+    ) * (HEAD ** (-0.5))
+    scores = jnp.exp(scores - jnp.max(scores, axis=1, keepdims=True))
+    attn = (scores / jnp.sum(scores, axis=1, keepdims=True)).astype(BF16)
+    f_ref[...] = jnp.dot(attn, value, preferred_element_type=F32)
 
 
 def reduce_dp(terms):
@@ -161,7 +177,8 @@
     low = teacher_gain - hi - mid
     gain_rows = jnp.stack([hi, mid, low] + [jnp.zeros_like(hi)] * 13).astype(BF16)
     shard = tie(jnp.concatenate([teacher_in, gain_rows], axis=0), near)
-    pair = jnp.stack([shard, flip(shard, "zl", 2)])
+    own = spread(shard, "x")
+    near_block = flip(shard, "zl", 1)
 
     student_normed = (normalize(student_in.astype(F32)) * student_gain).astype(BF16)
     pre_act = jnp.dot(student_normed, up_weight, preferred_element_type=F32)
@@ -172,16 +189,19 @@
     def by_core(mine, theirs):
         return jnp.where(first, jnp.stack([mine, theirs]), jnp.stack([theirs, mine]))
 
-    part = mp_scatter_x(mlp_term)
     given = flip(jnp.stack([near[1], far[1]]), "c")
-    given, part, pair = lax.optimization_barrier((given, part, pair))
+    given, own, near_block, mlp_term = lax.optimization_barrier(
+        (given, own, near_block, mlp_term)
+    )
     rows = jnp.concatenate([by_core(near[0], given[0]), by_core(far[0], given[1])])
     weight = lax.all_gather(rows, "y").reshape(6144, 384)
 
-    late = flip(pair, "zl", 1)
-    pair = spread(pair, "x")
-    part = mp_sum_zl(tie(part, rows))
-    late, part = lax.optimization_barrier((spread(tie(late, pair), "x"), part))
+    late = flip(jnp.stack([shard, near_block]), "zl", 2)
+    near_block = spread(near_block, "x")
+    part = mp_scatter_x_beside(tie(mlp_term, rows))
+    late, part = lax.optimization_barrier((late, part))
+    part = mp_sum_zl(part)
+    late, part = lax.optimization_barrier((spread(tie(late, near_block), "x"), part))
 
     place_z = jnp.stack([lax.axis_index("zl"), lax.axis_index("zh")])
     place_c = lax.axis_index("c").reshape(1)
@@ -191,32 +211,34 @@
     normed = pl.pallas_call(
         norm_kernel,
         out_shape=jax.ShapeDtypeStruct((256, 6144), BF16),
-        in_specs=[smem] + [vmem] * 2,
+        scratch_shapes=[pltpu.VMEM((16, 384), F32)],
+        in_specs=[smem] + [vmem] * 3,
         out_specs=vmem,
         compiler_params=params,
         cost_estimate=pl.CostEstimate(
             flops=1000, bytes_accessed=1000, transcendentals=0
         ),
         name="teacher_norm",
-    )(place_z, pair, late)
+    )(place_z, own, near_block, late)
     normed_other = shift(normed, "c", 1)
     mlp_sum = mp_gather_x(tie(part, normed))
     heads = pl.pallas_call(
         attention_kernel,
-        out_shape=jax.ShapeDtypeStruct((2, 256, 128), F32),
-        in_specs=[smem] + [vmem] * 4,
+        out_shape=jax.ShapeDtypeStruct((256, 128), F32),
+        in_specs=[smem] + [vmem] * 3,
         out_specs=vmem,
         compiler_params=params,
         cost_estimate=pl.CostEstimate(
-            flops=2 * 512 * 6144 * 384, bytes_accessed=11_000_000, transcendentals=131072
+            flops=2 * 256 * 6144 * 384, bytes_accessed=8_000_000, transcendentals=65536
         ),
         name="teacher_heads",
-    )(place_c, normed, normed_other, weight, qk_gain)
-    crossed = shift(heads[1], "c", 1)
+    )
+    crossed = shift(heads(place_c, normed_other, weight, qk_gain), "c", 1)
+    kept = heads(place_c, normed, weight, qk_gain)
     features = jnp.where(
         place_c[0] == 0,
-        jnp.concatenate([heads[0], crossed], axis=1),
-        jnp.concatenate([crossed, heads[0]], axis=1),
+        jnp.concatenate([kept, crossed], axis=1),
+        jnp.concatenate([crossed, kept], axis=1),
     )
 
     block_out = (student_in.astype(F32) + mlp_sum.astype(F32)).astype(BF16)

time: 231 us -> 234 us (1.013)
  waiting for transfers between devices: 74.6 us -> 56.7 us
  starting transfers between devices: 58.1 us -> 68.6 us
  local copies, waits for them, and re-layouts: 11.3 us -> 15.9 us
  blocking collectives: 49.6 us -> 53.4 us
  other arithmetic: 3.31 us -> 6.62 us
    ppermute x8 -> x11, starting transfers between devices: 28.6 us -> 40.9 us  [flip(): lax.ppermute(values, axes, [(i, i ^ bits) for i in range(SIZES[axes])])]
    ppermute x8 -> x11, waiting for transfers between devices: 42.7 us -> 34 us  [flip(): lax.ppermute(values, axes, [(i, i ^ bits) for i in range(SIZES[axes])])]
    all_to_all x6, waiting for transfers between devices: 29.3 us -> 21.1 us  [swap(): return lax.all_to_all(values, axis, split_axis=0, concat_axis=0)]
    all_to_all x1, blocking collectives: 33.5 us -> 37.1 us  [reduce_dp(): terms = lax.all_to_all(terms, ('zh', 'y'), split_axis=1, concat_axis=0)]
    unnamed x26 -> x40, local copies, waits for them, and re-layouts: 2.4 us -> 5.9 us
    pallas_call x1 -> x2, Pallas kernels: 7.35 us -> 8.84 us  [the longest x1 4.42 us: shards(): crossed = shift(heads(place_c, normed_other, weight, qk_gain), 'c', 1)]
    broadcast_in_dim x4 -> x5, local copies, waits for them, and re-layouts: 5.48 us -> 5.23 us  [spread(): jnp.broadcast_to(values[None], (SIZES[axis],) + values.shape)]
  transfers between devices with their start and end apart: 17 -> 20, of which waited for: 13 -> 13; matrix products, arithmetic and copies ran while one was open for 4% -> 5% of each run, Pallas kernels for 6% -> 6%
where the time goes in v9:
time: 234 us; the launch traced here: 233 us
  starting transfers between devices  68.6 us (29%)
  waiting for transfers between devices  56.7 us (24%)
  blocking collectives  53.4 us (23%)
  local copies, waits for them, and re-layouts  15.9 us (7%)
  between operations  14.7 us (6%)
  Pallas kernels  14 us (6%)
  other arithmetic  6.62 us (3%)
  matrix products  2.99 us (1%)
    ppermute x11, starting transfers between devices, flip(): lax.ppermute(values, axes, [(i, i ^ bits) for i in range(SIZES[axes])])  40.9 us
    all_to_all x1, blocking collectives, reduce_dp(): terms = lax.all_to_all(terms, ('zh', 'y'), split_axis=1, concat_axis=0)  37.1 us
    ppermute x11, waiting for transfers between devices, flip(): lax.ppermute(values, axes, [(i, i ^ bits) for i in range(SIZES[axes])])  34 us
    all_to_all x6, starting transfers between devices, swap(): return lax.all_to_all(values, axis, split_axis=0, concat_axis=0)  23.5 us
    all_to_all x6, waiting for transfers between devices, swap(): return lax.all_to_all(values, axis, split_axis=0, concat_axis=0)  21.1 us
    all_to_all x1, blocking collectives, swap(): return lax.all_to_all(values, axis, split_axis=0, concat_axis=0)  11.2 us
    unnamed x40, local copies, waits for them, and re-layouts  5.9 us
    broadcast_in_dim x5, local copies, waits for them, and re-layouts, spread(): jnp.broadcast_to(values[None], (SIZES[axis],) + values.shape)  5.23 us
  transfers between devices with their start and end apart: 20, of which 13 were waited for; matrix products, arithmetic and copies ran while one was open for 5% of the time, Pallas kernels for 6%

profile of v9, /device:TPU:8, one launch (start us, length us, event | category | flops | bytes accessed | tf_op | source)
XLA Modules:
  0.0 232.8 jit_solution(7637931363711850696)
XLA Ops:
  8.9 10.9 %collective-permute-start = (bf16[2,192,384]{2,1,0:T(8,128)(2,1)S(1)}, bf16[2,192,384]{2,1,0:T(8,128)(2,1)S(1)}, u32[]{:S(2)}, u32[]{:S(2)}) collective-permute-start(bf16[2,192,384]{2,1,0:T(8,128)(2,1)S(1)} %reverse_select_fusion), channel_id=1, source_target_pairs={{0,256},{256,0},{1,257},{257,1},{2,258},{258,2},{3,259},{259,3},{4... | collective-permute-start | bytes 884744 | tf_op jit(solution)/shard_map/ppermute | solution.py:40
  24.5 4.3 %all-to-all-start = ((bf16[4,272,384]{2,1,0:T(8,128)(2,1)}), bf16[4,272,384]{2,1,0:T(8,128)(2,1)S(1)}, u32[]{:S(2)}, u32[]{:S(2)}) async-start(bf16[4,272,384]{2,1,0:T(8,128)(2,1)} %broadcast_in_dim.14), calls=%async_computation | async-start | bytes 1671168 | tf_op jit(solution)/shard_map/all_to_all | solution.py:48
  29.9 3.5 %collective-permute-done = bf16[2,192,384]{2,1,0:T(8,128)(2,1)S(1)} collective-permute-done((bf16[2,192,384]{2,1,0:T(8,128)(2,1)S(1)}, bf16[2,192,384]{2,1,0:T(8,128)(2,1)S(1)}, u32[]{:S(2)}, u32[]{:S(2)}) %collective-permute-start) | collective-permute-done | bytes 294944 | tf_op jit(solution)/shard_map/ppermute | solution.py:40
  43.1 3.5 %all-to-all-start.1 = ((bf16[4,272,384]{2,1,0:T(8,128)(2,1)}), bf16[4,272,384]{2,1,0:T(8,128)(2,1)S(1)}, u32[]{:S(2)}, u32[]{:S(2)}) async-start(bf16[4,272,384]{2,1,0:T(8,128)(2,1)} %broadcast_in_dim.15), calls=%async_computation.1 | async-start | bytes 1671168 | tf_op jit(solution)/shard_map/all_to_all | solution.py:48
  47.4 4.3 %collective-permute-start.3 = (bf16[2,272,384]{2,1,0:T(8,128)(2,1)}, bf16[2,272,384]{2,1,0:T(8,128)(2,1)S(1)}, u32[]{:S(2)}, u32[]{:S(2)}) collective-permute-start(bf16[2,272,384]{2,1,0:T(8,128)(2,1)} %pad_maximum_fusion.2), channel_id=1, source_target_pairs={{0,8},{4,12},{8,0},{12,4},{1,9},{5,13},{9,1},{13,5},{2,10},{6,14},... | collective-permute-start | bytes 1253384 | tf_op jit(solution)/shard_map/ppermute | solution.py:40
  52.4 3.9 %collective-permute-start.4 = (bf16[64,1024]{1,0:T(8,128)(2,1)}, bf16[64,1024]{1,0:T(8,128)(2,1)}, u32[]{:S(2)}, u32[]{:S(2)}) collective-permute-start(bf16[64,1024]{1,0:T(8,128)(2,1)} %get-tuple-element.29), channel_id=1, source_target_pairs={{0,1},{1,0},{2,3},{3,2},{4,5},{5,4},{6,7},{7,6},{8,9},{9,8},{10,11... | collective-permute-start | bytes 393224 | tf_op jit(solution)/shard_map/ppermute | solution.py:40
  56.3 4.6 %collective-permute-start.5 = (bf16[64,1024]{1,0:T(8,128)(2,1)}, bf16[64,1024]{1,0:T(8,128)(2,1)}, u32[]{:S(2)}, u32[]{:S(2)}) collective-permute-start(bf16[64,1024]{1,0:T(8,128)(2,1)} %get-tuple-element.31), channel_id=1, source_target_pairs={{0,2},{1,3},{2,0},{3,1},{4,6},{5,7},{6,4},{7,5},{8,10},{9,11},{10,... | collective-permute-start | bytes 393224 | tf_op jit(solution)/shard_map/ppermute | solution.py:40
  65.1 4.0 %collective-permute-done.6 = bf16[64,1024]{1,0:T(8,128)(2,1)} collective-permute-done((bf16[64,1024]{1,0:T(8,128)(2,1)S(1)}, bf16[64,1024]{1,0:T(8,128)(2,1)}, u32[]{:S(2)}, u32[]{:S(2)}) %collective-permute-start.6) | collective-permute-done | bytes 131104 | tf_op jit(solution)/shard_map/ppermute | solution.py:40
  71.7 3.6 %all-to-all-start.2 = ((bf16[4,2,272,384]{3,2,1,0:T(8,128)(2,1)}), bf16[4,2,272,384]{3,2,1,0:T(8,128)(2,1)S(1)}, u32[]{:S(2)}, u32[]{:S(2)}) async-start(bf16[4,2,272,384]{3,2,1,0:T(8,128)(2,1)} %broadcast_in_dim.16), calls=%async_computation.2 | async-start | bytes 3342336 | tf_op jit(solution)/shard_map/all_to_all | solution.py:48
  77.8 4.4 %collective-permute-done.7 = bf16[64,1024]{1,0:T(8,128)(2,1)S(1)} collective-permute-done((bf16[64,1024]{1,0:T(8,128)(2,1)S(1)}, bf16[64,1024]{1,0:T(8,128)(2,1)S(1)}, u32[]{:S(2)}, u32[]{:S(2)}) %collective-permute-start.7) | collective-permute-done | bytes 131104 | tf_op jit(solution)/shard_map/ppermute | solution.py:40
  85.0 6.4 %collective-permute-done.8 = bf16[64,1024]{1,0:T(8,128)(2,1)} collective-permute-done((bf16[64,1024]{1,0:T(8,128)(2,1)S(1)}, bf16[64,1024]{1,0:T(8,128)(2,1)}, u32[]{:S(2)}, u32[]{:S(2)}) %collective-permute-start.8) | collective-permute-done | bytes 131104 | tf_op jit(solution)/shard_map/ppermute | solution.py:40
  93.0 3.6 %all-to-all-done.2.late_ref = bf16[4,2,272,384]{3,2,1,0:T(8,128)(2,1)S(1)} async-done(((bf16[4,2,272,384]{3,2,1,0:T(8,128)(2,1)}), bf16[4,2,272,384]{3,2,1,0:T(8,128)(2,1)S(1)}, u32[]{:S(2)}, u32[]{:S(2)}) %all-to-all-start.2) | async-done | bytes 1671200 | tf_op jit(solution)/shard_map/all_to_all | solution.py:48
  97.8 5.1 %teacher_norm.1.n_ref = bf16[256,6144]{1,0:T(8,128)(2,1)} custom-call(s32[2]{0:T(128)S(1)} %pad_add_fusion.place, bf16[4,272,384]{2,1,0:T(8,128)(2,1)S(1)} %all-to-all-done.own_ref, bf16[4,272,384]{2,1,0:T(8,128)(2,1)S(1)} %copy-done.4, bf16[4,2,272,384]{3,2,1,0:T(8,128)(2,1)S(1)} %all-to-all-done.2.late_ref), custom_call_target="tpu_custom_call" | custom-call | flops 1000 | bytes 1000 | tf_op jit(solution)/shard_map/teacher_norm/pallas_call | solution.py:211
  113.3 4.4 %teacher_heads.3 = f32[256,128]{1,0:T(8,128)S(1)} custom-call(s32[1]{0:T(128)} %bitcast.11.place, bf16[256,6144]{1,0:T(8,128)(2,1)} %collective-permute-done.9.n_ref, bf16[6144,384]{1,0:T(8,128)(2,1)S(1)} %bitcast.55, f32[2,128]{1,0:T(2,128)S(1)} %copy-done.5), custom_call_target="tpu_custom_call" | custom-call | flops 1207959552 | bytes 8000000 | tf_op jit(solution)/shard_map/teacher_heads/pallas_call | solution.py:236
  122.4 4.4 %teacher_heads.2 = f32[256,128]{1,0:T(8,128)S(1)} custom-call(s32[1]{0:T(128)} %bitcast.11.place, bf16[256,6144]{1,0:T(8,128)(2,1)} %teacher_norm.1.n_ref, bf16[6144,384]{1,0:T(8,128)(2,1)S(1)} %bitcast.56, f32[2,128]{1,0:T(2,128)S(1)} %copy-done.5), custom_call_target="tpu_custom_call" | custom-call | flops 1207959552 | bytes 8000000 | tf_op jit(solution)/shard_map/teacher_heads/pallas_call | solution.py:237
  127.8 4.9 %all-to-all-start.4 = ((f32[16,2,256]{2,1,0:T(2,128)}), f32[16,2,256]{2,1,0:T(2,128)S(1)}, u32[]{:S(2)}, u32[]{:S(2)}) async-start(f32[16,2,256]{2,1,0:T(2,128)} %broadcast_in_dim.18), calls=%async_computation.4 | async-start | bytes 65536 | tf_op jit(solution)/shard_map/all_to_all | solution.py:48
  133.0 7.8 %all-to-all-done.4 = f32[16,2,256]{2,1,0:T(2,128)S(1)} async-done(((f32[16,2,256]{2,1,0:T(2,128)}), f32[16,2,256]{2,1,0:T(2,128)S(1)}, u32[]{:S(2)}, u32[]{:S(2)}) %all-to-all-start.4) | async-done | bytes 32800 | tf_op jit(solution)/shard_map/all_to_all | solution.py:48
  141.3 11.2 %all_to_all.53 = bf16[4,64,1024]{2,1,0:T(8,128)(2,1)S(1)} all-to-all(bf16[4,64,1024]{2,1,0:T(8,128)(2,1)S(1)} %bitcast.58), channel_id=1, replica_groups=mesh['zh'=2,'y'=8,'c'=2,'zl'=4,'x'=4] {'x'}, dimensions={0} | all-to-all | bytes 1048576 | tf_op jit(solution)/shard_map/all_to_all | solution.py:48
  154.9 4.6 %collective-permute-done.11 = bf16[64,1024]{1,0:T(8,128)(2,1)S(1)} collective-permute-done((bf16[64,1024]{1,0:T(8,128)(2,1)S(1)}, bf16[64,1024]{1,0:T(8,128)(2,1)S(1)}, u32[]{:S(2)}, u32[]{:S(2)}) %collective-permute-start.11) | collective-permute-done | bytes 131104 | tf_op jit(solution)/shard_map/ppermute | solution.py:40
  162.1 6.4 %collective-permute-done.12 = bf16[64,1024]{1,0:T(8,128)(2,1)S(1)} collective-permute-done((bf16[64,1024]{1,0:T(8,128)(2,1)S(1)}, bf16[64,1024]{1,0:T(8,128)(2,1)S(1)}, u32[]{:S(2)}, u32[]{:S(2)}) %collective-permute-start.12) | collective-permute-done | bytes 131104 | tf_op jit(solution)/shard_map/ppermute | solution.py:40
  169.4 3.8 %all-to-all-start.6 = ((bf16[4,64,1024]{2,1,0:T(8,128)(2,1)}), bf16[4,64,1024]{2,1,0:T(8,128)(2,1)S(1)}, u32[]{:S(2)}, u32[]{:S(2)}) async-start(bf16[4,64,1024]{2,1,0:T(8,128)(2,1)} %broadcast_in_dim.19), calls=%async_computation.6 | async-start | bytes 1048576 | tf_op jit(solution)/shard_map/all_to_all | solution.py:48
  173.6 7.4 %all-to-all-done.6 = bf16[4,64,1024]{2,1,0:T(8,128)(2,1)S(1)} async-done(((bf16[4,64,1024]{2,1,0:T(8,128)(2,1)}), bf16[4,64,1024]{2,1,0:T(8,128)(2,1)S(1)}, u32[]{:S(2)}, u32[]{:S(2)}) %all-to-all-start.6) | async-done | bytes 524320 | tf_op jit(solution)/shard_map/all_to_all | solution.py:48
  182.6 5.0 %all_to_all.54 = bf16[1,3,16,2,32,256]{5,4,2,1,0,3:T(8,128)(2,1)S(1)} all-to-all(bf16[1,3,16,2,32,256]{5,4,2,1,0,3:T(8,128)(2,1)S(1)} %copy.35), channel_id=1, replica_groups=mesh['zh'=2,'y'=8,'c'=2,'zl'=4,'x'=4] {'c'}, dimensions={3} | all-to-all | bytes 3145728 | tf_op jit(solution)/shard_map/all_to_all | solution.py:152
  188.1 37.1 %all_to_all.55 = bf16[1,3,16,32,256]{4,3,1,0,2:T(8,128)(2,1)S(1)} all-to-all(bf16[1,3,16,32,256]{4,3,1,0,2:T(8,128)(2,1)S(1)} %copy.34), channel_id=1, replica_groups=mesh['zh'=2,'y'=8,'c'=2,'zl'=4,'x'=4] {'zh','y'}, dimensions={2} | all-to-all | bytes 1572864 | tf_op jit(solution)/shard_map/all_to_all | solution.py:154
  (122 shorter events, 58.8 us)
Async XLA Ops:
  7.2 28.8 %copy-start = (bf16[256,1024]{1,0:T(8,128)(2,1)S(1)}, bf16[256,1024]{1,0:T(8,128)(2,1)}, u32[]{:S(2)}) copy-start(bf16[256,1024]{1,0:T(8,128)(2,1)} %param.16) | copy-start | bytes 1572868
  7.2 12.6 %copy-start.14 = (f32[384]{0:T(512)S(1)}, f32[384]{0:T(512)}, u32[]{:S(2)}) copy-start(f32[384]{0:T(512)} %param.10) | copy-start | bytes 4612
  7.2 12.7 %copy-start.11 = (bf16[256,384]{1,0:T(8,128)(2,1)S(1)}, bf16[256,384]{1,0:T(8,128)(2,1)}, u32[]{:S(2)}) copy-start(bf16[256,384]{1,0:T(8,128)(2,1)} %param.9) | copy-start | bytes 589828
  8.9 24.5 %collective-permute-start = (bf16[2,192,384]{2,1,0:T(8,128)(2,1)S(1)}, bf16[2,192,384]{2,1,0:T(8,128)(2,1)S(1)}, u32[]{:S(2)}, u32[]{:S(2)}) collective-permute-start(bf16[2,192,384]{2,1,0:T(8,128)(2,1)S(1)} %reverse_select_fusion), channel_id=1, source_target_pairs={{0,256},{256,0},{1,257},{257,1},{2,258},{258,2},{3,259},{259,3},{4... | collective-permute-start | bytes 884744 | tf_op jit(solution)/shard_map/ppermute | solution.py:40
  20.1 18.7 %collective-permute-start.2 = (bf16[272,384]{1,0:T(8,128)(2,1)S(1)}, bf16[272,384]{1,0:T(8,128)(2,1)S(1)}, u32[]{:S(2)}, u32[]{:S(2)}) collective-permute-start(bf16[272,384]{1,0:T(8,128)(2,1)S(1)} %concatenate.14), channel_id=1, source_target_pairs={{0,4},{4,0},{8,12},{12,8},{1,5},{5,1},{9,13},{13,9},{2,6},{6,2},{1... | collective-permute-start | bytes 626696 | tf_op jit(solution)/shard_map/ppermute | solution.py:40
  24.5 16.5 %all-to-all-start = ((bf16[4,272,384]{2,1,0:T(8,128)(2,1)}), bf16[4,272,384]{2,1,0:T(8,128)(2,1)S(1)}, u32[]{:S(2)}, u32[]{:S(2)}) async-start(bf16[4,272,384]{2,1,0:T(8,128)(2,1)} %broadcast_in_dim.14), calls=%async_computation | async-start | bytes 1671168 | tf_op jit(solution)/shard_map/all_to_all | solution.py:48
  28.7 82.3 %all-gather.3.cloned.1.call-start = ((), (), s32[]{:S(2)}) async-start(), calls=%async_computation.9 | async-start | bytes 5308416 | tf_op jit(solution)/shard_map/all_gather | solution.py:197
  33.5 5.3 %collective-permute-start.1 = (bf16[2,192,384]{2,1,0:T(8,128)(2,1)S(1)}, bf16[2,192,384]{2,1,0:T(8,128)(2,1)S(1)}, u32[]{:S(2)}, u32[]{:S(2)}) collective-permute-start(bf16[2,192,384]{2,1,0:T(8,128)(2,1)S(1)} %pad_maximum_fusion.3), channel_id=1, source_target_pairs={{0,16},{16,0},{1,17},{17,1},{2,18},{18,2},{3,19},{19,3},{4,20},{20... | collective-permute-start | bytes 884744 | tf_op jit(solution)/shard_map/ppermute | solution.py:40
  43.1 27.1 %all-to-all-start.1 = ((bf16[4,272,384]{2,1,0:T(8,128)(2,1)}), bf16[4,272,384]{2,1,0:T(8,128)(2,1)S(1)}, u32[]{:S(2)}, u32[]{:S(2)}) async-start(bf16[4,272,384]{2,1,0:T(8,128)(2,1)} %broadcast_in_dim.15), calls=%async_computation.1 | async-start | bytes 1671168 | tf_op jit(solution)/shard_map/all_to_all | solution.py:48
  47.4 22.8 %collective-permute-start.3 = (bf16[2,272,384]{2,1,0:T(8,128)(2,1)}, bf16[2,272,384]{2,1,0:T(8,128)(2,1)S(1)}, u32[]{:S(2)}, u32[]{:S(2)}) collective-permute-start(bf16[2,272,384]{2,1,0:T(8,128)(2,1)} %pad_maximum_fusion.2), channel_id=1, source_target_pairs={{0,8},{4,12},{8,0},{12,4},{1,9},{5,13},{9,1},{13,5},{2,10},{6,14},... | collective-permute-start | bytes 1253384 | tf_op jit(solution)/shard_map/ppermute | solution.py:40
  52.4 10.4 %collective-permute-start.4 = (bf16[64,1024]{1,0:T(8,128)(2,1)}, bf16[64,1024]{1,0:T(8,128)(2,1)}, u32[]{:S(2)}, u32[]{:S(2)}) collective-permute-start(bf16[64,1024]{1,0:T(8,128)(2,1)} %get-tuple-element.29), channel_id=1, source_target_pairs={{0,1},{1,0},{2,3},{3,2},{4,5},{5,4},{6,7},{7,6},{8,9},{9,8},{10,11... | collective-permute-start | bytes 393224 | tf_op jit(solution)/shard_map/ppermute | solution.py:40
  56.3 8.8 %collective-permute-start.5 = (bf16[64,1024]{1,0:T(8,128)(2,1)}, bf16[64,1024]{1,0:T(8,128)(2,1)}, u32[]{:S(2)}, u32[]{:S(2)}) collective-permute-start(bf16[64,1024]{1,0:T(8,128)(2,1)} %get-tuple-element.31), channel_id=1, source_target_pairs={{0,2},{1,3},{2,0},{3,1},{4,6},{5,7},{6,4},{7,5},{8,10},{9,11},{10,... | collective-permute-start | bytes 393224 | tf_op jit(solution)/shard_map/ppermute | solution.py:40
  60.9 8.2 %collective-permute-start.6 = (bf16[64,1024]{1,0:T(8,128)(2,1)S(1)}, bf16[64,1024]{1,0:T(8,128)(2,1)}, u32[]{:S(2)}, u32[]{:S(2)}) collective-permute-start(bf16[64,1024]{1,0:T(8,128)(2,1)S(1)} %get-tuple-element.30), channel_id=1, source_target_pairs={{0,3},{1,2},{2,1},{3,0},{4,7},{5,6},{6,5},{7,4},{8,11},{9,10},{10,... | collective-permute-start | bytes 393224 | tf_op jit(solution)/shard_map/ppermute | solution.py:40
  71.7 25.0 %all-to-all-start.2 = ((bf16[4,2,272,384]{3,2,1,0:T(8,128)(2,1)}), bf16[4,2,272,384]{3,2,1,0:T(8,128)(2,1)S(1)}, u32[]{:S(2)}, u32[]{:S(2)}) async-start(bf16[4,2,272,384]{3,2,1,0:T(8,128)(2,1)} %broadcast_in_dim.16), calls=%async_computation.2 | async-start | bytes 3342336 | tf_op jit(solution)/shard_map/all_to_all | solution.py:48
  75.3 6.9 %collective-permute-start.7 = (bf16[64,1024]{1,0:T(8,128)(2,1)S(1)}, bf16[64,1024]{1,0:T(8,128)(2,1)S(1)}, u32[]{:S(2)}, u32[]{:S(2)}) collective-permute-start(bf16[64,1024]{1,0:T(8,128)(2,1)S(1)} %fusion.14), channel_id=1, source_target_pairs={{0,4},{4,0},{8,12},{12,8},{1,5},{5,1},{9,13},{13,9},{2,6},{6,2},{1... | collective-permute-start | bytes 393224 | tf_op jit(solution)/shard_map/ppermute | solution.py:40
  82.2 9.3 %collective-permute-start.8 = (bf16[64,1024]{1,0:T(8,128)(2,1)S(1)}, bf16[64,1024]{1,0:T(8,128)(2,1)}, u32[]{:S(2)}, u32[]{:S(2)}) collective-permute-start(bf16[64,1024]{1,0:T(8,128)(2,1)S(1)} %add_convert_fusion.3), channel_id=1, source_target_pairs={{0,8},{4,12},{8,0},{12,4},{1,9},{5,13},{9,1},{13,5},{2,10},{6,14},... | collective-permute-start | bytes 393224 | tf_op jit(solution)/shard_map/ppermute | solution.py:40
  103.0 8.0 %collective-permute-start.9 = (bf16[256,6144]{1,0:T(8,128)(2,1)}, bf16[256,6144]{1,0:T(8,128)(2,1)}, u32[]{:S(2)}, u32[]{:S(2)}) collective-permute-start(bf16[256,6144]{1,0:T(8,128)(2,1)} %teacher_norm.1.n_ref), channel_id=1, source_target_pairs={{0,16},{16,0},{1,17},{17,1},{2,18},{18,2},{3,19},{19,3},{4,20},{20... | collective-permute-start | bytes 9437192 | tf_op jit(solution)/shard_map/ppermute | solution.py:36
  105.9 13.9 %all-to-all-start.3 = ((bf16[4,64,1024]{2,1,0:T(8,128)(2,1)}), bf16[4,64,1024]{2,1,0:T(8,128)(2,1)S(1)}, u32[]{:S(2)}, u32[]{:S(2)}) async-start(bf16[4,64,1024]{2,1,0:T(8,128)(2,1)} %broadcast_in_dim.17), calls=%async_computation.3 | async-start | bytes 1048576 | tf_op jit(solution)/shard_map/all_to_all | solution.py:48
  117.8 9.1 %collective-permute-start.10 = (f32[256,128]{1,0:T(8,128)S(1)}, f32[256,128]{1,0:T(8,128)S(1)}, u32[]{:S(2)}, u32[]{:S(2)}) collective-permute-start(f32[256,128]{1,0:T(8,128)S(1)} %teacher_heads.3), channel_id=1, source_target_pairs={{0,16},{16,0},{1,17},{17,1},{2,18},{18,2},{3,19},{19,3},{4,20},{20... | collective-permute-start | bytes 393224 | tf_op jit(solution)/shard_map/ppermute | solution.py:36
  127.8 13.1 %all-to-all-start.4 = ((f32[16,2,256]{2,1,0:T(2,128)}), f32[16,2,256]{2,1,0:T(2,128)S(1)}, u32[]{:S(2)}, u32[]{:S(2)}) async-start(f32[16,2,256]{2,1,0:T(2,128)} %broadcast_in_dim.18), calls=%async_computation.4 | async-start | bytes 65536 | tf_op jit(solution)/shard_map/all_to_all | solution.py:48
  152.6 6.9 %collective-permute-start.11 = (bf16[64,1024]{1,0:T(8,128)(2,1)S(1)}, bf16[64,1024]{1,0:T(8,128)(2,1)S(1)}, u32[]{:S(2)}, u32[]{:S(2)}) collective-permute-start(bf16[64,1024]{1,0:T(8,128)(2,1)S(1)} %reduce_sum.106), channel_id=1, source_target_pairs={{0,4},{4,0},{8,12},{12,8},{1,5},{5,1},{9,13},{13,9},{2,6},{6,2},{1... | collective-permute-start | bytes 393224 | tf_op jit(solution)/shard_map/ppermute | solution.py:40
  159.5 8.9 %collective-permute-start.12 = (bf16[64,1024]{1,0:T(8,128)(2,1)S(1)}, bf16[64,1024]{1,0:T(8,128)(2,1)S(1)}, u32[]{:S(2)}, u32[]{:S(2)}) collective-permute-start(bf16[64,1024]{1,0:T(8,128)(2,1)S(1)} %add_convert_fusion.1), channel_id=1, source_target_pairs={{0,8},{4,12},{8,0},{12,4},{1,9},{5,13},{9,1},{13,5},{2,10},{6,14},... | collective-permute-start | bytes 393224 | tf_op jit(solution)/shard_map/ppermute | solution.py:40
  169.4 11.7 %copy-start.19 = (f32[1024]{0:T(1024)S(1)}, f32[1024]{0:T(1024)}, u32[]{:S(2)}) copy-start(f32[1024]{0:T(1024)} %param.14) | copy-start | bytes 12292
  169.4 11.7 %all-to-all-start.6 = ((bf16[4,64,1024]{2,1,0:T(8,128)(2,1)}), bf16[4,64,1024]{2,1,0:T(8,128)(2,1)S(1)}, u32[]{:S(2)}, u32[]{:S(2)}) async-start(bf16[4,64,1024]{2,1,0:T(8,128)(2,1)} %broadcast_in_dim.19), calls=%async_computation.6 | async-start | bytes 1048576 | tf_op jit(solution)/shard_map/all_to_all | solution.py:48
  (16 other events, 106.6 us)
Sparse Core Ops, SparseCore 0:
  42.2 58.8 all-gather.2

commit v10 on v9

--- a/solution.py
+++ b/solution.py
@@ -92,13 +92,13 @@
     return mean, spreads / (count * 16)
 
 
-def norm_kernel(place, own_ref, near_ref, late_ref, n_ref, gain_ref):
+def norm_kernel(place, own_ref, far_ref, late_ref, n_ref, gain_ref):
     my_zl, my_zh = place[0], place[1]
     blocks = []
     for x in range(4):
         blocks.append((own_ref, (x,), 0, x))
-        blocks.append((near_ref, (x,), 1, x))
-        blocks.append((late_ref, (x, 0), 2, x))
+        blocks.append((far_ref, (x,), 2, x))
+        blocks.append((late_ref, (x, 0), 1, x))
         blocks.append((late_ref, (x, 1), 3, x))
     for k, (ref, at, dz, x) in enumerate(blocks):
         gains = ref[(*at, slice(256, 272), slice(None))].astype(F32)
@@ -132,18 +132,19 @@
             ).astype(BF16)
 
 
-def attention_kernel(place, n_ref, w_ref, qg_ref, f_ref):
+def attention_kernel(place, own_ref, other_ref, w_ref, qg_ref, f_ref):
     gain = jnp.where(place[0] == 0, qg_ref[0:1, :], qg_ref[1:2, :])
-    projected = jnp.dot(n_ref[...], w_ref[...], preferred_element_type=F32)
-    query = (normalize(projected[:, :128]) * gain).astype(BF16)
-    key = (normalize(projected[:, 128:256]) * gain).astype(BF16)
-    value = projected[:, 256:].astype(BF16)
-    scores = lax.dot_general(
-        query, key, (((1,), (1,)), ((), ())), preferred_element_type=F32
-    ) * (HEAD ** (-0.5))
-    scores = jnp.exp(scores - jnp.max(scores, axis=1, keepdims=True))
-    attn = (scores / jnp.sum(scores, axis=1, keepdims=True)).astype(BF16)
-    f_ref[...] = jnp.dot(attn, value, preferred_element_type=F32)
+    for image, ref in enumerate((own_ref, other_ref)):
+        projected = jnp.dot(ref[...], w_ref[...], preferred_element_type=F32)
+        query = (normalize(projected[:, :128]) * gain).astype(BF16)
+        key = (normalize(projected[:, 128:256]) * gain).astype(BF16)
+        value = projected[:, 256:].astype(BF16)
+        scores = lax.dot_general(
+            query, key, (((1,), (1,)), ((), ())), preferred_element_type=F32
+        ) * (HEAD ** (-0.5))
+        scores = jnp.exp(scores - jnp.max(scores, axis=1, keepdims=True))
+        attn = (scores / jnp.sum(scores, axis=1, keepdims=True)).astype(BF16)
+        f_ref[image] = jnp.dot(attn, value, preferred_element_type=F32)
 
 
 def reduce_dp(terms):
@@ -178,7 +179,7 @@
     gain_rows = jnp.stack([hi, mid, low] + [jnp.zeros_like(hi)] * 13).astype(BF16)
     shard = tie(jnp.concatenate([teacher_in, gain_rows], axis=0), near)
     own = spread(shard, "x")
-    near_block = flip(shard, "zl", 1)
+    far_block = flip(shard, "zl", 2)
 
     student_normed = (normalize(student_in.astype(F32)) * student_gain).astype(BF16)
     pre_act = jnp.dot(student_normed, up_weight, preferred_element_type=F32)
@@ -190,18 +191,16 @@
         return jnp.where(first, jnp.stack([mine, theirs]), jnp.stack([theirs, mine]))
 
     given = flip(jnp.stack([near[1], far[1]]), "c")
-    given, own, near_block, mlp_term = lax.optimization_barrier(
-        (given, own, near_block, mlp_term)
+    given, own, far_block, mlp_term = lax.optimization_barrier(
+        (given, own, far_block, mlp_term)
     )
     rows = jnp.concatenate([by_core(near[0], given[0]), by_core(far[0], given[1])])
     weight = lax.all_gather(rows, "y").reshape(6144, 384)
 
-    late = flip(jnp.stack([shard, near_block]), "zl", 2)
-    near_block = spread(near_block, "x")
+    late = flip(jnp.stack([shard, far_block]), "zl", 1)
+    far_block = spread(far_block, "x")
     part = mp_scatter_x_beside(tie(mlp_term, rows))
-    late, part = lax.optimization_barrier((late, part))
-    part = mp_sum_zl(part)
-    late, part = lax.optimization_barrier((spread(tie(late, near_block), "x"), part))
+    late, part = lax.optimization_barrier((spread(tie(late, far_block), "x"), part))
 
     place_z = jnp.stack([lax.axis_index("zl"), lax.axis_index("zh")])
     place_c = lax.axis_index("c").reshape(1)
@@ -219,26 +218,25 @@
             flops=1000, bytes_accessed=1000, transcendentals=0
         ),
         name="teacher_norm",
-    )(place_z, own, near_block, late)
+    )(place_z, own, far_block, late)
     normed_other = shift(normed, "c", 1)
-    mlp_sum = mp_gather_x(tie(part, normed))
+    mlp_sum = mp_gather_x(mp_sum_zl(tie(part, normed)))
     heads = pl.pallas_call(
         attention_kernel,
-        out_shape=jax.ShapeDtypeStruct((256, 128), F32),
-        in_specs=[smem] + [vmem] * 3,
+        out_shape=jax.ShapeDtypeStruct((2, 256, 128), F32),
+        in_specs=[smem] + [vmem] * 4,
         out_specs=vmem,
         compiler_params=params,
         cost_estimate=pl.CostEstimate(
-            flops=2 * 256 * 6144 * 384, bytes_accessed=8_000_000, transcendentals=65536
+            flops=2 * 512 * 6144 * 384, bytes_accessed=11_000_000, transcendentals=131072
         ),
         name="teacher_heads",
-    )
-    crossed = shift(heads(place_c, normed_other, weight, qk_gain), "c", 1)
-    kept = heads(place_c, normed, weight, qk_gain)
+    )(place_c, normed, normed_other, weight, qk_gain)
+    crossed = shift(heads[1], "c", 1)
     features = jnp.where(
         place_c[0] == 0,
-        jnp.concatenate([kept, crossed], axis=1),
-        jnp.concatenate([crossed, kept], axis=1),
+        jnp.concatenate([heads[0], crossed], axis=1),
+        jnp.concatenate([crossed, heads[0]], axis=1),
     )
 
     block_out = (student_in.astype(F32) + mlp_sum.astype(F32)).astype(BF16)

time: 234 us -> 248 us (1.060)
  waiting for transfers between devices: 56.7 us -> 74.7 us
  blocking collectives: 53.4 us -> 49.5 us
  starting transfers between devices: 68.6 us -> 71.1 us
    ppermute x11, waiting for transfers between devices: 34 us -> 59.1 us  [flip(): lax.ppermute(values, axes, [(i, i ^ bits) for i in range(SIZES[axes])])]
    all_to_all x6, waiting for transfers between devices: 21.1 us -> 14.4 us  [swap(): return lax.all_to_all(values, axis, split_axis=0, concat_axis=0)]
    all_to_all x1, blocking collectives: 37.1 us -> 33.4 us  [reduce_dp(): terms = lax.all_to_all(terms, ('zh', 'y'), split_axis=1, concat_axis=0)]
    all_to_all x6, starting transfers between devices: 23.5 us -> 27 us  [swap(): return lax.all_to_all(values, axis, split_axis=0, concat_axis=0)]
    unnamed x40 -> x50, local copies, waits for them, and re-layouts: 5.9 us -> 4.26 us
    pallas_call x2 -> x1, Pallas kernels: 8.84 us -> 7.4 us  [shards(): pl.pallas_call(attention_kernel, out_shape=jax.ShapeDtypeStruct((2, 256,...]
  transfers between devices with their start and end apart: 20 -> 20, of which waited for: 13 -> 12; matrix products, arithmetic and copies ran while one was open for 5% -> 4% of each run, Pallas kernels for 6% -> 5%
where the time goes in v10:
time: 248 us; the launch traced here: 247 us
  waiting for transfers between devices  74.7 us (30%)
  starting transfers between devices  71.1 us (29%)
  blocking collectives  49.5 us (20%)
  local copies, waits for them, and re-layouts  15.6 us (6%)
  between operations  14.7 us (6%)
  Pallas kernels  12.5 us (5%)
  matrix products  4.63 us (2%)
  other arithmetic  4.24 us (2%)
    ppermute x11, waiting for transfers between devices, flip(): lax.ppermute(values, axes, [(i, i ^ bits) for i in range(SIZES[axes])])  59.1 us
    ppermute x11, starting transfers between devices, flip(): lax.ppermute(values, axes, [(i, i ^ bits) for i in range(SIZES[axes])])  40 us
    all_to_all x1, blocking collectives, reduce_dp(): terms = lax.all_to_all(terms, ('zh', 'y'), split_axis=1, concat_axis=0)  33.4 us
    all_to_all x6, starting transfers between devices, swap(): return lax.all_to_all(values, axis, split_axis=0, concat_axis=0)  27 us
    all_to_all x6, waiting for transfers between devices, swap(): return lax.all_to_all(values, axis, split_axis=0, concat_axis=0)  14.4 us
    all_to_all x1, blocking collectives, swap(): return lax.all_to_all(values, axis, split_axis=0, concat_axis=0)  11.1 us
    pallas_call x1, Pallas kernels, shards(): pl.pallas_call(attention_kernel, out_shape=jax.ShapeDtypeStruct((2, 256,...  7.4 us
    broadcast_in_dim x5, local copies, waits for them, and re-layouts, spread(): jnp.broadcast_to(values[None], (SIZES[axis],) + values.shape)  5.22 us
  transfers between devices with their start and end apart: 20, of which 12 were waited for; matrix products, arithmetic and copies ran while one was open for 4% of the time, Pallas kernels for 5%

profile of v10, /device:TPU:8, one launch (start us, length us, event | category | flops | bytes accessed | tf_op | source)
XLA Modules:
  0.0 247.0 jit_solution(8352701567588817680)
XLA Ops:
  8.9 10.9 %collective-permute-start = (bf16[2,192,384]{2,1,0:T(8,128)(2,1)S(1)}, bf16[2,192,384]{2,1,0:T(8,128)(2,1)}, u32[]{:S(2)}, u32[]{:S(2)}) collective-permute-start(bf16[2,192,384]{2,1,0:T(8,128)(2,1)S(1)} %reverse_select_fusion), channel_id=1, source_target_pairs={{0,256},{256,0},{1,257},{257,1},{2,258},{258,2},{3,259},{259,3},{4... | collective-permute-start | bytes 884744 | tf_op jit(solution)/shard_map/ppermute | solution.py:40
  20.1 4.3 %collective-permute-start.2 = (bf16[272,384]{1,0:T(8,128)(2,1)S(1)}, bf16[272,384]{1,0:T(8,128)(2,1)S(1)}, u32[]{:S(2)}, u32[]{:S(2)}) collective-permute-start(bf16[272,384]{1,0:T(8,128)(2,1)S(1)} %concatenate.14), channel_id=1, source_target_pairs={{0,8},{4,12},{8,0},{12,4},{1,9},{5,13},{9,1},{13,5},{2,10},{6,14},... | collective-permute-start | bytes 626696 | tf_op jit(solution)/shard_map/ppermute | solution.py:40
  25.4 4.3 %all-to-all-start = ((bf16[4,272,384]{2,1,0:T(8,128)(2,1)}), bf16[4,272,384]{2,1,0:T(8,128)(2,1)S(1)}, u32[]{:S(2)}, u32[]{:S(2)}) async-start(bf16[4,272,384]{2,1,0:T(8,128)(2,1)} %broadcast_in_dim.14), calls=%async_computation | async-start | bytes 1671168 | tf_op jit(solution)/shard_map/all_to_all | solution.py:48
  37.2 6.0 %collective-permute-done.2 = bf16[272,384]{1,0:T(8,128)(2,1)S(1)} collective-permute-done((bf16[272,384]{1,0:T(8,128)(2,1)S(1)}, bf16[272,384]{1,0:T(8,128)(2,1)S(1)}, u32[]{:S(2)}, u32[]{:S(2)}) %collective-permute-start.2) | collective-permute-done | bytes 208928 | tf_op jit(solution)/shard_map/ppermute | solution.py:40
  46.4 4.3 %all-to-all-start.1 = ((bf16[4,272,384]{2,1,0:T(8,128)(2,1)}), bf16[4,272,384]{2,1,0:T(8,128)(2,1)S(1)}, u32[]{:S(2)}, u32[]{:S(2)}) async-start(bf16[4,272,384]{2,1,0:T(8,128)(2,1)} %broadcast_in_dim.15), calls=%async_computation.1 | async-start | bytes 1671168 | tf_op jit(solution)/shard_map/all_to_all | solution.py:48
  52.7 11.2 %collective-permute-done.3 = bf16[2,272,384]{2,1,0:T(8,128)(2,1)S(1)} collective-permute-done((bf16[2,272,384]{2,1,0:T(8,128)(2,1)S(1)}, bf16[2,272,384]{2,1,0:T(8,128)(2,1)S(1)}, u32[]{:S(2)}, u32[]{:S(2)}) %collective-permute-start.3) | collective-permute-done | bytes 417824 | tf_op jit(solution)/shard_map/ppermute | solution.py:40
  65.5 4.5 %all-to-all-start.2 = ((bf16[4,2,272,384]{3,2,1,0:T(8,128)(2,1)}), bf16[4,2,272,384]{3,2,1,0:T(8,128)(2,1)S(1)}, u32[]{:S(2)}, u32[]{:S(2)}) async-start(bf16[4,2,272,384]{3,2,1,0:T(8,128)(2,1)} %broadcast_in_dim.16), calls=%async_computation.2 | async-start | bytes 3342336 | tf_op jit(solution)/shard_map/all_to_all | solution.py:48
  70.7 3.9 %collective-permute-start.4 = (bf16[64,1024]{1,0:T(8,128)(2,1)}, bf16[64,1024]{1,0:T(8,128)(2,1)S(1)}, u32[]{:S(2)}, u32[]{:S(2)}) collective-permute-start(bf16[64,1024]{1,0:T(8,128)(2,1)} %get-tuple-element.25), channel_id=1, source_target_pairs={{0,1},{1,0},{2,3},{3,2},{4,5},{5,4},{6,7},{7,6},{8,9},{9,8},{10,11... | collective-permute-start | bytes 393224 | tf_op jit(solution)/shard_map/ppermute | solution.py:40
  74.7 4.6 %collective-permute-start.5 = (bf16[64,1024]{1,0:T(8,128)(2,1)}, bf16[64,1024]{1,0:T(8,128)(2,1)S(1)}, u32[]{:S(2)}, u32[]{:S(2)}) collective-permute-start(bf16[64,1024]{1,0:T(8,128)(2,1)} %get-tuple-element.27), channel_id=1, source_target_pairs={{0,2},{1,3},{2,0},{3,1},{4,6},{5,7},{6,4},{7,5},{8,10},{9,11},{10,... | collective-permute-start | bytes 393224 | tf_op jit(solution)/shard_map/ppermute | solution.py:40
  81.3 12.0 %collective-permute-done.4 = bf16[64,1024]{1,0:T(8,128)(2,1)S(1)} collective-permute-done((bf16[64,1024]{1,0:T(8,128)(2,1)}, bf16[64,1024]{1,0:T(8,128)(2,1)S(1)}, u32[]{:S(2)}, u32[]{:S(2)}) %collective-permute-start.4) | collective-permute-done | bytes 131104 | tf_op jit(solution)/shard_map/ppermute | solution.py:40
  98.4 5.2 %teacher_norm.1.own_ref = bf16[256,6144]{1,0:T(8,128)(2,1)} custom-call(s32[2]{0:T(128)S(1)} %pad_add_fusion.place, bf16[4,272,384]{2,1,0:T(8,128)(2,1)S(1)} %all-to-all-done.own_ref, bf16[4,272,384]{2,1,0:T(8,128)(2,1)S(1)} %copy-done.3, bf16[4,2,272,384]{3,2,1,0:T(8,128)(2,1)S(1)} %all-to-all-done.2.late_ref), custom_call_target="tpu_custom_call" | custom-call | flops 1000 | bytes 1000 | tf_op jit(solution)/shard_map/teacher_norm/pallas_call | solution.py:210
  108.2 5.3 %collective-permute-done.7 = bf16[64,1024]{1,0:T(8,128)(2,1)S(1)} collective-permute-done((bf16[64,1024]{1,0:T(8,128)(2,1)S(1)}, bf16[64,1024]{1,0:T(8,128)(2,1)S(1)}, u32[]{:S(2)}, u32[]{:S(2)}) %collective-permute-start.7) | collective-permute-done | bytes 131104 | tf_op jit(solution)/shard_map/ppermute | solution.py:40
  116.9 7.3 %collective-permute-done.8 = bf16[64,1024]{1,0:T(8,128)(2,1)S(1)} collective-permute-done((bf16[64,1024]{1,0:T(8,128)(2,1)S(1)}, bf16[64,1024]{1,0:T(8,128)(2,1)S(1)}, u32[]{:S(2)}, u32[]{:S(2)}) %collective-permute-start.8) | collective-permute-done | bytes 131104 | tf_op jit(solution)/shard_map/ppermute | solution.py:40
  125.1 3.5 %all-to-all-start.3 = ((bf16[4,64,1024]{2,1,0:T(8,128)(2,1)}), bf16[4,64,1024]{2,1,0:T(8,128)(2,1)S(1)}, u32[]{:S(2)}, u32[]{:S(2)}) async-start(bf16[4,64,1024]{2,1,0:T(8,128)(2,1)} %broadcast_in_dim.17), calls=%async_computation.3 | async-start | bytes 1048576 | tf_op jit(solution)/shard_map/all_to_all | solution.py:48
  130.9 7.4 %teacher_heads.1 = f32[2,256,128]{2,1,0:T(8,128)S(1)} custom-call(s32[1]{0:T(128)} %bitcast.11.place, bf16[256,6144]{1,0:T(8,128)(2,1)} %teacher_norm.1.own_ref, bf16[256,6144]{1,0:T(8,128)(2,1)} %collective-permute-done.9.other_ref, bf16[6144,384]{1,0:T(8,128)(2,1)S(1)} %bitcast.59, f32[2,128]{1,0:T(2,128)S(1)} %copy-done.4), custom_call_target="tpu_custom_call" | custom-call | flops 2415919104 | bytes 11000000 | tf_op jit(solution)/shard_map/teacher_heads/pallas_call | solution.py:224
  142.7 6.6 %all-to-all-start.4 = ((f32[16,2,256]{2,1,0:T(2,128)}), f32[16,2,256]{2,1,0:T(2,128)S(1)}, u32[]{:S(2)}, u32[]{:S(2)}) async-start(f32[16,2,256]{2,1,0:T(2,128)} %broadcast_in_dim.18), calls=%async_computation.4 | async-start | bytes 65536 | tf_op jit(solution)/shard_map/all_to_all | solution.py:48
  149.7 7.8 %all-to-all-done.4 = f32[16,2,256]{2,1,0:T(2,128)S(1)} async-done(((f32[16,2,256]{2,1,0:T(2,128)}), f32[16,2,256]{2,1,0:T(2,128)S(1)}, u32[]{:S(2)}, u32[]{:S(2)}) %all-to-all-start.4) | async-done | bytes 32800 | tf_op jit(solution)/shard_map/all_to_all | solution.py:48
  157.9 11.1 %all_to_all.53 = bf16[4,64,1024]{2,1,0:T(8,128)(2,1)S(1)} all-to-all(bf16[4,64,1024]{2,1,0:T(8,128)(2,1)S(1)} %bitcast.61), channel_id=1, replica_groups=mesh['zh'=2,'y'=8,'c'=2,'zl'=4,'x'=4] {'x'}, dimensions={0} | all-to-all | bytes 1048576 | tf_op jit(solution)/shard_map/all_to_all | solution.py:48
  171.3 4.7 %collective-permute-done.11 = bf16[64,1024]{1,0:T(8,128)(2,1)S(1)} collective-permute-done((bf16[64,1024]{1,0:T(8,128)(2,1)S(1)}, bf16[64,1024]{1,0:T(8,128)(2,1)S(1)}, u32[]{:S(2)}, u32[]{:S(2)}) %collective-permute-start.11) | collective-permute-done | bytes 131104 | tf_op jit(solution)/shard_map/ppermute | solution.py:40
  178.6 6.4 %collective-permute-done.12 = bf16[64,1024]{1,0:T(8,128)(2,1)S(1)} collective-permute-done((bf16[64,1024]{1,0:T(8,128)(2,1)S(1)}, bf16[64,1024]{1,0:T(8,128)(2,1)S(1)}, u32[]{:S(2)}, u32[]{:S(2)}) %collective-permute-start.12) | collective-permute-done | bytes 131104 | tf_op jit(solution)/shard_map/ppermute | solution.py:40
  185.8 3.8 %all-to-all-start.6 = ((bf16[4,64,1024]{2,1,0:T(8,128)(2,1)}), bf16[4,64,1024]{2,1,0:T(8,128)(2,1)S(1)}, u32[]{:S(2)}, u32[]{:S(2)}) async-start(bf16[4,64,1024]{2,1,0:T(8,128)(2,1)} %broadcast_in_dim.19), calls=%async_computation.6 | async-start | bytes 1048576 | tf_op jit(solution)/shard_map/all_to_all | solution.py:48
  190.9 6.6 %all-to-all-done.6 = bf16[4,64,1024]{2,1,0:T(8,128)(2,1)S(1)} async-done(((bf16[4,64,1024]{2,1,0:T(8,128)(2,1)}), bf16[4,64,1024]{2,1,0:T(8,128)(2,1)S(1)}, u32[]{:S(2)}, u32[]{:S(2)}) %all-to-all-start.6) | async-done | bytes 524320 | tf_op jit(solution)/shard_map/all_to_all | solution.py:48
  200.6 5.0 %all_to_all.54 = bf16[1,3,16,2,32,256]{5,4,2,1,0,3:T(8,128)(2,1)S(1)} all-to-all(bf16[1,3,16,2,32,256]{5,4,2,1,0,3:T(8,128)(2,1)S(1)} %copy.35), channel_id=1, replica_groups=mesh['zh'=2,'y'=8,'c'=2,'zl'=4,'x'=4] {'c'}, dimensions={3} | all-to-all | bytes 3145728 | tf_op jit(solution)/shard_map/all_to_all | solution.py:153
  206.1 33.4 %all_to_all.55 = bf16[1,3,16,32,256]{4,3,1,0,2:T(8,128)(2,1)S(1)} all-to-all(bf16[1,3,16,32,256]{4,3,1,0,2:T(8,128)(2,1)S(1)} %copy.34), channel_id=1, replica_groups=mesh['zh'=2,'y'=8,'c'=2,'zl'=4,'x'=4] {'zh','y'}, dimensions={2} | all-to-all | bytes 1572864 | tf_op jit(solution)/shard_map/all_to_all | solution.py:155
  (132 shorter events, 52.3 us)
Async XLA Ops:
  7.2 29.7 %copy-start = (bf16[256,1024]{1,0:T(8,128)(2,1)S(1)}, bf16[256,1024]{1,0:T(8,128)(2,1)}, u32[]{:S(2)}) copy-start(bf16[256,1024]{1,0:T(8,128)(2,1)} %param.16) | copy-start | bytes 1572868
  7.2 12.7 %copy-start.16 = (bf16[256,384]{1,0:T(8,128)(2,1)S(1)}, bf16[256,384]{1,0:T(8,128)(2,1)}, u32[]{:S(2)}) copy-start(bf16[256,384]{1,0:T(8,128)(2,1)} %param.9) | copy-start | bytes 589828
  8.9 24.6 %collective-permute-start = (bf16[2,192,384]{2,1,0:T(8,128)(2,1)S(1)}, bf16[2,192,384]{2,1,0:T(8,128)(2,1)}, u32[]{:S(2)}, u32[]{:S(2)}) collective-permute-start(bf16[2,192,384]{2,1,0:T(8,128)(2,1)S(1)} %reverse_select_fusion), channel_id=1, source_target_pairs={{0,256},{256,0},{1,257},{257,1},{2,258},{258,2},{3,259},{259,3},{4... | collective-permute-start | bytes 884744 | tf_op jit(solution)/shard_map/ppermute | solution.py:40
  20.1 23.2 %collective-permute-start.2 = (bf16[272,384]{1,0:T(8,128)(2,1)S(1)}, bf16[272,384]{1,0:T(8,128)(2,1)S(1)}, u32[]{:S(2)}, u32[]{:S(2)}) collective-permute-start(bf16[272,384]{1,0:T(8,128)(2,1)S(1)} %concatenate.14), channel_id=1, source_target_pairs={{0,8},{4,12},{8,0},{12,4},{1,9},{5,13},{9,1},{13,5},{2,10},{6,14},... | collective-permute-start | bytes 626696 | tf_op jit(solution)/shard_map/ppermute | solution.py:40
  25.4 17.9 %all-to-all-start = ((bf16[4,272,384]{2,1,0:T(8,128)(2,1)}), bf16[4,272,384]{2,1,0:T(8,128)(2,1)S(1)}, u32[]{:S(2)}, u32[]{:S(2)}) async-start(bf16[4,272,384]{2,1,0:T(8,128)(2,1)} %broadcast_in_dim.14), calls=%async_computation | async-start | bytes 1671168 | tf_op jit(solution)/shard_map/all_to_all | solution.py:48
  29.7 98.9 %all-gather.3.cloned.1.call-start = ((), (), s32[]{:S(2)}) async-start(), calls=%async_computation.9 | async-start | bytes 5308416 | tf_op jit(solution)/shard_map/all_gather | solution.py:198
  34.5 8.7 %collective-permute-start.1 = (bf16[2,192,384]{2,1,0:T(8,128)(2,1)S(1)}, bf16[2,192,384]{2,1,0:T(8,128)(2,1)}, u32[]{:S(2)}, u32[]{:S(2)}) collective-permute-start(bf16[2,192,384]{2,1,0:T(8,128)(2,1)S(1)} %pad_maximum_fusion.3), channel_id=1, source_target_pairs={{0,16},{16,0},{1,17},{17,1},{2,18},{18,2},{3,19},{19,3},{4,20},{20... | collective-permute-start | bytes 884744 | tf_op jit(solution)/shard_map/ppermute | solution.py:40
  37.2 32.8 %copy-start.8 = (bf16[256,1024]{1,0:T(8,128)(2,1)}, bf16[256,1024]{1,0:T(8,128)(2,1)S(1)}, u32[]{:S(2)}) copy-start(bf16[256,1024]{1,0:T(8,128)(2,1)S(1)} %convolution_convert_fusion.4) | copy-start | bytes 1572868
  46.4 17.5 %all-to-all-start.1 = ((bf16[4,272,384]{2,1,0:T(8,128)(2,1)}), bf16[4,272,384]{2,1,0:T(8,128)(2,1)S(1)}, u32[]{:S(2)}, u32[]{:S(2)}) async-start(bf16[4,272,384]{2,1,0:T(8,128)(2,1)} %broadcast_in_dim.15), calls=%async_computation.1 | async-start | bytes 1671168 | tf_op jit(solution)/shard_map/all_to_all | solution.py:48
  50.8 13.2 %collective-permute-start.3 = (bf16[2,272,384]{2,1,0:T(8,128)(2,1)S(1)}, bf16[2,272,384]{2,1,0:T(8,128)(2,1)S(1)}, u32[]{:S(2)}, u32[]{:S(2)}) collective-permute-start(bf16[2,272,384]{2,1,0:T(8,128)(2,1)S(1)} %pad_maximum_fusion.2), channel_id=1, source_target_pairs={{0,4},{4,0},{8,12},{12,8},{1,5},{5,1},{9,13},{13,9},{2,6},{6,2},{1... | collective-permute-start | bytes 1253384 | tf_op jit(solution)/shard_map/ppermute | solution.py:40
  65.5 31.8 %all-to-all-start.2 = ((bf16[4,2,272,384]{3,2,1,0:T(8,128)(2,1)}), bf16[4,2,272,384]{3,2,1,0:T(8,128)(2,1)S(1)}, u32[]{:S(2)}, u32[]{:S(2)}) async-start(bf16[4,2,272,384]{3,2,1,0:T(8,128)(2,1)} %broadcast_in_dim.16), calls=%async_computation.2 | async-start | bytes 3342336 | tf_op jit(solution)/shard_map/all_to_all | solution.py:48
  70.7 22.6 %collective-permute-start.4 = (bf16[64,1024]{1,0:T(8,128)(2,1)}, bf16[64,1024]{1,0:T(8,128)(2,1)S(1)}, u32[]{:S(2)}, u32[]{:S(2)}) collective-permute-start(bf16[64,1024]{1,0:T(8,128)(2,1)} %get-tuple-element.25), channel_id=1, source_target_pairs={{0,1},{1,0},{2,3},{3,2},{4,5},{5,4},{6,7},{7,6},{8,9},{9,8},{10,11... | collective-permute-start | bytes 393224 | tf_op jit(solution)/shard_map/ppermute | solution.py:40
  74.7 21.5 %collective-permute-start.5 = (bf16[64,1024]{1,0:T(8,128)(2,1)}, bf16[64,1024]{1,0:T(8,128)(2,1)S(1)}, u32[]{:S(2)}, u32[]{:S(2)}) collective-permute-start(bf16[64,1024]{1,0:T(8,128)(2,1)} %get-tuple-element.27), channel_id=1, source_target_pairs={{0,2},{1,3},{2,0},{3,1},{4,6},{5,7},{6,4},{7,5},{8,10},{9,11},{10,... | collective-permute-start | bytes 393224 | tf_op jit(solution)/shard_map/ppermute | solution.py:40
  79.3 17.0 %collective-permute-start.6 = (bf16[64,1024]{1,0:T(8,128)(2,1)}, bf16[64,1024]{1,0:T(8,128)(2,1)}, u32[]{:S(2)}, u32[]{:S(2)}) collective-permute-start(bf16[64,1024]{1,0:T(8,128)(2,1)} %get-tuple-element.26), channel_id=1, source_target_pairs={{0,3},{1,2},{2,1},{3,0},{4,7},{5,6},{6,5},{7,4},{8,11},{9,10},{10,... | collective-permute-start | bytes 393224 | tf_op jit(solution)/shard_map/ppermute | solution.py:40
  103.6 25.0 %copy-start.4 = (f32[2,128]{1,0:T(2,128)S(1)}, f32[2,128]{1,0:T(2,128)}, u32[]{:S(2)}) copy-start(f32[2,128]{1,0:T(2,128)} %qg_ref.1) | copy-start | bytes 3076
  103.6 25.0 %collective-permute-start.9 = (bf16[256,6144]{1,0:T(8,128)(2,1)}, bf16[256,6144]{1,0:T(8,128)(2,1)}, u32[]{:S(2)}, u32[]{:S(2)}) collective-permute-start(bf16[256,6144]{1,0:T(8,128)(2,1)} %teacher_norm.1.own_ref), channel_id=1, source_target_pairs={{0,16},{16,0},{1,17},{17,1},{2,18},{18,2},{3,19},{19,3},{4,20},{20... | collective-permute-start | bytes 9437192 | tf_op jit(solution)/shard_map/ppermute | solution.py:36
  105.6 7.8 %collective-permute-start.7 = (bf16[64,1024]{1,0:T(8,128)(2,1)S(1)}, bf16[64,1024]{1,0:T(8,128)(2,1)S(1)}, u32[]{:S(2)}, u32[]{:S(2)}) collective-permute-start(bf16[64,1024]{1,0:T(8,128)(2,1)S(1)} %fusion.14), channel_id=1, source_target_pairs={{0,4},{4,0},{8,12},{12,8},{1,5},{5,1},{9,13},{13,9},{2,6},{6,2},{1... | collective-permute-start | bytes 393224 | tf_op jit(solution)/shard_map/ppermute | solution.py:40
  113.5 10.7 %collective-permute-start.8 = (bf16[64,1024]{1,0:T(8,128)(2,1)S(1)}, bf16[64,1024]{1,0:T(8,128)(2,1)S(1)}, u32[]{:S(2)}, u32[]{:S(2)}) collective-permute-start(bf16[64,1024]{1,0:T(8,128)(2,1)S(1)} %add_convert_fusion.3), channel_id=1, source_target_pairs={{0,8},{4,12},{8,0},{12,4},{1,9},{5,13},{9,1},{13,5},{2,10},{6,14},... | collective-permute-start | bytes 393224 | tf_op jit(solution)/shard_map/ppermute | solution.py:40
  125.1 15.4 %all-to-all-start.3 = ((bf16[4,64,1024]{2,1,0:T(8,128)(2,1)}), bf16[4,64,1024]{2,1,0:T(8,128)(2,1)S(1)}, u32[]{:S(2)}, u32[]{:S(2)}) async-start(bf16[4,64,1024]{2,1,0:T(8,128)(2,1)} %broadcast_in_dim.17), calls=%async_computation.3 | async-start | bytes 1048576 | tf_op jit(solution)/shard_map/all_to_all | solution.py:48
  138.4 3.4 %collective-permute-start.10 = (f32[256,128]{1,0:T(8,128)S(1)}, f32[256,128]{1,0:T(8,128)S(1)}, u32[]{:S(2)}, u32[]{:S(2)}) collective-permute-start(f32[256,128]{1,0:T(8,128)S(1)} %get-tuple-element.34), channel_id=1, source_target_pairs={{0,16},{16,0},{1,17},{17,1},{2,18},{18,2},{3,19},{19,3},{4,20},{20... | collective-permute-start | bytes 393224 | tf_op jit(solution)/shard_map/ppermute | solution.py:36
  142.7 14.8 %all-to-all-start.4 = ((f32[16,2,256]{2,1,0:T(2,128)}), f32[16,2,256]{2,1,0:T(2,128)S(1)}, u32[]{:S(2)}, u32[]{:S(2)}) async-start(f32[16,2,256]{2,1,0:T(2,128)} %broadcast_in_dim.18), calls=%async_computation.4 | async-start | bytes 65536 | tf_op jit(solution)/shard_map/all_to_all | solution.py:48
  169.2 6.9 %collective-permute-start.11 = (bf16[64,1024]{1,0:T(8,128)(2,1)S(1)}, bf16[64,1024]{1,0:T(8,128)(2,1)S(1)}, u32[]{:S(2)}, u32[]{:S(2)}) collective-permute-start(bf16[64,1024]{1,0:T(8,128)(2,1)S(1)} %reduce_sum.106), channel_id=1, source_target_pairs={{0,4},{4,0},{8,12},{12,8},{1,5},{5,1},{9,13},{13,9},{2,6},{6,2},{1... | collective-permute-start | bytes 393224 | tf_op jit(solution)/shard_map/ppermute | solution.py:40
  176.1 8.9 %collective-permute-start.12 = (bf16[64,1024]{1,0:T(8,128)(2,1)S(1)}, bf16[64,1024]{1,0:T(8,128)(2,1)S(1)}, u32[]{:S(2)}, u32[]{:S(2)}) collective-permute-start(bf16[64,1024]{1,0:T(8,128)(2,1)S(1)} %add_convert_fusion.1), channel_id=1, source_target_pairs={{0,8},{4,12},{8,0},{12,4},{1,9},{5,13},{9,1},{13,5},{2,10},{6,14},... | collective-permute-start | bytes 393224 | tf_op jit(solution)/shard_map/ppermute | solution.py:40
  185.8 11.7 %all-to-all-start.6 = ((bf16[4,64,1024]{2,1,0:T(8,128)(2,1)}), bf16[4,64,1024]{2,1,0:T(8,128)(2,1)S(1)}, u32[]{:S(2)}, u32[]{:S(2)}) async-start(bf16[4,64,1024]{2,1,0:T(8,128)(2,1)} %broadcast_in_dim.19), calls=%async_computation.6 | async-start | bytes 1048576 | tf_op jit(solution)/shard_map/all_to_all | solution.py:48
  (21 other events, 140.4 us)
Sparse Core Ops, SparseCore 0:
  45.5 58.5 all-gather.2

commit v11 on v8

--- a/solution.py
+++ b/solution.py
@@ -81,12 +81,17 @@
     return mean, spreads / (count * 16)
 
 
-def norm_kernel(place, pair_ref, late_ref, n_ref):
+def norm_kernel(place, pair_ref, late_ref, n_ref, gain_ref):
     my_zl, my_zh = place[0], place[1]
     blocks = []
-    for dz in range(4):
-        for x in range(4):
-            blocks.append(((pair_ref, late_ref)[dz % 2], (x, dz // 2), dz, x))
+    for x in range(4):
+        blocks.append((pair_ref, (x, 0), 0, x))
+        blocks.append((pair_ref, (x, 1), 1, x))
+        blocks.append((late_ref, (x, 0), 2, x))
+        blocks.append((late_ref, (x, 1), 3, x))
+    for k, (ref, at, dz, x) in enumerate(blocks):
+        gains = ref[(*at, slice(256, 272), slice(None))].astype(F32)
+        gain_ref[k : k + 1, :] = gains[0:1] + gains[1:2] + gains[2:3]
     width = 16 * 384
 
     def fold(values):
@@ -95,23 +100,24 @@
     @pl.loop(0, 8)
     def _(t):
         rows = pl.ds(pl.multiple_of(t * 32, 32), 32)
+
+        def read(ref, at):
+            return ref[(*at, rows, slice(None))].astype(F32)
+
         total = jnp.zeros((32, 128), F32)
-        for ref, (i, j), dz, x in blocks:
-            total += fold(ref[i, j, rows, :].astype(F32))
+        for ref, at, dz, x in blocks:
+            total += fold(read(ref, at))
         mean = jnp.sum(total, axis=1, keepdims=True) / width
         total = jnp.zeros((32, 128), F32)
-        for ref, (i, j), dz, x in blocks:
-            d = ref[i, j, rows, :].astype(F32) - mean
+        for ref, at, dz, x in blocks:
+            d = read(ref, at) - mean
             total += fold(d * d)
         rstd = lax.rsqrt(jnp.sum(total, axis=1, keepdims=True) / width + EPSILON)
-        for ref, (i, j), dz, x in blocks:
-            gains = ref[i, j, 256:272, :].astype(F32)
-            gain = gains[0:1] + gains[1:2] + gains[2:3]
+        for k, (ref, at, dz, x) in enumerate(blocks):
             zl = my_zl ^ dz
             spot = ((zl & 1) * 4 + x) * 2 + ((zl >> 1) ^ my_zh)
-            d = ref[i, j, rows, :].astype(F32) - mean
             n_ref[rows, pl.ds(pl.multiple_of(spot * 384, 128), 384)] = (
-                d * rstd * gain
+                (read(ref, at) - mean) * rstd * gain_ref[k : k + 1, :]
             ).astype(BF16)
 
 
@@ -130,13 +136,23 @@
         f_ref[image] = jnp.dot(attn, value, preferred_element_type=F32)
 
 
+def reduce_zh(term):
+    low = lax.axis_index("zh") == 0
+    theirs = flip(jnp.where(low, term[1], term[0]), "zh")
+    mine = jnp.where(low, term[0], term[1])
+    return (mine.astype(F32) + theirs.astype(F32)).astype(BF16)
+
+
 def reduce_dp(terms):
     k = terms.shape[0]
-    terms = terms.reshape(k, 16, 2, 32, 256)
-    terms = lax.all_to_all(terms, "c", split_axis=2, concat_axis=0)
+    terms = terms.reshape(k, 2, 8, 2, 32, 256)
+    terms = lax.all_to_all(terms, "c", split_axis=3, concat_axis=0)
     terms = sum_parts(terms).astype(BF16)
-    terms = lax.all_to_all(terms, ("zh", "y"), split_axis=1, concat_axis=0)
-    return sum_parts(terms).astype(BF16)
+    upper = reduce_zh(terms[:, :, :, :16].transpose(1, 2, 0, 3, 4))
+    lower = swap(terms[:, :, :, 16:].transpose(2, 1, 0, 3, 4), "y")
+    upper = sum_parts(swap(upper, "y")).astype(BF16)
+    lower = reduce_zh(sum_parts(lower).astype(BF16))
+    return jnp.concatenate([upper, lower], axis=1)
 
 
 def shards(
@@ -161,7 +177,7 @@
     low = teacher_gain - hi - mid
     gain_rows = jnp.stack([hi, mid, low] + [jnp.zeros_like(hi)] * 13).astype(BF16)
     shard = tie(jnp.concatenate([teacher_in, gain_rows], axis=0), near)
-    pair = jnp.stack([shard, flip(shard, "zl", 2)])
+    pair = jnp.stack([shard, flip(shard, "zl", 1)])
 
     student_normed = (normalize(student_in.astype(F32)) * student_gain).astype(BF16)
     pre_act = jnp.dot(student_normed, up_weight, preferred_element_type=F32)
@@ -178,7 +194,7 @@
     rows = jnp.concatenate([by_core(near[0], given[0]), by_core(far[0], given[1])])
     weight = lax.all_gather(rows, "y").reshape(6144, 384)
 
-    late = flip(pair, "zl", 1)
+    late = flip(pair, "zl", 2)
     pair = spread(pair, "x")
     part = mp_sum_zl(tie(part, rows))
     late, part = lax.optimization_barrier((spread(tie(late, pair), "x"), part))
@@ -191,6 +207,7 @@
     normed = pl.pallas_call(
         norm_kernel,
         out_shape=jax.ShapeDtypeStruct((256, 6144), BF16),
+        scratch_shapes=[pltpu.VMEM((16, 384), F32)],
         in_specs=[smem] + [vmem] * 2,
         out_specs=vmem,
         compiler_params=params,

time: 231 us -> 239 us (1.035)
  blocking collectives: 49.6 us -> 16.1 us
  starting transfers between devices: 58.1 us -> 85.6 us
  waiting for transfers between devices: 74.6 us -> 82.4 us
  matrix products: 4.83 us -> 7.38 us
    all_to_all x2 -> x1, blocking collectives: 38.5 us -> 5 us  [reduce_dp(): terms = lax.all_to_all(terms, 'c', split_axis=3, concat_axis=0)]
    all_to_all x6 -> x8, starting transfers between devices: 25.3 us -> 40.8 us  [swap(): return lax.all_to_all(values, axis, split_axis=0, concat_axis=0)]
    ppermute x8 -> x10, waiting for transfers between devices: 42.7 us -> 57.2 us  [flip(): lax.ppermute(values, axes, [(i, i ^ bits) for i in range(SIZES[axes])])]
    ppermute x8 -> x10, starting transfers between devices: 28.6 us -> 40.6 us  [flip(): lax.ppermute(values, axes, [(i, i ^ bits) for i in range(SIZES[axes])])]
    all_to_all x6 -> x8, waiting for transfers between devices: 29.3 us -> 22.6 us  [swap(): return lax.all_to_all(values, axis, split_axis=0, concat_axis=0)]
  transfers between devices with their start and end apart: 17 -> 21, of which waited for: 13 -> 15; matrix products, arithmetic and copies ran while one was open for 4% -> 6% of each run, Pallas kernels for 6% -> 6%
where the time goes in v11:
time: 239 us; the launch traced here: 237 us
  starting transfers between devices  85.6 us (36%)
  waiting for transfers between devices  82.4 us (34%)
  blocking collectives  16.1 us (7%)
  between operations  14.6 us (6%)
  Pallas kernels  13.4 us (6%)
  local copies, waits for them, and re-layouts  12.1 us (5%)
  matrix products  7.38 us (3%)
  other arithmetic  5.68 us (2%)
    ppermute x10, waiting for transfers between devices, flip(): lax.ppermute(values, axes, [(i, i ^ bits) for i in range(SIZES[axes])])  57.2 us
    all_to_all x8, starting transfers between devices, swap(): return lax.all_to_all(values, axis, split_axis=0, concat_axis=0)  40.8 us
    ppermute x10, starting transfers between devices, flip(): lax.ppermute(values, axes, [(i, i ^ bits) for i in range(SIZES[axes])])  40.6 us
    all_to_all x8, waiting for transfers between devices, swap(): return lax.all_to_all(values, axis, split_axis=0, concat_axis=0)  22.6 us
    all_to_all x1, blocking collectives, swap(): return lax.all_to_all(values, axis, split_axis=0, concat_axis=0)  11.1 us
    pallas_call x1, Pallas kernels, shards(): pl.pallas_call(attention_kernel, out_shape=jax.ShapeDtypeStruct((2, 256,...  7.35 us
    pallas_call x1, Pallas kernels, shards(): pl.pallas_call(norm_kernel, out_shape=jax.ShapeDtypeStruct((256, 6144), B...  6.06 us
    broadcast_in_dim x4, local copies, waits for them, and re-layouts, spread(): jnp.broadcast_to(values[None], (SIZES[axis],) + values.shape)  5.46 us
  transfers between devices with their start and end apart: 21, of which 15 were waited for; matrix products, arithmetic and copies ran while one was open for 6% of the time, Pallas kernels for 6%

profile of v11, /device:TPU:8, one launch (start us, length us, event | category | flops | bytes accessed | tf_op | source)
XLA Modules:
  0.0 237.2 jit_solution(4929983173056293597)
XLA Ops:
  8.9 10.9 %collective-permute-start = (bf16[2,192,384]{2,1,0:T(8,128)(2,1)S(1)}, bf16[2,192,384]{2,1,0:T(8,128)(2,1)S(1)}, u32[]{:S(2)}, u32[]{:S(2)}) collective-permute-start(bf16[2,192,384]{2,1,0:T(8,128)(2,1)S(1)} %reverse_select_fusion), channel_id=1, source_target_pairs={{0,256},{256,0},{1,257},{257,1},{2,258},{258,2},{3,259},{259,3},{4... | collective-permute-start | bytes 884744 | tf_op jit(solution)/shard_map/ppermute | solution.py:40
  26.5 4.3 %all-to-all-start = ((bf16[4,64,1024]{2,1,0:T(8,128)(2,1)}), bf16[4,64,1024]{2,1,0:T(8,128)(2,1)S(1)}, u32[]{:S(2)}, u32[]{:S(2)}) async-start(bf16[4,64,1024]{2,1,0:T(8,128)(2,1)} %bitcast.1), calls=%async_computation | async-start | bytes 1048576 | tf_op jit(solution)/shard_map/all_to_all | solution.py:48
  42.5 4.3 %all-to-all-start.1 = ((bf16[4,2,272,384]{3,2,1,0:T(8,128)(2,1)}), bf16[4,2,272,384]{3,2,1,0:T(8,128)(2,1)S(1)}, u32[]{:S(2)}, u32[]{:S(2)}) async-start(bf16[4,2,272,384]{3,2,1,0:T(8,128)(2,1)} %broadcast_in_dim.10), calls=%async_computation.1 | async-start | bytes 3342336 | tf_op jit(solution)/shard_map/all_to_all | solution.py:48
  50.2 18.7 %collective-permute-done.3 = bf16[2,272,384]{2,1,0:T(8,128)(2,1)} collective-permute-done((bf16[2,272,384]{2,1,0:T(8,128)(2,1)S(1)}, bf16[2,272,384]{2,1,0:T(8,128)(2,1)}, u32[]{:S(2)}, u32[]{:S(2)}) %collective-permute-start.3) | collective-permute-done | bytes 417824 | tf_op jit(solution)/shard_map/ppermute | solution.py:40
  71.2 4.5 %all-to-all-start.2 = ((bf16[4,2,272,384]{3,2,1,0:T(8,128)(2,1)}), bf16[4,2,272,384]{3,2,1,0:T(8,128)(2,1)}, u32[]{:S(2)}, u32[]{:S(2)}) async-start(bf16[4,2,272,384]{3,2,1,0:T(8,128)(2,1)} %broadcast_in_dim.11), calls=%async_computation.2 | async-start | bytes 3342336 | tf_op jit(solution)/shard_map/all_to_all | solution.py:48
  77.7 4.9 %collective-permute-done.4 = bf16[64,1024]{1,0:T(8,128)(2,1)S(1)} collective-permute-done((bf16[64,1024]{1,0:T(8,128)(2,1)S(1)}, bf16[64,1024]{1,0:T(8,128)(2,1)S(1)}, u32[]{:S(2)}, u32[]{:S(2)}) %collective-permute-start.4) | collective-permute-done | bytes 131104 | tf_op jit(solution)/shard_map/ppermute | solution.py:40
  86.1 5.9 %collective-permute-done.5 = bf16[64,1024]{1,0:T(8,128)(2,1)S(1)} collective-permute-done((bf16[64,1024]{1,0:T(8,128)(2,1)S(1)}, bf16[64,1024]{1,0:T(8,128)(2,1)S(1)}, u32[]{:S(2)}, u32[]{:S(2)}) %collective-permute-start.5) | collective-permute-done | bytes 131104 | tf_op jit(solution)/shard_map/ppermute | solution.py:40
  92.0 5.1 %all-to-all-done.2.late_ref = bf16[4,2,272,384]{3,2,1,0:T(8,128)(2,1)} async-done(((bf16[4,2,272,384]{3,2,1,0:T(8,128)(2,1)}), bf16[4,2,272,384]{3,2,1,0:T(8,128)(2,1)}, u32[]{:S(2)}, u32[]{:S(2)}) %all-to-all-start.2) | async-done | bytes 1671200 | tf_op jit(solution)/shard_map/all_to_all | solution.py:48
  97.1 6.1 %teacher_norm.1.own_ref = bf16[256,6144]{1,0:T(8,128)(2,1)} custom-call(s32[2]{0:T(128)S(1)} %pad_add_fusion.place, bf16[4,2,272,384]{3,2,1,0:T(8,128)(2,1)S(1)} %all-to-all-done.1.pair_ref, bf16[4,2,272,384]{3,2,1,0:T(8,128)(2,1)} %all-to-all-done.2.late_ref), custom_call_target="tpu_custom_call" | custom-call | flops 1000 | bytes 1000 | tf_op jit(solution)/shard_map/teacher_norm/pallas_call | solution.py:207
  113.6 7.4 %teacher_heads.1 = f32[2,256,128]{2,1,0:T(8,128)S(1)} custom-call(s32[1]{0:T(128)} %bitcast.7.place, bf16[256,6144]{1,0:T(8,128)(2,1)} %teacher_norm.1.own_ref, bf16[256,6144]{1,0:T(8,128)(2,1)} %collective-permute-done.6.other_ref, bf16[6144,384]{1,0:T(8,128)(2,1)S(1)} %bitcast.79, f32[2,128]{1,0:T(2,128)S(1)} %copy-done.2), custom_call_target="tpu_custom_call" | custom-call | flops 2415919104 | bytes 11000000 | tf_op jit(solution)/shard_map/teacher_heads/pallas_call | solution.py:221
  125.3 5.8 %all-to-all-start.4 = ((f32[16,2,256]{2,1,0:T(2,128)}), f32[16,2,256]{2,1,0:T(2,128)S(1)}, u32[]{:S(2)}, u32[]{:S(2)}) async-start(f32[16,2,256]{2,1,0:T(2,128)} %broadcast_in_dim.13), calls=%async_computation.4 | async-start | bytes 65536 | tf_op jit(solution)/shard_map/all_to_all | solution.py:48
  132.1 7.1 %all-to-all-done.4 = f32[16,2,256]{2,1,0:T(2,128)S(1)} async-done(((f32[16,2,256]{2,1,0:T(2,128)}), f32[16,2,256]{2,1,0:T(2,128)S(1)}, u32[]{:S(2)}, u32[]{:S(2)}) %all-to-all-start.4) | async-done | bytes 32800 | tf_op jit(solution)/shard_map/all_to_all | solution.py:48
  140.6 11.1 %all_to_all.54 = bf16[4,64,1024]{2,1,0:T(8,128)(2,1)S(1)} all-to-all(bf16[4,64,1024]{2,1,0:T(8,128)(2,1)S(1)} %bitcast.80), channel_id=1, replica_groups=mesh['zh'=2,'y'=8,'c'=2,'zl'=4,'x'=4] {'x'}, dimensions={0} | all-to-all | bytes 1048576 | tf_op jit(solution)/shard_map/all_to_all | solution.py:48
  154.1 4.6 %collective-permute-done.8 = bf16[64,1024]{1,0:T(8,128)(2,1)S(1)} collective-permute-done((bf16[64,1024]{1,0:T(8,128)(2,1)S(1)}, bf16[64,1024]{1,0:T(8,128)(2,1)S(1)}, u32[]{:S(2)}, u32[]{:S(2)}) %collective-permute-start.8) | collective-permute-done | bytes 131104 | tf_op jit(solution)/shard_map/ppermute | solution.py:40
  161.3 6.4 %collective-permute-done.9 = bf16[64,1024]{1,0:T(8,128)(2,1)S(1)} collective-permute-done((bf16[64,1024]{1,0:T(8,128)(2,1)S(1)}, bf16[64,1024]{1,0:T(8,128)(2,1)S(1)}, u32[]{:S(2)}, u32[]{:S(2)}) %collective-permute-start.9) | collective-permute-done | bytes 131104 | tf_op jit(solution)/shard_map/ppermute | solution.py:40
  168.6 3.6 %all-to-all-start.6 = ((bf16[4,64,1024]{2,1,0:T(8,128)(2,1)}), bf16[4,64,1024]{2,1,0:T(8,128)(2,1)S(1)}, u32[]{:S(2)}, u32[]{:S(2)}) async-start(bf16[4,64,1024]{2,1,0:T(8,128)(2,1)} %broadcast_in_dim.14), calls=%async_computation.6 | async-start | bytes 1048576 | tf_op jit(solution)/shard_map/all_to_all | solution.py:48
  173.5 6.6 %all-to-all-done.6 = bf16[4,64,1024]{2,1,0:T(8,128)(2,1)S(1)} async-done(((bf16[4,64,1024]{2,1,0:T(8,128)(2,1)}), bf16[4,64,1024]{2,1,0:T(8,128)(2,1)S(1)}, u32[]{:S(2)}, u32[]{:S(2)}) %all-to-all-start.6) | async-done | bytes 524320 | tf_op jit(solution)/shard_map/all_to_all | solution.py:48
  181.7 5.0 %all_to_all.55 = bf16[1,3,2,8,2,32,256]{6,5,3,2,1,0,4:T(8,128)(2,1)S(1)} all-to-all(bf16[1,3,2,8,2,32,256]{6,5,3,2,1,0,4:T(8,128)(2,1)S(1)} %copy.59), channel_id=1, replica_groups=mesh['zh'=2,'y'=8,'c'=2,'zl'=4,'x'=4] {'c'}, dimensions={4} | all-to-all | bytes 3145728 | tf_op jit(solution)/shard_map/all_to_all | solution.py:149
  188.0 7.6 %all-to-all-start.9 = ((bf16[8,2,3,16,256]{4,3,2,1,0:T(8,128)(2,1)}), bf16[8,2,3,16,256]{4,3,2,1,0:T(8,128)(2,1)S(1)}, u32[]{:S(2)}, u32[]{:S(2)}) async-start(bf16[8,2,3,16,256]{4,3,2,1,0:T(8,128)(2,1)} %copy.58), calls=%async_computation.9 | async-start | bytes 786432 | tf_op jit(solution)/shard_map/all_to_all | solution.py:48
  195.6 6.4 %collective-permute-start.10 = (bf16[8,3,16,256]{3,2,0,1:T(8,128)(2,1)S(1)}, bf16[8,3,16,256]{3,2,0,1:T(8,128)(2,1)S(1)}, u32[]{:S(2)}, u32[]{:S(2)}) collective-permute-start(bf16[8,3,16,256]{3,2,0,1:T(8,128)(2,1)S(1)} %fusion.13), channel_id=1, source_target_pairs={{0,256},{256,0},{1,257},{257,1},{2,258},{258,2},{3,259},{259,3},{4... | collective-permute-start | bytes 589832 | tf_op jit(solution)/shard_map/ppermute | solution.py:40
  202.0 10.1 %collective-permute-done.10 = bf16[8,3,16,256]{3,2,0,1:T(8,128)(2,1)S(1)} collective-permute-done((bf16[8,3,16,256]{3,2,0,1:T(8,128)(2,1)S(1)}, bf16[8,3,16,256]{3,2,0,1:T(8,128)(2,1)S(1)}, u32[]{:S(2)}, u32[]{:S(2)}) %collective-permute-start.10) | collective-permute-done | bytes 196640 | tf_op jit(solution)/shard_map/ppermute | solution.py:40
  212.8 7.2 %all-to-all-start.8 = ((bf16[8,3,16,256]{3,2,1,0:T(8,128)(2,1)}), bf16[8,3,16,256]{3,2,1,0:T(8,128)(2,1)S(1)}, u32[]{:S(2)}, u32[]{:S(2)}) async-start(bf16[8,3,16,256]{3,2,1,0:T(8,128)(2,1)} %copy.57), calls=%async_computation.8 | async-start | bytes 393216 | tf_op jit(solution)/shard_map/all_to_all | solution.py:48
  220.1 4.5 %collective-permute-start.11 = (bf16[3,16,256]{2,1,0:T(8,128)(2,1)S(1)}, bf16[3,16,256]{2,1,0:T(8,128)(2,1)S(1)}, u32[]{:S(2)}, u32[]{:S(2)}) collective-permute-start(bf16[3,16,256]{2,1,0:T(8,128)(2,1)S(1)} %select_bitcast_fusion), channel_id=1, source_target_pairs={{0,256},{256,0},{1,257},{257,1},{2,258},{258,2},{3,259},{259,3},{4... | collective-permute-start | bytes 73736 | tf_op jit(solution)/shard_map/ppermute | solution.py:40
  224.6 3.7 %all-to-all-done.8 = bf16[8,3,16,256]{3,2,1,0:T(8,128)(2,1)S(1)} async-done(((bf16[8,3,16,256]{3,2,1,0:T(8,128)(2,1)}), bf16[8,3,16,256]{3,2,1,0:T(8,128)(2,1)S(1)}, u32[]{:S(2)}, u32[]{:S(2)}) %all-to-all-start.8) | async-done | bytes 196640 | tf_op jit(solution)/shard_map/all_to_all | solution.py:48
  (108 shorter events, 61.0 us)
Async XLA Ops:
  7.2 18.2 %copy-start = (bf16[256,1024]{1,0:T(8,128)(2,1)S(1)}, bf16[256,1024]{1,0:T(8,128)(2,1)}, u32[]{:S(2)}) copy-start(bf16[256,1024]{1,0:T(8,128)(2,1)} %param.16) | copy-start | bytes 1572868
  7.2 16.3 %copy-start.3 = (bf16[256,1024]{1,0:T(8,128)(2,1)S(1)}, bf16[256,1024]{1,0:T(8,128)(2,1)}, u32[]{:S(2)}) copy-start(bf16[256,1024]{1,0:T(8,128)(2,1)} %param.13) | copy-start | bytes 1572868
  8.9 24.5 %collective-permute-start = (bf16[2,192,384]{2,1,0:T(8,128)(2,1)S(1)}, bf16[2,192,384]{2,1,0:T(8,128)(2,1)S(1)}, u32[]{:S(2)}, u32[]{:S(2)}) collective-permute-start(bf16[2,192,384]{2,1,0:T(8,128)(2,1)S(1)} %reverse_select_fusion), channel_id=1, source_target_pairs={{0,256},{256,0},{1,257},{257,1},{2,258},{258,2},{3,259},{259,3},{4... | collective-permute-start | bytes 884744 | tf_op jit(solution)/shard_map/ppermute | solution.py:40
  20.1 18.8 %collective-permute-start.2 = (bf16[272,384]{1,0:T(8,128)(2,1)S(1)}, bf16[272,384]{1,0:T(8,128)(2,1)}, u32[]{:S(2)}, u32[]{:S(2)}) collective-permute-start(bf16[272,384]{1,0:T(8,128)(2,1)S(1)} %concatenate.17), channel_id=1, source_target_pairs={{0,4},{4,0},{8,12},{12,8},{1,5},{5,1},{9,13},{13,9},{2,6},{6,2},{1... | collective-permute-start | bytes 626696 | tf_op jit(solution)/shard_map/ppermute | solution.py:40
  26.5 13.4 %all-to-all-start = ((bf16[4,64,1024]{2,1,0:T(8,128)(2,1)}), bf16[4,64,1024]{2,1,0:T(8,128)(2,1)S(1)}, u32[]{:S(2)}, u32[]{:S(2)}) async-start(bf16[4,64,1024]{2,1,0:T(8,128)(2,1)} %bitcast.1), calls=%async_computation | async-start | bytes 1048576 | tf_op jit(solution)/shard_map/all_to_all | solution.py:48
  30.8 80.4 %all-gather.3.cloned.1.call-start = ((), (), s32[]{:S(2)}) async-start(), calls=%async_computation.10 | async-start | bytes 5308416 | tf_op jit(solution)/shard_map/all_gather | solution.py:195
  34.3 5.8 %collective-permute-start.1 = (bf16[2,192,384]{2,1,0:T(8,128)(2,1)}, bf16[2,192,384]{2,1,0:T(8,128)(2,1)S(1)}, u32[]{:S(2)}, u32[]{:S(2)}) collective-permute-start(bf16[2,192,384]{2,1,0:T(8,128)(2,1)} %pad_maximum_fusion.3), channel_id=1, source_target_pairs={{0,16},{16,0},{1,17},{17,1},{2,18},{18,2},{3,19},{19,3},{4,20},{20... | collective-permute-start | bytes 884744 | tf_op jit(solution)/shard_map/ppermute | solution.py:40
  42.5 26.4 %all-to-all-start.1 = ((bf16[4,2,272,384]{3,2,1,0:T(8,128)(2,1)}), bf16[4,2,272,384]{3,2,1,0:T(8,128)(2,1)S(1)}, u32[]{:S(2)}, u32[]{:S(2)}) async-start(bf16[4,2,272,384]{3,2,1,0:T(8,128)(2,1)} %broadcast_in_dim.10), calls=%async_computation.1 | async-start | bytes 3342336 | tf_op jit(solution)/shard_map/all_to_all | solution.py:48
  46.8 22.1 %collective-permute-start.3 = (bf16[2,272,384]{2,1,0:T(8,128)(2,1)S(1)}, bf16[2,272,384]{2,1,0:T(8,128)(2,1)}, u32[]{:S(2)}, u32[]{:S(2)}) collective-permute-start(bf16[2,272,384]{2,1,0:T(8,128)(2,1)S(1)} %pad_maximum_fusion.2), channel_id=1, source_target_pairs={{0,8},{4,12},{8,0},{12,4},{1,9},{5,13},{9,1},{13,5},{2,10},{6,14},... | collective-permute-start | bytes 1253384 | tf_op jit(solution)/shard_map/ppermute | solution.py:40
  71.2 25.9 %all-to-all-start.2 = ((bf16[4,2,272,384]{3,2,1,0:T(8,128)(2,1)}), bf16[4,2,272,384]{3,2,1,0:T(8,128)(2,1)}, u32[]{:S(2)}, u32[]{:S(2)}) async-start(bf16[4,2,272,384]{3,2,1,0:T(8,128)(2,1)} %broadcast_in_dim.11), calls=%async_computation.2 | async-start | bytes 3342336 | tf_op jit(solution)/shard_map/all_to_all | solution.py:48
  75.8 6.8 %collective-permute-start.4 = (bf16[64,1024]{1,0:T(8,128)(2,1)S(1)}, bf16[64,1024]{1,0:T(8,128)(2,1)S(1)}, u32[]{:S(2)}, u32[]{:S(2)}) collective-permute-start(bf16[64,1024]{1,0:T(8,128)(2,1)S(1)} %reduce_sum.125), channel_id=1, source_target_pairs={{0,4},{4,0},{8,12},{12,8},{1,5},{5,1},{9,13},{13,9},{2,6},{6,2},{1... | collective-permute-start | bytes 393224 | tf_op jit(solution)/shard_map/ppermute | solution.py:40
  82.7 9.3 %collective-permute-start.5 = (bf16[64,1024]{1,0:T(8,128)(2,1)S(1)}, bf16[64,1024]{1,0:T(8,128)(2,1)S(1)}, u32[]{:S(2)}, u32[]{:S(2)}) collective-permute-start(bf16[64,1024]{1,0:T(8,128)(2,1)S(1)} %add_convert_fusion.3), channel_id=1, source_target_pairs={{0,8},{4,12},{8,0},{12,4},{1,9},{5,13},{9,1},{13,5},{2,10},{6,14},... | collective-permute-start | bytes 393224 | tf_op jit(solution)/shard_map/ppermute | solution.py:40
  103.2 8.0 %collective-permute-start.6 = (bf16[256,6144]{1,0:T(8,128)(2,1)}, bf16[256,6144]{1,0:T(8,128)(2,1)}, u32[]{:S(2)}, u32[]{:S(2)}) collective-permute-start(bf16[256,6144]{1,0:T(8,128)(2,1)} %teacher_norm.1.own_ref), channel_id=1, source_target_pairs={{0,16},{16,0},{1,17},{17,1},{2,18},{18,2},{3,19},{19,3},{4,20},{20... | collective-permute-start | bytes 9437192 | tf_op jit(solution)/shard_map/ppermute | solution.py:36
  106.1 17.0 %all-to-all-start.3 = ((bf16[4,64,1024]{2,1,0:T(8,128)(2,1)}), bf16[4,64,1024]{2,1,0:T(8,128)(2,1)S(1)}, u32[]{:S(2)}, u32[]{:S(2)}) async-start(bf16[4,64,1024]{2,1,0:T(8,128)(2,1)} %broadcast_in_dim.12), calls=%async_computation.3 | async-start | bytes 1048576 | tf_op jit(solution)/shard_map/all_to_all | solution.py:48
  121.0 3.4 %collective-permute-start.7 = (f32[256,128]{1,0:T(8,128)S(1)}, f32[256,128]{1,0:T(8,128)S(1)}, u32[]{:S(2)}, u32[]{:S(2)}) collective-permute-start(f32[256,128]{1,0:T(8,128)S(1)} %get-tuple-element.31), channel_id=1, source_target_pairs={{0,16},{16,0},{1,17},{17,1},{2,18},{18,2},{3,19},{19,3},{4,20},{20... | collective-permute-start | bytes 393224 | tf_op jit(solution)/shard_map/ppermute | solution.py:36
  125.3 13.9 %all-to-all-start.4 = ((f32[16,2,256]{2,1,0:T(2,128)}), f32[16,2,256]{2,1,0:T(2,128)S(1)}, u32[]{:S(2)}, u32[]{:S(2)}) async-start(f32[16,2,256]{2,1,0:T(2,128)} %broadcast_in_dim.13), calls=%async_computation.4 | async-start | bytes 65536 | tf_op jit(solution)/shard_map/all_to_all | solution.py:48
  151.7 20.5 %copy-start.5 = (f32[256,256]{1,0:T(8,128)S(1)}, f32[256,256]{1,0:T(8,128)}, u32[]{:S(2)}) copy-start(f32[256,256]{1,0:T(8,128)} %fusion.43) | copy-start | bytes 786436
  151.8 6.9 %collective-permute-start.8 = (bf16[64,1024]{1,0:T(8,128)(2,1)S(1)}, bf16[64,1024]{1,0:T(8,128)(2,1)S(1)}, u32[]{:S(2)}, u32[]{:S(2)}) collective-permute-start(bf16[64,1024]{1,0:T(8,128)(2,1)S(1)} %reduce_sum.131), channel_id=1, source_target_pairs={{0,4},{4,0},{8,12},{12,8},{1,5},{5,1},{9,13},{13,9},{2,6},{6,2},{1... | collective-permute-start | bytes 393224 | tf_op jit(solution)/shard_map/ppermute | solution.py:40
  158.7 9.0 %collective-permute-start.9 = (bf16[64,1024]{1,0:T(8,128)(2,1)S(1)}, bf16[64,1024]{1,0:T(8,128)(2,1)S(1)}, u32[]{:S(2)}, u32[]{:S(2)}) collective-permute-start(bf16[64,1024]{1,0:T(8,128)(2,1)S(1)} %add_convert_fusion.1), channel_id=1, source_target_pairs={{0,8},{4,12},{8,0},{12,4},{1,9},{5,13},{9,1},{13,5},{2,10},{6,14},... | collective-permute-start | bytes 393224 | tf_op jit(solution)/shard_map/ppermute | solution.py:40
  168.6 11.5 %all-to-all-start.6 = ((bf16[4,64,1024]{2,1,0:T(8,128)(2,1)}), bf16[4,64,1024]{2,1,0:T(8,128)(2,1)S(1)}, u32[]{:S(2)}, u32[]{:S(2)}) async-start(bf16[4,64,1024]{2,1,0:T(8,128)(2,1)} %broadcast_in_dim.14), calls=%async_computation.6 | async-start | bytes 1048576 | tf_op jit(solution)/shard_map/all_to_all | solution.py:48
  188.0 24.8 %all-to-all-start.9 = ((bf16[8,2,3,16,256]{4,3,2,1,0:T(8,128)(2,1)}), bf16[8,2,3,16,256]{4,3,2,1,0:T(8,128)(2,1)S(1)}, u32[]{:S(2)}, u32[]{:S(2)}) async-start(bf16[8,2,3,16,256]{4,3,2,1,0:T(8,128)(2,1)} %copy.58), calls=%async_computation.9 | async-start | bytes 786432 | tf_op jit(solution)/shard_map/all_to_all | solution.py:48
  195.6 16.4 %collective-permute-start.10 = (bf16[8,3,16,256]{3,2,0,1:T(8,128)(2,1)S(1)}, bf16[8,3,16,256]{3,2,0,1:T(8,128)(2,1)S(1)}, u32[]{:S(2)}, u32[]{:S(2)}) collective-permute-start(bf16[8,3,16,256]{3,2,0,1:T(8,128)(2,1)S(1)} %fusion.13), channel_id=1, source_target_pairs={{0,256},{256,0},{1,257},{257,1},{2,258},{258,2},{3,259},{259,3},{4... | collective-permute-start | bytes 589832 | tf_op jit(solution)/shard_map/ppermute | solution.py:40
  212.8 15.5 %all-to-all-start.8 = ((bf16[8,3,16,256]{3,2,1,0:T(8,128)(2,1)}), bf16[8,3,16,256]{3,2,1,0:T(8,128)(2,1)S(1)}, u32[]{:S(2)}, u32[]{:S(2)}) async-start(bf16[8,3,16,256]{3,2,1,0:T(8,128)(2,1)} %copy.57), calls=%async_computation.8 | async-start | bytes 393216 | tf_op jit(solution)/shard_map/all_to_all | solution.py:48
  220.1 9.6 %collective-permute-start.11 = (bf16[3,16,256]{2,1,0:T(8,128)(2,1)S(1)}, bf16[3,16,256]{2,1,0:T(8,128)(2,1)S(1)}, u32[]{:S(2)}, u32[]{:S(2)}) collective-permute-start(bf16[3,16,256]{2,1,0:T(8,128)(2,1)S(1)} %select_bitcast_fusion), channel_id=1, source_target_pairs={{0,256},{256,0},{1,257},{257,1},{2,258},{258,2},{3,259},{259,3},{4... | collective-permute-start | bytes 73736 | tf_op jit(solution)/shard_map/ppermute | solution.py:40
  (7 other events, 62.9 us)
Sparse Core Ops, SparseCore 0:
  41.2 60.5 all-gather.2

commit v12 on v10

--- a/solution.py
+++ b/solution.py
@@ -61,15 +61,15 @@
     return sum_parts(swap(term.reshape(4, rows // 4, cols), "x")).astype(BF16)
 
 
-def mp_scatter_x_beside(term):
+def spread_and_scatter_x(block, term):
     rows, cols = term.shape
-    term = term.reshape(4, rows // 4, cols)
-    x = lax.axis_index("x")
-    total = lax.dynamic_index_in_dim(term, x, 0, False).astype(F32)
-    for bits in (1, 2, 3):
-        given = lax.dynamic_index_in_dim(term, x ^ bits, 0, False)
-        total += flip(given, "x", bits).astype(F32)
-    return total.astype(BF16)
+    term = term.reshape(4, rows // 4, 4, cols // 4).transpose(0, 2, 1, 3)
+    term = jnp.pad(term.reshape(4, rows, cols // 4), ((0, 0), (0, 16), (0, 0)))
+    block = jnp.broadcast_to(block[None], (4,) + block.shape)
+    block = swap(jnp.concatenate([block, term], axis=2), "x")
+    part = sum_parts(block[:, :rows, 384:]).astype(BF16)
+    part = part.reshape(4, rows // 4, cols // 4).transpose(1, 0, 2)
+    return block, part.reshape(rows // 4, cols)
 
 
 def mp_sum_zl(part):
@@ -101,7 +101,7 @@
         blocks.append((late_ref, (x, 0), 1, x))
         blocks.append((late_ref, (x, 1), 3, x))
     for k, (ref, at, dz, x) in enumerate(blocks):
-        gains = ref[(*at, slice(256, 272), slice(None))].astype(F32)
+        gains = ref[(*at, slice(256, 272), slice(0, 384))].astype(F32)
         gain_ref[k : k + 1, :] = gains[0:1] + gains[1:2] + gains[2:3]
     width = 16 * 384
 
@@ -113,7 +113,7 @@
         rows = pl.ds(pl.multiple_of(t * 32, 32), 32)
 
         def read(ref, at):
-            return ref[(*at, rows, slice(None))].astype(F32)
+            return ref[(*at, rows, slice(0, 384))].astype(F32)
 
         total = jnp.zeros((32, 128), F32)
         for ref, at, dz, x in blocks:
@@ -198,9 +198,9 @@
     weight = lax.all_gather(rows, "y").reshape(6144, 384)
 
     late = flip(jnp.stack([shard, far_block]), "zl", 1)
-    far_block = spread(far_block, "x")
-    part = mp_scatter_x_beside(tie(mlp_term, rows))
-    late, part = lax.optimization_barrier((spread(tie(late, far_block), "x"), part))
+    far_block, part = spread_and_scatter_x(far_block, mlp_term)
+    late = spread(tie(late, far_block), "x")
+    late, part = lax.optimization_barrier((late, mp_sum_zl(part)))
 
     place_z = jnp.stack([lax.axis_index("zl"), lax.axis_index("zh")])
     place_c = lax.axis_index("c").reshape(1)
@@ -220,7 +220,7 @@
         name="teacher_norm",
     )(place_z, own, far_block, late)
     normed_other = shift(normed, "c", 1)
-    mlp_sum = mp_gather_x(mp_sum_zl(tie(part, normed)))
+    mlp_sum = mp_gather_x(tie(part, normed))
     heads = pl.pallas_call(
         attention_kernel,
         out_shape=jax.ShapeDtypeStruct((2, 256, 128), F32),

time: 248 us -> 229 us (0.923)
  starting transfers between devices: 71.1 us -> 58.1 us
  waiting for transfers between devices: 74.7 us -> 68.9 us
  local copies, waits for them, and re-layouts: 15.6 us -> 12.4 us
  other arithmetic: 4.24 us -> 7.03 us
    ppermute x11 -> x8, waiting for transfers between devices: 59.1 us -> 43.6 us  [flip(): lax.ppermute(values, axes, [(i, i ^ bits) for i in range(SIZES[axes])])]
    ppermute x11 -> x8, starting transfers between devices: 40 us -> 28.6 us  [flip(): lax.ppermute(values, axes, [(i, i ^ bits) for i in range(SIZES[axes])])]
    all_to_all x6, waiting for transfers between devices: 14.4 us -> 22.7 us  [swap(): return lax.all_to_all(values, axis, split_axis=0, concat_axis=0)]
    broadcast_in_dim x5 -> x4, local copies, waits for them, and re-layouts: 5.22 us -> 5.09 us  [spread(): jnp.broadcast_to(values[None], (SIZES[axis],) + values.shape)]
  transfers between devices with their start and end apart: 20 -> 17, of which waited for: 12 -> 13; matrix products, arithmetic and copies ran while one was open for 4% -> 5% of each run, Pallas kernels for 5% -> 6%
where the time goes in v12:
time: 229 us; the launch traced here: 228 us
  waiting for transfers between devices  68.9 us (30%)
  starting transfers between devices  58.1 us (25%)
  blocking collectives  49.5 us (22%)
  between operations  14.6 us (6%)
  Pallas kernels  13.4 us (6%)
  local copies, waits for them, and re-layouts  12.4 us (5%)
  other arithmetic  7.03 us (3%)
  matrix products  3.81 us (2%)
    ppermute x8, waiting for transfers between devices, flip(): lax.ppermute(values, axes, [(i, i ^ bits) for i in range(SIZES[axes])])  43.6 us
    all_to_all x1, blocking collectives, reduce_dp(): terms = lax.all_to_all(terms, ('zh', 'y'), split_axis=1, concat_axis=0)  33.4 us
    ppermute x8, starting transfers between devices, flip(): lax.ppermute(values, axes, [(i, i ^ bits) for i in range(SIZES[axes])])  28.6 us
    all_to_all x6, starting transfers between devices, swap(): return lax.all_to_all(values, axis, split_axis=0, concat_axis=0)  25.3 us
    all_to_all x6, waiting for transfers between devices, swap(): return lax.all_to_all(values, axis, split_axis=0, concat_axis=0)  22.7 us
    all_to_all x1, blocking collectives, swap(): return lax.all_to_all(values, axis, split_axis=0, concat_axis=0)  11.1 us
    pallas_call x1, Pallas kernels, shards(): pl.pallas_call(attention_kernel, out_shape=jax.ShapeDtypeStruct((2, 256,...  7.35 us
    pallas_call x1, Pallas kernels, shards(): pl.pallas_call(norm_kernel, out_shape=jax.ShapeDtypeStruct((256, 6144), B...  6.07 us
  transfers between devices with their start and end apart: 17, of which 13 were waited for; matrix products, arithmetic and copies ran while one was open for 5% of the time, Pallas kernels for 6%

profile of v12, /device:TPU:8, one launch (start us, length us, event | category | flops | bytes accessed | tf_op | source)
XLA Modules:
  0.0 227.9 jit_solution(10596810366526182052)
XLA Ops:
  8.9 10.9 %collective-permute-start = (bf16[2,192,384]{2,1,0:T(8,128)(2,1)S(1)}, bf16[2,192,384]{2,1,0:T(8,128)(2,1)S(1)}, u32[]{:S(2)}, u32[]{:S(2)}) collective-permute-start(bf16[2,192,384]{2,1,0:T(8,128)(2,1)S(1)} %reverse_select_fusion), channel_id=1, source_target_pairs={{0,256},{256,0},{1,257},{257,1},{2,258},{258,2},{3,259},{259,3},{4... | collective-permute-start | bytes 884744 | tf_op jit(solution)/shard_map/ppermute | solution.py:40
  20.1 4.3 %collective-permute-start.2 = (bf16[272,384]{1,0:T(8,128)(2,1)S(1)}, bf16[272,384]{1,0:T(8,128)(2,1)S(1)}, u32[]{:S(2)}, u32[]{:S(2)}) collective-permute-start(bf16[272,384]{1,0:T(8,128)(2,1)S(1)} %concatenate.17), channel_id=1, source_target_pairs={{0,8},{4,12},{8,0},{12,4},{1,9},{5,13},{9,1},{13,5},{2,10},{6,14},... | collective-permute-start | bytes 626696 | tf_op jit(solution)/shard_map/ppermute | solution.py:40
  25.4 4.3 %all-to-all-start = ((bf16[4,272,384]{2,1,0:T(8,128)(2,1)}), bf16[4,272,384]{2,1,0:T(8,128)(2,1)S(1)}, u32[]{:S(2)}, u32[]{:S(2)}) async-start(bf16[4,272,384]{2,1,0:T(8,128)(2,1)} %broadcast_in_dim.14), calls=%async_computation | async-start | bytes 1671168 | tf_op jit(solution)/shard_map/all_to_all | solution.py:48
  30.2 3.3 %collective-permute-done = bf16[2,192,384]{2,1,0:T(8,128)(2,1)S(1)} collective-permute-done((bf16[2,192,384]{2,1,0:T(8,128)(2,1)S(1)}, bf16[2,192,384]{2,1,0:T(8,128)(2,1)S(1)}, u32[]{:S(2)}, u32[]{:S(2)}) %collective-permute-start) | collective-permute-done | bytes 294944 | tf_op jit(solution)/shard_map/ppermute | solution.py:40
  36.2 7.0 %collective-permute-done.2 = bf16[272,384]{1,0:T(8,128)(2,1)S(1)} collective-permute-done((bf16[272,384]{1,0:T(8,128)(2,1)S(1)}, bf16[272,384]{1,0:T(8,128)(2,1)S(1)}, u32[]{:S(2)}, u32[]{:S(2)}) %collective-permute-start.2) | collective-permute-done | bytes 208928 | tf_op jit(solution)/shard_map/ppermute | solution.py:40
  47.2 4.3 %all-to-all-start.1 = ((bf16[4,272,640]{2,1,0:T(8,128)(2,1)}), bf16[4,272,640]{2,1,0:T(8,128)(2,1)S(1)}, u32[]{:S(2)}, u32[]{:S(2)}) async-start(bf16[4,272,640]{2,1,0:T(8,128)(2,1)} %fusion.1), calls=%async_computation.1 | async-start | bytes 2785280 | tf_op jit(solution)/shard_map/all_to_all | solution.py:48
  54.4 11.4 %collective-permute-done.3 = bf16[2,272,384]{2,1,0:T(8,128)(2,1)} collective-permute-done((bf16[2,272,384]{2,1,0:T(8,128)(2,1)S(1)}, bf16[2,272,384]{2,1,0:T(8,128)(2,1)}, u32[]{:S(2)}, u32[]{:S(2)}) %collective-permute-start.3) | collective-permute-done | bytes 417824 | tf_op jit(solution)/shard_map/ppermute | solution.py:40
  65.8 4.7 %all-to-all-done.1.far_ref = bf16[4,272,640]{2,1,0:T(8,128)(2,1)S(1)} async-done(((bf16[4,272,640]{2,1,0:T(8,128)(2,1)}), bf16[4,272,640]{2,1,0:T(8,128)(2,1)S(1)}, u32[]{:S(2)}, u32[]{:S(2)}) %all-to-all-start.1) | async-done | bytes 1392672 | tf_op jit(solution)/shard_map/all_to_all | solution.py:48
  72.8 4.4 %all-to-all-start.2 = ((bf16[4,2,272,384]{3,2,1,0:T(8,128)(2,1)}), bf16[4,2,272,384]{3,2,1,0:T(8,128)(2,1)}, u32[]{:S(2)}, u32[]{:S(2)}) async-start(bf16[4,2,272,384]{3,2,1,0:T(8,128)(2,1)} %broadcast_in_dim.16), calls=%async_computation.2 | async-start | bytes 3342336 | tf_op jit(solution)/shard_map/all_to_all | solution.py:48
  79.3 4.9 %collective-permute-done.4 = bf16[64,1024]{1,0:T(8,128)(2,1)S(1)} collective-permute-done((bf16[64,1024]{1,0:T(8,128)(2,1)S(1)}, bf16[64,1024]{1,0:T(8,128)(2,1)S(1)}, u32[]{:S(2)}, u32[]{:S(2)}) %collective-permute-start.4) | collective-permute-done | bytes 131104 | tf_op jit(solution)/shard_map/ppermute | solution.py:40
  87.1 6.0 %collective-permute-done.5 = bf16[64,1024]{1,0:T(8,128)(2,1)} collective-permute-done((bf16[64,1024]{1,0:T(8,128)(2,1)S(1)}, bf16[64,1024]{1,0:T(8,128)(2,1)}, u32[]{:S(2)}, u32[]{:S(2)}) %collective-permute-start.5) | collective-permute-done | bytes 131104 | tf_op jit(solution)/shard_map/ppermute | solution.py:40
  94.8 3.6 %all-to-all-done.2.late_ref = bf16[4,2,272,384]{3,2,1,0:T(8,128)(2,1)} async-done(((bf16[4,2,272,384]{3,2,1,0:T(8,128)(2,1)}), bf16[4,2,272,384]{3,2,1,0:T(8,128)(2,1)}, u32[]{:S(2)}, u32[]{:S(2)}) %all-to-all-start.2) | async-done | bytes 1671200 | tf_op jit(solution)/shard_map/all_to_all | solution.py:48
  98.4 6.1 %teacher_norm.1.own_ref = bf16[256,6144]{1,0:T(8,128)(2,1)} custom-call(s32[2]{0:T(128)S(1)} %pad_add_fusion.place, bf16[4,272,384]{2,1,0:T(8,128)(2,1)S(1)} %all-to-all-done.own_ref, bf16[4,272,640]{2,1,0:T(8,128)(2,1)S(1)} %all-to-all-done.1.far_ref, bf16[4,2,272,384]{3,2,1,0:T(8,128)(2,1)} %all-to-all-done.2.late_ref), custom_call_target="tpu_custom_call" | custom-call | flops 1000 | bytes 1000 | tf_op jit(solution)/shard_map/teacher_norm/pallas_call | solution.py:210
  107.4 3.5 %all-to-all-start.3 = ((bf16[4,64,1024]{2,1,0:T(8,128)(2,1)}), bf16[4,64,1024]{2,1,0:T(8,128)(2,1)S(1)}, u32[]{:S(2)}, u32[]{:S(2)}) async-start(bf16[4,64,1024]{2,1,0:T(8,128)(2,1)} %broadcast_in_dim.17), calls=%async_computation.3 | async-start | bytes 1048576 | tf_op jit(solution)/shard_map/all_to_all | solution.py:48
  114.8 7.3 %teacher_heads.1 = f32[2,256,128]{2,1,0:T(8,128)S(1)} custom-call(s32[1]{0:T(128)} %bitcast.10.place, bf16[256,6144]{1,0:T(8,128)(2,1)} %teacher_norm.1.own_ref, bf16[256,6144]{1,0:T(8,128)(2,1)} %collective-permute-done.6.other_ref, bf16[6144,384]{1,0:T(8,128)(2,1)S(1)} %bitcast.57, f32[2,128]{1,0:T(2,128)S(1)} %copy-done.2), custom_call_target="tpu_custom_call" | custom-call | flops 2415919104 | bytes 11000000 | tf_op jit(solution)/shard_map/teacher_heads/pallas_call | solution.py:224
  126.5 5.0 %all-to-all-start.4 = ((f32[16,2,256]{2,1,0:T(2,128)}), f32[16,2,256]{2,1,0:T(2,128)S(1)}, u32[]{:S(2)}, u32[]{:S(2)}) async-start(f32[16,2,256]{2,1,0:T(2,128)} %broadcast_in_dim.18), calls=%async_computation.4 | async-start | bytes 65536 | tf_op jit(solution)/shard_map/all_to_all | solution.py:48
  131.9 7.8 %all-to-all-done.4 = f32[16,2,256]{2,1,0:T(2,128)S(1)} async-done(((f32[16,2,256]{2,1,0:T(2,128)}), f32[16,2,256]{2,1,0:T(2,128)S(1)}, u32[]{:S(2)}, u32[]{:S(2)}) %all-to-all-start.4) | async-done | bytes 32800 | tf_op jit(solution)/shard_map/all_to_all | solution.py:48
  140.2 11.1 %all_to_all.53 = bf16[4,64,1024]{2,1,0:T(8,128)(2,1)S(1)} all-to-all(bf16[4,64,1024]{2,1,0:T(8,128)(2,1)S(1)} %bitcast.59), channel_id=1, replica_groups=mesh['zh'=2,'y'=8,'c'=2,'zl'=4,'x'=4] {'x'}, dimensions={0} | all-to-all | bytes 1048576 | tf_op jit(solution)/shard_map/all_to_all | solution.py:48
  153.6 4.6 %collective-permute-done.8 = bf16[64,1024]{1,0:T(8,128)(2,1)S(1)} collective-permute-done((bf16[64,1024]{1,0:T(8,128)(2,1)S(1)}, bf16[64,1024]{1,0:T(8,128)(2,1)S(1)}, u32[]{:S(2)}, u32[]{:S(2)}) %collective-permute-start.8) | collective-permute-done | bytes 131104 | tf_op jit(solution)/shard_map/ppermute | solution.py:40
  160.9 6.4 %collective-permute-done.9 = bf16[64,1024]{1,0:T(8,128)(2,1)S(1)} collective-permute-done((bf16[64,1024]{1,0:T(8,128)(2,1)S(1)}, bf16[64,1024]{1,0:T(8,128)(2,1)S(1)}, u32[]{:S(2)}, u32[]{:S(2)}) %collective-permute-start.9) | collective-permute-done | bytes 131104 | tf_op jit(solution)/shard_map/ppermute | solution.py:40
  168.1 3.8 %all-to-all-start.6 = ((bf16[4,64,1024]{2,1,0:T(8,128)(2,1)}), bf16[4,64,1024]{2,1,0:T(8,128)(2,1)S(1)}, u32[]{:S(2)}, u32[]{:S(2)}) async-start(bf16[4,64,1024]{2,1,0:T(8,128)(2,1)} %broadcast_in_dim.19), calls=%async_computation.6 | async-start | bytes 1048576 | tf_op jit(solution)/shard_map/all_to_all | solution.py:48
  173.1 6.6 %all-to-all-done.6 = bf16[4,64,1024]{2,1,0:T(8,128)(2,1)S(1)} async-done(((bf16[4,64,1024]{2,1,0:T(8,128)(2,1)}), bf16[4,64,1024]{2,1,0:T(8,128)(2,1)S(1)}, u32[]{:S(2)}, u32[]{:S(2)}) %all-to-all-start.6) | async-done | bytes 524320 | tf_op jit(solution)/shard_map/all_to_all | solution.py:48
  181.4 5.0 %all_to_all.54 = bf16[1,3,16,2,32,256]{5,4,2,1,0,3:T(8,128)(2,1)S(1)} all-to-all(bf16[1,3,16,2,32,256]{5,4,2,1,0,3:T(8,128)(2,1)S(1)} %copy.48), channel_id=1, replica_groups=mesh['zh'=2,'y'=8,'c'=2,'zl'=4,'x'=4] {'c'}, dimensions={3} | all-to-all | bytes 3145728 | tf_op jit(solution)/shard_map/all_to_all | solution.py:153
  186.9 33.4 %all_to_all.55 = bf16[1,3,16,32,256]{4,3,1,0,2:T(8,128)(2,1)S(1)} all-to-all(bf16[1,3,16,32,256]{4,3,1,0,2:T(8,128)(2,1)S(1)} %copy.47), channel_id=1, replica_groups=mesh['zh'=2,'y'=8,'c'=2,'zl'=4,'x'=4] {'zh','y'}, dimensions={2} | all-to-all | bytes 1572864 | tf_op jit(solution)/shard_map/all_to_all | solution.py:155
  (107 shorter events, 43.5 us)
Async XLA Ops:
  7.2 28.7 %copy-start = (bf16[256,1024]{1,0:T(8,128)(2,1)S(1)}, bf16[256,1024]{1,0:T(8,128)(2,1)}, u32[]{:S(2)}) copy-start(bf16[256,1024]{1,0:T(8,128)(2,1)} %param.16) | copy-start | bytes 1572868
  7.2 12.6 %copy-start.11 = (f32[384]{0:T(512)S(1)}, f32[384]{0:T(512)}, u32[]{:S(2)}) copy-start(f32[384]{0:T(512)} %param.10) | copy-start | bytes 4612
  7.2 12.7 %copy-start.10 = (bf16[256,384]{1,0:T(8,128)(2,1)S(1)}, bf16[256,384]{1,0:T(8,128)(2,1)}, u32[]{:S(2)}) copy-start(bf16[256,384]{1,0:T(8,128)(2,1)} %param.9) | copy-start | bytes 589828
  8.9 24.6 %collective-permute-start = (bf16[2,192,384]{2,1,0:T(8,128)(2,1)S(1)}, bf16[2,192,384]{2,1,0:T(8,128)(2,1)S(1)}, u32[]{:S(2)}, u32[]{:S(2)}) collective-permute-start(bf16[2,192,384]{2,1,0:T(8,128)(2,1)S(1)} %reverse_select_fusion), channel_id=1, source_target_pairs={{0,256},{256,0},{1,257},{257,1},{2,258},{258,2},{3,259},{259,3},{4... | collective-permute-start | bytes 884744 | tf_op jit(solution)/shard_map/ppermute | solution.py:40
  19.9 9.8 %copy-start.3 = (bf16[256,1024]{1,0:T(8,128)(2,1)S(1)}, bf16[256,1024]{1,0:T(8,128)(2,1)}, u32[]{:S(2)}) copy-start(bf16[256,1024]{1,0:T(8,128)(2,1)} %param.13) | copy-start | bytes 1572868
  20.1 23.2 %collective-permute-start.2 = (bf16[272,384]{1,0:T(8,128)(2,1)S(1)}, bf16[272,384]{1,0:T(8,128)(2,1)S(1)}, u32[]{:S(2)}, u32[]{:S(2)}) collective-permute-start(bf16[272,384]{1,0:T(8,128)(2,1)S(1)} %concatenate.17), channel_id=1, source_target_pairs={{0,8},{4,12},{8,0},{12,4},{1,9},{5,13},{9,1},{13,5},{2,10},{6,14},... | collective-permute-start | bytes 626696 | tf_op jit(solution)/shard_map/ppermute | solution.py:40
  25.4 17.9 %all-to-all-start = ((bf16[4,272,384]{2,1,0:T(8,128)(2,1)}), bf16[4,272,384]{2,1,0:T(8,128)(2,1)S(1)}, u32[]{:S(2)}, u32[]{:S(2)}) async-start(bf16[4,272,384]{2,1,0:T(8,128)(2,1)} %broadcast_in_dim.14), calls=%async_computation | async-start | bytes 1671168 | tf_op jit(solution)/shard_map/all_to_all | solution.py:48
  29.7 82.8 %all-gather.3.cloned.1.call-start = ((), (), s32[]{:S(2)}) async-start(), calls=%async_computation.9 | async-start | bytes 5308416 | tf_op jit(solution)/shard_map/all_gather | solution.py:198
  33.6 9.7 %collective-permute-start.1 = (bf16[2,192,384]{2,1,0:T(8,128)(2,1)S(1)}, bf16[2,192,384]{2,1,0:T(8,128)(2,1)}, u32[]{:S(2)}, u32[]{:S(2)}) collective-permute-start(bf16[2,192,384]{2,1,0:T(8,128)(2,1)S(1)} %pad_maximum_fusion.3), channel_id=1, source_target_pairs={{0,16},{16,0},{1,17},{17,1},{2,18},{18,2},{3,19},{19,3},{4,20},{20... | collective-permute-start | bytes 884744 | tf_op jit(solution)/shard_map/ppermute | solution.py:40
  47.2 23.3 %all-to-all-start.1 = ((bf16[4,272,640]{2,1,0:T(8,128)(2,1)}), bf16[4,272,640]{2,1,0:T(8,128)(2,1)S(1)}, u32[]{:S(2)}, u32[]{:S(2)}) async-start(bf16[4,272,640]{2,1,0:T(8,128)(2,1)} %fusion.1), calls=%async_computation.1 | async-start | bytes 2785280 | tf_op jit(solution)/shard_map/all_to_all | solution.py:48
  52.5 13.3 %collective-permute-start.3 = (bf16[2,272,384]{2,1,0:T(8,128)(2,1)S(1)}, bf16[2,272,384]{2,1,0:T(8,128)(2,1)}, u32[]{:S(2)}, u32[]{:S(2)}) collective-permute-start(bf16[2,272,384]{2,1,0:T(8,128)(2,1)S(1)} %pad_maximum_fusion.2), channel_id=1, source_target_pairs={{0,4},{4,0},{8,12},{12,8},{1,5},{5,1},{9,13},{13,9},{2,6},{6,2},{1... | collective-permute-start | bytes 1253384 | tf_op jit(solution)/shard_map/ppermute | solution.py:40
  72.8 25.5 %all-to-all-start.2 = ((bf16[4,2,272,384]{3,2,1,0:T(8,128)(2,1)}), bf16[4,2,272,384]{3,2,1,0:T(8,128)(2,1)}, u32[]{:S(2)}, u32[]{:S(2)}) async-start(bf16[4,2,272,384]{3,2,1,0:T(8,128)(2,1)} %broadcast_in_dim.16), calls=%async_computation.2 | async-start | bytes 3342336 | tf_op jit(solution)/shard_map/all_to_all | solution.py:48
  77.4 6.9 %collective-permute-start.4 = (bf16[64,1024]{1,0:T(8,128)(2,1)S(1)}, bf16[64,1024]{1,0:T(8,128)(2,1)S(1)}, u32[]{:S(2)}, u32[]{:S(2)}) collective-permute-start(bf16[64,1024]{1,0:T(8,128)(2,1)S(1)} %bitcast.67), channel_id=1, source_target_pairs={{0,4},{4,0},{8,12},{12,8},{1,5},{5,1},{9,13},{13,9},{2,6},{6,2},{1... | collective-permute-start | bytes 393224 | tf_op jit(solution)/shard_map/ppermute | solution.py:40
  84.3 8.9 %collective-permute-start.5 = (bf16[64,1024]{1,0:T(8,128)(2,1)S(1)}, bf16[64,1024]{1,0:T(8,128)(2,1)}, u32[]{:S(2)}, u32[]{:S(2)}) collective-permute-start(bf16[64,1024]{1,0:T(8,128)(2,1)S(1)} %add_convert_fusion.3), channel_id=1, source_target_pairs={{0,8},{4,12},{8,0},{12,4},{1,9},{5,13},{9,1},{13,5},{2,10},{6,14},... | collective-permute-start | bytes 393224 | tf_op jit(solution)/shard_map/ppermute | solution.py:40
  94.8 11.7 %copy-start.8 = (bf16[64,1024]{1,0:T(8,128)(2,1)S(1)}, bf16[64,1024]{1,0:T(8,128)(2,1)}, u32[]{:S(2)}) copy-start(bf16[64,1024]{1,0:T(8,128)(2,1)} %add_convert_fusion.2) | copy-start | bytes 393220
  104.4 8.0 %collective-permute-start.6 = (bf16[256,6144]{1,0:T(8,128)(2,1)}, bf16[256,6144]{1,0:T(8,128)(2,1)}, u32[]{:S(2)}, u32[]{:S(2)}) collective-permute-start(bf16[256,6144]{1,0:T(8,128)(2,1)} %teacher_norm.1.own_ref), channel_id=1, source_target_pairs={{0,16},{16,0},{1,17},{17,1},{2,18},{18,2},{3,19},{19,3},{4,20},{20... | collective-permute-start | bytes 9437192 | tf_op jit(solution)/shard_map/ppermute | solution.py:36
  107.4 17.0 %all-to-all-start.3 = ((bf16[4,64,1024]{2,1,0:T(8,128)(2,1)}), bf16[4,64,1024]{2,1,0:T(8,128)(2,1)S(1)}, u32[]{:S(2)}, u32[]{:S(2)}) async-start(bf16[4,64,1024]{2,1,0:T(8,128)(2,1)} %broadcast_in_dim.17), calls=%async_computation.3 | async-start | bytes 1048576 | tf_op jit(solution)/shard_map/all_to_all | solution.py:48
  122.2 9.4 %copy-start.4 = (bf16[1024,256]{1,0:T(8,128)(2,1)S(1)}, bf16[1024,256]{1,0:T(8,128)(2,1)}, u32[]{:S(2)}) copy-start(bf16[1024,256]{1,0:T(8,128)(2,1)} %param.17) | copy-start | bytes 1572868
  122.2 3.4 %collective-permute-start.7 = (f32[256,128]{1,0:T(8,128)S(1)}, f32[256,128]{1,0:T(8,128)S(1)}, u32[]{:S(2)}, u32[]{:S(2)}) collective-permute-start(f32[256,128]{1,0:T(8,128)S(1)} %get-tuple-element.29), channel_id=1, source_target_pairs={{0,16},{16,0},{1,17},{17,1},{2,18},{18,2},{3,19},{19,3},{4,20},{20... | collective-permute-start | bytes 393224 | tf_op jit(solution)/shard_map/ppermute | solution.py:36
  126.5 13.2 %all-to-all-start.4 = ((f32[16,2,256]{2,1,0:T(2,128)}), f32[16,2,256]{2,1,0:T(2,128)S(1)}, u32[]{:S(2)}, u32[]{:S(2)}) async-start(f32[16,2,256]{2,1,0:T(2,128)} %broadcast_in_dim.18), calls=%async_computation.4 | async-start | bytes 65536 | tf_op jit(solution)/shard_map/all_to_all | solution.py:48
  151.4 6.9 %collective-permute-start.8 = (bf16[64,1024]{1,0:T(8,128)(2,1)S(1)}, bf16[64,1024]{1,0:T(8,128)(2,1)S(1)}, u32[]{:S(2)}, u32[]{:S(2)}) collective-permute-start(bf16[64,1024]{1,0:T(8,128)(2,1)S(1)} %reduce_sum.119), channel_id=1, source_target_pairs={{0,4},{4,0},{8,12},{12,8},{1,5},{5,1},{9,13},{13,9},{2,6},{6,2},{1... | collective-permute-start | bytes 393224 | tf_op jit(solution)/shard_map/ppermute | solution.py:40
  158.3 9.0 %collective-permute-start.9 = (bf16[64,1024]{1,0:T(8,128)(2,1)S(1)}, bf16[64,1024]{1,0:T(8,128)(2,1)S(1)}, u32[]{:S(2)}, u32[]{:S(2)}) collective-permute-start(bf16[64,1024]{1,0:T(8,128)(2,1)S(1)} %add_convert_fusion.1), channel_id=1, source_target_pairs={{0,8},{4,12},{8,0},{12,4},{1,9},{5,13},{9,1},{13,5},{2,10},{6,14},... | collective-permute-start | bytes 393224 | tf_op jit(solution)/shard_map/ppermute | solution.py:40
  168.1 11.7 %copy-start.6 = (f32[256,256]{1,0:T(8,128)S(1)}, f32[256,256]{1,0:T(8,128)}, u32[]{:S(2)}) copy-start(f32[256,256]{1,0:T(8,128)} %copy-done.5) | copy-start | bytes 786436
  168.1 11.7 %all-to-all-start.6 = ((bf16[4,64,1024]{2,1,0:T(8,128)(2,1)}), bf16[4,64,1024]{2,1,0:T(8,128)(2,1)S(1)}, u32[]{:S(2)}, u32[]{:S(2)}) async-start(bf16[4,64,1024]{2,1,0:T(8,128)(2,1)} %broadcast_in_dim.19), calls=%async_computation.6 | async-start | bytes 1048576 | tf_op jit(solution)/shard_map/all_to_all | solution.py:48
  (7 other events, 34.4 us)
Sparse Core Ops, SparseCore 0:
  45.5 58.5 all-gather.2

commit v13 on v12

--- a/solution.py
+++ b/solution.py
@@ -132,19 +132,18 @@
             ).astype(BF16)
 
 
-def attention_kernel(place, own_ref, other_ref, w_ref, qg_ref, f_ref):
+def attention_kernel(place, n_ref, w_ref, qg_ref, f_ref):
     gain = jnp.where(place[0] == 0, qg_ref[0:1, :], qg_ref[1:2, :])
-    for image, ref in enumerate((own_ref, other_ref)):
-        projected = jnp.dot(ref[...], w_ref[...], preferred_element_type=F32)
-        query = (normalize(projected[:, :128]) * gain).astype(BF16)
-        key = (normalize(projected[:, 128:256]) * gain).astype(BF16)
-        value = projected[:, 256:].astype(BF16)
-        scores = lax.dot_general(
-            query, key, (((1,), (1,)), ((), ())), preferred_element_type=F32
-        ) * (HEAD ** (-0.5))
-        scores = jnp.exp(scores - jnp.max(scores, axis=1, keepdims=True))
-        attn = (scores / jnp.sum(scores, axis=1, keepdims=True)).astype(BF16)
-        f_ref[image] = jnp.dot(attn, value, preferred_element_type=F32)
+    projected = jnp.dot(n_ref[...], w_ref[...], preferred_element_type=F32)
+    query = (normalize(projected[:, :128]) * gain).astype(BF16)
+    key = (normalize(projected[:, 128:256]) * gain).astype(BF16)
+    value = projected[:, 256:].astype(BF16)
+    scores = lax.dot_general(
+        query, key, (((1,), (1,)), ((), ())), preferred_element_type=F32
+    ) * (HEAD ** (-0.5))
+    scores = jnp.exp(scores - jnp.max(scores, axis=1, keepdims=True))
+    attn = (scores / jnp.sum(scores, axis=1, keepdims=True)).astype(BF16)
+    f_ref[...] = jnp.dot(attn, value, preferred_element_type=F32)
 
 
 def reduce_dp(terms):
@@ -199,14 +198,15 @@
 
     late = flip(jnp.stack([shard, far_block]), "zl", 1)
     far_block, part = spread_and_scatter_x(far_block, mlp_term)
-    late = spread(tie(late, far_block), "x")
+    late = jnp.broadcast_to(late[None], (4,) + late.shape)
+    late = swap(tie(late, far_block), "x")
     late, part = lax.optimization_barrier((late, mp_sum_zl(part)))
 
     place_z = jnp.stack([lax.axis_index("zl"), lax.axis_index("zh")])
     place_c = lax.axis_index("c").reshape(1)
     smem = pl.BlockSpec(memory_space=pltpu.SMEM)
     vmem = pl.BlockSpec(memory_space=pltpu.VMEM)
-    params = pltpu.CompilerParams(vmem_limit_bytes=40 * 1024 * 1024)
+    params = pltpu.CompilerParams(vmem_limit_bytes=24 * 1024 * 1024)
     normed = pl.pallas_call(
         norm_kernel,
         out_shape=jax.ShapeDtypeStruct((256, 6144), BF16),
@@ -223,20 +223,21 @@
     mlp_sum = mp_gather_x(tie(part, normed))
     heads = pl.pallas_call(
         attention_kernel,
-        out_shape=jax.ShapeDtypeStruct((2, 256, 128), F32),
-        in_specs=[smem] + [vmem] * 4,
+        out_shape=jax.ShapeDtypeStruct((256, 128), F32),
+        in_specs=[smem] + [vmem] * 3,
         out_specs=vmem,
         compiler_params=params,
         cost_estimate=pl.CostEstimate(
-            flops=2 * 512 * 6144 * 384, bytes_accessed=11_000_000, transcendentals=131072
+            flops=2 * 256 * 6144 * 384, bytes_accessed=8_000_000, transcendentals=65536
         ),
         name="teacher_heads",
-    )(place_c, normed, normed_other, weight, qk_gain)
-    crossed = shift(heads[1], "c", 1)
+    )
+    kept = heads(place_c, normed, weight, qk_gain)
+    crossed = shift(heads(place_c, tie(normed_other, kept), weight, qk_gain), "c", 1)
     features = jnp.where(
         place_c[0] == 0,
-        jnp.concatenate([heads[0], crossed], axis=1),
-        jnp.concatenate([crossed, heads[0]], axis=1),
+        jnp.concatenate([kept, crossed], axis=1),
+        jnp.concatenate([crossed, kept], axis=1),
     )
 
     block_out = (student_in.astype(F32) + mlp_sum.astype(F32)).astype(BF16)

time: 229 us -> 230 us (level)
    broadcast_in_dim x4 -> x3, local copies, waits for them, and re-layouts: 5.09 us -> 2.71 us  [spread(): jnp.broadcast_to(values[None], (SIZES[axis],) + values.shape)]
    broadcast_in_dim x0 -> x1, local copies, waits for them, and re-layouts: none -> 2.38 us  [shards(): late = jnp.broadcast_to(late[None], (4,) + late.shape)]
    pallas_call x1 -> x2, Pallas kernels: 7.35 us -> 8.87 us  [the longest x1 4.51 us: shards(): kept = heads(place_c, normed, weight, qk_gain)]
  transfers between devices with their start and end apart: 17 -> 17, of which waited for: 13 -> 12; matrix products, arithmetic and copies ran while one was open for 5% -> 5% of each run, Pallas kernels for 6% -> 7%
where the time goes in v13:
time: 230 us; the launch traced here: 229 us
  waiting for transfers between devices  67.1 us (29%)
  starting transfers between devices  59.9 us (26%)
  blocking collectives  49.2 us (21%)
  Pallas kernels  14.9 us (6%)
  between operations  14.6 us (6%)
  local copies, waits for them, and re-layouts  12.4 us (5%)
  other arithmetic  7.03 us (3%)
  matrix products  3.81 us (2%)
    ppermute x8, waiting for transfers between devices, flip(): lax.ppermute(values, axes, [(i, i ^ bits) for i in range(SIZES[axes])])  43.6 us
    all_to_all x1, blocking collectives, reduce_dp(): terms = lax.all_to_all(terms, ('zh', 'y'), split_axis=1, concat_axis=0)  33.1 us
    ppermute x8, starting transfers between devices, flip(): lax.ppermute(values, axes, [(i, i ^ bits) for i in range(SIZES[axes])])  28.6 us
    all_to_all x6, starting transfers between devices, swap(): return lax.all_to_all(values, axis, split_axis=0, concat_axis=0)  26.7 us
    all_to_all x6, waiting for transfers between devices, swap(): return lax.all_to_all(values, axis, split_axis=0, concat_axis=0)  22.7 us
    all_to_all x1, blocking collectives, swap(): return lax.all_to_all(values, axis, split_axis=0, concat_axis=0)  11.1 us
    pallas_call x1, Pallas kernels, shards(): pl.pallas_call(norm_kernel, out_shape=jax.ShapeDtypeStruct((256, 6144), B...  6.07 us
    all_to_all x1, blocking collectives, reduce_dp(): terms = lax.all_to_all(terms, 'c', split_axis=2, concat_axis=0)  5 us
  transfers between devices with their start and end apart: 17, of which 12 were waited for; matrix products, arithmetic and copies ran while one was open for 5% of the time, Pallas kernels for 7%

profile of v13, /device:TPU:8, one launch (start us, length us, event | category | flops | bytes accessed | tf_op | source)
XLA Modules:
  0.0 229.1 jit_solution(9678769391931955083)
XLA Ops:
  8.9 10.9 %collective-permute-start = (bf16[2,192,384]{2,1,0:T(8,128)(2,1)S(1)}, bf16[2,192,384]{2,1,0:T(8,128)(2,1)S(1)}, u32[]{:S(2)}, u32[]{:S(2)}) collective-permute-start(bf16[2,192,384]{2,1,0:T(8,128)(2,1)S(1)} %reverse_select_fusion), channel_id=1, source_target_pairs={{0,256},{256,0},{1,257},{257,1},{2,258},{258,2},{3,259},{259,3},{4... | collective-permute-start | bytes 884744 | tf_op jit(solution)/shard_map/ppermute | solution.py:40
  20.1 4.3 %collective-permute-start.2 = (bf16[272,384]{1,0:T(8,128)(2,1)S(1)}, bf16[272,384]{1,0:T(8,128)(2,1)S(1)}, u32[]{:S(2)}, u32[]{:S(2)}) collective-permute-start(bf16[272,384]{1,0:T(8,128)(2,1)S(1)} %concatenate.17), channel_id=1, source_target_pairs={{0,8},{4,12},{8,0},{12,4},{1,9},{5,13},{9,1},{13,5},{2,10},{6,14},... | collective-permute-start | bytes 626696 | tf_op jit(solution)/shard_map/ppermute | solution.py:40
  25.4 4.3 %all-to-all-start = ((bf16[4,272,384]{2,1,0:T(8,128)(2,1)}), bf16[4,272,384]{2,1,0:T(8,128)(2,1)S(1)}, u32[]{:S(2)}, u32[]{:S(2)}) async-start(bf16[4,272,384]{2,1,0:T(8,128)(2,1)} %broadcast_in_dim.14), calls=%async_computation | async-start | bytes 1671168 | tf_op jit(solution)/shard_map/all_to_all | solution.py:48
  36.2 7.0 %collective-permute-done.2 = bf16[272,384]{1,0:T(8,128)(2,1)S(1)} collective-permute-done((bf16[272,384]{1,0:T(8,128)(2,1)S(1)}, bf16[272,384]{1,0:T(8,128)(2,1)S(1)}, u32[]{:S(2)}, u32[]{:S(2)}) %collective-permute-start.2) | collective-permute-done | bytes 208928 | tf_op jit(solution)/shard_map/ppermute | solution.py:40
  47.2 4.3 %all-to-all-start.1 = ((bf16[4,272,640]{2,1,0:T(8,128)(2,1)}), bf16[4,272,640]{2,1,0:T(8,128)(2,1)S(1)}, u32[]{:S(2)}, u32[]{:S(2)}) async-start(bf16[4,272,640]{2,1,0:T(8,128)(2,1)} %fusion.1), calls=%async_computation.1 | async-start | bytes 2785280 | tf_op jit(solution)/shard_map/all_to_all | solution.py:48
  54.4 11.4 %collective-permute-done.3 = bf16[2,272,384]{2,1,0:T(8,128)(2,1)} collective-permute-done((bf16[2,272,384]{2,1,0:T(8,128)(2,1)S(1)}, bf16[2,272,384]{2,1,0:T(8,128)(2,1)}, u32[]{:S(2)}, u32[]{:S(2)}) %collective-permute-start.3) | collective-permute-done | bytes 417824 | tf_op jit(solution)/shard_map/ppermute | solution.py:40
  65.8 4.7 %all-to-all-done.1.far_ref = bf16[4,272,640]{2,1,0:T(8,128)(2,1)S(1)} async-done(((bf16[4,272,640]{2,1,0:T(8,128)(2,1)}), bf16[4,272,640]{2,1,0:T(8,128)(2,1)S(1)}, u32[]{:S(2)}, u32[]{:S(2)}) %all-to-all-start.1) | async-done | bytes 1392672 | tf_op jit(solution)/shard_map/all_to_all | solution.py:48
  72.8 4.4 %all-to-all-start.2 = ((bf16[4,2,272,384]{3,2,1,0:T(8,128)(2,1)}), bf16[4,2,272,384]{3,2,1,0:T(8,128)(2,1)}, u32[]{:S(2)}, u32[]{:S(2)}) async-start(bf16[4,2,272,384]{3,2,1,0:T(8,128)(2,1)} %broadcast_in_dim.15), calls=%async_computation.2 | async-start | bytes 3342336 | tf_op jit(solution)/shard_map/all_to_all | solution.py:48
  79.3 4.9 %collective-permute-done.4 = bf16[64,1024]{1,0:T(8,128)(2,1)S(1)} collective-permute-done((bf16[64,1024]{1,0:T(8,128)(2,1)S(1)}, bf16[64,1024]{1,0:T(8,128)(2,1)S(1)}, u32[]{:S(2)}, u32[]{:S(2)}) %collective-permute-start.4) | collective-permute-done | bytes 131104 | tf_op jit(solution)/shard_map/ppermute | solution.py:40
  87.1 6.0 %collective-permute-done.5 = bf16[64,1024]{1,0:T(8,128)(2,1)} collective-permute-done((bf16[64,1024]{1,0:T(8,128)(2,1)S(1)}, bf16[64,1024]{1,0:T(8,128)(2,1)}, u32[]{:S(2)}, u32[]{:S(2)}) %collective-permute-start.5) | collective-permute-done | bytes 131104 | tf_op jit(solution)/shard_map/ppermute | solution.py:40
  94.8 3.6 %all-to-all-done.2.late_ref = bf16[4,2,272,384]{3,2,1,0:T(8,128)(2,1)} async-done(((bf16[4,2,272,384]{3,2,1,0:T(8,128)(2,1)}), bf16[4,2,272,384]{3,2,1,0:T(8,128)(2,1)}, u32[]{:S(2)}, u32[]{:S(2)}) %all-to-all-start.2) | async-done | bytes 1671200 | tf_op jit(solution)/shard_map/all_to_all | solution.py:48
  98.4 6.1 %teacher_norm.1.n_ref = bf16[256,6144]{1,0:T(8,128)(2,1)} custom-call(s32[2]{0:T(128)S(1)} %pad_add_fusion.place, bf16[4,272,384]{2,1,0:T(8,128)(2,1)S(1)} %all-to-all-done.own_ref, bf16[4,272,640]{2,1,0:T(8,128)(2,1)S(1)} %all-to-all-done.1.far_ref, bf16[4,2,272,384]{3,2,1,0:T(8,128)(2,1)} %all-to-all-done.2.late_ref), custom_call_target="tpu_custom_call" | custom-call | flops 1000 | bytes 1000 | tf_op jit(solution)/shard_map/teacher_norm/pallas_call | solution.py:210
  107.4 3.5 %all-to-all-start.3 = ((bf16[4,64,1024]{2,1,0:T(8,128)(2,1)}), bf16[4,64,1024]{2,1,0:T(8,128)(2,1)S(1)}, u32[]{:S(2)}, u32[]{:S(2)}) async-start(bf16[4,64,1024]{2,1,0:T(8,128)(2,1)} %broadcast_in_dim.17), calls=%async_computation.3 | async-start | bytes 1048576 | tf_op jit(solution)/shard_map/all_to_all | solution.py:48
  113.2 4.5 %teacher_heads.2 = f32[256,128]{1,0:T(8,128)S(1)} custom-call(s32[1]{0:T(128)} %bitcast.10.place, bf16[256,6144]{1,0:T(8,128)(2,1)} %teacher_norm.1.n_ref, bf16[6144,384]{1,0:T(8,128)(2,1)S(1)} %bitcast.53, f32[2,128]{1,0:T(2,128)S(1)} %copy-done.3), custom_call_target="tpu_custom_call" | custom-call | flops 1207959552 | bytes 8000000 | tf_op jit(solution)/shard_map/teacher_heads/pallas_call | solution.py:235
  117.8 4.4 %teacher_heads.3 = f32[256,128]{1,0:T(8,128)S(1)} custom-call(s32[1]{0:T(128)} %bitcast.10.place, bf16[256,6144]{1,0:T(8,128)(2,1)} %collective-permute-done.6.n_ref, bf16[6144,384]{1,0:T(8,128)(2,1)S(1)} %bitcast.54, f32[2,128]{1,0:T(2,128)S(1)} %copy-done.3), custom_call_target="tpu_custom_call" | custom-call | flops 1207959552 | bytes 8000000 | tf_op jit(solution)/shard_map/teacher_heads/pallas_call | solution.py:236
  126.6 6.5 %all-to-all-start.4 = ((f32[16,2,256]{2,1,0:T(2,128)}), f32[16,2,256]{2,1,0:T(2,128)S(1)}, u32[]{:S(2)}, u32[]{:S(2)}) async-start(f32[16,2,256]{2,1,0:T(2,128)} %broadcast_in_dim.18), calls=%async_computation.4 | async-start | bytes 65536 | tf_op jit(solution)/shard_map/all_to_all | solution.py:48
  133.4 7.8 %all-to-all-done.4 = f32[16,2,256]{2,1,0:T(2,128)S(1)} async-done(((f32[16,2,256]{2,1,0:T(2,128)}), f32[16,2,256]{2,1,0:T(2,128)S(1)}, u32[]{:S(2)}, u32[]{:S(2)}) %all-to-all-start.4) | async-done | bytes 32800 | tf_op jit(solution)/shard_map/all_to_all | solution.py:48
  141.7 11.1 %all_to_all.53 = bf16[4,64,1024]{2,1,0:T(8,128)(2,1)S(1)} all-to-all(bf16[4,64,1024]{2,1,0:T(8,128)(2,1)S(1)} %bitcast.56), channel_id=1, replica_groups=mesh['zh'=2,'y'=8,'c'=2,'zl'=4,'x'=4] {'x'}, dimensions={0} | all-to-all | bytes 1048576 | tf_op jit(solution)/shard_map/all_to_all | solution.py:48
  155.2 4.6 %collective-permute-done.8 = bf16[64,1024]{1,0:T(8,128)(2,1)S(1)} collective-permute-done((bf16[64,1024]{1,0:T(8,128)(2,1)S(1)}, bf16[64,1024]{1,0:T(8,128)(2,1)S(1)}, u32[]{:S(2)}, u32[]{:S(2)}) %collective-permute-start.8) | collective-permute-done | bytes 131104 | tf_op jit(solution)/shard_map/ppermute | solution.py:40
  162.4 6.4 %collective-permute-done.9 = bf16[64,1024]{1,0:T(8,128)(2,1)S(1)} collective-permute-done((bf16[64,1024]{1,0:T(8,128)(2,1)S(1)}, bf16[64,1024]{1,0:T(8,128)(2,1)S(1)}, u32[]{:S(2)}, u32[]{:S(2)}) %collective-permute-start.9) | collective-permute-done | bytes 131104 | tf_op jit(solution)/shard_map/ppermute | solution.py:40
  169.6 3.8 %all-to-all-start.6 = ((bf16[4,64,1024]{2,1,0:T(8,128)(2,1)}), bf16[4,64,1024]{2,1,0:T(8,128)(2,1)S(1)}, u32[]{:S(2)}, u32[]{:S(2)}) async-start(bf16[4,64,1024]{2,1,0:T(8,128)(2,1)} %broadcast_in_dim.19), calls=%async_computation.6 | async-start | bytes 1048576 | tf_op jit(solution)/shard_map/all_to_all | solution.py:48
  174.7 6.6 %all-to-all-done.6 = bf16[4,64,1024]{2,1,0:T(8,128)(2,1)S(1)} async-done(((bf16[4,64,1024]{2,1,0:T(8,128)(2,1)}), bf16[4,64,1024]{2,1,0:T(8,128)(2,1)S(1)}, u32[]{:S(2)}, u32[]{:S(2)}) %all-to-all-start.6) | async-done | bytes 524320 | tf_op jit(solution)/shard_map/all_to_all | solution.py:48
  182.9 5.0 %all_to_all.54 = bf16[1,3,16,2,32,256]{5,4,2,1,0,3:T(8,128)(2,1)S(1)} all-to-all(bf16[1,3,16,2,32,256]{5,4,2,1,0,3:T(8,128)(2,1)S(1)} %copy.48), channel_id=1, replica_groups=mesh['zh'=2,'y'=8,'c'=2,'zl'=4,'x'=4] {'c'}, dimensions={3} | all-to-all | bytes 3145728 | tf_op jit(solution)/shard_map/all_to_all | solution.py:152
  188.4 33.1 %all_to_all.55 = bf16[1,3,16,32,256]{4,3,1,0,2:T(8,128)(2,1)S(1)} all-to-all(bf16[1,3,16,32,256]{4,3,1,0,2:T(8,128)(2,1)S(1)} %copy.47), channel_id=1, replica_groups=mesh['zh'=2,'y'=8,'c'=2,'zl'=4,'x'=4] {'zh','y'}, dimensions={2} | all-to-all | bytes 1572864 | tf_op jit(solution)/shard_map/all_to_all | solution.py:154
  (109 shorter events, 45.3 us)
Async XLA Ops:
  7.2 28.7 %copy-start = (bf16[256,1024]{1,0:T(8,128)(2,1)S(1)}, bf16[256,1024]{1,0:T(8,128)(2,1)}, u32[]{:S(2)}) copy-start(bf16[256,1024]{1,0:T(8,128)(2,1)} %param.16) | copy-start | bytes 1572868
  7.2 12.6 %copy-start.12 = (f32[384]{0:T(512)S(1)}, f32[384]{0:T(512)}, u32[]{:S(2)}) copy-start(f32[384]{0:T(512)} %param.10) | copy-start | bytes 4612
  7.2 12.7 %copy-start.11 = (bf16[256,384]{1,0:T(8,128)(2,1)S(1)}, bf16[256,384]{1,0:T(8,128)(2,1)}, u32[]{:S(2)}) copy-start(bf16[256,384]{1,0:T(8,128)(2,1)} %param.9) | copy-start | bytes 589828
  8.9 24.6 %collective-permute-start = (bf16[2,192,384]{2,1,0:T(8,128)(2,1)S(1)}, bf16[2,192,384]{2,1,0:T(8,128)(2,1)S(1)}, u32[]{:S(2)}, u32[]{:S(2)}) collective-permute-start(bf16[2,192,384]{2,1,0:T(8,128)(2,1)S(1)} %reverse_select_fusion), channel_id=1, source_target_pairs={{0,256},{256,0},{1,257},{257,1},{2,258},{258,2},{3,259},{259,3},{4... | collective-permute-start | bytes 884744 | tf_op jit(solution)/shard_map/ppermute | solution.py:40
  19.9 9.8 %copy-start.4 = (bf16[256,1024]{1,0:T(8,128)(2,1)S(1)}, bf16[256,1024]{1,0:T(8,128)(2,1)}, u32[]{:S(2)}) copy-start(bf16[256,1024]{1,0:T(8,128)(2,1)} %param.13) | copy-start | bytes 1572868
  20.1 23.2 %collective-permute-start.2 = (bf16[272,384]{1,0:T(8,128)(2,1)S(1)}, bf16[272,384]{1,0:T(8,128)(2,1)S(1)}, u32[]{:S(2)}, u32[]{:S(2)}) collective-permute-start(bf16[272,384]{1,0:T(8,128)(2,1)S(1)} %concatenate.17), channel_id=1, source_target_pairs={{0,8},{4,12},{8,0},{12,4},{1,9},{5,13},{9,1},{13,5},{2,10},{6,14},... | collective-permute-start | bytes 626696 | tf_op jit(solution)/shard_map/ppermute | solution.py:40
  25.4 17.9 %all-to-all-start = ((bf16[4,272,384]{2,1,0:T(8,128)(2,1)}), bf16[4,272,384]{2,1,0:T(8,128)(2,1)S(1)}, u32[]{:S(2)}, u32[]{:S(2)}) async-start(bf16[4,272,384]{2,1,0:T(8,128)(2,1)} %broadcast_in_dim.14), calls=%async_computation | async-start | bytes 1671168 | tf_op jit(solution)/shard_map/all_to_all | solution.py:48
  29.7 81.2 %all-gather.3.cloned.1.call-start = ((), (), s32[]{:S(2)}) async-start(), calls=%async_computation.9 | async-start | bytes 5308416 | tf_op jit(solution)/shard_map/all_gather | solution.py:197
  33.6 9.7 %collective-permute-start.1 = (bf16[2,192,384]{2,1,0:T(8,128)(2,1)S(1)}, bf16[2,192,384]{2,1,0:T(8,128)(2,1)}, u32[]{:S(2)}, u32[]{:S(2)}) collective-permute-start(bf16[2,192,384]{2,1,0:T(8,128)(2,1)S(1)} %pad_maximum_fusion.3), channel_id=1, source_target_pairs={{0,16},{16,0},{1,17},{17,1},{2,18},{18,2},{3,19},{19,3},{4,20},{20... | collective-permute-start | bytes 884744 | tf_op jit(solution)/shard_map/ppermute | solution.py:40
  47.2 23.3 %all-to-all-start.1 = ((bf16[4,272,640]{2,1,0:T(8,128)(2,1)}), bf16[4,272,640]{2,1,0:T(8,128)(2,1)S(1)}, u32[]{:S(2)}, u32[]{:S(2)}) async-start(bf16[4,272,640]{2,1,0:T(8,128)(2,1)} %fusion.1), calls=%async_computation.1 | async-start | bytes 2785280 | tf_op jit(solution)/shard_map/all_to_all | solution.py:48
  52.5 13.3 %collective-permute-start.3 = (bf16[2,272,384]{2,1,0:T(8,128)(2,1)S(1)}, bf16[2,272,384]{2,1,0:T(8,128)(2,1)}, u32[]{:S(2)}, u32[]{:S(2)}) collective-permute-start(bf16[2,272,384]{2,1,0:T(8,128)(2,1)S(1)} %pad_maximum_fusion.2), channel_id=1, source_target_pairs={{0,4},{4,0},{8,12},{12,8},{1,5},{5,1},{9,13},{13,9},{2,6},{6,2},{1... | collective-permute-start | bytes 1253384 | tf_op jit(solution)/shard_map/ppermute | solution.py:40
  72.8 25.5 %all-to-all-start.2 = ((bf16[4,2,272,384]{3,2,1,0:T(8,128)(2,1)}), bf16[4,2,272,384]{3,2,1,0:T(8,128)(2,1)}, u32[]{:S(2)}, u32[]{:S(2)}) async-start(bf16[4,2,272,384]{3,2,1,0:T(8,128)(2,1)} %broadcast_in_dim.15), calls=%async_computation.2 | async-start | bytes 3342336 | tf_op jit(solution)/shard_map/all_to_all | solution.py:48
  77.4 6.9 %collective-permute-start.4 = (bf16[64,1024]{1,0:T(8,128)(2,1)S(1)}, bf16[64,1024]{1,0:T(8,128)(2,1)S(1)}, u32[]{:S(2)}, u32[]{:S(2)}) collective-permute-start(bf16[64,1024]{1,0:T(8,128)(2,1)S(1)} %bitcast.64), channel_id=1, source_target_pairs={{0,4},{4,0},{8,12},{12,8},{1,5},{5,1},{9,13},{13,9},{2,6},{6,2},{1... | collective-permute-start | bytes 393224 | tf_op jit(solution)/shard_map/ppermute | solution.py:40
  84.3 8.9 %collective-permute-start.5 = (bf16[64,1024]{1,0:T(8,128)(2,1)S(1)}, bf16[64,1024]{1,0:T(8,128)(2,1)}, u32[]{:S(2)}, u32[]{:S(2)}) collective-permute-start(bf16[64,1024]{1,0:T(8,128)(2,1)S(1)} %add_convert_fusion.3), channel_id=1, source_target_pairs={{0,8},{4,12},{8,0},{12,4},{1,9},{5,13},{9,1},{13,5},{2,10},{6,14},... | collective-permute-start | bytes 393224 | tf_op jit(solution)/shard_map/ppermute | solution.py:40
  94.8 11.7 %copy-start.9 = (bf16[64,1024]{1,0:T(8,128)(2,1)S(1)}, bf16[64,1024]{1,0:T(8,128)(2,1)}, u32[]{:S(2)}) copy-start(bf16[64,1024]{1,0:T(8,128)(2,1)} %add_convert_fusion.2) | copy-start | bytes 393220
  104.4 13.3 %collective-permute-start.6 = (bf16[256,6144]{1,0:T(8,128)(2,1)}, bf16[256,6144]{1,0:T(8,128)(2,1)}, u32[]{:S(2)}, u32[]{:S(2)}) collective-permute-start(bf16[256,6144]{1,0:T(8,128)(2,1)} %teacher_norm.1.n_ref), channel_id=1, source_target_pairs={{0,16},{16,0},{1,17},{17,1},{2,18},{18,2},{3,19},{19,3},{4,20},{20... | collective-permute-start | bytes 9437192 | tf_op jit(solution)/shard_map/ppermute | solution.py:36
  107.4 17.3 %all-to-all-start.3 = ((bf16[4,64,1024]{2,1,0:T(8,128)(2,1)}), bf16[4,64,1024]{2,1,0:T(8,128)(2,1)S(1)}, u32[]{:S(2)}, u32[]{:S(2)}) async-start(bf16[4,64,1024]{2,1,0:T(8,128)(2,1)} %broadcast_in_dim.17), calls=%async_computation.3 | async-start | bytes 1048576 | tf_op jit(solution)/shard_map/all_to_all | solution.py:48
  122.1 11.0 %copy-start.5 = (bf16[1024,256]{1,0:T(8,128)(2,1)S(1)}, bf16[1024,256]{1,0:T(8,128)(2,1)}, u32[]{:S(2)}) copy-start(bf16[1024,256]{1,0:T(8,128)(2,1)} %param.17) | copy-start | bytes 1572868
  122.1 3.5 %collective-permute-start.7 = (f32[256,128]{1,0:T(8,128)S(1)}, f32[256,128]{1,0:T(8,128)S(1)}, u32[]{:S(2)}, u32[]{:S(2)}) collective-permute-start(f32[256,128]{1,0:T(8,128)S(1)} %teacher_heads.3), channel_id=1, source_target_pairs={{0,16},{16,0},{1,17},{17,1},{2,18},{18,2},{3,19},{19,3},{4,20},{20... | collective-permute-start | bytes 393224 | tf_op jit(solution)/shard_map/ppermute | solution.py:36
  126.6 14.6 %all-to-all-start.4 = ((f32[16,2,256]{2,1,0:T(2,128)}), f32[16,2,256]{2,1,0:T(2,128)S(1)}, u32[]{:S(2)}, u32[]{:S(2)}) async-start(f32[16,2,256]{2,1,0:T(2,128)} %broadcast_in_dim.18), calls=%async_computation.4 | async-start | bytes 65536 | tf_op jit(solution)/shard_map/all_to_all | solution.py:48
  152.9 6.9 %collective-permute-start.8 = (bf16[64,1024]{1,0:T(8,128)(2,1)S(1)}, bf16[64,1024]{1,0:T(8,128)(2,1)S(1)}, u32[]{:S(2)}, u32[]{:S(2)}) collective-permute-start(bf16[64,1024]{1,0:T(8,128)(2,1)S(1)} %reduce_sum.119), channel_id=1, source_target_pairs={{0,4},{4,0},{8,12},{12,8},{1,5},{5,1},{9,13},{13,9},{2,6},{6,2},{1... | collective-permute-start | bytes 393224 | tf_op jit(solution)/shard_map/ppermute | solution.py:40
  159.8 9.0 %collective-permute-start.9 = (bf16[64,1024]{1,0:T(8,128)(2,1)S(1)}, bf16[64,1024]{1,0:T(8,128)(2,1)S(1)}, u32[]{:S(2)}, u32[]{:S(2)}) collective-permute-start(bf16[64,1024]{1,0:T(8,128)(2,1)S(1)} %add_convert_fusion.1), channel_id=1, source_target_pairs={{0,8},{4,12},{8,0},{12,4},{1,9},{5,13},{9,1},{13,5},{2,10},{6,14},... | collective-permute-start | bytes 393224 | tf_op jit(solution)/shard_map/ppermute | solution.py:40
  169.6 11.7 %copy-start.7 = (f32[256,256]{1,0:T(8,128)S(1)}, f32[256,256]{1,0:T(8,128)}, u32[]{:S(2)}) copy-start(f32[256,256]{1,0:T(8,128)} %copy-done.6) | copy-start | bytes 786436
  169.6 11.7 %all-to-all-start.6 = ((bf16[4,64,1024]{2,1,0:T(8,128)(2,1)}), bf16[4,64,1024]{2,1,0:T(8,128)(2,1)S(1)}, u32[]{:S(2)}, u32[]{:S(2)}) async-start(bf16[4,64,1024]{2,1,0:T(8,128)(2,1)} %broadcast_in_dim.19), calls=%async_computation.6 | async-start | bytes 1048576 | tf_op jit(solution)/shard_map/all_to_all | solution.py:48
  (8 other events, 37.3 us)
Sparse Core Ops, SparseCore 0:
  45.5 58.5 all-gather.2

commit v14 on v12

--- a/solution.py
+++ b/solution.py
@@ -108,18 +108,18 @@
     def fold(values):
         return values[:, :128] + values[:, 128:256] + values[:, 256:]
 
-    @pl.loop(0, 8)
+    @pl.loop(0, 4)
     def _(t):
-        rows = pl.ds(pl.multiple_of(t * 32, 32), 32)
+        rows = pl.ds(pl.multiple_of(t * 64, 64), 64)
 
         def read(ref, at):
             return ref[(*at, rows, slice(0, 384))].astype(F32)
 
-        total = jnp.zeros((32, 128), F32)
+        total = jnp.zeros((64, 128), F32)
         for ref, at, dz, x in blocks:
             total += fold(read(ref, at))
         mean = jnp.sum(total, axis=1, keepdims=True) / width
-        total = jnp.zeros((32, 128), F32)
+        total = jnp.zeros((64, 128), F32)
         for ref, at, dz, x in blocks:
             d = read(ref, at) - mean
             total += fold(d * d)
@@ -134,8 +134,13 @@
 
 def attention_kernel(place, own_ref, other_ref, w_ref, qg_ref, f_ref):
     gain = jnp.where(place[0] == 0, qg_ref[0:1, :], qg_ref[1:2, :])
-    for image, ref in enumerate((own_ref, other_ref)):
-        projected = jnp.dot(ref[...], w_ref[...], preferred_element_type=F32)
+    both = jnp.dot(
+        jnp.concatenate([own_ref[...], other_ref[...]], axis=0),
+        w_ref[...],
+        preferred_element_type=F32,
+    )
+    for image in range(2):
+        projected = both[256 * image : 256 * image + 256]
         query = (normalize(projected[:, :128]) * gain).astype(BF16)
         key = (normalize(projected[:, 128:256]) * gain).astype(BF16)
         value = projected[:, 256:].astype(BF16)
@@ -172,15 +177,17 @@
     first = lax.axis_index("c") == 0
     weight = qkv_weight.reshape(192, 3, 2, 128).transpose(2, 0, 1, 3).reshape(2, 192, 384)
     near = jnp.where(first, weight, weight[::-1])
-    far = flip(near, "zh")
     hi = lax.reduce_precision(teacher_gain, 8, 7)
     mid = lax.reduce_precision(teacher_gain - hi, 8, 7)
     low = teacher_gain - hi - mid
     gain_rows = jnp.stack([hi, mid, low] + [jnp.zeros_like(hi)] * 13).astype(BF16)
     shard = tie(jnp.concatenate([teacher_in, gain_rows], axis=0), near)
-    own = spread(shard, "x")
+    own = jnp.broadcast_to(shard[None], (4,) + shard.shape)
+    own, near = lax.optimization_barrier((own, near))
+    own = swap(own, "x")
     far_block = flip(shard, "zl", 2)
 
+    far = flip(near, "zh")
     student_normed = (normalize(student_in.astype(F32)) * student_gain).astype(BF16)
     pre_act = jnp.dot(student_normed, up_weight, preferred_element_type=F32)
     gated, slope = gelu_parts(pre_act)

time: 229 us -> 231 us (level)
  starting transfers between devices: 58.1 us -> 64.7 us
  waiting for transfers between devices: 68.9 us -> 64 us
    ppermute x8, starting transfers between devices: 28.6 us -> 34.4 us  [flip(): lax.ppermute(values, axes, [(i, i ^ bits) for i in range(SIZES[axes])])]
    all_to_all x6, waiting for transfers between devices: 22.7 us -> 19.4 us  [swap(): return lax.all_to_all(values, axis, split_axis=0, concat_axis=0)]
    broadcast_in_dim x4 -> x3, local copies, waits for them, and re-layouts: 5.09 us -> 4.1 us  [spread(): jnp.broadcast_to(values[None], (SIZES[axis],) + values.shape)]
  transfers between devices with their start and end apart: 17 -> 17, of which waited for: 13 -> 13; matrix products, arithmetic and copies ran while one was open for 5% -> 5% of each run, Pallas kernels for 6% -> 5%
where the time goes in v14:
time: 231 us; the launch traced here: 230 us
  starting transfers between devices  64.7 us (28%)
  waiting for transfers between devices  64 us (28%)
  blocking collectives  51.1 us (22%)
  between operations  14.6 us (6%)
  Pallas kernels  12.7 us (5%)
  local copies, waits for them, and re-layouts  12.4 us (5%)
  other arithmetic  7.03 us (3%)
  matrix products  3.81 us (2%)
    ppermute x8, waiting for transfers between devices, flip(): lax.ppermute(values, axes, [(i, i ^ bits) for i in range(SIZES[axes])])  42 us
    all_to_all x1, blocking collectives, reduce_dp(): terms = lax.all_to_all(terms, ('zh', 'y'), split_axis=1, concat_axis=0)  35 us
    ppermute x8, starting transfers between devices, flip(): lax.ppermute(values, axes, [(i, i ^ bits) for i in range(SIZES[axes])])  34.4 us
    all_to_all x6, starting transfers between devices, swap(): return lax.all_to_all(values, axis, split_axis=0, concat_axis=0)  26.1 us
    all_to_all x6, waiting for transfers between devices, swap(): return lax.all_to_all(values, axis, split_axis=0, concat_axis=0)  19.4 us
    all_to_all x1, blocking collectives, swap(): return lax.all_to_all(values, axis, split_axis=0, concat_axis=0)  11.1 us
    pallas_call x1, Pallas kernels, shards(): pl.pallas_call(attention_kernel, out_shape=jax.ShapeDtypeStruct((2, 256,...  6.97 us
    pallas_call x1, Pallas kernels, shards(): pl.pallas_call(norm_kernel, out_shape=jax.ShapeDtypeStruct((256, 6144), B...  5.68 us
  transfers between devices with their start and end apart: 17, of which 13 were waited for; matrix products, arithmetic and copies ran while one was open for 5% of the time, Pallas kernels for 5%

profile of v14, /device:TPU:8, one launch (start us, length us, event | category | flops | bytes accessed | tf_op | source)
XLA Modules:
  0.0 230.3 jit_solution(16637295697864689422)
XLA Ops:
  9.2 6.1 %collective-permute-start.2 = (bf16[272,384]{1,0:T(8,128)(2,1)S(1)}, bf16[272,384]{1,0:T(8,128)(2,1)S(1)}, u32[]{:S(2)}, u32[]{:S(2)}) collective-permute-start(bf16[272,384]{1,0:T(8,128)(2,1)S(1)} %concatenate.17), channel_id=1, source_target_pairs={{0,8},{4,12},{8,0},{12,4},{1,9},{5,13},{9,1},{13,5},{2,10},{6,14},... | collective-permute-start | bytes 626696 | tf_op jit(solution)/shard_map/ppermute | solution.py:40
  16.2 9.1 %collective-permute-start = (bf16[2,192,384]{2,1,0:T(8,128)(2,1)S(1)}, bf16[2,192,384]{2,1,0:T(8,128)(2,1)S(1)}, u32[]{:S(2)}, u32[]{:S(2)}) collective-permute-start(bf16[2,192,384]{2,1,0:T(8,128)(2,1)S(1)} %reverse_select_fusion), channel_id=1, source_target_pairs={{0,256},{256,0},{1,257},{257,1},{2,258},{258,2},{3,259},{259,3},{4... | collective-permute-start | bytes 884744 | tf_op jit(solution)/shard_map/ppermute | solution.py:40
  25.4 4.3 %all-to-all-start = ((bf16[4,272,384]{2,1,0:T(8,128)(2,1)}), bf16[4,272,384]{2,1,0:T(8,128)(2,1)S(1)}, u32[]{:S(2)}, u32[]{:S(2)}) async-start(bf16[4,272,384]{2,1,0:T(8,128)(2,1)} %broadcast_in_dim.14), calls=%async_computation | async-start | bytes 1671168 | tf_op jit(solution)/shard_map/all_to_all | solution.py:48
  30.2 9.8 %collective-permute-done = bf16[2,192,384]{2,1,0:T(8,128)(2,1)S(1)} collective-permute-done((bf16[2,192,384]{2,1,0:T(8,128)(2,1)S(1)}, bf16[2,192,384]{2,1,0:T(8,128)(2,1)S(1)}, u32[]{:S(2)}, u32[]{:S(2)}) %collective-permute-start) | collective-permute-done | bytes 294944 | tf_op jit(solution)/shard_map/ppermute | solution.py:40
  47.5 4.3 %all-to-all-start.1 = ((bf16[4,272,640]{2,1,0:T(8,128)(2,1)}), bf16[4,272,640]{2,1,0:T(8,128)(2,1)S(1)}, u32[]{:S(2)}, u32[]{:S(2)}) async-start(bf16[4,272,640]{2,1,0:T(8,128)(2,1)} %fusion.1), calls=%async_computation.1 | async-start | bytes 2785280 | tf_op jit(solution)/shard_map/all_to_all | solution.py:48
  52.8 5.2 %collective-permute-start.3 = (bf16[2,272,384]{2,1,0:T(8,128)(2,1)S(1)}, bf16[2,272,384]{2,1,0:T(8,128)(2,1)}, u32[]{:S(2)}, u32[]{:S(2)}) collective-permute-start(bf16[2,272,384]{2,1,0:T(8,128)(2,1)S(1)} %pad_maximum_fusion.2), channel_id=1, source_target_pairs={{0,4},{4,0},{8,12},{12,8},{1,5},{5,1},{9,13},{13,9},{2,6},{6,2},{1... | collective-permute-start | bytes 1253384 | tf_op jit(solution)/shard_map/ppermute | solution.py:40
  58.1 9.8 %collective-permute-done.3 = bf16[2,272,384]{2,1,0:T(8,128)(2,1)} collective-permute-done((bf16[2,272,384]{2,1,0:T(8,128)(2,1)S(1)}, bf16[2,272,384]{2,1,0:T(8,128)(2,1)}, u32[]{:S(2)}, u32[]{:S(2)}) %collective-permute-start.3) | collective-permute-done | bytes 417824 | tf_op jit(solution)/shard_map/ppermute | solution.py:40
  67.8 3.1 %all-to-all-done.1.far_ref = bf16[4,272,640]{2,1,0:T(8,128)(2,1)S(1)} async-done(((bf16[4,272,640]{2,1,0:T(8,128)(2,1)}), bf16[4,272,640]{2,1,0:T(8,128)(2,1)S(1)}, u32[]{:S(2)}, u32[]{:S(2)}) %all-to-all-start.1) | async-done | bytes 1392672 | tf_op jit(solution)/shard_map/all_to_all | solution.py:48
  73.3 4.4 %all-to-all-start.2 = ((bf16[4,2,272,384]{3,2,1,0:T(8,128)(2,1)}), bf16[4,2,272,384]{3,2,1,0:T(8,128)(2,1)}, u32[]{:S(2)}, u32[]{:S(2)}) async-start(bf16[4,2,272,384]{3,2,1,0:T(8,128)(2,1)} %broadcast_in_dim.16), calls=%async_computation.2 | async-start | bytes 3342336 | tf_op jit(solution)/shard_map/all_to_all | solution.py:48
  77.8 5.2 %collective-permute-start.4 = (bf16[64,1024]{1,0:T(8,128)(2,1)S(1)}, bf16[64,1024]{1,0:T(8,128)(2,1)S(1)}, u32[]{:S(2)}, u32[]{:S(2)}) collective-permute-start(bf16[64,1024]{1,0:T(8,128)(2,1)S(1)} %bitcast.67), channel_id=1, source_target_pairs={{0,4},{4,0},{8,12},{12,8},{1,5},{5,1},{9,13},{13,9},{2,6},{6,2},{1... | collective-permute-start | bytes 393224 | tf_op jit(solution)/shard_map/ppermute | solution.py:40
  83.1 2.9 %collective-permute-done.4 = bf16[64,1024]{1,0:T(8,128)(2,1)S(1)} collective-permute-done((bf16[64,1024]{1,0:T(8,128)(2,1)S(1)}, bf16[64,1024]{1,0:T(8,128)(2,1)S(1)}, u32[]{:S(2)}, u32[]{:S(2)}) %collective-permute-start.4) | collective-permute-done | bytes 131104 | tf_op jit(solution)/shard_map/ppermute | solution.py:40
  88.0 7.6 %collective-permute-done.5 = bf16[64,1024]{1,0:T(8,128)(2,1)} collective-permute-done((bf16[64,1024]{1,0:T(8,128)(2,1)S(1)}, bf16[64,1024]{1,0:T(8,128)(2,1)}, u32[]{:S(2)}, u32[]{:S(2)}) %collective-permute-start.5) | collective-permute-done | bytes 131104 | tf_op jit(solution)/shard_map/ppermute | solution.py:40
  99.0 5.7 %teacher_norm.1.own_ref = bf16[256,6144]{1,0:T(8,128)(2,1)} custom-call(s32[2]{0:T(128)S(1)} %pad_add_fusion.place, bf16[4,272,384]{2,1,0:T(8,128)(2,1)S(1)} %all-to-all-done.own_ref, bf16[4,272,640]{2,1,0:T(8,128)(2,1)S(1)} %all-to-all-done.1.far_ref, bf16[4,2,272,384]{3,2,1,0:T(8,128)(2,1)} %all-to-all-done.2.late_ref), custom_call_target="tpu_custom_call" | custom-call | flops 1000 | bytes 1000 | tf_op jit(solution)/shard_map/teacher_norm/pallas_call | solution.py:217
  107.6 3.5 %all-to-all-start.3 = ((bf16[4,64,1024]{2,1,0:T(8,128)(2,1)}), bf16[4,64,1024]{2,1,0:T(8,128)(2,1)S(1)}, u32[]{:S(2)}, u32[]{:S(2)}) async-start(bf16[4,64,1024]{2,1,0:T(8,128)(2,1)} %broadcast_in_dim.17), calls=%async_computation.3 | async-start | bytes 1048576 | tf_op jit(solution)/shard_map/all_to_all | solution.py:48
  115.0 7.0 %teacher_heads.1 = f32[2,256,128]{2,1,0:T(8,128)S(1)} custom-call(s32[1]{0:T(128)} %bitcast.10.place, bf16[256,6144]{1,0:T(8,128)(2,1)} %teacher_norm.1.own_ref, bf16[256,6144]{1,0:T(8,128)(2,1)} %collective-permute-done.6.other_ref, bf16[6144,384]{1,0:T(8,128)(2,1)S(1)} %bitcast.57, f32[2,128]{1,0:T(2,128)S(1)} %copy-done.2), custom_call_target="tpu_custom_call" | custom-call | flops 2415919104 | bytes 11000000 | tf_op jit(solution)/shard_map/teacher_heads/pallas_call | solution.py:231
  126.4 6.0 %all-to-all-start.4 = ((f32[16,2,256]{2,1,0:T(2,128)}), f32[16,2,256]{2,1,0:T(2,128)S(1)}, u32[]{:S(2)}, u32[]{:S(2)}) async-start(f32[16,2,256]{2,1,0:T(2,128)} %broadcast_in_dim.18), calls=%async_computation.4 | async-start | bytes 65536 | tf_op jit(solution)/shard_map/all_to_all | solution.py:48
  132.7 7.8 %all-to-all-done.4 = f32[16,2,256]{2,1,0:T(2,128)S(1)} async-done(((f32[16,2,256]{2,1,0:T(2,128)}), f32[16,2,256]{2,1,0:T(2,128)S(1)}, u32[]{:S(2)}, u32[]{:S(2)}) %all-to-all-start.4) | async-done | bytes 32800 | tf_op jit(solution)/shard_map/all_to_all | solution.py:48
  141.0 11.1 %all_to_all.53 = bf16[4,64,1024]{2,1,0:T(8,128)(2,1)S(1)} all-to-all(bf16[4,64,1024]{2,1,0:T(8,128)(2,1)S(1)} %bitcast.59), channel_id=1, replica_groups=mesh['zh'=2,'y'=8,'c'=2,'zl'=4,'x'=4] {'x'}, dimensions={0} | all-to-all | bytes 1048576 | tf_op jit(solution)/shard_map/all_to_all | solution.py:48
  154.4 4.6 %collective-permute-done.8 = bf16[64,1024]{1,0:T(8,128)(2,1)S(1)} collective-permute-done((bf16[64,1024]{1,0:T(8,128)(2,1)S(1)}, bf16[64,1024]{1,0:T(8,128)(2,1)S(1)}, u32[]{:S(2)}, u32[]{:S(2)}) %collective-permute-start.8) | collective-permute-done | bytes 131104 | tf_op jit(solution)/shard_map/ppermute | solution.py:40
  161.7 6.4 %collective-permute-done.9 = bf16[64,1024]{1,0:T(8,128)(2,1)S(1)} collective-permute-done((bf16[64,1024]{1,0:T(8,128)(2,1)S(1)}, bf16[64,1024]{1,0:T(8,128)(2,1)S(1)}, u32[]{:S(2)}, u32[]{:S(2)}) %collective-permute-start.9) | collective-permute-done | bytes 131104 | tf_op jit(solution)/shard_map/ppermute | solution.py:40
  168.9 3.6 %all-to-all-start.6 = ((bf16[4,64,1024]{2,1,0:T(8,128)(2,1)}), bf16[4,64,1024]{2,1,0:T(8,128)(2,1)S(1)}, u32[]{:S(2)}, u32[]{:S(2)}) async-start(bf16[4,64,1024]{2,1,0:T(8,128)(2,1)} %broadcast_in_dim.19), calls=%async_computation.6 | async-start | bytes 1048576 | tf_op jit(solution)/shard_map/all_to_all | solution.py:48
  173.8 6.8 %all-to-all-done.6 = bf16[4,64,1024]{2,1,0:T(8,128)(2,1)S(1)} async-done(((bf16[4,64,1024]{2,1,0:T(8,128)(2,1)}), bf16[4,64,1024]{2,1,0:T(8,128)(2,1)S(1)}, u32[]{:S(2)}, u32[]{:S(2)}) %all-to-all-start.6) | async-done | bytes 524320 | tf_op jit(solution)/shard_map/all_to_all | solution.py:48
  182.2 5.0 %all_to_all.54 = bf16[1,3,16,2,32,256]{5,4,2,1,0,3:T(8,128)(2,1)S(1)} all-to-all(bf16[1,3,16,2,32,256]{5,4,2,1,0,3:T(8,128)(2,1)S(1)} %copy.48), channel_id=1, replica_groups=mesh['zh'=2,'y'=8,'c'=2,'zl'=4,'x'=4] {'c'}, dimensions={3} | all-to-all | bytes 3145728 | tf_op jit(solution)/shard_map/all_to_all | solution.py:158
  187.7 35.0 %all_to_all.55 = bf16[1,3,16,32,256]{4,3,1,0,2:T(8,128)(2,1)S(1)} all-to-all(bf16[1,3,16,32,256]{4,3,1,0,2:T(8,128)(2,1)S(1)} %copy.47), channel_id=1, replica_groups=mesh['zh'=2,'y'=8,'c'=2,'zl'=4,'x'=4] {'zh','y'}, dimensions={2} | all-to-all | bytes 1572864 | tf_op jit(solution)/shard_map/all_to_all | solution.py:160
  (107 shorter events, 41.3 us)
Async XLA Ops:
  7.2 35.2 %copy-start = (bf16[256,1024]{1,0:T(8,128)(2,1)S(1)}, bf16[256,1024]{1,0:T(8,128)(2,1)}, u32[]{:S(2)}) copy-start(bf16[256,1024]{1,0:T(8,128)(2,1)} %param.16) | copy-start | bytes 1572868
  9.0 20.7 %copy-start.3 = (bf16[256,1024]{1,0:T(8,128)(2,1)S(1)}, bf16[256,1024]{1,0:T(8,128)(2,1)}, u32[]{:S(2)}) copy-start(bf16[256,1024]{1,0:T(8,128)(2,1)} %param.13) | copy-start | bytes 1572868
  9.2 33.6 %collective-permute-start.2 = (bf16[272,384]{1,0:T(8,128)(2,1)S(1)}, bf16[272,384]{1,0:T(8,128)(2,1)S(1)}, u32[]{:S(2)}, u32[]{:S(2)}) collective-permute-start(bf16[272,384]{1,0:T(8,128)(2,1)S(1)} %concatenate.17), channel_id=1, source_target_pairs={{0,8},{4,12},{8,0},{12,4},{1,9},{5,13},{9,1},{13,5},{2,10},{6,14},... | collective-permute-start | bytes 626696 | tf_op jit(solution)/shard_map/ppermute | solution.py:40
  16.2 23.7 %collective-permute-start = (bf16[2,192,384]{2,1,0:T(8,128)(2,1)S(1)}, bf16[2,192,384]{2,1,0:T(8,128)(2,1)S(1)}, u32[]{:S(2)}, u32[]{:S(2)}) collective-permute-start(bf16[2,192,384]{2,1,0:T(8,128)(2,1)S(1)} %reverse_select_fusion), channel_id=1, source_target_pairs={{0,256},{256,0},{1,257},{257,1},{2,258},{258,2},{3,259},{259,3},{4... | collective-permute-start | bytes 884744 | tf_op jit(solution)/shard_map/ppermute | solution.py:40
  25.4 18.3 %all-to-all-start = ((bf16[4,272,384]{2,1,0:T(8,128)(2,1)}), bf16[4,272,384]{2,1,0:T(8,128)(2,1)S(1)}, u32[]{:S(2)}, u32[]{:S(2)}) async-start(bf16[4,272,384]{2,1,0:T(8,128)(2,1)} %broadcast_in_dim.14), calls=%async_computation | async-start | bytes 1671168 | tf_op jit(solution)/shard_map/all_to_all | solution.py:48
  29.7 12.3 %copy-start.13 = (f32[1024]{0:T(1024)S(1)}, f32[1024]{0:T(1024)}, u32[]{:S(2)}) copy-start(f32[1024]{0:T(1024)} %param.14) | copy-start | bytes 12292
  29.7 83.0 %all-gather.3.cloned.1.call-start = ((), (), s32[]{:S(2)}) async-start(), calls=%async_computation.9 | async-start | bytes 5308416 | tf_op jit(solution)/shard_map/all_gather | solution.py:205
  29.7 12.3 %copy-start.12 = (bf16[1024,256]{1,0:T(8,128)(2,1)S(1)}, bf16[1024,256]{1,0:T(8,128)(2,1)}, u32[]{:S(2)}) copy-start(bf16[1024,256]{1,0:T(8,128)(2,1)} %param.15) | copy-start | bytes 1572868
  40.1 3.6 %collective-permute-start.1 = (bf16[2,192,384]{2,1,0:T(8,128)(2,1)S(1)}, bf16[2,192,384]{2,1,0:T(8,128)(2,1)}, u32[]{:S(2)}, u32[]{:S(2)}) collective-permute-start(bf16[2,192,384]{2,1,0:T(8,128)(2,1)S(1)} %pad_maximum_fusion.3), channel_id=1, source_target_pairs={{0,16},{16,0},{1,17},{17,1},{2,18},{18,2},{3,19},{19,3},{4,20},{20... | collective-permute-start | bytes 884744 | tf_op jit(solution)/shard_map/ppermute | solution.py:40
  47.5 23.4 %all-to-all-start.1 = ((bf16[4,272,640]{2,1,0:T(8,128)(2,1)}), bf16[4,272,640]{2,1,0:T(8,128)(2,1)S(1)}, u32[]{:S(2)}, u32[]{:S(2)}) async-start(bf16[4,272,640]{2,1,0:T(8,128)(2,1)} %fusion.1), calls=%async_computation.1 | async-start | bytes 2785280 | tf_op jit(solution)/shard_map/all_to_all | solution.py:48
  52.8 15.0 %collective-permute-start.3 = (bf16[2,272,384]{2,1,0:T(8,128)(2,1)S(1)}, bf16[2,272,384]{2,1,0:T(8,128)(2,1)}, u32[]{:S(2)}, u32[]{:S(2)}) collective-permute-start(bf16[2,272,384]{2,1,0:T(8,128)(2,1)S(1)} %pad_maximum_fusion.2), channel_id=1, source_target_pairs={{0,4},{4,0},{8,12},{12,8},{1,5},{5,1},{9,13},{13,9},{2,6},{6,2},{1... | collective-permute-start | bytes 1253384 | tf_op jit(solution)/shard_map/ppermute | solution.py:40
  73.3 25.7 %all-to-all-start.2 = ((bf16[4,2,272,384]{3,2,1,0:T(8,128)(2,1)}), bf16[4,2,272,384]{3,2,1,0:T(8,128)(2,1)}, u32[]{:S(2)}, u32[]{:S(2)}) async-start(bf16[4,2,272,384]{3,2,1,0:T(8,128)(2,1)} %broadcast_in_dim.16), calls=%async_computation.2 | async-start | bytes 3342336 | tf_op jit(solution)/shard_map/all_to_all | solution.py:48
  77.8 8.2 %collective-permute-start.4 = (bf16[64,1024]{1,0:T(8,128)(2,1)S(1)}, bf16[64,1024]{1,0:T(8,128)(2,1)S(1)}, u32[]{:S(2)}, u32[]{:S(2)}) collective-permute-start(bf16[64,1024]{1,0:T(8,128)(2,1)S(1)} %bitcast.67), channel_id=1, source_target_pairs={{0,4},{4,0},{8,12},{12,8},{1,5},{5,1},{9,13},{13,9},{2,6},{6,2},{1... | collective-permute-start | bytes 393224 | tf_op jit(solution)/shard_map/ppermute | solution.py:40
  86.0 9.6 %collective-permute-start.5 = (bf16[64,1024]{1,0:T(8,128)(2,1)S(1)}, bf16[64,1024]{1,0:T(8,128)(2,1)}, u32[]{:S(2)}, u32[]{:S(2)}) collective-permute-start(bf16[64,1024]{1,0:T(8,128)(2,1)S(1)} %add_convert_fusion.3), channel_id=1, source_target_pairs={{0,8},{4,12},{8,0},{12,4},{1,9},{5,13},{9,1},{13,5},{2,10},{6,14},... | collective-permute-start | bytes 393224 | tf_op jit(solution)/shard_map/ppermute | solution.py:40
  97.3 9.4 %copy-start.8 = (bf16[64,1024]{1,0:T(8,128)(2,1)S(1)}, bf16[64,1024]{1,0:T(8,128)(2,1)}, u32[]{:S(2)}) copy-start(bf16[64,1024]{1,0:T(8,128)(2,1)} %add_convert_fusion.2) | copy-start | bytes 393220
  104.7 8.0 %collective-permute-start.6 = (bf16[256,6144]{1,0:T(8,128)(2,1)}, bf16[256,6144]{1,0:T(8,128)(2,1)}, u32[]{:S(2)}, u32[]{:S(2)}) collective-permute-start(bf16[256,6144]{1,0:T(8,128)(2,1)} %teacher_norm.1.own_ref), channel_id=1, source_target_pairs={{0,16},{16,0},{1,17},{17,1},{2,18},{18,2},{3,19},{19,3},{4,20},{20... | collective-permute-start | bytes 9437192 | tf_op jit(solution)/shard_map/ppermute | solution.py:36
  107.6 16.6 %all-to-all-start.3 = ((bf16[4,64,1024]{2,1,0:T(8,128)(2,1)}), bf16[4,64,1024]{2,1,0:T(8,128)(2,1)S(1)}, u32[]{:S(2)}, u32[]{:S(2)}) async-start(bf16[4,64,1024]{2,1,0:T(8,128)(2,1)} %broadcast_in_dim.17), calls=%async_computation.3 | async-start | bytes 1048576 | tf_op jit(solution)/shard_map/all_to_all | solution.py:48
  122.0 10.4 %copy-start.4 = (bf16[1024,256]{1,0:T(8,128)(2,1)S(1)}, bf16[1024,256]{1,0:T(8,128)(2,1)}, u32[]{:S(2)}) copy-start(bf16[1024,256]{1,0:T(8,128)(2,1)} %param.17) | copy-start | bytes 1572868
  122.0 3.4 %collective-permute-start.7 = (f32[256,128]{1,0:T(8,128)S(1)}, f32[256,128]{1,0:T(8,128)S(1)}, u32[]{:S(2)}, u32[]{:S(2)}) collective-permute-start(f32[256,128]{1,0:T(8,128)S(1)} %get-tuple-element.33), channel_id=1, source_target_pairs={{0,16},{16,0},{1,17},{17,1},{2,18},{18,2},{3,19},{19,3},{4,20},{20... | collective-permute-start | bytes 393224 | tf_op jit(solution)/shard_map/ppermute | solution.py:36
  126.4 14.2 %all-to-all-start.4 = ((f32[16,2,256]{2,1,0:T(2,128)}), f32[16,2,256]{2,1,0:T(2,128)S(1)}, u32[]{:S(2)}, u32[]{:S(2)}) async-start(f32[16,2,256]{2,1,0:T(2,128)} %broadcast_in_dim.18), calls=%async_computation.4 | async-start | bytes 65536 | tf_op jit(solution)/shard_map/all_to_all | solution.py:48
  152.2 6.9 %collective-permute-start.8 = (bf16[64,1024]{1,0:T(8,128)(2,1)S(1)}, bf16[64,1024]{1,0:T(8,128)(2,1)S(1)}, u32[]{:S(2)}, u32[]{:S(2)}) collective-permute-start(bf16[64,1024]{1,0:T(8,128)(2,1)S(1)} %reduce_sum.119), channel_id=1, source_target_pairs={{0,4},{4,0},{8,12},{12,8},{1,5},{5,1},{9,13},{13,9},{2,6},{6,2},{1... | collective-permute-start | bytes 393224 | tf_op jit(solution)/shard_map/ppermute | solution.py:40
  159.1 9.0 %collective-permute-start.9 = (bf16[64,1024]{1,0:T(8,128)(2,1)S(1)}, bf16[64,1024]{1,0:T(8,128)(2,1)S(1)}, u32[]{:S(2)}, u32[]{:S(2)}) collective-permute-start(bf16[64,1024]{1,0:T(8,128)(2,1)S(1)} %add_convert_fusion.1), channel_id=1, source_target_pairs={{0,8},{4,12},{8,0},{12,4},{1,9},{5,13},{9,1},{13,5},{2,10},{6,14},... | collective-permute-start | bytes 393224 | tf_op jit(solution)/shard_map/ppermute | solution.py:40
  168.9 11.7 %copy-start.6 = (f32[256,256]{1,0:T(8,128)S(1)}, f32[256,256]{1,0:T(8,128)}, u32[]{:S(2)}) copy-start(f32[256,256]{1,0:T(8,128)} %copy-done.5) | copy-start | bytes 786436
  168.9 11.7 %all-to-all-start.6 = ((bf16[4,64,1024]{2,1,0:T(8,128)(2,1)}), bf16[4,64,1024]{2,1,0:T(8,128)(2,1)S(1)}, u32[]{:S(2)}, u32[]{:S(2)}) async-start(bf16[4,64,1024]{2,1,0:T(8,128)(2,1)} %broadcast_in_dim.19), calls=%async_computation.6 | async-start | bytes 1048576 | tf_op jit(solution)/shard_map/all_to_all | solution.py:48
  (7 other events, 20.8 us)
Sparse Core Ops, SparseCore 0:
  45.9 60.3 all-gather.2

commit v15 on v14

--- a/solution.py
+++ b/solution.py
@@ -59,6 +59,24 @@
 def mp_scatter_x(term):
     rows, cols = term.shape
     return sum_parts(swap(term.reshape(4, rows // 4, cols), "x")).astype(BF16)
+
+
+def copies_kernel(in_ref, out_ref):
+    for i in range(4):
+        out_ref[i] = in_ref[...]
+
+
+def four_copies(values):
+    vmem = pl.BlockSpec(memory_space=pltpu.VMEM)
+    return pl.pallas_call(
+        copies_kernel,
+        out_shape=jax.ShapeDtypeStruct((4,) + values.shape, values.dtype),
+        in_specs=[vmem],
+        out_specs=vmem,
+        compiler_params=pltpu.CompilerParams(vmem_limit_bytes=16 * 1024 * 1024),
+        cost_estimate=pl.CostEstimate(flops=0, bytes_accessed=3_000_000, transcendentals=0),
+        name="four_copies",
+    )(values)
 
 
 def spread_and_scatter_x(block, term):
@@ -177,17 +195,15 @@
     first = lax.axis_index("c") == 0
     weight = qkv_weight.reshape(192, 3, 2, 128).transpose(2, 0, 1, 3).reshape(2, 192, 384)
     near = jnp.where(first, weight, weight[::-1])
+    far = flip(near, "zh")
     hi = lax.reduce_precision(teacher_gain, 8, 7)
     mid = lax.reduce_precision(teacher_gain - hi, 8, 7)
     low = teacher_gain - hi - mid
     gain_rows = jnp.stack([hi, mid, low] + [jnp.zeros_like(hi)] * 13).astype(BF16)
     shard = tie(jnp.concatenate([teacher_in, gain_rows], axis=0), near)
-    own = jnp.broadcast_to(shard[None], (4,) + shard.shape)
-    own, near = lax.optimization_barrier((own, near))
-    own = swap(own, "x")
+    own = spread(shard, "x")
     far_block = flip(shard, "zl", 2)
 
-    far = flip(near, "zh")
     student_normed = (normalize(student_in.astype(F32)) * student_gain).astype(BF16)
     pre_act = jnp.dot(student_normed, up_weight, preferred_element_type=F32)
     gated, slope = gelu_parts(pre_act)
@@ -206,7 +222,7 @@
 
     late = flip(jnp.stack([shard, far_block]), "zl", 1)
     far_block, part = spread_and_scatter_x(far_block, mlp_term)
-    late = spread(tie(late, far_block), "x")
+    late = swap(tie(four_copies(late), far_block), "x")
     late, part = lax.optimization_barrier((late, mp_sum_zl(part)))
 
     place_z = jnp.stack([lax.axis_index("zl"), lax.axis_index("zh")])

time: 231 us -> 226 us (0.978)
  starting transfers between devices: 64.7 us -> 57.9 us
  waiting for transfers between devices: 64 us -> 67.8 us
    ppermute x8, starting transfers between devices: 34.4 us -> 28.6 us  [flip(): lax.ppermute(values, axes, [(i, i ^ bits) for i in range(SIZES[axes])])]
  transfers between devices with their start and end apart: 17 -> 17, of which waited for: 13 -> 13; matrix products, arithmetic and copies ran while one was open for 5% -> 4% of each run, Pallas kernels for 5% -> 6%
where the time goes in v15:
time: 226 us; the launch traced here: 225 us
  waiting for transfers between devices  67.8 us (30%)
  starting transfers between devices  57.9 us (26%)
  blocking collectives  49.6 us (22%)
  between operations  14.6 us (6%)
  Pallas kernels  12.8 us (6%)
  local copies, waits for them, and re-layouts  11.3 us (5%)
  other arithmetic  7.02 us (3%)
  matrix products  3.81 us (2%)
    ppermute x8, waiting for transfers between devices, flip(): lax.ppermute(values, axes, [(i, i ^ bits) for i in range(SIZES[axes])])  43.5 us
    all_to_all x1, blocking collectives, reduce_dp(): terms = lax.all_to_all(terms, ('zh', 'y'), split_axis=1, concat_axis=0)  33.5 us
    ppermute x8, starting transfers between devices, flip(): lax.ppermute(values, axes, [(i, i ^ bits) for i in range(SIZES[axes])])  28.6 us
    all_to_all x6, starting transfers between devices, swap(): return lax.all_to_all(values, axis, split_axis=0, concat_axis=0)  25.1 us
    all_to_all x6, waiting for transfers between devices, swap(): return lax.all_to_all(values, axis, split_axis=0, concat_axis=0)  21.7 us
    all_to_all x1, blocking collectives, swap(): return lax.all_to_all(values, axis, split_axis=0, concat_axis=0)  11.1 us
    pallas_call x1, Pallas kernels, shards(): pl.pallas_call(attention_kernel, out_shape=jax.ShapeDtypeStruct((2, 256,...  6.97 us
    pallas_call x1, Pallas kernels, shards(): pl.pallas_call(norm_kernel, out_shape=jax.ShapeDtypeStruct((256, 6144), B...  5.67 us
  transfers between devices with their start and end apart: 17, of which 13 were waited for; matrix products, arithmetic and copies ran while one was open for 4% of the time, Pallas kernels for 6%

profile of v15, /device:TPU:8, one launch (start us, length us, event | category | flops | bytes accessed | tf_op | source)
XLA Modules:
  0.0 224.7 jit_solution(8870479495223821974)
XLA Ops:
  8.9 10.9 %collective-permute-start = (bf16[2,192,384]{2,1,0:T(8,128)(2,1)S(1)}, bf16[2,192,384]{2,1,0:T(8,128)(2,1)S(1)}, u32[]{:S(2)}, u32[]{:S(2)}) collective-permute-start(bf16[2,192,384]{2,1,0:T(8,128)(2,1)S(1)} %reverse_select_fusion), channel_id=1, source_target_pairs={{0,256},{256,0},{1,257},{257,1},{2,258},{258,2},{3,259},{259,3},{4... | collective-permute-start | bytes 884744 | tf_op jit(solution)/shard_map/ppermute | solution.py:40
  20.1 4.3 %collective-permute-start.2 = (bf16[272,384]{1,0:T(8,128)(2,1)S(1)}, bf16[272,384]{1,0:T(8,128)(2,1)S(1)}, u32[]{:S(2)}, u32[]{:S(2)}) collective-permute-start(bf16[272,384]{1,0:T(8,128)(2,1)S(1)} %concatenate.17), channel_id=1, source_target_pairs={{0,8},{4,12},{8,0},{12,4},{1,9},{5,13},{9,1},{13,5},{2,10},{6,14},... | collective-permute-start | bytes 626696 | tf_op jit(solution)/shard_map/ppermute | solution.py:40
  25.4 4.3 %all-to-all-start = ((bf16[4,272,384]{2,1,0:T(8,128)(2,1)}), bf16[4,272,384]{2,1,0:T(8,128)(2,1)S(1)}, u32[]{:S(2)}, u32[]{:S(2)}) async-start(bf16[4,272,384]{2,1,0:T(8,128)(2,1)} %broadcast_in_dim.12), calls=%async_computation | async-start | bytes 1671168 | tf_op jit(solution)/shard_map/all_to_all | solution.py:48
  30.2 3.3 %collective-permute-done = bf16[2,192,384]{2,1,0:T(8,128)(2,1)S(1)} collective-permute-done((bf16[2,192,384]{2,1,0:T(8,128)(2,1)S(1)}, bf16[2,192,384]{2,1,0:T(8,128)(2,1)S(1)}, u32[]{:S(2)}, u32[]{:S(2)}) %collective-permute-start) | collective-permute-done | bytes 294944 | tf_op jit(solution)/shard_map/ppermute | solution.py:40
  36.2 7.0 %collective-permute-done.2 = bf16[272,384]{1,0:T(8,128)(2,1)S(1)} collective-permute-done((bf16[272,384]{1,0:T(8,128)(2,1)S(1)}, bf16[272,384]{1,0:T(8,128)(2,1)S(1)}, u32[]{:S(2)}, u32[]{:S(2)}) %collective-permute-start.2) | collective-permute-done | bytes 208928 | tf_op jit(solution)/shard_map/ppermute | solution.py:40
  47.2 4.3 %all-to-all-start.1 = ((bf16[4,272,640]{2,1,0:T(8,128)(2,1)}), bf16[4,272,640]{2,1,0:T(8,128)(2,1)S(1)}, u32[]{:S(2)}, u32[]{:S(2)}) async-start(bf16[4,272,640]{2,1,0:T(8,128)(2,1)} %fusion.1), calls=%async_computation.1 | async-start | bytes 2785280 | tf_op jit(solution)/shard_map/all_to_all | solution.py:48
  54.4 11.2 %collective-permute-done.3.in_ref = bf16[2,272,384]{2,1,0:T(8,128)(2,1)S(1)} collective-permute-done((bf16[2,272,384]{2,1,0:T(8,128)(2,1)S(1)}, bf16[2,272,384]{2,1,0:T(8,128)(2,1)S(1)}, u32[]{:S(2)}, u32[]{:S(2)}) %collective-permute-start.3) | collective-permute-done | bytes 417824 | tf_op jit(solution)/shard_map/ppermute | solution.py:40
  67.0 3.4 %all-to-all-done.1.far_ref = bf16[4,272,640]{2,1,0:T(8,128)(2,1)S(1)} async-done(((bf16[4,272,640]{2,1,0:T(8,128)(2,1)}), bf16[4,272,640]{2,1,0:T(8,128)(2,1)S(1)}, u32[]{:S(2)}, u32[]{:S(2)}) %all-to-all-start.1) | async-done | bytes 1392672 | tf_op jit(solution)/shard_map/all_to_all | solution.py:48
  70.5 4.4 %all-to-all-start.2 = ((bf16[4,2,272,384]{3,2,1,0:T(8,128)(2,1)}), bf16[4,2,272,384]{3,2,1,0:T(8,128)(2,1)}, u32[]{:S(2)}, u32[]{:S(2)}) async-start(bf16[4,2,272,384]{3,2,1,0:T(8,128)(2,1)} %copy-done.1), calls=%async_computation.2 | async-start | bytes 3342336 | tf_op jit(solution)/shard_map/all_to_all | solution.py:48
  76.9 4.9 %collective-permute-done.4 = bf16[64,1024]{1,0:T(8,128)(2,1)S(1)} collective-permute-done((bf16[64,1024]{1,0:T(8,128)(2,1)S(1)}, bf16[64,1024]{1,0:T(8,128)(2,1)S(1)}, u32[]{:S(2)}, u32[]{:S(2)}) %collective-permute-start.4) | collective-permute-done | bytes 131104 | tf_op jit(solution)/shard_map/ppermute | solution.py:40
  84.8 6.1 %collective-permute-done.5 = bf16[64,1024]{1,0:T(8,128)(2,1)} collective-permute-done((bf16[64,1024]{1,0:T(8,128)(2,1)S(1)}, bf16[64,1024]{1,0:T(8,128)(2,1)}, u32[]{:S(2)}, u32[]{:S(2)}) %collective-permute-start.5) | collective-permute-done | bytes 131104 | tf_op jit(solution)/shard_map/ppermute | solution.py:40
  92.4 3.6 %all-to-all-done.2.late_ref = bf16[4,2,272,384]{3,2,1,0:T(8,128)(2,1)} async-done(((bf16[4,2,272,384]{3,2,1,0:T(8,128)(2,1)}), bf16[4,2,272,384]{3,2,1,0:T(8,128)(2,1)}, u32[]{:S(2)}, u32[]{:S(2)}) %all-to-all-start.2) | async-done | bytes 1671200 | tf_op jit(solution)/shard_map/all_to_all | solution.py:48
  96.0 5.7 %teacher_norm.1.own_ref = bf16[256,6144]{1,0:T(8,128)(2,1)} custom-call(s32[2]{0:T(128)S(1)} %pad_add_fusion.place, bf16[4,272,384]{2,1,0:T(8,128)(2,1)S(1)} %all-to-all-done.own_ref, bf16[4,272,640]{2,1,0:T(8,128)(2,1)S(1)} %all-to-all-done.1.far_ref, bf16[4,2,272,384]{3,2,1,0:T(8,128)(2,1)} %all-to-all-done.2.late_ref), custom_call_target="tpu_custom_call" | custom-call | flops 1000 | bytes 1000 | tf_op jit(solution)/shard_map/teacher_norm/pallas_call | solution.py:233
  104.6 3.5 %all-to-all-start.3 = ((bf16[4,64,1024]{2,1,0:T(8,128)(2,1)}), bf16[4,64,1024]{2,1,0:T(8,128)(2,1)S(1)}, u32[]{:S(2)}, u32[]{:S(2)}) async-start(bf16[4,64,1024]{2,1,0:T(8,128)(2,1)} %broadcast_in_dim.14), calls=%async_computation.3 | async-start | bytes 1048576 | tf_op jit(solution)/shard_map/all_to_all | solution.py:48
  112.0 7.0 %teacher_heads.1 = f32[2,256,128]{2,1,0:T(8,128)S(1)} custom-call(s32[1]{0:T(128)} %bitcast.10.place, bf16[256,6144]{1,0:T(8,128)(2,1)} %teacher_norm.1.own_ref, bf16[256,6144]{1,0:T(8,128)(2,1)} %collective-permute-done.6.other_ref, bf16[6144,384]{1,0:T(8,128)(2,1)S(1)} %bitcast.57, f32[2,128]{1,0:T(2,128)S(1)} %copy-done.3), custom_call_target="tpu_custom_call" | custom-call | flops 2415919104 | bytes 11000000 | tf_op jit(solution)/shard_map/teacher_heads/pallas_call | solution.py:247
  123.4 5.0 %all-to-all-start.4 = ((f32[16,2,256]{2,1,0:T(2,128)}), f32[16,2,256]{2,1,0:T(2,128)S(1)}, u32[]{:S(2)}, u32[]{:S(2)}) async-start(f32[16,2,256]{2,1,0:T(2,128)} %broadcast_in_dim.15), calls=%async_computation.4 | async-start | bytes 65536 | tf_op jit(solution)/shard_map/all_to_all | solution.py:48
  128.7 7.8 %all-to-all-done.4 = f32[16,2,256]{2,1,0:T(2,128)S(1)} async-done(((f32[16,2,256]{2,1,0:T(2,128)}), f32[16,2,256]{2,1,0:T(2,128)S(1)}, u32[]{:S(2)}, u32[]{:S(2)}) %all-to-all-start.4) | async-done | bytes 32800 | tf_op jit(solution)/shard_map/all_to_all | solution.py:48
  137.0 11.1 %all_to_all.53 = bf16[4,64,1024]{2,1,0:T(8,128)(2,1)S(1)} all-to-all(bf16[4,64,1024]{2,1,0:T(8,128)(2,1)S(1)} %bitcast.59), channel_id=1, replica_groups=mesh['zh'=2,'y'=8,'c'=2,'zl'=4,'x'=4] {'x'}, dimensions={0} | all-to-all | bytes 1048576 | tf_op jit(solution)/shard_map/all_to_all | solution.py:48
  150.5 4.6 %collective-permute-done.8 = bf16[64,1024]{1,0:T(8,128)(2,1)S(1)} collective-permute-done((bf16[64,1024]{1,0:T(8,128)(2,1)S(1)}, bf16[64,1024]{1,0:T(8,128)(2,1)S(1)}, u32[]{:S(2)}, u32[]{:S(2)}) %collective-permute-start.8) | collective-permute-done | bytes 131104 | tf_op jit(solution)/shard_map/ppermute | solution.py:40
  157.7 6.4 %collective-permute-done.9 = bf16[64,1024]{1,0:T(8,128)(2,1)S(1)} collective-permute-done((bf16[64,1024]{1,0:T(8,128)(2,1)S(1)}, bf16[64,1024]{1,0:T(8,128)(2,1)S(1)}, u32[]{:S(2)}, u32[]{:S(2)}) %collective-permute-start.9) | collective-permute-done | bytes 131104 | tf_op jit(solution)/shard_map/ppermute | solution.py:40
  164.9 3.6 %all-to-all-start.6 = ((bf16[4,64,1024]{2,1,0:T(8,128)(2,1)}), bf16[4,64,1024]{2,1,0:T(8,128)(2,1)S(1)}, u32[]{:S(2)}, u32[]{:S(2)}) async-start(bf16[4,64,1024]{2,1,0:T(8,128)(2,1)} %broadcast_in_dim.16), calls=%async_computation.6 | async-start | bytes 1048576 | tf_op jit(solution)/shard_map/all_to_all | solution.py:48
  169.8 6.8 %all-to-all-done.6 = bf16[4,64,1024]{2,1,0:T(8,128)(2,1)S(1)} async-done(((bf16[4,64,1024]{2,1,0:T(8,128)(2,1)}), bf16[4,64,1024]{2,1,0:T(8,128)(2,1)S(1)}, u32[]{:S(2)}, u32[]{:S(2)}) %all-to-all-start.6) | async-done | bytes 524320 | tf_op jit(solution)/shard_map/all_to_all | solution.py:48
  178.2 5.0 %all_to_all.54 = bf16[1,3,16,2,32,256]{5,4,2,1,0,3:T(8,128)(2,1)S(1)} all-to-all(bf16[1,3,16,2,32,256]{5,4,2,1,0,3:T(8,128)(2,1)S(1)} %copy.48), channel_id=1, replica_groups=mesh['zh'=2,'y'=8,'c'=2,'zl'=4,'x'=4] {'c'}, dimensions={3} | all-to-all | bytes 3145728 | tf_op jit(solution)/shard_map/all_to_all | solution.py:176
  183.7 33.5 %all_to_all.55 = bf16[1,3,16,32,256]{4,3,1,0,2:T(8,128)(2,1)S(1)} all-to-all(bf16[1,3,16,32,256]{4,3,1,0,2:T(8,128)(2,1)S(1)} %copy.47), channel_id=1, replica_groups=mesh['zh'=2,'y'=8,'c'=2,'zl'=4,'x'=4] {'zh','y'}, dimensions={2} | all-to-all | bytes 1572864 | tf_op jit(solution)/shard_map/all_to_all | solution.py:178
  (109 shorter events, 42.5 us)
Async XLA Ops:
  7.2 28.7 %copy-start = (bf16[256,1024]{1,0:T(8,128)(2,1)S(1)}, bf16[256,1024]{1,0:T(8,128)(2,1)}, u32[]{:S(2)}) copy-start(bf16[256,1024]{1,0:T(8,128)(2,1)} %param.16) | copy-start | bytes 1572868
  7.2 12.6 %copy-start.12 = (f32[384]{0:T(512)S(1)}, f32[384]{0:T(512)}, u32[]{:S(2)}) copy-start(f32[384]{0:T(512)} %param.10) | copy-start | bytes 4612
  7.2 12.7 %copy-start.11 = (bf16[256,384]{1,0:T(8,128)(2,1)S(1)}, bf16[256,384]{1,0:T(8,128)(2,1)}, u32[]{:S(2)}) copy-start(bf16[256,384]{1,0:T(8,128)(2,1)} %param.9) | copy-start | bytes 589828
  8.9 24.6 %collective-permute-start = (bf16[2,192,384]{2,1,0:T(8,128)(2,1)S(1)}, bf16[2,192,384]{2,1,0:T(8,128)(2,1)S(1)}, u32[]{:S(2)}, u32[]{:S(2)}) collective-permute-start(bf16[2,192,384]{2,1,0:T(8,128)(2,1)S(1)} %reverse_select_fusion), channel_id=1, source_target_pairs={{0,256},{256,0},{1,257},{257,1},{2,258},{258,2},{3,259},{259,3},{4... | collective-permute-start | bytes 884744 | tf_op jit(solution)/shard_map/ppermute | solution.py:40
  19.9 9.8 %copy-start.4 = (bf16[256,1024]{1,0:T(8,128)(2,1)S(1)}, bf16[256,1024]{1,0:T(8,128)(2,1)}, u32[]{:S(2)}) copy-start(bf16[256,1024]{1,0:T(8,128)(2,1)} %param.13) | copy-start | bytes 1572868
  20.1 23.2 %collective-permute-start.2 = (bf16[272,384]{1,0:T(8,128)(2,1)S(1)}, bf16[272,384]{1,0:T(8,128)(2,1)S(1)}, u32[]{:S(2)}, u32[]{:S(2)}) collective-permute-start(bf16[272,384]{1,0:T(8,128)(2,1)S(1)} %concatenate.17), channel_id=1, source_target_pairs={{0,8},{4,12},{8,0},{12,4},{1,9},{5,13},{9,1},{13,5},{2,10},{6,14},... | collective-permute-start | bytes 626696 | tf_op jit(solution)/shard_map/ppermute | solution.py:40
  25.4 17.9 %all-to-all-start = ((bf16[4,272,384]{2,1,0:T(8,128)(2,1)}), bf16[4,272,384]{2,1,0:T(8,128)(2,1)S(1)}, u32[]{:S(2)}, u32[]{:S(2)}) async-start(bf16[4,272,384]{2,1,0:T(8,128)(2,1)} %broadcast_in_dim.12), calls=%async_computation | async-start | bytes 1671168 | tf_op jit(solution)/shard_map/all_to_all | solution.py:48
  29.7 80.0 %all-gather.3.cloned.1.call-start = ((), (), s32[]{:S(2)}) async-start(), calls=%async_computation.9 | async-start | bytes 5308416 | tf_op jit(solution)/shard_map/all_gather | solution.py:221
  33.6 9.7 %collective-permute-start.1 = (bf16[2,192,384]{2,1,0:T(8,128)(2,1)S(1)}, bf16[2,192,384]{2,1,0:T(8,128)(2,1)}, u32[]{:S(2)}, u32[]{:S(2)}) collective-permute-start(bf16[2,192,384]{2,1,0:T(8,128)(2,1)S(1)} %pad_maximum_fusion.3), channel_id=1, source_target_pairs={{0,16},{16,0},{1,17},{17,1},{2,18},{18,2},{3,19},{19,3},{4,20},{20... | collective-permute-start | bytes 884744 | tf_op jit(solution)/shard_map/ppermute | solution.py:40
  47.2 23.3 %all-to-all-start.1 = ((bf16[4,272,640]{2,1,0:T(8,128)(2,1)}), bf16[4,272,640]{2,1,0:T(8,128)(2,1)S(1)}, u32[]{:S(2)}, u32[]{:S(2)}) async-start(bf16[4,272,640]{2,1,0:T(8,128)(2,1)} %fusion.1), calls=%async_computation.1 | async-start | bytes 2785280 | tf_op jit(solution)/shard_map/all_to_all | solution.py:48
  52.5 13.2 %collective-permute-start.3 = (bf16[2,272,384]{2,1,0:T(8,128)(2,1)S(1)}, bf16[2,272,384]{2,1,0:T(8,128)(2,1)S(1)}, u32[]{:S(2)}, u32[]{:S(2)}) collective-permute-start(bf16[2,272,384]{2,1,0:T(8,128)(2,1)S(1)} %pad_maximum_fusion.2), channel_id=1, source_target_pairs={{0,4},{4,0},{8,12},{12,8},{1,5},{5,1},{9,13},{13,9},{2,6},{6,2},{1... | collective-permute-start | bytes 1253384 | tf_op jit(solution)/shard_map/ppermute | solution.py:40
  70.5 25.5 %all-to-all-start.2 = ((bf16[4,2,272,384]{3,2,1,0:T(8,128)(2,1)}), bf16[4,2,272,384]{3,2,1,0:T(8,128)(2,1)}, u32[]{:S(2)}, u32[]{:S(2)}) async-start(bf16[4,2,272,384]{3,2,1,0:T(8,128)(2,1)} %copy-done.1), calls=%async_computation.2 | async-start | bytes 3342336 | tf_op jit(solution)/shard_map/all_to_all | solution.py:48
  75.0 6.9 %collective-permute-start.4 = (bf16[64,1024]{1,0:T(8,128)(2,1)S(1)}, bf16[64,1024]{1,0:T(8,128)(2,1)S(1)}, u32[]{:S(2)}, u32[]{:S(2)}) collective-permute-start(bf16[64,1024]{1,0:T(8,128)(2,1)S(1)} %bitcast.67), channel_id=1, source_target_pairs={{0,4},{4,0},{8,12},{12,8},{1,5},{5,1},{9,13},{13,9},{2,6},{6,2},{1... | collective-permute-start | bytes 393224 | tf_op jit(solution)/shard_map/ppermute | solution.py:40
  81.9 8.9 %collective-permute-start.5 = (bf16[64,1024]{1,0:T(8,128)(2,1)S(1)}, bf16[64,1024]{1,0:T(8,128)(2,1)}, u32[]{:S(2)}, u32[]{:S(2)}) collective-permute-start(bf16[64,1024]{1,0:T(8,128)(2,1)S(1)} %add_convert_fusion.3), channel_id=1, source_target_pairs={{0,8},{4,12},{8,0},{12,4},{1,9},{5,13},{9,1},{13,5},{2,10},{6,14},... | collective-permute-start | bytes 393224 | tf_op jit(solution)/shard_map/ppermute | solution.py:40
  92.4 11.3 %copy-start.9 = (bf16[64,1024]{1,0:T(8,128)(2,1)S(1)}, bf16[64,1024]{1,0:T(8,128)(2,1)}, u32[]{:S(2)}) copy-start(bf16[64,1024]{1,0:T(8,128)(2,1)} %add_convert_fusion.2) | copy-start | bytes 393220
  101.7 8.0 %collective-permute-start.6 = (bf16[256,6144]{1,0:T(8,128)(2,1)}, bf16[256,6144]{1,0:T(8,128)(2,1)}, u32[]{:S(2)}, u32[]{:S(2)}) collective-permute-start(bf16[256,6144]{1,0:T(8,128)(2,1)} %teacher_norm.1.own_ref), channel_id=1, source_target_pairs={{0,16},{16,0},{1,17},{17,1},{2,18},{18,2},{3,19},{19,3},{4,20},{20... | collective-permute-start | bytes 9437192 | tf_op jit(solution)/shard_map/ppermute | solution.py:36
  104.6 16.7 %all-to-all-start.3 = ((bf16[4,64,1024]{2,1,0:T(8,128)(2,1)}), bf16[4,64,1024]{2,1,0:T(8,128)(2,1)S(1)}, u32[]{:S(2)}, u32[]{:S(2)}) async-start(bf16[4,64,1024]{2,1,0:T(8,128)(2,1)} %broadcast_in_dim.14), calls=%async_computation.3 | async-start | bytes 1048576 | tf_op jit(solution)/shard_map/all_to_all | solution.py:48
  119.0 9.4 %copy-start.5 = (bf16[1024,256]{1,0:T(8,128)(2,1)S(1)}, bf16[1024,256]{1,0:T(8,128)(2,1)}, u32[]{:S(2)}) copy-start(bf16[1024,256]{1,0:T(8,128)(2,1)} %param.17) | copy-start | bytes 1572868
  119.1 3.4 %collective-permute-start.7 = (f32[256,128]{1,0:T(8,128)S(1)}, f32[256,128]{1,0:T(8,128)S(1)}, u32[]{:S(2)}, u32[]{:S(2)}) collective-permute-start(f32[256,128]{1,0:T(8,128)S(1)} %get-tuple-element.29), channel_id=1, source_target_pairs={{0,16},{16,0},{1,17},{17,1},{2,18},{18,2},{3,19},{19,3},{4,20},{20... | collective-permute-start | bytes 393224 | tf_op jit(solution)/shard_map/ppermute | solution.py:36
  123.4 13.2 %all-to-all-start.4 = ((f32[16,2,256]{2,1,0:T(2,128)}), f32[16,2,256]{2,1,0:T(2,128)S(1)}, u32[]{:S(2)}, u32[]{:S(2)}) async-start(f32[16,2,256]{2,1,0:T(2,128)} %broadcast_in_dim.15), calls=%async_computation.4 | async-start | bytes 65536 | tf_op jit(solution)/shard_map/all_to_all | solution.py:48
  148.2 6.9 %collective-permute-start.8 = (bf16[64,1024]{1,0:T(8,128)(2,1)S(1)}, bf16[64,1024]{1,0:T(8,128)(2,1)S(1)}, u32[]{:S(2)}, u32[]{:S(2)}) collective-permute-start(bf16[64,1024]{1,0:T(8,128)(2,1)S(1)} %reduce_sum.119), channel_id=1, source_target_pairs={{0,4},{4,0},{8,12},{12,8},{1,5},{5,1},{9,13},{13,9},{2,6},{6,2},{1... | collective-permute-start | bytes 393224 | tf_op jit(solution)/shard_map/ppermute | solution.py:40
  155.1 9.0 %collective-permute-start.9 = (bf16[64,1024]{1,0:T(8,128)(2,1)S(1)}, bf16[64,1024]{1,0:T(8,128)(2,1)S(1)}, u32[]{:S(2)}, u32[]{:S(2)}) collective-permute-start(bf16[64,1024]{1,0:T(8,128)(2,1)S(1)} %add_convert_fusion.1), channel_id=1, source_target_pairs={{0,8},{4,12},{8,0},{12,4},{1,9},{5,13},{9,1},{13,5},{2,10},{6,14},... | collective-permute-start | bytes 393224 | tf_op jit(solution)/shard_map/ppermute | solution.py:40
  164.9 11.7 %copy-start.7 = (f32[256,256]{1,0:T(8,128)S(1)}, f32[256,256]{1,0:T(8,128)}, u32[]{:S(2)}) copy-start(f32[256,256]{1,0:T(8,128)} %copy-done.6) | copy-start | bytes 786436
  164.9 11.7 %all-to-all-start.6 = ((bf16[4,64,1024]{2,1,0:T(8,128)(2,1)}), bf16[4,64,1024]{2,1,0:T(8,128)(2,1)S(1)}, u32[]{:S(2)}, u32[]{:S(2)}) async-start(bf16[4,64,1024]{2,1,0:T(8,128)(2,1)} %broadcast_in_dim.16), calls=%async_computation.6 | async-start | bytes 1048576 | tf_op jit(solution)/shard_map/all_to_all | solution.py:48
  (8 other events, 35.6 us)
Sparse Core Ops, SparseCore 0:
  45.5 58.5 all-gather.2

commit v16 on v15

--- a/solution.py
+++ b/solution.py
@@ -98,7 +98,7 @@
 
 def mp_gather_x(part):
     rows, cols = part.shape
-    return spread(part, "x").reshape(4 * rows, cols)
+    return swap(four_copies(part), "x").reshape(4 * rows, cols)
 
 
 def merge_stats(stats, count):
@@ -210,14 +210,13 @@
     activ = gated.astype(BF16)
     mlp_term = jnp.dot(activ, down_weight, preferred_element_type=F32).astype(BF16)
 
-    def by_core(mine, theirs):
-        return jnp.where(first, jnp.stack([mine, theirs]), jnp.stack([theirs, mine]))
-
     given = flip(jnp.stack([near[1], far[1]]), "c")
     given, own, far_block, mlp_term = lax.optimization_barrier(
         (given, own, far_block, mlp_term)
     )
-    rows = jnp.concatenate([by_core(near[0], given[0]), by_core(far[0], given[1])])
+    mine = jnp.stack([near[0], far[0]])
+    from_first = (jnp.arange(2) == 0)[None, :, None, None]
+    rows = jnp.where(from_first == first, mine[:, None], given[:, None]).reshape(4, 192, 384)
     weight = lax.all_gather(rows, "y").reshape(6144, 384)
 
     late = flip(jnp.stack([shard, far_block]), "zl", 1)

time: 226 us -> 227 us (level)
  waiting for transfers between devices: 67.8 us -> 65.2 us
    ppermute x8, waiting for transfers between devices: 43.5 us -> 40.4 us  [flip(): lax.ppermute(values, axes, [(i, i ^ bits) for i in range(SIZES[axes])])]
  transfers between devices with their start and end apart: 17 -> 17, of which waited for: 13 -> 13; matrix products, arithmetic and copies ran while one was open for 4% -> 5% of each run, Pallas kernels for 6% -> 6%
where the time goes in v16:
time: 227 us; the launch traced here: 226 us
  waiting for transfers between devices  65.2 us (29%)
  starting transfers between devices  58.2 us (26%)
  blocking collectives  50.4 us (22%)
  between operations  14.6 us (6%)
  Pallas kernels  14.5 us (6%)
  local copies, waits for them, and re-layouts  10.7 us (5%)
  other arithmetic  7.12 us (3%)
  matrix products  4.85 us (2%)
    ppermute x8, waiting for transfers between devices, flip(): lax.ppermute(values, axes, [(i, i ^ bits) for i in range(SIZES[axes])])  40.4 us
    all_to_all x1, blocking collectives, reduce_dp(): terms = lax.all_to_all(terms, ('zh', 'y'), split_axis=1, concat_axis=0)  34.3 us
    ppermute x8, starting transfers between devices, flip(): lax.ppermute(values, axes, [(i, i ^ bits) for i in range(SIZES[axes])])  28.7 us
    all_to_all x6, starting transfers between devices, swap(): return lax.all_to_all(values, axis, split_axis=0, concat_axis=0)  25.2 us
    all_to_all x6, waiting for transfers between devices, swap(): return lax.all_to_all(values, axis, split_axis=0, concat_axis=0)  22.2 us
    all_to_all x1, blocking collectives, swap(): return lax.all_to_all(values, axis, split_axis=0, concat_axis=0)  11.1 us
    pallas_call x1, Pallas kernels, shards(): pl.pallas_call(attention_kernel, out_shape=jax.ShapeDtypeStruct((2, 256,...  6.97 us
    pallas_call x1, Pallas kernels, shards(): pl.pallas_call(norm_kernel, out_shape=jax.ShapeDtypeStruct((256, 6144), B...  5.68 us
  transfers between devices with their start and end apart: 17, of which 13 were waited for; matrix products, arithmetic and copies ran while one was open for 5% of the time, Pallas kernels for 6%

profile of v16, /device:TPU:8, one launch (start us, length us, event | category | flops | bytes accessed | tf_op | source)
XLA Modules:
  0.0 225.5 jit_solution(6948781282749192491)
XLA Ops:
  8.9 10.9 %collective-permute-start = (bf16[2,192,384]{2,1,0:T(8,128)(2,1)S(1)}, bf16[2,192,384]{2,1,0:T(8,128)(2,1)}, u32[]{:S(2)}, u32[]{:S(2)}) collective-permute-start(bf16[2,192,384]{2,1,0:T(8,128)(2,1)S(1)} %reverse_select_fusion), channel_id=1, source_target_pairs={{0,256},{256,0},{1,257},{257,1},{2,258},{258,2},{3,259},{259,3},{4... | collective-permute-start | bytes 884744 | tf_op jit(solution)/shard_map/ppermute | solution.py:40
  20.1 4.4 %collective-permute-start.2 = (bf16[272,384]{1,0:T(8,128)(2,1)S(1)}, bf16[272,384]{1,0:T(8,128)(2,1)S(1)}, u32[]{:S(2)}, u32[]{:S(2)}) collective-permute-start(bf16[272,384]{1,0:T(8,128)(2,1)S(1)} %concatenate.14), channel_id=1, source_target_pairs={{0,8},{4,12},{8,0},{12,4},{1,9},{5,13},{9,1},{13,5},{2,10},{6,14},... | collective-permute-start | bytes 626696 | tf_op jit(solution)/shard_map/ppermute | solution.py:40
  25.5 4.4 %all-to-all-start = ((bf16[4,272,384]{2,1,0:T(8,128)(2,1)}), bf16[4,272,384]{2,1,0:T(8,128)(2,1)S(1)}, u32[]{:S(2)}, u32[]{:S(2)}) async-start(bf16[4,272,384]{2,1,0:T(8,128)(2,1)} %broadcast_in_dim.40), calls=%async_computation | async-start | bytes 1671168 | tf_op jit(solution)/shard_map/all_to_all | solution.py:48
  37.7 5.6 %collective-permute-done.2 = bf16[272,384]{1,0:T(8,128)(2,1)S(1)} collective-permute-done((bf16[272,384]{1,0:T(8,128)(2,1)S(1)}, bf16[272,384]{1,0:T(8,128)(2,1)S(1)}, u32[]{:S(2)}, u32[]{:S(2)}) %collective-permute-start.2) | collective-permute-done | bytes 208928 | tf_op jit(solution)/shard_map/ppermute | solution.py:40
  47.2 4.3 %all-to-all-start.1 = ((bf16[4,272,640]{2,1,0:T(8,128)(2,1)}), bf16[4,272,640]{2,1,0:T(8,128)(2,1)S(1)}, u32[]{:S(2)}, u32[]{:S(2)}) async-start(bf16[4,272,640]{2,1,0:T(8,128)(2,1)} %fusion.1), calls=%async_computation.1 | async-start | bytes 2785280 | tf_op jit(solution)/shard_map/all_to_all | solution.py:48
  54.4 11.2 %collective-permute-done.3.in_ref = bf16[2,272,384]{2,1,0:T(8,128)(2,1)S(1)} collective-permute-done((bf16[2,272,384]{2,1,0:T(8,128)(2,1)S(1)}, bf16[2,272,384]{2,1,0:T(8,128)(2,1)S(1)}, u32[]{:S(2)}, u32[]{:S(2)}) %collective-permute-start.3) | collective-permute-done | bytes 417824 | tf_op jit(solution)/shard_map/ppermute | solution.py:40
  67.0 3.4 %all-to-all-done.1.far_ref = bf16[4,272,640]{2,1,0:T(8,128)(2,1)S(1)} async-done(((bf16[4,272,640]{2,1,0:T(8,128)(2,1)}), bf16[4,272,640]{2,1,0:T(8,128)(2,1)S(1)}, u32[]{:S(2)}, u32[]{:S(2)}) %all-to-all-start.1) | async-done | bytes 1392672 | tf_op jit(solution)/shard_map/all_to_all | solution.py:48
  70.4 4.4 %all-to-all-start.2 = ((bf16[4,2,272,384]{3,2,1,0:T(8,128)(2,1)}), bf16[4,2,272,384]{3,2,1,0:T(8,128)(2,1)}, u32[]{:S(2)}, u32[]{:S(2)}) async-start(bf16[4,2,272,384]{3,2,1,0:T(8,128)(2,1)} %copy-done.1), calls=%async_computation.2 | async-start | bytes 3342336 | tf_op jit(solution)/shard_map/all_to_all | solution.py:48
  76.9 4.9 %collective-permute-done.4 = bf16[64,1024]{1,0:T(8,128)(2,1)S(1)} collective-permute-done((bf16[64,1024]{1,0:T(8,128)(2,1)S(1)}, bf16[64,1024]{1,0:T(8,128)(2,1)S(1)}, u32[]{:S(2)}, u32[]{:S(2)}) %collective-permute-start.4) | collective-permute-done | bytes 131104 | tf_op jit(solution)/shard_map/ppermute | solution.py:40
  81.9 2.8 %collective-permute-start.5 = (bf16[64,1024]{1,0:T(8,128)(2,1)S(1)}, bf16[64,1024]{1,0:T(8,128)(2,1)}, u32[]{:S(2)}, u32[]{:S(2)}) collective-permute-start(bf16[64,1024]{1,0:T(8,128)(2,1)S(1)} %add_convert_fusion.3), channel_id=1, source_target_pairs={{0,8},{4,12},{8,0},{12,4},{1,9},{5,13},{9,1},{13,5},{2,10},{6,14},... | collective-permute-start | bytes 393224 | tf_op jit(solution)/shard_map/ppermute | solution.py:40
  84.7 6.1 %collective-permute-done.5 = bf16[64,1024]{1,0:T(8,128)(2,1)} collective-permute-done((bf16[64,1024]{1,0:T(8,128)(2,1)S(1)}, bf16[64,1024]{1,0:T(8,128)(2,1)}, u32[]{:S(2)}, u32[]{:S(2)}) %collective-permute-start.5) | collective-permute-done | bytes 131104 | tf_op jit(solution)/shard_map/ppermute | solution.py:40
  91.8 4.2 %all-to-all-done.2.late_ref = bf16[4,2,272,384]{3,2,1,0:T(8,128)(2,1)} async-done(((bf16[4,2,272,384]{3,2,1,0:T(8,128)(2,1)}), bf16[4,2,272,384]{3,2,1,0:T(8,128)(2,1)}, u32[]{:S(2)}, u32[]{:S(2)}) %all-to-all-start.2) | async-done | bytes 1671200 | tf_op jit(solution)/shard_map/all_to_all | solution.py:48
  96.0 5.7 %teacher_norm.1.own_ref = bf16[256,6144]{1,0:T(8,128)(2,1)} custom-call(s32[2]{0:T(128)S(1)} %pad_add_fusion.place, bf16[4,272,384]{2,1,0:T(8,128)(2,1)S(1)} %all-to-all-done.own_ref, bf16[4,272,640]{2,1,0:T(8,128)(2,1)S(1)} %all-to-all-done.1.far_ref, bf16[4,2,272,384]{3,2,1,0:T(8,128)(2,1)} %all-to-all-done.2.late_ref), custom_call_target="tpu_custom_call" | custom-call | flops 1000 | bytes 1000 | tf_op jit(solution)/shard_map/teacher_norm/pallas_call | solution.py:232
  104.6 3.5 %all-to-all-start.3 = ((bf16[4,64,1024]{2,1,0:T(8,128)(2,1)}), bf16[4,64,1024]{2,1,0:T(8,128)(2,1)S(1)}, u32[]{:S(2)}, u32[]{:S(2)}) async-start(bf16[4,64,1024]{2,1,0:T(8,128)(2,1)} %four_copies.4), calls=%async_computation.3 | async-start | bytes 1048576 | tf_op jit(solution)/shard_map/all_to_all | solution.py:48
  112.0 7.0 %teacher_heads.1 = f32[2,256,128]{2,1,0:T(8,128)S(1)} custom-call(s32[1]{0:T(128)} %bitcast.10.place, bf16[256,6144]{1,0:T(8,128)(2,1)} %teacher_norm.1.own_ref, bf16[256,6144]{1,0:T(8,128)(2,1)} %collective-permute-done.6.other_ref, bf16[6144,384]{1,0:T(8,128)(2,1)S(1)} %bitcast.63, f32[2,128]{1,0:T(2,128)S(1)} %copy-done.3), custom_call_target="tpu_custom_call" | custom-call | flops 2415919104 | bytes 11000000 | tf_op jit(solution)/shard_map/teacher_heads/pallas_call | solution.py:246
  123.4 5.0 %all-to-all-start.4 = ((f32[16,2,256]{2,1,0:T(2,128)}), f32[16,2,256]{2,1,0:T(2,128)S(1)}, u32[]{:S(2)}, u32[]{:S(2)}) async-start(f32[16,2,256]{2,1,0:T(2,128)} %broadcast_in_dim.72), calls=%async_computation.4 | async-start | bytes 65536 | tf_op jit(solution)/shard_map/all_to_all | solution.py:48
  128.7 7.8 %all-to-all-done.4 = f32[16,2,256]{2,1,0:T(2,128)S(1)} async-done(((f32[16,2,256]{2,1,0:T(2,128)}), f32[16,2,256]{2,1,0:T(2,128)S(1)}, u32[]{:S(2)}, u32[]{:S(2)}) %all-to-all-start.4) | async-done | bytes 32800 | tf_op jit(solution)/shard_map/all_to_all | solution.py:48
  137.0 11.1 %all_to_all.53 = bf16[4,64,1024]{2,1,0:T(8,128)(2,1)S(1)} all-to-all(bf16[4,64,1024]{2,1,0:T(8,128)(2,1)S(1)} %bitcast.67), channel_id=1, replica_groups=mesh['zh'=2,'y'=8,'c'=2,'zl'=4,'x'=4] {'x'}, dimensions={0} | all-to-all | bytes 1048576 | tf_op jit(solution)/shard_map/all_to_all | solution.py:48
  150.4 4.6 %collective-permute-done.8 = bf16[64,1024]{1,0:T(8,128)(2,1)S(1)} collective-permute-done((bf16[64,1024]{1,0:T(8,128)(2,1)S(1)}, bf16[64,1024]{1,0:T(8,128)(2,1)S(1)}, u32[]{:S(2)}, u32[]{:S(2)}) %collective-permute-start.8) | collective-permute-done | bytes 131104 | tf_op jit(solution)/shard_map/ppermute | solution.py:40
  157.7 6.4 %collective-permute-done.9 = bf16[64,1024]{1,0:T(8,128)(2,1)S(1)} collective-permute-done((bf16[64,1024]{1,0:T(8,128)(2,1)S(1)}, bf16[64,1024]{1,0:T(8,128)(2,1)S(1)}, u32[]{:S(2)}, u32[]{:S(2)}) %collective-permute-start.9) | collective-permute-done | bytes 131104 | tf_op jit(solution)/shard_map/ppermute | solution.py:40
  164.9 3.6 %all-to-all-start.6 = ((bf16[4,64,1024]{2,1,0:T(8,128)(2,1)}), bf16[4,64,1024]{2,1,0:T(8,128)(2,1)S(1)}, u32[]{:S(2)}, u32[]{:S(2)}) async-start(bf16[4,64,1024]{2,1,0:T(8,128)(2,1)} %four_copies.5), calls=%async_computation.6 | async-start | bytes 1048576 | tf_op jit(solution)/shard_map/all_to_all | solution.py:48
  169.8 6.8 %all-to-all-done.6 = bf16[4,64,1024]{2,1,0:T(8,128)(2,1)S(1)} async-done(((bf16[4,64,1024]{2,1,0:T(8,128)(2,1)}), bf16[4,64,1024]{2,1,0:T(8,128)(2,1)S(1)}, u32[]{:S(2)}, u32[]{:S(2)}) %all-to-all-start.6) | async-done | bytes 524320 | tf_op jit(solution)/shard_map/all_to_all | solution.py:48
  178.2 5.0 %all_to_all.54 = bf16[1,3,16,2,32,256]{5,4,2,1,0,3:T(8,128)(2,1)S(1)} all-to-all(bf16[1,3,16,2,32,256]{5,4,2,1,0,3:T(8,128)(2,1)S(1)} %copy.45), channel_id=1, replica_groups=mesh['zh'=2,'y'=8,'c'=2,'zl'=4,'x'=4] {'c'}, dimensions={3} | all-to-all | bytes 3145728 | tf_op jit(solution)/shard_map/all_to_all | solution.py:176
  183.6 34.3 %all_to_all.55 = bf16[1,3,16,32,256]{4,3,1,0,2:T(8,128)(2,1)S(1)} all-to-all(bf16[1,3,16,32,256]{4,3,1,0,2:T(8,128)(2,1)S(1)} %copy.44), channel_id=1, replica_groups=mesh['zh'=2,'y'=8,'c'=2,'zl'=4,'x'=4] {'zh','y'}, dimensions={2} | all-to-all | bytes 1572864 | tf_op jit(solution)/shard_map/all_to_all | solution.py:178
  (111 shorter events, 43.5 us)
Async XLA Ops:
  7.2 30.0 %copy-start = (bf16[256,1024]{1,0:T(8,128)(2,1)S(1)}, bf16[256,1024]{1,0:T(8,128)(2,1)}, u32[]{:S(2)}) copy-start(bf16[256,1024]{1,0:T(8,128)(2,1)} %param.16) | copy-start | bytes 1572868
  7.2 12.6 %copy-start.12 = (f32[384]{0:T(512)S(1)}, f32[384]{0:T(512)}, u32[]{:S(2)}) copy-start(f32[384]{0:T(512)} %param.10) | copy-start | bytes 4612
  7.2 12.7 %copy-start.11 = (bf16[256,384]{1,0:T(8,128)(2,1)S(1)}, bf16[256,384]{1,0:T(8,128)(2,1)}, u32[]{:S(2)}) copy-start(bf16[256,384]{1,0:T(8,128)(2,1)} %param.9) | copy-start | bytes 589828
  8.9 24.6 %collective-permute-start = (bf16[2,192,384]{2,1,0:T(8,128)(2,1)S(1)}, bf16[2,192,384]{2,1,0:T(8,128)(2,1)}, u32[]{:S(2)}, u32[]{:S(2)}) collective-permute-start(bf16[2,192,384]{2,1,0:T(8,128)(2,1)S(1)} %reverse_select_fusion), channel_id=1, source_target_pairs={{0,256},{256,0},{1,257},{257,1},{2,258},{258,2},{3,259},{259,3},{4... | collective-permute-start | bytes 884744 | tf_op jit(solution)/shard_map/ppermute | solution.py:40
  20.1 9.9 %copy-start.4 = (bf16[256,1024]{1,0:T(8,128)(2,1)S(1)}, bf16[256,1024]{1,0:T(8,128)(2,1)}, u32[]{:S(2)}) copy-start(bf16[256,1024]{1,0:T(8,128)(2,1)} %param.13) | copy-start | bytes 1572868
  20.1 23.2 %collective-permute-start.2 = (bf16[272,384]{1,0:T(8,128)(2,1)S(1)}, bf16[272,384]{1,0:T(8,128)(2,1)S(1)}, u32[]{:S(2)}, u32[]{:S(2)}) collective-permute-start(bf16[272,384]{1,0:T(8,128)(2,1)S(1)} %concatenate.14), channel_id=1, source_target_pairs={{0,8},{4,12},{8,0},{12,4},{1,9},{5,13},{9,1},{13,5},{2,10},{6,14},... | collective-permute-start | bytes 626696 | tf_op jit(solution)/shard_map/ppermute | solution.py:40
  25.5 17.8 %all-to-all-start = ((bf16[4,272,384]{2,1,0:T(8,128)(2,1)}), bf16[4,272,384]{2,1,0:T(8,128)(2,1)S(1)}, u32[]{:S(2)}, u32[]{:S(2)}) async-start(bf16[4,272,384]{2,1,0:T(8,128)(2,1)} %broadcast_in_dim.40), calls=%async_computation | async-start | bytes 1671168 | tf_op jit(solution)/shard_map/all_to_all | solution.py:48
  29.9 79.8 %all-gather.2.cloned.1.call-start = ((), (), s32[]{:S(2)}) async-start(), calls=%async_computation.9 | async-start | bytes 5308416 | tf_op jit(solution)/shard_map/all_gather | solution.py:220
  35.3 8.0 %collective-permute-start.1 = (bf16[2,192,384]{2,1,0:T(8,128)(2,1)}, bf16[2,192,384]{2,1,0:T(8,128)(2,1)}, u32[]{:S(2)}, u32[]{:S(2)}) collective-permute-start(bf16[2,192,384]{2,1,0:T(8,128)(2,1)} %pad_maximum_fusion.2), channel_id=1, source_target_pairs={{0,16},{16,0},{1,17},{17,1},{2,18},{18,2},{3,19},{19,3},{4,20},{20... | collective-permute-start | bytes 884744 | tf_op jit(solution)/shard_map/ppermute | solution.py:40
  47.2 23.3 %all-to-all-start.1 = ((bf16[4,272,640]{2,1,0:T(8,128)(2,1)}), bf16[4,272,640]{2,1,0:T(8,128)(2,1)S(1)}, u32[]{:S(2)}, u32[]{:S(2)}) async-start(bf16[4,272,640]{2,1,0:T(8,128)(2,1)} %fusion.1), calls=%async_computation.1 | async-start | bytes 2785280 | tf_op jit(solution)/shard_map/all_to_all | solution.py:48
  52.4 13.2 %collective-permute-start.3 = (bf16[2,272,384]{2,1,0:T(8,128)(2,1)S(1)}, bf16[2,272,384]{2,1,0:T(8,128)(2,1)S(1)}, u32[]{:S(2)}, u32[]{:S(2)}) collective-permute-start(bf16[2,272,384]{2,1,0:T(8,128)(2,1)S(1)} %pad_maximum_fusion.1), channel_id=1, source_target_pairs={{0,4},{4,0},{8,12},{12,8},{1,5},{5,1},{9,13},{13,9},{2,6},{6,2},{1... | collective-permute-start | bytes 1253384 | tf_op jit(solution)/shard_map/ppermute | solution.py:40
  70.4 25.6 %all-to-all-start.2 = ((bf16[4,2,272,384]{3,2,1,0:T(8,128)(2,1)}), bf16[4,2,272,384]{3,2,1,0:T(8,128)(2,1)}, u32[]{:S(2)}, u32[]{:S(2)}) async-start(bf16[4,2,272,384]{3,2,1,0:T(8,128)(2,1)} %copy-done.1), calls=%async_computation.2 | async-start | bytes 3342336 | tf_op jit(solution)/shard_map/all_to_all | solution.py:48
  75.0 6.9 %collective-permute-start.4 = (bf16[64,1024]{1,0:T(8,128)(2,1)S(1)}, bf16[64,1024]{1,0:T(8,128)(2,1)S(1)}, u32[]{:S(2)}, u32[]{:S(2)}) collective-permute-start(bf16[64,1024]{1,0:T(8,128)(2,1)S(1)} %bitcast.75), channel_id=1, source_target_pairs={{0,4},{4,0},{8,12},{12,8},{1,5},{5,1},{9,13},{13,9},{2,6},{6,2},{1... | collective-permute-start | bytes 393224 | tf_op jit(solution)/shard_map/ppermute | solution.py:40
  81.9 8.9 %collective-permute-start.5 = (bf16[64,1024]{1,0:T(8,128)(2,1)S(1)}, bf16[64,1024]{1,0:T(8,128)(2,1)}, u32[]{:S(2)}, u32[]{:S(2)}) collective-permute-start(bf16[64,1024]{1,0:T(8,128)(2,1)S(1)} %add_convert_fusion.3), channel_id=1, source_target_pairs={{0,8},{4,12},{8,0},{12,4},{1,9},{5,13},{9,1},{13,5},{2,10},{6,14},... | collective-permute-start | bytes 393224 | tf_op jit(solution)/shard_map/ppermute | solution.py:40
  101.7 8.0 %copy-start.3 = (f32[2,128]{1,0:T(2,128)S(1)}, f32[2,128]{1,0:T(2,128)}, u32[]{:S(2)}) copy-start(f32[2,128]{1,0:T(2,128)} %qg_ref.1) | copy-start | bytes 3076
  101.7 8.0 %collective-permute-start.6 = (bf16[256,6144]{1,0:T(8,128)(2,1)}, bf16[256,6144]{1,0:T(8,128)(2,1)}, u32[]{:S(2)}, u32[]{:S(2)}) collective-permute-start(bf16[256,6144]{1,0:T(8,128)(2,1)} %teacher_norm.1.own_ref), channel_id=1, source_target_pairs={{0,16},{16,0},{1,17},{17,1},{2,18},{18,2},{3,19},{19,3},{4,20},{20... | collective-permute-start | bytes 9437192 | tf_op jit(solution)/shard_map/ppermute | solution.py:36
  104.6 16.7 %all-to-all-start.3 = ((bf16[4,64,1024]{2,1,0:T(8,128)(2,1)}), bf16[4,64,1024]{2,1,0:T(8,128)(2,1)S(1)}, u32[]{:S(2)}, u32[]{:S(2)}) async-start(bf16[4,64,1024]{2,1,0:T(8,128)(2,1)} %four_copies.4), calls=%async_computation.3 | async-start | bytes 1048576 | tf_op jit(solution)/shard_map/all_to_all | solution.py:48
  119.0 9.4 %copy-start.5 = (bf16[1024,256]{1,0:T(8,128)(2,1)S(1)}, bf16[1024,256]{1,0:T(8,128)(2,1)}, u32[]{:S(2)}) copy-start(bf16[1024,256]{1,0:T(8,128)(2,1)} %param.17) | copy-start | bytes 1572868
  119.0 3.4 %collective-permute-start.7 = (f32[256,128]{1,0:T(8,128)S(1)}, f32[256,128]{1,0:T(8,128)S(1)}, u32[]{:S(2)}, u32[]{:S(2)}) collective-permute-start(f32[256,128]{1,0:T(8,128)S(1)} %get-tuple-element.27), channel_id=1, source_target_pairs={{0,16},{16,0},{1,17},{17,1},{2,18},{18,2},{3,19},{19,3},{4,20},{20... | collective-permute-start | bytes 393224 | tf_op jit(solution)/shard_map/ppermute | solution.py:36
  123.4 13.2 %all-to-all-start.4 = ((f32[16,2,256]{2,1,0:T(2,128)}), f32[16,2,256]{2,1,0:T(2,128)S(1)}, u32[]{:S(2)}, u32[]{:S(2)}) async-start(f32[16,2,256]{2,1,0:T(2,128)} %broadcast_in_dim.72), calls=%async_computation.4 | async-start | bytes 65536 | tf_op jit(solution)/shard_map/all_to_all | solution.py:48
  148.2 6.9 %collective-permute-start.8 = (bf16[64,1024]{1,0:T(8,128)(2,1)S(1)}, bf16[64,1024]{1,0:T(8,128)(2,1)S(1)}, u32[]{:S(2)}, u32[]{:S(2)}) collective-permute-start(bf16[64,1024]{1,0:T(8,128)(2,1)S(1)} %reduce_sum.119), channel_id=1, source_target_pairs={{0,4},{4,0},{8,12},{12,8},{1,5},{5,1},{9,13},{13,9},{2,6},{6,2},{1... | collective-permute-start | bytes 393224 | tf_op jit(solution)/shard_map/ppermute | solution.py:40
  155.1 9.0 %collective-permute-start.9 = (bf16[64,1024]{1,0:T(8,128)(2,1)S(1)}, bf16[64,1024]{1,0:T(8,128)(2,1)S(1)}, u32[]{:S(2)}, u32[]{:S(2)}) collective-permute-start(bf16[64,1024]{1,0:T(8,128)(2,1)S(1)} %add_convert_fusion.1), channel_id=1, source_target_pairs={{0,8},{4,12},{8,0},{12,4},{1,9},{5,13},{9,1},{13,5},{2,10},{6,14},... | collective-permute-start | bytes 393224 | tf_op jit(solution)/shard_map/ppermute | solution.py:40
  164.9 11.7 %copy-start.7 = (f32[256,256]{1,0:T(8,128)S(1)}, f32[256,256]{1,0:T(8,128)}, u32[]{:S(2)}) copy-start(f32[256,256]{1,0:T(8,128)} %copy-done.6) | copy-start | bytes 786436
  164.9 11.7 %all-to-all-start.6 = ((bf16[4,64,1024]{2,1,0:T(8,128)(2,1)}), bf16[4,64,1024]{2,1,0:T(8,128)(2,1)S(1)}, u32[]{:S(2)}, u32[]{:S(2)}) async-start(bf16[4,64,1024]{2,1,0:T(8,128)(2,1)} %four_copies.5), calls=%async_computation.6 | async-start | bytes 1048576 | tf_op jit(solution)/shard_map/all_to_all | solution.py:48
  (7 other events, 21.0 us)
Sparse Core Ops, SparseCore 0:
  45.5 58.5 all-gather.1

commit v17 on v15

--- a/solution.py
+++ b/solution.py
@@ -172,11 +172,12 @@
 
 def reduce_dp(terms):
     k = terms.shape[0]
-    terms = terms.reshape(k, 16, 2, 32, 256)
-    terms = lax.all_to_all(terms, "c", split_axis=2, concat_axis=0)
-    terms = sum_parts(terms).astype(BF16)
-    terms = lax.all_to_all(terms, ("zh", "y"), split_axis=1, concat_axis=0)
-    return sum_parts(terms).astype(BF16)
+    terms = terms.reshape(k, 16, 2, 32, 256).transpose(1, 0, 2, 3, 4)
+    first = lax.axis_index("c") == 0
+    theirs = flip(jnp.where(first, terms[:, :, 1], terms[:, :, 0]), "c")
+    mine = jnp.where(first, terms[:, :, 0], terms[:, :, 1])
+    terms = (mine.astype(F32) + theirs.astype(F32)).astype(BF16)
+    return sum_parts(swap(terms, ("zh", "y"))).astype(BF16)
 
 
 def shards(

time: 226 us -> 225 us (level)
  blocking collectives: 49.6 us -> 44.6 us
    all_to_all x2 -> x0, blocking collectives: 38.5 us -> none  [the longest x1 33.5 us: reduce_dp(): terms = lax.all_to_all(terms, ('zh', 'y'), split_axis=1, concat_axis=0)]
    all_to_all x1 -> x2, blocking collectives: 11.1 us -> 44.6 us  [swap(): return lax.all_to_all(values, axis, split_axis=0, concat_axis=0)]
    ppermute x8 -> x9, waiting for transfers between devices: 43.5 us -> 45.8 us  [flip(): lax.ppermute(values, axes, [(i, i ^ bits) for i in range(SIZES[axes])])]
    ppermute x8 -> x9, starting transfers between devices: 28.6 us -> 30.5 us  [flip(): lax.ppermute(values, axes, [(i, i ^ bits) for i in range(SIZES[axes])])]
  transfers between devices with their start and end apart: 17 -> 18, of which waited for: 13 -> 14; matrix products, arithmetic and copies ran while one was open for 4% -> 4% of each run, Pallas kernels for 6% -> 6%
where the time goes in v17:
time: 225 us; the launch traced here: 224 us
  waiting for transfers between devices  70 us (31%)
  starting transfers between devices  59.8 us (27%)
  blocking collectives  44.6 us (20%)
  between operations  14.6 us (6%)
  Pallas kernels  12.8 us (6%)
  local copies, waits for them, and re-layouts  11 us (5%)
  other arithmetic  7.07 us (3%)
  matrix products  3.82 us (2%)
    ppermute x9, waiting for transfers between devices, flip(): lax.ppermute(values, axes, [(i, i ^ bits) for i in range(SIZES[axes])])  45.8 us
    all_to_all x2, blocking collectives, swap(): return lax.all_to_all(values, axis, split_axis=0, concat_axis=0)  44.6 us
    ppermute x9, starting transfers between devices, flip(): lax.ppermute(values, axes, [(i, i ^ bits) for i in range(SIZES[axes])])  30.5 us
    all_to_all x6, starting transfers between devices, swap(): return lax.all_to_all(values, axis, split_axis=0, concat_axis=0)  25.1 us
    all_to_all x6, waiting for transfers between devices, swap(): return lax.all_to_all(values, axis, split_axis=0, concat_axis=0)  21.7 us
    pallas_call x1, Pallas kernels, shards(): pl.pallas_call(attention_kernel, out_shape=jax.ShapeDtypeStruct((2, 256,...  6.97 us
    pallas_call x1, Pallas kernels, shards(): pl.pallas_call(norm_kernel, out_shape=jax.ShapeDtypeStruct((256, 6144), B...  5.67 us
  transfers between devices with their start and end apart: 18, of which 14 were waited for; matrix products, arithmetic and copies ran while one was open for 4% of the time, Pallas kernels for 6%

profile of v17, /device:TPU:8, one launch (start us, length us, event | category | flops | bytes accessed | tf_op | source)
XLA Modules:
  0.0 223.8 jit_solution(4896214755483588588)
XLA Ops:
  8.9 10.9 %collective-permute-start = (bf16[2,192,384]{2,1,0:T(8,128)(2,1)S(1)}, bf16[2,192,384]{2,1,0:T(8,128)(2,1)S(1)}, u32[]{:S(2)}, u32[]{:S(2)}) collective-permute-start(bf16[2,192,384]{2,1,0:T(8,128)(2,1)S(1)} %reverse_select_fusion), channel_id=1, source_target_pairs={{0,256},{256,0},{1,257},{257,1},{2,258},{258,2},{3,259},{259,3},{4... | collective-permute-start | bytes 884744 | tf_op jit(solution)/shard_map/ppermute | solution.py:40
  20.1 4.3 %collective-permute-start.2 = (bf16[272,384]{1,0:T(8,128)(2,1)S(1)}, bf16[272,384]{1,0:T(8,128)(2,1)S(1)}, u32[]{:S(2)}, u32[]{:S(2)}) collective-permute-start(bf16[272,384]{1,0:T(8,128)(2,1)S(1)} %concatenate.17), channel_id=1, source_target_pairs={{0,8},{4,12},{8,0},{12,4},{1,9},{5,13},{9,1},{13,5},{2,10},{6,14},... | collective-permute-start | bytes 626696 | tf_op jit(solution)/shard_map/ppermute | solution.py:40
  25.4 4.3 %all-to-all-start = ((bf16[4,272,384]{2,1,0:T(8,128)(2,1)}), bf16[4,272,384]{2,1,0:T(8,128)(2,1)S(1)}, u32[]{:S(2)}, u32[]{:S(2)}) async-start(bf16[4,272,384]{2,1,0:T(8,128)(2,1)} %broadcast_in_dim.10), calls=%async_computation | async-start | bytes 1671168 | tf_op jit(solution)/shard_map/all_to_all | solution.py:48
  30.2 3.3 %collective-permute-done = bf16[2,192,384]{2,1,0:T(8,128)(2,1)S(1)} collective-permute-done((bf16[2,192,384]{2,1,0:T(8,128)(2,1)S(1)}, bf16[2,192,384]{2,1,0:T(8,128)(2,1)S(1)}, u32[]{:S(2)}, u32[]{:S(2)}) %collective-permute-start) | collective-permute-done | bytes 294944 | tf_op jit(solution)/shard_map/ppermute | solution.py:40
  36.2 7.0 %collective-permute-done.2 = bf16[272,384]{1,0:T(8,128)(2,1)S(1)} collective-permute-done((bf16[272,384]{1,0:T(8,128)(2,1)S(1)}, bf16[272,384]{1,0:T(8,128)(2,1)S(1)}, u32[]{:S(2)}, u32[]{:S(2)}) %collective-permute-start.2) | collective-permute-done | bytes 208928 | tf_op jit(solution)/shard_map/ppermute | solution.py:40
  47.2 4.3 %all-to-all-start.1 = ((bf16[4,272,640]{2,1,0:T(8,128)(2,1)}), bf16[4,272,640]{2,1,0:T(8,128)(2,1)S(1)}, u32[]{:S(2)}, u32[]{:S(2)}) async-start(bf16[4,272,640]{2,1,0:T(8,128)(2,1)} %fusion.2), calls=%async_computation.1 | async-start | bytes 2785280 | tf_op jit(solution)/shard_map/all_to_all | solution.py:48
  54.4 11.2 %collective-permute-done.3.in_ref = bf16[2,272,384]{2,1,0:T(8,128)(2,1)S(1)} collective-permute-done((bf16[2,272,384]{2,1,0:T(8,128)(2,1)S(1)}, bf16[2,272,384]{2,1,0:T(8,128)(2,1)S(1)}, u32[]{:S(2)}, u32[]{:S(2)}) %collective-permute-start.3) | collective-permute-done | bytes 417824 | tf_op jit(solution)/shard_map/ppermute | solution.py:40
  67.0 3.4 %all-to-all-done.1.far_ref = bf16[4,272,640]{2,1,0:T(8,128)(2,1)S(1)} async-done(((bf16[4,272,640]{2,1,0:T(8,128)(2,1)}), bf16[4,272,640]{2,1,0:T(8,128)(2,1)S(1)}, u32[]{:S(2)}, u32[]{:S(2)}) %all-to-all-start.1) | async-done | bytes 1392672 | tf_op jit(solution)/shard_map/all_to_all | solution.py:48
  70.5 4.4 %all-to-all-start.2 = ((bf16[4,2,272,384]{3,2,1,0:T(8,128)(2,1)}), bf16[4,2,272,384]{3,2,1,0:T(8,128)(2,1)}, u32[]{:S(2)}, u32[]{:S(2)}) async-start(bf16[4,2,272,384]{3,2,1,0:T(8,128)(2,1)} %copy-done.1), calls=%async_computation.2 | async-start | bytes 3342336 | tf_op jit(solution)/shard_map/all_to_all | solution.py:48
  76.9 4.9 %collective-permute-done.4 = bf16[64,1024]{1,0:T(8,128)(2,1)S(1)} collective-permute-done((bf16[64,1024]{1,0:T(8,128)(2,1)S(1)}, bf16[64,1024]{1,0:T(8,128)(2,1)S(1)}, u32[]{:S(2)}, u32[]{:S(2)}) %collective-permute-start.4) | collective-permute-done | bytes 131104 | tf_op jit(solution)/shard_map/ppermute | solution.py:40
  81.9 2.8 %collective-permute-start.5 = (bf16[64,1024]{1,0:T(8,128)(2,1)S(1)}, bf16[64,1024]{1,0:T(8,128)(2,1)}, u32[]{:S(2)}, u32[]{:S(2)}) collective-permute-start(bf16[64,1024]{1,0:T(8,128)(2,1)S(1)} %add_convert_fusion.3), channel_id=1, source_target_pairs={{0,8},{4,12},{8,0},{12,4},{1,9},{5,13},{9,1},{13,5},{2,10},{6,14},... | collective-permute-start | bytes 393224 | tf_op jit(solution)/shard_map/ppermute | solution.py:40
  84.8 6.1 %collective-permute-done.5 = bf16[64,1024]{1,0:T(8,128)(2,1)} collective-permute-done((bf16[64,1024]{1,0:T(8,128)(2,1)S(1)}, bf16[64,1024]{1,0:T(8,128)(2,1)}, u32[]{:S(2)}, u32[]{:S(2)}) %collective-permute-start.5) | collective-permute-done | bytes 131104 | tf_op jit(solution)/shard_map/ppermute | solution.py:40
  92.4 3.6 %all-to-all-done.2.late_ref = bf16[4,2,272,384]{3,2,1,0:T(8,128)(2,1)} async-done(((bf16[4,2,272,384]{3,2,1,0:T(8,128)(2,1)}), bf16[4,2,272,384]{3,2,1,0:T(8,128)(2,1)}, u32[]{:S(2)}, u32[]{:S(2)}) %all-to-all-start.2) | async-done | bytes 1671200 | tf_op jit(solution)/shard_map/all_to_all | solution.py:48
  96.0 5.7 %teacher_norm.1.own_ref = bf16[256,6144]{1,0:T(8,128)(2,1)} custom-call(s32[2]{0:T(128)S(1)} %pad_add_fusion.place, bf16[4,272,384]{2,1,0:T(8,128)(2,1)S(1)} %all-to-all-done.own_ref, bf16[4,272,640]{2,1,0:T(8,128)(2,1)S(1)} %all-to-all-done.1.far_ref, bf16[4,2,272,384]{3,2,1,0:T(8,128)(2,1)} %all-to-all-done.2.late_ref), custom_call_target="tpu_custom_call" | custom-call | flops 1000 | bytes 1000 | tf_op jit(solution)/shard_map/teacher_norm/pallas_call | solution.py:234
  104.6 3.5 %all-to-all-start.3 = ((bf16[4,64,1024]{2,1,0:T(8,128)(2,1)}), bf16[4,64,1024]{2,1,0:T(8,128)(2,1)S(1)}, u32[]{:S(2)}, u32[]{:S(2)}) async-start(bf16[4,64,1024]{2,1,0:T(8,128)(2,1)} %broadcast_in_dim.12), calls=%async_computation.3 | async-start | bytes 1048576 | tf_op jit(solution)/shard_map/all_to_all | solution.py:48
  112.0 7.0 %teacher_heads.1 = f32[2,256,128]{2,1,0:T(8,128)S(1)} custom-call(s32[1]{0:T(128)} %bitcast.10.place, bf16[256,6144]{1,0:T(8,128)(2,1)} %teacher_norm.1.own_ref, bf16[256,6144]{1,0:T(8,128)(2,1)} %collective-permute-done.6.other_ref, bf16[6144,384]{1,0:T(8,128)(2,1)S(1)} %bitcast.63, f32[2,128]{1,0:T(2,128)S(1)} %copy-done.3), custom_call_target="tpu_custom_call" | custom-call | flops 2415919104 | bytes 11000000 | tf_op jit(solution)/shard_map/teacher_heads/pallas_call | solution.py:248
  123.4 5.0 %all-to-all-start.4 = ((f32[16,2,256]{2,1,0:T(2,128)}), f32[16,2,256]{2,1,0:T(2,128)S(1)}, u32[]{:S(2)}, u32[]{:S(2)}) async-start(f32[16,2,256]{2,1,0:T(2,128)} %broadcast_in_dim.13), calls=%async_computation.4 | async-start | bytes 65536 | tf_op jit(solution)/shard_map/all_to_all | solution.py:48
  128.7 7.8 %all-to-all-done.4 = f32[16,2,256]{2,1,0:T(2,128)S(1)} async-done(((f32[16,2,256]{2,1,0:T(2,128)}), f32[16,2,256]{2,1,0:T(2,128)S(1)}, u32[]{:S(2)}, u32[]{:S(2)}) %all-to-all-start.4) | async-done | bytes 32800 | tf_op jit(solution)/shard_map/all_to_all | solution.py:48
  137.0 11.1 %all_to_all.40 = bf16[4,64,1024]{2,1,0:T(8,128)(2,1)S(1)} all-to-all(bf16[4,64,1024]{2,1,0:T(8,128)(2,1)S(1)} %bitcast.64), channel_id=1, replica_groups=mesh['zh'=2,'y'=8,'c'=2,'zl'=4,'x'=4] {'x'}, dimensions={0} | all-to-all | bytes 1048576 | tf_op jit(solution)/shard_map/all_to_all | solution.py:48
  150.4 4.6 %collective-permute-done.8 = bf16[64,1024]{1,0:T(8,128)(2,1)S(1)} collective-permute-done((bf16[64,1024]{1,0:T(8,128)(2,1)S(1)}, bf16[64,1024]{1,0:T(8,128)(2,1)S(1)}, u32[]{:S(2)}, u32[]{:S(2)}) %collective-permute-start.8) | collective-permute-done | bytes 131104 | tf_op jit(solution)/shard_map/ppermute | solution.py:40
  157.7 6.4 %collective-permute-done.9 = bf16[64,1024]{1,0:T(8,128)(2,1)S(1)} collective-permute-done((bf16[64,1024]{1,0:T(8,128)(2,1)S(1)}, bf16[64,1024]{1,0:T(8,128)(2,1)S(1)}, u32[]{:S(2)}, u32[]{:S(2)}) %collective-permute-start.9) | collective-permute-done | bytes 131104 | tf_op jit(solution)/shard_map/ppermute | solution.py:40
  164.9 3.6 %all-to-all-start.6 = ((bf16[4,64,1024]{2,1,0:T(8,128)(2,1)}), bf16[4,64,1024]{2,1,0:T(8,128)(2,1)S(1)}, u32[]{:S(2)}, u32[]{:S(2)}) async-start(bf16[4,64,1024]{2,1,0:T(8,128)(2,1)} %broadcast_in_dim.14), calls=%async_computation.6 | async-start | bytes 1048576 | tf_op jit(solution)/shard_map/all_to_all | solution.py:48
  169.8 6.8 %all-to-all-done.6 = bf16[4,64,1024]{2,1,0:T(8,128)(2,1)S(1)} async-done(((bf16[4,64,1024]{2,1,0:T(8,128)(2,1)}), bf16[4,64,1024]{2,1,0:T(8,128)(2,1)S(1)}, u32[]{:S(2)}, u32[]{:S(2)}) %all-to-all-start.6) | async-done | bytes 524320 | tf_op jit(solution)/shard_map/all_to_all | solution.py:48
  182.7 33.5 %all_to_all.41 = bf16[16,3,32,256]{3,2,1,0:T(8,128)(2,1)S(1)} all-to-all(bf16[16,3,32,256]{3,2,1,0:T(8,128)(2,1)S(1)} %fusion.1), channel_id=1, replica_groups=mesh['zh'=2,'y'=8,'c'=2,'zl'=4,'x'=4] {'zh','y'}, dimensions={0} | all-to-all | bytes 1572864 | tf_op jit(solution)/shard_map/all_to_all | solution.py:48
  (109 shorter events, 43.7 us)
Async XLA Ops:
  7.2 28.7 %copy-start = (bf16[256,1024]{1,0:T(8,128)(2,1)S(1)}, bf16[256,1024]{1,0:T(8,128)(2,1)}, u32[]{:S(2)}) copy-start(bf16[256,1024]{1,0:T(8,128)(2,1)} %param.16) | copy-start | bytes 1572868
  7.2 12.6 %copy-start.12 = (f32[384]{0:T(512)S(1)}, f32[384]{0:T(512)}, u32[]{:S(2)}) copy-start(f32[384]{0:T(512)} %param.10) | copy-start | bytes 4612
  7.2 12.7 %copy-start.11 = (bf16[256,384]{1,0:T(8,128)(2,1)S(1)}, bf16[256,384]{1,0:T(8,128)(2,1)}, u32[]{:S(2)}) copy-start(bf16[256,384]{1,0:T(8,128)(2,1)} %param.9) | copy-start | bytes 589828
  8.9 24.6 %collective-permute-start = (bf16[2,192,384]{2,1,0:T(8,128)(2,1)S(1)}, bf16[2,192,384]{2,1,0:T(8,128)(2,1)S(1)}, u32[]{:S(2)}, u32[]{:S(2)}) collective-permute-start(bf16[2,192,384]{2,1,0:T(8,128)(2,1)S(1)} %reverse_select_fusion), channel_id=1, source_target_pairs={{0,256},{256,0},{1,257},{257,1},{2,258},{258,2},{3,259},{259,3},{4... | collective-permute-start | bytes 884744 | tf_op jit(solution)/shard_map/ppermute | solution.py:40
  19.9 9.8 %copy-start.4 = (bf16[256,1024]{1,0:T(8,128)(2,1)S(1)}, bf16[256,1024]{1,0:T(8,128)(2,1)}, u32[]{:S(2)}) copy-start(bf16[256,1024]{1,0:T(8,128)(2,1)} %param.13) | copy-start | bytes 1572868
  20.1 23.2 %collective-permute-start.2 = (bf16[272,384]{1,0:T(8,128)(2,1)S(1)}, bf16[272,384]{1,0:T(8,128)(2,1)S(1)}, u32[]{:S(2)}, u32[]{:S(2)}) collective-permute-start(bf16[272,384]{1,0:T(8,128)(2,1)S(1)} %concatenate.17), channel_id=1, source_target_pairs={{0,8},{4,12},{8,0},{12,4},{1,9},{5,13},{9,1},{13,5},{2,10},{6,14},... | collective-permute-start | bytes 626696 | tf_op jit(solution)/shard_map/ppermute | solution.py:40
  25.4 17.9 %all-to-all-start = ((bf16[4,272,384]{2,1,0:T(8,128)(2,1)}), bf16[4,272,384]{2,1,0:T(8,128)(2,1)S(1)}, u32[]{:S(2)}, u32[]{:S(2)}) async-start(bf16[4,272,384]{2,1,0:T(8,128)(2,1)} %broadcast_in_dim.10), calls=%async_computation | async-start | bytes 1671168 | tf_op jit(solution)/shard_map/all_to_all | solution.py:48
  29.7 80.0 %all-gather.3.cloned.1.call-start = ((), (), s32[]{:S(2)}) async-start(), calls=%async_computation.8 | async-start | bytes 5308416 | tf_op jit(solution)/shard_map/all_gather | solution.py:222
  33.6 9.7 %collective-permute-start.1 = (bf16[2,192,384]{2,1,0:T(8,128)(2,1)S(1)}, bf16[2,192,384]{2,1,0:T(8,128)(2,1)}, u32[]{:S(2)}, u32[]{:S(2)}) collective-permute-start(bf16[2,192,384]{2,1,0:T(8,128)(2,1)S(1)} %pad_maximum_fusion.3), channel_id=1, source_target_pairs={{0,16},{16,0},{1,17},{17,1},{2,18},{18,2},{3,19},{19,3},{4,20},{20... | collective-permute-start | bytes 884744 | tf_op jit(solution)/shard_map/ppermute | solution.py:40
  47.2 23.3 %all-to-all-start.1 = ((bf16[4,272,640]{2,1,0:T(8,128)(2,1)}), bf16[4,272,640]{2,1,0:T(8,128)(2,1)S(1)}, u32[]{:S(2)}, u32[]{:S(2)}) async-start(bf16[4,272,640]{2,1,0:T(8,128)(2,1)} %fusion.2), calls=%async_computation.1 | async-start | bytes 2785280 | tf_op jit(solution)/shard_map/all_to_all | solution.py:48
  52.5 13.2 %collective-permute-start.3 = (bf16[2,272,384]{2,1,0:T(8,128)(2,1)S(1)}, bf16[2,272,384]{2,1,0:T(8,128)(2,1)S(1)}, u32[]{:S(2)}, u32[]{:S(2)}) collective-permute-start(bf16[2,272,384]{2,1,0:T(8,128)(2,1)S(1)} %pad_maximum_fusion.2), channel_id=1, source_target_pairs={{0,4},{4,0},{8,12},{12,8},{1,5},{5,1},{9,13},{13,9},{2,6},{6,2},{1... | collective-permute-start | bytes 1253384 | tf_op jit(solution)/shard_map/ppermute | solution.py:40
  70.5 25.5 %all-to-all-start.2 = ((bf16[4,2,272,384]{3,2,1,0:T(8,128)(2,1)}), bf16[4,2,272,384]{3,2,1,0:T(8,128)(2,1)}, u32[]{:S(2)}, u32[]{:S(2)}) async-start(bf16[4,2,272,384]{3,2,1,0:T(8,128)(2,1)} %copy-done.1), calls=%async_computation.2 | async-start | bytes 3342336 | tf_op jit(solution)/shard_map/all_to_all | solution.py:48
  75.0 6.9 %collective-permute-start.4 = (bf16[64,1024]{1,0:T(8,128)(2,1)S(1)}, bf16[64,1024]{1,0:T(8,128)(2,1)S(1)}, u32[]{:S(2)}, u32[]{:S(2)}) collective-permute-start(bf16[64,1024]{1,0:T(8,128)(2,1)S(1)} %bitcast.72), channel_id=1, source_target_pairs={{0,4},{4,0},{8,12},{12,8},{1,5},{5,1},{9,13},{13,9},{2,6},{6,2},{1... | collective-permute-start | bytes 393224 | tf_op jit(solution)/shard_map/ppermute | solution.py:40
  81.9 8.9 %collective-permute-start.5 = (bf16[64,1024]{1,0:T(8,128)(2,1)S(1)}, bf16[64,1024]{1,0:T(8,128)(2,1)}, u32[]{:S(2)}, u32[]{:S(2)}) collective-permute-start(bf16[64,1024]{1,0:T(8,128)(2,1)S(1)} %add_convert_fusion.3), channel_id=1, source_target_pairs={{0,8},{4,12},{8,0},{12,4},{1,9},{5,13},{9,1},{13,5},{2,10},{6,14},... | collective-permute-start | bytes 393224 | tf_op jit(solution)/shard_map/ppermute | solution.py:40
  92.4 11.3 %copy-start.9 = (bf16[64,1024]{1,0:T(8,128)(2,1)S(1)}, bf16[64,1024]{1,0:T(8,128)(2,1)}, u32[]{:S(2)}) copy-start(bf16[64,1024]{1,0:T(8,128)(2,1)} %add_convert_fusion.2) | copy-start | bytes 393220
  101.7 8.0 %collective-permute-start.6 = (bf16[256,6144]{1,0:T(8,128)(2,1)}, bf16[256,6144]{1,0:T(8,128)(2,1)}, u32[]{:S(2)}, u32[]{:S(2)}) collective-permute-start(bf16[256,6144]{1,0:T(8,128)(2,1)} %teacher_norm.1.own_ref), channel_id=1, source_target_pairs={{0,16},{16,0},{1,17},{17,1},{2,18},{18,2},{3,19},{19,3},{4,20},{20... | collective-permute-start | bytes 9437192 | tf_op jit(solution)/shard_map/ppermute | solution.py:36
  104.6 16.7 %all-to-all-start.3 = ((bf16[4,64,1024]{2,1,0:T(8,128)(2,1)}), bf16[4,64,1024]{2,1,0:T(8,128)(2,1)S(1)}, u32[]{:S(2)}, u32[]{:S(2)}) async-start(bf16[4,64,1024]{2,1,0:T(8,128)(2,1)} %broadcast_in_dim.12), calls=%async_computation.3 | async-start | bytes 1048576 | tf_op jit(solution)/shard_map/all_to_all | solution.py:48
  119.0 3.4 %collective-permute-start.7 = (f32[256,128]{1,0:T(8,128)S(1)}, f32[256,128]{1,0:T(8,128)S(1)}, u32[]{:S(2)}, u32[]{:S(2)}) collective-permute-start(f32[256,128]{1,0:T(8,128)S(1)} %get-tuple-element.29), channel_id=1, source_target_pairs={{0,16},{16,0},{1,17},{17,1},{2,18},{18,2},{3,19},{19,3},{4,20},{20... | collective-permute-start | bytes 393224 | tf_op jit(solution)/shard_map/ppermute | solution.py:36
  123.4 13.2 %all-to-all-start.4 = ((f32[16,2,256]{2,1,0:T(2,128)}), f32[16,2,256]{2,1,0:T(2,128)S(1)}, u32[]{:S(2)}, u32[]{:S(2)}) async-start(f32[16,2,256]{2,1,0:T(2,128)} %broadcast_in_dim.13), calls=%async_computation.4 | async-start | bytes 65536 | tf_op jit(solution)/shard_map/all_to_all | solution.py:48
  148.2 6.9 %collective-permute-start.8 = (bf16[64,1024]{1,0:T(8,128)(2,1)S(1)}, bf16[64,1024]{1,0:T(8,128)(2,1)S(1)}, u32[]{:S(2)}, u32[]{:S(2)}) collective-permute-start(bf16[64,1024]{1,0:T(8,128)(2,1)S(1)} %reduce_sum.107), channel_id=1, source_target_pairs={{0,4},{4,0},{8,12},{12,8},{1,5},{5,1},{9,13},{13,9},{2,6},{6,2},{1... | collective-permute-start | bytes 393224 | tf_op jit(solution)/shard_map/ppermute | solution.py:40
  155.1 9.0 %collective-permute-start.9 = (bf16[64,1024]{1,0:T(8,128)(2,1)S(1)}, bf16[64,1024]{1,0:T(8,128)(2,1)S(1)}, u32[]{:S(2)}, u32[]{:S(2)}) collective-permute-start(bf16[64,1024]{1,0:T(8,128)(2,1)S(1)} %add_convert_fusion.1), channel_id=1, source_target_pairs={{0,8},{4,12},{8,0},{12,4},{1,9},{5,13},{9,1},{13,5},{2,10},{6,14},... | collective-permute-start | bytes 393224 | tf_op jit(solution)/shard_map/ppermute | solution.py:40
  164.9 11.7 %copy-start.7 = (f32[256,256]{1,0:T(8,128)S(1)}, f32[256,256]{1,0:T(8,128)}, u32[]{:S(2)}) copy-start(f32[256,256]{1,0:T(8,128)} %copy-done.6) | copy-start | bytes 786436
  164.9 11.7 %all-to-all-start.6 = ((bf16[4,64,1024]{2,1,0:T(8,128)(2,1)}), bf16[4,64,1024]{2,1,0:T(8,128)(2,1)S(1)}, u32[]{:S(2)}, u32[]{:S(2)}) async-start(bf16[4,64,1024]{2,1,0:T(8,128)(2,1)} %broadcast_in_dim.14), calls=%async_computation.6 | async-start | bytes 1048576 | tf_op jit(solution)/shard_map/all_to_all | solution.py:48
  178.1 4.2 %collective-permute-start.10 = (bf16[16,3,32,256]{3,2,1,0:T(8,128)(2,1)S(1)}, bf16[16,3,32,256]{3,2,1,0:T(8,128)(2,1)S(1)}, u32[]{:S(2)}, u32[]{:S(2)}) collective-permute-start(bf16[16,3,32,256]{3,2,1,0:T(8,128)(2,1)S(1)} %select_bitcast_fusion), channel_id=1, source_target_pairs={{0,16},{16,0},{1,17},{17,1},{2,18},{18,2},{3,19},{19,3},{4,20},{20... | collective-permute-start | bytes 2359304 | tf_op jit(solution)/shard_map/ppermute | solution.py:40
  (9 other events, 45.0 us)
Sparse Core Ops, SparseCore 0:
  45.5 58.5 all-gather.2
